TPU v7x, 512 devices: a whole 4x8x8 slice. The times are simulated.
512 devices in a mesh: dom: 32 (over x_lo, y, core), blk: 16 (over x_hi, z).
Axes of the slice: x: 4 (x_hi: 2, x_lo: 2; x = x_hi * 2 + x_lo), y: 8, z: 8, core: 2. Of those that a mesh axis runs over, the one named last changes fastest.
Arguments:
- features: bfloat16 [196608, 256], P(('dom', 'blk')), may hold values from -6 to 6
- weight: bfloat16 [256, 256], replicated, may hold values from -0.375 to 0.375
- bias: float32 [256], replicated, may hold values from -3 to 3
- cotangent: bfloat16 [196608, 256], P(('dom', 'blk')), may hold values from -6 to 6
- in_tiles: bfloat16 [32, 16, 16, 4, 128, 128], P('dom', 'blk'), may hold values from -0.125 to 0.125
- in_pos: int32 [32, 16, 16, 4], P('dom', 'blk'), may hold values from 0 to 8, as said below
- in_count: int32 [32, 16, 16], P('dom', 'blk'), may hold values from 1 to 4, as said below
- cut_tiles: bfloat16 [32, 16, 32, 128, 128], P('dom', 'blk'), may hold values from -0.125 to 0.125
- send_blk: int32 [32, 16, 32], P('dom', 'blk'), may hold values from 0 to 2
- send_live: int32 [32, 16, 32], P('dom', 'blk'), may hold values from 0 to 1, as said below
- recv_dst: int32 [32, 16, 32], P('dom', 'blk'), may hold values from 0 to 2
Outputs:
- hidden: bfloat16 [196608, 256], P(('dom', 'blk'))
- grad_features: bfloat16 [196608, 256], P(('dom', 'blk'))
Inputs may be any that keep to these rules, and one draw needn't show every extreme that they name: The first in_count[p, b, c] entries of in_pos[p, b, c] are distinct; later slots, and their tiles, are ignored. in_count[p, b, b] = 4. send_live[p, b, p] = 0 and send_live[p, b, q] = 1 for q = (p + 1) modulo the number of parts. Where it is 0 the slot's cut tile, send_blk and recv_dst are ignored.
All inputs are finite; a program needn't handle non-finite values.
Results may differ from a plain program's by a relative error of at most 0.007.
Values may be sent and summed in bfloat16 or wider, within the bound.
No kernel may reach another device: no remote copies, remote signals or barrier semaphores. Data moves between devices by JAX's collectives and lax.ppermute only.
A program may use at most 64 MiB of HBM per device.

v0:
```python
import jax
import jax.numpy as jnp
from jax import lax
from jax.sharding import PartitionSpec as P


def passed_along(value, axis, by):
    peers = lax.axis_size(axis)
    return lax.ppermute(value, axis, [(i, (i + by) % peers) for i in range(peers)])


def silu_parts(preact):
    sigmoid = 1.0 / (1.0 + jnp.exp(-preact))
    return (preact * sigmoid, sigmoid * (1.0 + preact * (1.0 - sigmoid)))


def spread_rows(onehot, products):
    return jnp.einsum("kr,kxf->rxf", onehot, products, precision=lax.Precision.HIGHEST)


def on_device(
    features,
    weight,
    bias,
    cotangent,
    in_tiles,
    in_pos,
    in_count,
    cut_tiles,
    send_blk,
    send_live,
    recv_dst,
):
    rows_dev, feat_width = features.shape
    tile_size = in_tiles.shape[-1]
    block_count = rows_dev // tile_size
    loop_size = lax.axis_size("blk")
    self_index = lax.axis_index("blk")
    tiles_all = in_tiles[0, 0]
    positions = in_pos[0, 0]
    live_counts = in_count[0, 0]
    block_ids = jnp.arange(block_count, dtype=jnp.int32)
    slot_ids = jnp.arange(tiles_all.shape[1], dtype=jnp.int32)
    slot_live = slot_ids[None, :] < live_counts[:, None]
    target_index = positions // block_count
    source_index = positions % block_count
    target_onehot = ((target_index[..., None] == block_ids) & slot_live[..., None]).astype(
        jnp.float32
    )
    source_onehot = ((source_index[..., None] == block_ids) & slot_live[..., None]).astype(
        jnp.float32
    )

    def forward_term(source_blocks, source):
        source_rows = source_blocks[source_index[source]]
        products = jnp.einsum(
            "kxy,kyf->kxf", tiles_all[source], source_rows, preferred_element_type=jnp.float32
        )
        return spread_rows(target_onehot[source], products)

    def backward_term(grad_blocks, source):
        target_rows = grad_blocks[target_index[source]]
        products = jnp.einsum(
            "kxy,kxf->kyf", tiles_all[source], target_rows, preferred_element_type=jnp.float32
        )
        return spread_rows(source_onehot[source], products)

    projected = jnp.dot(features, weight, preferred_element_type=jnp.float32).astype(jnp.bfloat16)
    proj_blocks = projected.reshape(block_count, tile_size, feat_width)
    zero_sum = jnp.zeros((block_count, tile_size, feat_width), jnp.float32)

    def single_step(step_index, carried):
        moving, running = carried
        running = running + forward_term(moving, (self_index - step_index) % loop_size)
        moving = passed_along(moving, "blk", 1)
        return (moving, running)

    moving, running = lax.fori_loop(0, loop_size - 1, single_step, (proj_blocks, zero_sum))
    intra_sum = running + forward_term(moving, (self_index - loop_size + 1) % loop_size)
    cut_live = send_live[0, 0] > 0
    outgoing = jnp.where(
        cut_live[:, None, None], proj_blocks[send_blk[0, 0]], jnp.zeros((), jnp.bfloat16)
    )
    incoming = lax.all_to_all(outgoing, "dom", split_axis=0, concat_axis=0, tiled=True)
    recv_onehot = (recv_dst[0, 0][:, None] == block_ids).astype(jnp.float32)
    cross_terms = jnp.einsum(
        "pxy,pyf->pxf", cut_tiles[0, 0], incoming, preferred_element_type=jnp.float32
    )
    aggregate = (intra_sum + spread_rows(recv_onehot, cross_terms)).reshape(rows_dev, feat_width)
    activated, derivative = silu_parts(aggregate + bias)
    hidden = activated.astype(jnp.bfloat16)
    grad_pre = (cotangent.astype(jnp.float32) * derivative).astype(jnp.bfloat16)
    grad_blocks = grad_pre.reshape(block_count, tile_size, feat_width)

    def carry_step(step_index, running):
        running = running + backward_term(grad_blocks, (self_index - 1 - step_index) % loop_size)
        return passed_along(running, "blk", 1)

    running = lax.fori_loop(0, loop_size - 1, carry_step, zero_sum)
    intra_back = running + backward_term(grad_blocks, self_index)
    far_rows = grad_blocks[recv_dst[0, 0]]
    returned = jnp.einsum(
        "pxy,pxf->pyf", cut_tiles[0, 0], far_rows, preferred_element_type=jnp.float32
    ).astype(jnp.bfloat16)
    arrived_back = lax.all_to_all(returned, "dom", split_axis=0, concat_axis=0, tiled=True)
    arrived = lax.optimization_barrier(arrived_back).astype(jnp.float32)
    send_onehot = ((send_blk[0, 0][:, None] == block_ids) & cut_live[:, None]).astype(jnp.float32)
    back_sum = intra_back + spread_rows(send_onehot, arrived)
    back_rows = back_sum.reshape(rows_dev, feat_width).astype(jnp.bfloat16)
    grad_features = jnp.dot(back_rows, weight.T, preferred_element_type=jnp.float32).astype(
        jnp.bfloat16
    )
    return (hidden, grad_features)


def solution(mesh):
    in_specs = (
        P(("dom", "blk"), None),
        P(),
        P(),
        P(("dom", "blk"), None),
        P("dom", "blk", None, None, None, None),
        P("dom", "blk", None, None),
        P("dom", "blk", None),
        P("dom", "blk", None, None, None),
        P("dom", "blk", None),
        P("dom", "blk", None),
        P("dom", "blk", None),
    )
    out_specs = (P(("dom", "blk"), None), P(("dom", "blk"), None))
    return jax.shard_map(
        on_device, mesh=mesh, in_specs=in_specs, out_specs=out_specs, check_vma=False
    )
```

profile of v0, /device:TPU:12, one launch (start us, length us, event | category | flops | bytes accessed | tf_op | source)
XLA Modules:
  0.0 584.7 jit_solution(6647476878674387367)
XLA Ops:
  2.6 2.0 gather_fusion.3
  4.6 4.1 copy.59
  8.7 3.1 broadcast_select_fusion
  11.9 8.5 %all-to-all-start = ((bf16[32,128,256]{1,2,0:T(8,128)(2,1)}), bf16[32,128,256]{1,2,0:T(8,128)(2,1)}, u32[]{:S(2)}, u32[]{:S(2)}) async-start(bf16[32,128,256]{1,2,0:T(8,128)(2,1)} %broadcast_select_fusion), calls=%async_computation | async-start | bytes 4194304 | tf_op jit(solution)/shard_map/all_to_all | solution.py:84
  21.2 183.0 %while.34 = (s32[]{:T(128)}, bf16[3,128,256]{2,1,0:T(8,128)(2,1)S(1)}, f32[3,128,256]{2,0,1:T(4,128)S(1)}, s32[]{:T(128)}, f32[16,4,3]{2,1,0:T(4,128)S(1)}, /*in...) while((s32[]{:T(128)}, ...), condition=%wide.region_1.2_spmd.clone, body=%wide.region_0.1_spmd.clone.sunk | while | flops 38470684 | bytes 4069766 | solution.py:78
  21.2 4.3 collective-permute-start.1
  29.0 9.2 %collective-permute-done.1 = bf16[3,128,256]{2,1,0:T(8,128)(2,1)S(1)} collective-permute-done((bf16[3,128,256]{2,1,0:T(8,128)(2,1)S(1)}, bf16[3,128,256]{2,1,0:T(8,128)(2,1)S(1)}, u32[]{:S(2)}, u32[]{:S(2)}) %collective-permute-start.1) | collective-permute-done | bytes 196640 | tf_op jit(solution)/shard_map/while/body/eval_jaxpr/ppermute | solution.py:9
  38.2 1.9 collective-permute-start.1
  43.7 7.5 %collective-permute-done.1 = bf16[3,128,256]{2,1,0:T(8,128)(2,1)S(1)} collective-permute-done((bf16[3,128,256]{2,1,0:T(8,128)(2,1)S(1)}, bf16[3,128,256]{2,1,0:T(8,128)(2,1)S(1)}, u32[]{:S(2)}, u32[]{:S(2)}) %collective-permute-start.1) | collective-permute-done | bytes 196640 | tf_op jit(solution)/shard_map/while/body/eval_jaxpr/ppermute | solution.py:9
  51.2 1.9 collective-permute-start.1
  56.6 9.0 %collective-permute-done.1 = bf16[3,128,256]{2,1,0:T(8,128)(2,1)S(1)} collective-permute-done((bf16[3,128,256]{2,1,0:T(8,128)(2,1)S(1)}, bf16[3,128,256]{2,1,0:T(8,128)(2,1)S(1)}, u32[]{:S(2)}, u32[]{:S(2)}) %collective-permute-start.1) | collective-permute-done | bytes 196640 | tf_op jit(solution)/shard_map/while/body/eval_jaxpr/ppermute | solution.py:9
  65.7 1.9 collective-permute-start.1
  71.1 5.7 collective-permute-done.1
  76.9 1.9 collective-permute-start.1
  82.3 5.7 collective-permute-done.1
  88.1 1.9 collective-permute-start.1
  93.5 5.7 collective-permute-done.1
  99.3 1.9 collective-permute-start.1
  104.7 6.1 %collective-permute-done.1 = bf16[3,128,256]{2,1,0:T(8,128)(2,1)S(1)} collective-permute-done((bf16[3,128,256]{2,1,0:T(8,128)(2,1)S(1)}, bf16[3,128,256]{2,1,0:T(8,128)(2,1)S(1)}, u32[]{:S(2)}, u32[]{:S(2)}) %collective-permute-start.1) | collective-permute-done | bytes 196640 | tf_op jit(solution)/shard_map/while/body/eval_jaxpr/ppermute | solution.py:9
  110.8 1.9 collective-permute-start.1
  116.2 7.3 %collective-permute-done.1 = bf16[3,128,256]{2,1,0:T(8,128)(2,1)S(1)} collective-permute-done((bf16[3,128,256]{2,1,0:T(8,128)(2,1)S(1)}, bf16[3,128,256]{2,1,0:T(8,128)(2,1)S(1)}, u32[]{:S(2)}, u32[]{:S(2)}) %collective-permute-start.1) | collective-permute-done | bytes 196640 | tf_op jit(solution)/shard_map/while/body/eval_jaxpr/ppermute | solution.py:9
  123.5 1.9 collective-permute-start.1
  128.9 7.3 %collective-permute-done.1 = bf16[3,128,256]{2,1,0:T(8,128)(2,1)S(1)} collective-permute-done((bf16[3,128,256]{2,1,0:T(8,128)(2,1)S(1)}, bf16[3,128,256]{2,1,0:T(8,128)(2,1)S(1)}, u32[]{:S(2)}, u32[]{:S(2)}) %collective-permute-start.1) | collective-permute-done | bytes 196640 | tf_op jit(solution)/shard_map/while/body/eval_jaxpr/ppermute | solution.py:9
  136.2 1.9 collective-permute-start.1
  141.7 6.5 %collective-permute-done.1 = bf16[3,128,256]{2,1,0:T(8,128)(2,1)S(1)} collective-permute-done((bf16[3,128,256]{2,1,0:T(8,128)(2,1)S(1)}, bf16[3,128,256]{2,1,0:T(8,128)(2,1)S(1)}, u32[]{:S(2)}, u32[]{:S(2)}) %collective-permute-start.1) | collective-permute-done | bytes 196640 | tf_op jit(solution)/shard_map/while/body/eval_jaxpr/ppermute | solution.py:9
  148.2 1.9 collective-permute-start.1
  153.6 5.7 collective-permute-done.1
  159.4 1.9 collective-permute-start.1
  164.8 5.7 collective-permute-done.1
  170.6 1.9 collective-permute-start.1
  176.0 5.7 collective-permute-done.1
  187.2 5.7 collective-permute-done.1
  193.0 1.9 collective-permute-start.1
  198.4 5.7 collective-permute-done.1
  205.9 4.3 convolution_bitcast_fusion
  210.2 5.5 copy.60
  215.7 3.6 fusion.40
  222.0 2.1 convert_bitcast_fusion
  224.1 4.1 copy.69
  228.2 11.1 %all-to-all-start.1 = ((bf16[32,128,256]{2,1,0:T(8,128)(2,1)}), bf16[32,128,256]{2,1,0:T(8,128)(2,1)S(1)}, u32[]{:S(2)}, u32[]{:S(2)}) async-start(bf16[32,128,256]{2,1,0:T(8,128)(2,1)} %copy.69), calls=%async_computation.1 | async-start | bytes 4194304 | tf_op jit(solution)/shard_map/all_to_all | solution.py:105
  240.5 2.1 fusion.29
  242.6 48.1 %all-to-all-done.1 = bf16[32,128,256]{2,1,0:T(8,128)(2,1)S(1)} async-done(((bf16[32,128,256]{2,1,0:T(8,128)(2,1)}), bf16[32,128,256]{2,1,0:T(8,128)(2,1)S(1)}, u32[]{:S(2)}, u32[]{:S(2)}) %all-to-all-start.1) | async-done | bytes 2097184 | tf_op jit(solution)/shard_map/all_to_all | solution.py:105
  290.7 2.1 fusion.20
  292.9 289.8 %while.33 = (s32[]{:T(128)}, f32[3,128,256]{2,0,1:T(4,128)S(1)}, s32[]{:T(128)}, f32[16,4,3]{2,1,0:T(4,128)S(1)}, bf16[16,4,128,128]{3,2,1,0:T(8,128)(2,1)}, /*i...) while((s32[]{:T(128)}, f32[3,128,256]{2,0,1:T(4,128)S(1)}, ...), condition=%wide.region_3.4_spmd, body=%wide.region_2.3_spmd.sunk | while | flops 38372380 | bytes 4462972 | solution.py:99
  298.1 17.0 %collective-permute-done = f32[3,128,256]{2,0,1:T(4,128)S(1)} collective-permute-done((f32[3,128,256]{2,0,1:T(4,128)S(1)}, f32[3,128,256]{2,0,1:T(4,128)S(1)}, u32[]{:S(2)}, u32[]{:S(2)}) %collective-permute-start) | collective-permute-done | bytes 393248 | tf_op jit(solution)/shard_map/while/body/eval_jaxpr/ppermute | solution.py:9
  320.3 16.1 %collective-permute-done = f32[3,128,256]{2,0,1:T(4,128)S(1)} collective-permute-done((f32[3,128,256]{2,0,1:T(4,128)S(1)}, f32[3,128,256]{2,0,1:T(4,128)S(1)}, u32[]{:S(2)}, u32[]{:S(2)}) %collective-permute-start) | collective-permute-done | bytes 393248 | tf_op jit(solution)/shard_map/while/body/eval_jaxpr/ppermute | solution.py:9
  339.7 1.9 collective-permute-start
  341.7 15.2 %collective-permute-done = f32[3,128,256]{2,0,1:T(4,128)S(1)} collective-permute-done((f32[3,128,256]{2,0,1:T(4,128)S(1)}, f32[3,128,256]{2,0,1:T(4,128)S(1)}, u32[]{:S(2)}, u32[]{:S(2)}) %collective-permute-start) | collective-permute-done | bytes 393248 | tf_op jit(solution)/shard_map/while/body/eval_jaxpr/ppermute | solution.py:9
  362.1 14.3 %collective-permute-done = f32[3,128,256]{2,0,1:T(4,128)S(1)} collective-permute-done((f32[3,128,256]{2,0,1:T(4,128)S(1)}, f32[3,128,256]{2,0,1:T(4,128)S(1)}, u32[]{:S(2)}, u32[]{:S(2)}) %collective-permute-start) | collective-permute-done | bytes 393248 | tf_op jit(solution)/shard_map/while/body/eval_jaxpr/ppermute | solution.py:9
  379.6 1.9 collective-permute-start
  381.6 13.4 %collective-permute-done = f32[3,128,256]{2,0,1:T(4,128)S(1)} collective-permute-done((f32[3,128,256]{2,0,1:T(4,128)S(1)}, f32[3,128,256]{2,0,1:T(4,128)S(1)}, u32[]{:S(2)}, u32[]{:S(2)}) %collective-permute-start) | collective-permute-done | bytes 393248 | tf_op jit(solution)/shard_map/while/body/eval_jaxpr/ppermute | solution.py:9
  398.2 1.9 collective-permute-start
  400.1 12.8 %collective-permute-done = f32[3,128,256]{2,0,1:T(4,128)S(1)} collective-permute-done((f32[3,128,256]{2,0,1:T(4,128)S(1)}, f32[3,128,256]{2,0,1:T(4,128)S(1)}, u32[]{:S(2)}, u32[]{:S(2)}) %collective-permute-start) | collective-permute-done | bytes 393248 | tf_op jit(solution)/shard_map/while/body/eval_jaxpr/ppermute | solution.py:9
  416.1 1.9 collective-permute-start
  418.1 12.8 %collective-permute-done = f32[3,128,256]{2,0,1:T(4,128)S(1)} collective-permute-done((f32[3,128,256]{2,0,1:T(4,128)S(1)}, f32[3,128,256]{2,0,1:T(4,128)S(1)}, u32[]{:S(2)}, u32[]{:S(2)}) %collective-permute-start) | collective-permute-done | bytes 393248 | tf_op jit(solution)/shard_map/while/body/eval_jaxpr/ppermute | solution.py:9
  436.0 12.8 %collective-permute-done = f32[3,128,256]{2,0,1:T(4,128)S(1)} collective-permute-done((f32[3,128,256]{2,0,1:T(4,128)S(1)}, f32[3,128,256]{2,0,1:T(4,128)S(1)}, u32[]{:S(2)}, u32[]{:S(2)}) %collective-permute-start) | collective-permute-done | bytes 393248 | tf_op jit(solution)/shard_map/while/body/eval_jaxpr/ppermute | solution.py:9
  453.9 12.8 %collective-permute-done = f32[3,128,256]{2,0,1:T(4,128)S(1)} collective-permute-done((f32[3,128,256]{2,0,1:T(4,128)S(1)}, f32[3,128,256]{2,0,1:T(4,128)S(1)}, u32[]{:S(2)}, u32[]{:S(2)}) %collective-permute-start) | collective-permute-done | bytes 393248 | tf_op jit(solution)/shard_map/while/body/eval_jaxpr/ppermute | solution.py:9
  470.0 1.9 collective-permute-start
  471.9 12.8 %collective-permute-done = f32[3,128,256]{2,0,1:T(4,128)S(1)} collective-permute-done((f32[3,128,256]{2,0,1:T(4,128)S(1)}, f32[3,128,256]{2,0,1:T(4,128)S(1)}, u32[]{:S(2)}, u32[]{:S(2)}) %collective-permute-start) | collective-permute-done | bytes 393248 | tf_op jit(solution)/shard_map/while/body/eval_jaxpr/ppermute | solution.py:9
  489.9 13.2 %collective-permute-done = f32[3,128,256]{2,0,1:T(4,128)S(1)} collective-permute-done((f32[3,128,256]{2,0,1:T(4,128)S(1)}, f32[3,128,256]{2,0,1:T(4,128)S(1)}, u32[]{:S(2)}, u32[]{:S(2)}) %collective-permute-start) | collective-permute-done | bytes 393248 | tf_op jit(solution)/shard_map/while/body/eval_jaxpr/ppermute | solution.py:9
  508.2 14.3 %collective-permute-done = f32[3,128,256]{2,0,1:T(4,128)S(1)} collective-permute-done((f32[3,128,256]{2,0,1:T(4,128)S(1)}, f32[3,128,256]{2,0,1:T(4,128)S(1)}, u32[]{:S(2)}, u32[]{:S(2)}) %collective-permute-start) | collective-permute-done | bytes 393248 | tf_op jit(solution)/shard_map/while/body/eval_jaxpr/ppermute | solution.py:9
  527.7 15.4 %collective-permute-done = f32[3,128,256]{2,0,1:T(4,128)S(1)} collective-permute-done((f32[3,128,256]{2,0,1:T(4,128)S(1)}, f32[3,128,256]{2,0,1:T(4,128)S(1)}, u32[]{:S(2)}, u32[]{:S(2)}) %collective-permute-start) | collective-permute-done | bytes 393248 | tf_op jit(solution)/shard_map/while/body/eval_jaxpr/ppermute | solution.py:9
  548.3 16.4 %collective-permute-done = f32[3,128,256]{2,0,1:T(4,128)S(1)} collective-permute-done((f32[3,128,256]{2,0,1:T(4,128)S(1)}, f32[3,128,256]{2,0,1:T(4,128)S(1)}, u32[]{:S(2)}, u32[]{:S(2)}) %collective-permute-start) | collective-permute-done | bytes 393248 | tf_op jit(solution)/shard_map/while/body/eval_jaxpr/ppermute | solution.py:9
  569.9 12.8 %collective-permute-done = f32[3,128,256]{2,0,1:T(4,128)S(1)} collective-permute-done((f32[3,128,256]{2,0,1:T(4,128)S(1)}, f32[3,128,256]{2,0,1:T(4,128)S(1)}, u32[]{:S(2)}, u32[]{:S(2)}) %collective-permute-start) | collective-permute-done | bytes 393248 | tf_op jit(solution)/shard_map/while/body/eval_jaxpr/ppermute | solution.py:9
  (226 shorter events, 132.0 us)
Async XLA Ops:
  0.6 205.3 %copy-start = (bf16[1,1,32,128,128]{4,3,2,1,0:T(8,128)(2,1)S(1)}, bf16[1,1,32,128,128]{4,3,2,1,0:T(8,128)(2,1)}, u32[]{:S(2)}) copy-start(bf16[1,1,32,128,128]{4,3,2,1,0:T(8,128)(2,1)} %param.22) | copy-start | bytes 3145732
  4.6 4.1 copy-start.10
  11.9 8.6 %copy-start.9 = (s32[1,1,16]{2,1,0:T(1,128)S(1)}, s32[1,1,16]{2,1,0:T(1,128)}, u32[]{:S(2)}) copy-start(s32[1,1,16]{2,1,0:T(1,128)} %param.21) | copy-start | bytes 196
  11.9 8.7 %copy-start.7 = (s32[1,1,16,4]{2,3,1,0:T(4,128)S(1)}, s32[1,1,16,4]{2,3,1,0:T(4,128)}, u32[]{:S(2)}) copy-start(s32[1,1,16,4]{2,3,1,0:T(4,128)} %param.20) | copy-start | bytes 772
  11.9 194.0 %all-to-all-start = ((bf16[32,128,256]{1,2,0:T(8,128)(2,1)}), bf16[32,128,256]{1,2,0:T(8,128)(2,1)}, u32[]{:S(2)}, u32[]{:S(2)}) async-start(bf16[32,128,256]{1,2,0:T(8,128)(2,1)} %broadcast_select_fusion), calls=%async_computation | async-start | bytes 4194304 | tf_op jit(solution)/shard_map/all_to_all | solution.py:84
  21.2 17.0 %collective-permute-start.1 = (bf16[3,128,256]{2,1,0:T(8,128)(2,1)S(1)}, bf16[3,128,256]{2,1,0:T(8,128)(2,1)S(1)}, u32[]{:S(2)}, u32[]{:S(2)}) collective-permute-start(bf16[3,128,256]{2,1,0:T(8,128)(2,1)S(1)} %copy.100), channel_id=1, source_target_pairs={{0,1},{1,2},{2,3},{3,4},{4,5},{5,6},{6,7},{7,8},{8,9},{9,10},{10,1... | collective-permute-start | bytes 589832 | tf_op jit(solution)/shard_map/while/body/eval_jaxpr/ppermute | solution.py:9
  38.2 13.0 %collective-permute-start.1 = (bf16[3,128,256]{2,1,0:T(8,128)(2,1)S(1)}, bf16[3,128,256]{2,1,0:T(8,128)(2,1)S(1)}, u32[]{:S(2)}, u32[]{:S(2)}) collective-permute-start(bf16[3,128,256]{2,1,0:T(8,128)(2,1)S(1)} %copy.100), channel_id=1, source_target_pairs={{0,1},{1,2},{2,3},{3,4},{4,5},{5,6},{6,7},{7,8},{8,9},{9,10},{10,1... | collective-permute-start | bytes 589832 | tf_op jit(solution)/shard_map/while/body/eval_jaxpr/ppermute | solution.py:9
  51.2 14.4 %collective-permute-start.1 = (bf16[3,128,256]{2,1,0:T(8,128)(2,1)S(1)}, bf16[3,128,256]{2,1,0:T(8,128)(2,1)S(1)}, u32[]{:S(2)}, u32[]{:S(2)}) collective-permute-start(bf16[3,128,256]{2,1,0:T(8,128)(2,1)S(1)} %copy.100), channel_id=1, source_target_pairs={{0,1},{1,2},{2,3},{3,4},{4,5},{5,6},{6,7},{7,8},{8,9},{9,10},{10,1... | collective-permute-start | bytes 589832 | tf_op jit(solution)/shard_map/while/body/eval_jaxpr/ppermute | solution.py:9
  65.7 11.2 %collective-permute-start.1 = (bf16[3,128,256]{2,1,0:T(8,128)(2,1)S(1)}, bf16[3,128,256]{2,1,0:T(8,128)(2,1)S(1)}, u32[]{:S(2)}, u32[]{:S(2)}) collective-permute-start(bf16[3,128,256]{2,1,0:T(8,128)(2,1)S(1)} %copy.100), channel_id=1, source_target_pairs={{0,1},{1,2},{2,3},{3,4},{4,5},{5,6},{6,7},{7,8},{8,9},{9,10},{10,1... | collective-permute-start | bytes 589832 | tf_op jit(solution)/shard_map/while/body/eval_jaxpr/ppermute | solution.py:9
  76.9 11.2 %collective-permute-start.1 = (bf16[3,128,256]{2,1,0:T(8,128)(2,1)S(1)}, bf16[3,128,256]{2,1,0:T(8,128)(2,1)S(1)}, u32[]{:S(2)}, u32[]{:S(2)}) collective-permute-start(bf16[3,128,256]{2,1,0:T(8,128)(2,1)S(1)} %copy.100), channel_id=1, source_target_pairs={{0,1},{1,2},{2,3},{3,4},{4,5},{5,6},{6,7},{7,8},{8,9},{9,10},{10,1... | collective-permute-start | bytes 589832 | tf_op jit(solution)/shard_map/while/body/eval_jaxpr/ppermute | solution.py:9
  88.1 11.2 %collective-permute-start.1 = (bf16[3,128,256]{2,1,0:T(8,128)(2,1)S(1)}, bf16[3,128,256]{2,1,0:T(8,128)(2,1)S(1)}, u32[]{:S(2)}, u32[]{:S(2)}) collective-permute-start(bf16[3,128,256]{2,1,0:T(8,128)(2,1)S(1)} %copy.100), channel_id=1, source_target_pairs={{0,1},{1,2},{2,3},{3,4},{4,5},{5,6},{6,7},{7,8},{8,9},{9,10},{10,1... | collective-permute-start | bytes 589832 | tf_op jit(solution)/shard_map/while/body/eval_jaxpr/ppermute | solution.py:9
  99.3 11.5 %collective-permute-start.1 = (bf16[3,128,256]{2,1,0:T(8,128)(2,1)S(1)}, bf16[3,128,256]{2,1,0:T(8,128)(2,1)S(1)}, u32[]{:S(2)}, u32[]{:S(2)}) collective-permute-start(bf16[3,128,256]{2,1,0:T(8,128)(2,1)S(1)} %copy.100), channel_id=1, source_target_pairs={{0,1},{1,2},{2,3},{3,4},{4,5},{5,6},{6,7},{7,8},{8,9},{9,10},{10,1... | collective-permute-start | bytes 589832 | tf_op jit(solution)/shard_map/while/body/eval_jaxpr/ppermute | solution.py:9
  110.8 12.7 %collective-permute-start.1 = (bf16[3,128,256]{2,1,0:T(8,128)(2,1)S(1)}, bf16[3,128,256]{2,1,0:T(8,128)(2,1)S(1)}, u32[]{:S(2)}, u32[]{:S(2)}) collective-permute-start(bf16[3,128,256]{2,1,0:T(8,128)(2,1)S(1)} %copy.100), channel_id=1, source_target_pairs={{0,1},{1,2},{2,3},{3,4},{4,5},{5,6},{6,7},{7,8},{8,9},{9,10},{10,1... | collective-permute-start | bytes 589832 | tf_op jit(solution)/shard_map/while/body/eval_jaxpr/ppermute | solution.py:9
  123.5 12.8 %collective-permute-start.1 = (bf16[3,128,256]{2,1,0:T(8,128)(2,1)S(1)}, bf16[3,128,256]{2,1,0:T(8,128)(2,1)S(1)}, u32[]{:S(2)}, u32[]{:S(2)}) collective-permute-start(bf16[3,128,256]{2,1,0:T(8,128)(2,1)S(1)} %copy.100), channel_id=1, source_target_pairs={{0,1},{1,2},{2,3},{3,4},{4,5},{5,6},{6,7},{7,8},{8,9},{9,10},{10,1... | collective-permute-start | bytes 589832 | tf_op jit(solution)/shard_map/while/body/eval_jaxpr/ppermute | solution.py:9
  136.2 12.0 %collective-permute-start.1 = (bf16[3,128,256]{2,1,0:T(8,128)(2,1)S(1)}, bf16[3,128,256]{2,1,0:T(8,128)(2,1)S(1)}, u32[]{:S(2)}, u32[]{:S(2)}) collective-permute-start(bf16[3,128,256]{2,1,0:T(8,128)(2,1)S(1)} %copy.100), channel_id=1, source_target_pairs={{0,1},{1,2},{2,3},{3,4},{4,5},{5,6},{6,7},{7,8},{8,9},{9,10},{10,1... | collective-permute-start | bytes 589832 | tf_op jit(solution)/shard_map/while/body/eval_jaxpr/ppermute | solution.py:9
  148.2 11.2 %collective-permute-start.1 = (bf16[3,128,256]{2,1,0:T(8,128)(2,1)S(1)}, bf16[3,128,256]{2,1,0:T(8,128)(2,1)S(1)}, u32[]{:S(2)}, u32[]{:S(2)}) collective-permute-start(bf16[3,128,256]{2,1,0:T(8,128)(2,1)S(1)} %copy.100), channel_id=1, source_target_pairs={{0,1},{1,2},{2,3},{3,4},{4,5},{5,6},{6,7},{7,8},{8,9},{9,10},{10,1... | collective-permute-start | bytes 589832 | tf_op jit(solution)/shard_map/while/body/eval_jaxpr/ppermute | solution.py:9
  159.4 11.2 %collective-permute-start.1 = (bf16[3,128,256]{2,1,0:T(8,128)(2,1)S(1)}, bf16[3,128,256]{2,1,0:T(8,128)(2,1)S(1)}, u32[]{:S(2)}, u32[]{:S(2)}) collective-permute-start(bf16[3,128,256]{2,1,0:T(8,128)(2,1)S(1)} %copy.100), channel_id=1, source_target_pairs={{0,1},{1,2},{2,3},{3,4},{4,5},{5,6},{6,7},{7,8},{8,9},{9,10},{10,1... | collective-permute-start | bytes 589832 | tf_op jit(solution)/shard_map/while/body/eval_jaxpr/ppermute | solution.py:9
  170.6 11.2 %collective-permute-start.1 = (bf16[3,128,256]{2,1,0:T(8,128)(2,1)S(1)}, bf16[3,128,256]{2,1,0:T(8,128)(2,1)S(1)}, u32[]{:S(2)}, u32[]{:S(2)}) collective-permute-start(bf16[3,128,256]{2,1,0:T(8,128)(2,1)S(1)} %copy.100), channel_id=1, source_target_pairs={{0,1},{1,2},{2,3},{3,4},{4,5},{5,6},{6,7},{7,8},{8,9},{9,10},{10,1... | collective-permute-start | bytes 589832 | tf_op jit(solution)/shard_map/while/body/eval_jaxpr/ppermute | solution.py:9
  181.8 11.2 %collective-permute-start.1 = (bf16[3,128,256]{2,1,0:T(8,128)(2,1)S(1)}, bf16[3,128,256]{2,1,0:T(8,128)(2,1)S(1)}, u32[]{:S(2)}, u32[]{:S(2)}) collective-permute-start(bf16[3,128,256]{2,1,0:T(8,128)(2,1)S(1)} %copy.100), channel_id=1, source_target_pairs={{0,1},{1,2},{2,3},{3,4},{4,5},{5,6},{6,7},{7,8},{8,9},{9,10},{10,1... | collective-permute-start | bytes 589832 | tf_op jit(solution)/shard_map/while/body/eval_jaxpr/ppermute | solution.py:9
  193.0 11.2 %collective-permute-start.1 = (bf16[3,128,256]{2,1,0:T(8,128)(2,1)S(1)}, bf16[3,128,256]{2,1,0:T(8,128)(2,1)S(1)}, u32[]{:S(2)}, u32[]{:S(2)}) collective-permute-start(bf16[3,128,256]{2,1,0:T(8,128)(2,1)S(1)} %copy.100), channel_id=1, source_target_pairs={{0,1},{1,2},{2,3},{3,4},{4,5},{5,6},{6,7},{7,8},{8,9},{9,10},{10,1... | collective-permute-start | bytes 589832 | tf_op jit(solution)/shard_map/while/body/eval_jaxpr/ppermute | solution.py:9
  210.2 5.5 copy-start.5
  219.3 1.2 copy-start.4
  219.3 1.2 copy-start.8
  228.2 62.5 %copy-start.6 = (s32[1,1,32]{2,1,0:T(1,128)S(1)}, s32[1,1,32]{2,1,0:T(1,128)}, u32[]{:S(2)}) copy-start(s32[1,1,32]{2,1,0:T(1,128)} %param.23) | copy-start | bytes 388
  228.2 62.5 %all-to-all-start.1 = ((bf16[32,128,256]{2,1,0:T(8,128)(2,1)}), bf16[32,128,256]{2,1,0:T(8,128)(2,1)S(1)}, u32[]{:S(2)}, u32[]{:S(2)}) async-start(bf16[32,128,256]{2,1,0:T(8,128)(2,1)} %copy.69), calls=%async_computation.1 | async-start | bytes 4194304 | tf_op jit(solution)/shard_map/all_to_all | solution.py:105
  292.8 289.8 %copy-start.1 = (f32[3,128,256]{2,0,1:T(4,128)S(1)}, f32[3,128,256]{2,0,1:T(4,128)}, u32[]{:S(2)}) copy-start(f32[3,128,256]{2,0,1:T(4,128)} %fusion.20) | copy-start | bytes 1179652
  292.8 289.8 %copy-start.2 = (f32[4,128,256]{2,1,0:T(8,128)S(1)}, f32[4,128,256]{2,1,0:T(8,128)}, u32[]{:S(2)}) copy-start(f32[4,128,256]{2,1,0:T(8,128)} %fusion.29) | copy-start | bytes 1572868
  296.2 19.0 %collective-permute-start = (f32[3,128,256]{2,0,1:T(4,128)S(1)}, f32[3,128,256]{2,0,1:T(4,128)S(1)}, u32[]{:S(2)}, u32[]{:S(2)}) collective-permute-start(f32[3,128,256]{2,0,1:T(4,128)S(1)} %convolution_add_fusion.6), channel_id=1, source_target_pairs={{0,1},{1,2},{2,3},{3,4},{4,5},{5,6},{6,7},{7,8},{8,9},{9,10},{10,1... | collective-permute-start | bytes 1179656 | tf_op jit(solution)/shard_map/while/body/eval_jaxpr/ppermute | solution.py:9
  318.4 18.1 %collective-permute-start = (f32[3,128,256]{2,0,1:T(4,128)S(1)}, f32[3,128,256]{2,0,1:T(4,128)S(1)}, u32[]{:S(2)}, u32[]{:S(2)}) collective-permute-start(f32[3,128,256]{2,0,1:T(4,128)S(1)} %convolution_add_fusion.6), channel_id=1, source_target_pairs={{0,1},{1,2},{2,3},{3,4},{4,5},{5,6},{6,7},{7,8},{8,9},{9,10},{10,1... | collective-permute-start | bytes 1179656 | tf_op jit(solution)/shard_map/while/body/eval_jaxpr/ppermute | solution.py:9
  339.7 17.1 %collective-permute-start = (f32[3,128,256]{2,0,1:T(4,128)S(1)}, f32[3,128,256]{2,0,1:T(4,128)S(1)}, u32[]{:S(2)}, u32[]{:S(2)}) collective-permute-start(f32[3,128,256]{2,0,1:T(4,128)S(1)} %convolution_add_fusion.6), channel_id=1, source_target_pairs={{0,1},{1,2},{2,3},{3,4},{4,5},{5,6},{6,7},{7,8},{8,9},{9,10},{10,1... | collective-permute-start | bytes 1179656 | tf_op jit(solution)/shard_map/while/body/eval_jaxpr/ppermute | solution.py:9
  360.1 16.2 %collective-permute-start = (f32[3,128,256]{2,0,1:T(4,128)S(1)}, f32[3,128,256]{2,0,1:T(4,128)S(1)}, u32[]{:S(2)}, u32[]{:S(2)}) collective-permute-start(f32[3,128,256]{2,0,1:T(4,128)S(1)} %convolution_add_fusion.6), channel_id=1, source_target_pairs={{0,1},{1,2},{2,3},{3,4},{4,5},{5,6},{6,7},{7,8},{8,9},{9,10},{10,1... | collective-permute-start | bytes 1179656 | tf_op jit(solution)/shard_map/while/body/eval_jaxpr/ppermute | solution.py:9
  379.6 15.3 %collective-permute-start = (f32[3,128,256]{2,0,1:T(4,128)S(1)}, f32[3,128,256]{2,0,1:T(4,128)S(1)}, u32[]{:S(2)}, u32[]{:S(2)}) collective-permute-start(f32[3,128,256]{2,0,1:T(4,128)S(1)} %convolution_add_fusion.6), channel_id=1, source_target_pairs={{0,1},{1,2},{2,3},{3,4},{4,5},{5,6},{6,7},{7,8},{8,9},{9,10},{10,1... | collective-permute-start | bytes 1179656 | tf_op jit(solution)/shard_map/while/body/eval_jaxpr/ppermute | solution.py:9
  398.2 14.7 %collective-permute-start = (f32[3,128,256]{2,0,1:T(4,128)S(1)}, f32[3,128,256]{2,0,1:T(4,128)S(1)}, u32[]{:S(2)}, u32[]{:S(2)}) collective-permute-start(f32[3,128,256]{2,0,1:T(4,128)S(1)} %convolution_add_fusion.6), channel_id=1, source_target_pairs={{0,1},{1,2},{2,3},{3,4},{4,5},{5,6},{6,7},{7,8},{8,9},{9,10},{10,1... | collective-permute-start | bytes 1179656 | tf_op jit(solution)/shard_map/while/body/eval_jaxpr/ppermute | solution.py:9
  416.1 14.7 %collective-permute-start = (f32[3,128,256]{2,0,1:T(4,128)S(1)}, f32[3,128,256]{2,0,1:T(4,128)S(1)}, u32[]{:S(2)}, u32[]{:S(2)}) collective-permute-start(f32[3,128,256]{2,0,1:T(4,128)S(1)} %convolution_add_fusion.6), channel_id=1, source_target_pairs={{0,1},{1,2},{2,3},{3,4},{4,5},{5,6},{6,7},{7,8},{8,9},{9,10},{10,1... | collective-permute-start | bytes 1179656 | tf_op jit(solution)/shard_map/while/body/eval_jaxpr/ppermute | solution.py:9
  434.1 14.7 %collective-permute-start = (f32[3,128,256]{2,0,1:T(4,128)S(1)}, f32[3,128,256]{2,0,1:T(4,128)S(1)}, u32[]{:S(2)}, u32[]{:S(2)}) collective-permute-start(f32[3,128,256]{2,0,1:T(4,128)S(1)} %convolution_add_fusion.6), channel_id=1, source_target_pairs={{0,1},{1,2},{2,3},{3,4},{4,5},{5,6},{6,7},{7,8},{8,9},{9,10},{10,1... | collective-permute-start | bytes 1179656 | tf_op jit(solution)/shard_map/while/body/eval_jaxpr/ppermute | solution.py:9
  452.0 14.7 %collective-permute-start = (f32[3,128,256]{2,0,1:T(4,128)S(1)}, f32[3,128,256]{2,0,1:T(4,128)S(1)}, u32[]{:S(2)}, u32[]{:S(2)}) collective-permute-start(f32[3,128,256]{2,0,1:T(4,128)S(1)} %convolution_add_fusion.6), channel_id=1, source_target_pairs={{0,1},{1,2},{2,3},{3,4},{4,5},{5,6},{6,7},{7,8},{8,9},{9,10},{10,1... | collective-permute-start | bytes 1179656 | tf_op jit(solution)/shard_map/while/body/eval_jaxpr/ppermute | solution.py:9
  470.0 14.7 %collective-permute-start = (f32[3,128,256]{2,0,1:T(4,128)S(1)}, f32[3,128,256]{2,0,1:T(4,128)S(1)}, u32[]{:S(2)}, u32[]{:S(2)}) collective-permute-start(f32[3,128,256]{2,0,1:T(4,128)S(1)} %convolution_add_fusion.6), channel_id=1, source_target_pairs={{0,1},{1,2},{2,3},{3,4},{4,5},{5,6},{6,7},{7,8},{8,9},{9,10},{10,1... | collective-permute-start | bytes 1179656 | tf_op jit(solution)/shard_map/while/body/eval_jaxpr/ppermute | solution.py:9
  487.9 15.1 %collective-permute-start = (f32[3,128,256]{2,0,1:T(4,128)S(1)}, f32[3,128,256]{2,0,1:T(4,128)S(1)}, u32[]{:S(2)}, u32[]{:S(2)}) collective-permute-start(f32[3,128,256]{2,0,1:T(4,128)S(1)} %convolution_add_fusion.6), channel_id=1, source_target_pairs={{0,1},{1,2},{2,3},{3,4},{4,5},{5,6},{6,7},{7,8},{8,9},{9,10},{10,1... | collective-permute-start | bytes 1179656 | tf_op jit(solution)/shard_map/while/body/eval_jaxpr/ppermute | solution.py:9
  506.3 16.2 %collective-permute-start = (f32[3,128,256]{2,0,1:T(4,128)S(1)}, f32[3,128,256]{2,0,1:T(4,128)S(1)}, u32[]{:S(2)}, u32[]{:S(2)}) collective-permute-start(f32[3,128,256]{2,0,1:T(4,128)S(1)} %convolution_add_fusion.6), channel_id=1, source_target_pairs={{0,1},{1,2},{2,3},{3,4},{4,5},{5,6},{6,7},{7,8},{8,9},{9,10},{10,1... | collective-permute-start | bytes 1179656 | tf_op jit(solution)/shard_map/while/body/eval_jaxpr/ppermute | solution.py:9
  525.8 17.3 %collective-permute-start = (f32[3,128,256]{2,0,1:T(4,128)S(1)}, f32[3,128,256]{2,0,1:T(4,128)S(1)}, u32[]{:S(2)}, u32[]{:S(2)}) collective-permute-start(f32[3,128,256]{2,0,1:T(4,128)S(1)} %convolution_add_fusion.6), channel_id=1, source_target_pairs={{0,1},{1,2},{2,3},{3,4},{4,5},{5,6},{6,7},{7,8},{8,9},{9,10},{10,1... | collective-permute-start | bytes 1179656 | tf_op jit(solution)/shard_map/while/body/eval_jaxpr/ppermute | solution.py:9
  546.3 18.4 %collective-permute-start = (f32[3,128,256]{2,0,1:T(4,128)S(1)}, f32[3,128,256]{2,0,1:T(4,128)S(1)}, u32[]{:S(2)}, u32[]{:S(2)}) collective-permute-start(f32[3,128,256]{2,0,1:T(4,128)S(1)} %convolution_add_fusion.6), channel_id=1, source_target_pairs={{0,1},{1,2},{2,3},{3,4},{4,5},{5,6},{6,7},{7,8},{8,9},{9,10},{10,1... | collective-permute-start | bytes 1179656 | tf_op jit(solution)/shard_map/while/body/eval_jaxpr/ppermute | solution.py:9
  568.0 14.7 %collective-permute-start = (f32[3,128,256]{2,0,1:T(4,128)S(1)}, f32[3,128,256]{2,0,1:T(4,128)S(1)}, u32[]{:S(2)}, u32[]{:S(2)}) collective-permute-start(f32[3,128,256]{2,0,1:T(4,128)S(1)} %convolution_add_fusion.6), channel_id=1, source_target_pairs={{0,1},{1,2},{2,3},{3,4},{4,5},{5,6},{6,7},{7,8},{8,9},{9,10},{10,1... | collective-permute-start | bytes 1179656 | tf_op jit(solution)/shard_map/while/body/eval_jaxpr/ppermute | solution.py:9
  582.7 1.1 copy-start.3
where the time goes:
time: 587 us; the launch traced here: 585 us
  waiting for transfers between devices  359 us (61%)
  matrix products  102 us (17%)
  starting transfers between devices  79.6 us (14%)
  local copies, waits for them, and re-layouts  36.1 us (6%)
    ppermute x30, waiting for transfers between devices, passed_along(): lax.ppermute(value, axis, [(i, (i + by) % peers) for i in range(peers)])  311 us
    ppermute x30, starting transfers between devices, passed_along(): lax.ppermute(value, axis, [(i, (i + by) % peers) for i in range(peers)])  60 us
    dot_general x34, matrix products, spread_rows(): jnp.einsum('kr,kxf->rxf', onehot, products, precision=lax.Precision.HIGHEST)  56.3 us
    all_to_all x1, waiting for transfers between devices, on_device(): lax.all_to_all(returned, 'dom', split_axis=0, concat_axis=0, tiled=True)  48.1 us
    dot_general x16, matrix products, backward_term(): jnp.einsum('kxy,kxf->kyf', tiles_all[source], target_rows, preferred_elem...  19.7 us
    dot_general x16, matrix products, forward_term(): jnp.einsum('kxy,kyf->kxf', tiles_all[source], source_rows, preferred_elem...  17.8 us
  transfers between devices with their start and end apart: 32, of which 31 were waited for; matrix products, arithmetic and copies ran while one was open for 10% of the time, Pallas kernels for 0%

commit v1 on v0

v1 whole, which is shorter than its diff:
```python
import jax
import jax.numpy as jnp
from jax import lax
from jax.experimental import pallas as pl
from jax.experimental.pallas import tpu as pltpu
from jax.sharding import PartitionSpec as P

BF, F32, I32 = jnp.bfloat16, jnp.float32, jnp.int32
TILE = 128
FAR = 2
STEPS = 4
VMEM_LIMIT = 40 * 1024 * 1024


def spec(space):
    return pl.BlockSpec(memory_space=space)


def silu_parts(preact):
    sigmoid = 1.0 / (1.0 + jnp.exp(-preact))
    return (preact * sigmoid, sigmoid * (1.0 + preact * (1.0 - sigmoid)))


def project_kernel(blk_ref, live_ref, features_ref, weight_ref, projected_ref, outgoing_ref):
    projected_ref[...] = jnp.dot(
        features_ref[...], weight_ref[...], preferred_element_type=F32
    ).astype(BF)

    def fill(part, carried):
        @pl.when(live_ref[part] > 0)
        def _():
            row = pl.multiple_of(blk_ref[part] * TILE, TILE)
            outgoing_ref[part] = projected_ref[pl.ds(row, TILE), :]

        @pl.when(live_ref[part] <= 0)
        def _():
            outgoing_ref[part] = jnp.zeros(outgoing_ref.shape[1:], BF)

        return carried

    lax.fori_loop(0, outgoing_ref.shape[0], fill, 0)


def spread_kernel(ring, blocks, pos_ref, count_ref, dst_ref, place_ref, tiles_ref, cut_ref, *outs):
    ahead, back = outs[:ring], outs[ring : 2 * ring]
    cut_ahead, cut_back = outs[2 * ring :]
    rows = blocks * TILE
    place = place_ref[0]
    for offset in range(ring):
        ahead[offset][...] = jnp.zeros(ahead[offset].shape, BF)
        back[offset][...] = jnp.zeros(back[offset].shape, BF)
        spot = lax.rem(place + offset, ring)
        for half in range(FAR):
            source = half * ring + spot

            def put(slot, carried, offset=offset, half=half, source=source):
                position = pos_ref[source * tiles_ref.shape[1] + slot]
                target = pl.multiple_of(position // blocks * TILE, TILE)
                origin = pl.multiple_of(half * rows + position % blocks * TILE, TILE)
                tile = tiles_ref[source, slot]
                ahead[offset][pl.ds(target, TILE), pl.ds(origin, TILE)] = tile
                back[offset][pl.ds(origin, TILE), pl.ds(target, TILE)] = (
                    tile.astype(F32).T.astype(BF)
                )
                return carried

            lax.fori_loop(0, count_ref[source], put, 0)
    cut_ahead[...] = jnp.zeros(cut_ahead.shape, BF)
    cut_back[...] = jnp.zeros(cut_back.shape, BF)

    def put_cut(part, carried):
        target = pl.multiple_of(dst_ref[part] * TILE, TILE)
        origin = pl.multiple_of(part * TILE, TILE)
        tile = cut_ref[part]
        cut_ahead[pl.ds(target, TILE), pl.ds(origin, TILE)] = tile
        cut_back[pl.ds(origin, TILE), pl.ds(target, TILE)] = tile.astype(F32).T.astype(BF)
        return carried

    lax.fori_loop(0, cut_ref.shape[0], put_cut, 0)


def middle_kernel(
    sum_ref,
    mat_ref,
    low_ref,
    high_ref,
    bias_ref,
    cotangent_ref,
    ahead_ref,
    far_ref,
    back_ref,
    hidden_ref,
    grad_ref,
    terms_ref,
    total,
):
    step = pl.program_id(0)
    rows = sum_ref.shape[0]
    width = sum_ref.shape[1]

    @pl.when(step == 0)
    def _():
        total[...] = (
            sum_ref[...]
            + jnp.dot(mat_ref[:, :rows], low_ref[...], preferred_element_type=F32)
            + jnp.dot(mat_ref[:, rows:], high_ref[...], preferred_element_type=F32)
        )

    @pl.when(step < STEPS)
    def _():
        arrived = far_ref[...].reshape(-1, width)
        total[...] += jnp.dot(ahead_ref[...], arrived, preferred_element_type=F32)

    @pl.when(step == STEPS - 1)
    def _():
        activated, derivative = silu_parts(total[...] + bias_ref[...])
        hidden_ref[...] = activated.astype(BF)
        grad_ref[...] = (cotangent_ref[...].astype(F32) * derivative).astype(BF)

    @pl.when(step >= STEPS)
    def _():
        product = jnp.dot(back_ref[...], grad_ref[...], preferred_element_type=F32)
        terms_ref[...] = product.astype(BF).reshape(terms_ref.shape)


def last_kernel(blk_ref, live_ref, own_ref, other_ref, weight_ref, arrived_ref, out_ref, total):
    step = pl.program_id(0)
    chunk = arrived_ref.shape[0]

    @pl.when(step == 0)
    def _():
        total[...] = own_ref[...] + other_ref[...].astype(F32)

    def add(slot, carried):
        part = step * chunk + slot

        @pl.when(live_ref[part] > 0)
        def _():
            row = pl.ds(pl.multiple_of(blk_ref[part] * TILE, TILE), TILE)
            total[row, :] += arrived_ref[slot].astype(F32)

        return carried

    lax.fori_loop(0, chunk, add, 0)

    @pl.when(step == STEPS - 1)
    def _():
        out_ref[...] = lax.dot_general(
            total[...].astype(BF),
            weight_ref[...],
            (((1,), (1,)), ((), ())),
            preferred_element_type=F32,
        ).astype(BF)


def on_device(
    features,
    weight,
    bias,
    cotangent,
    in_tiles,
    in_pos,
    in_count,
    cut_tiles,
    send_blk,
    send_live,
    recv_dst,
):
    rows, width = features.shape
    blocks = rows // TILE
    peers = lax.axis_size("blk")
    parts = lax.axis_size("dom")
    ring = peers // FAR
    reach = ring // 2
    me = lax.axis_index("blk")
    place, half = me % ring, me // ring
    smem, vmem = spec(pltpu.SMEM), spec(pltpu.VMEM)
    params = pltpu.CompilerParams(vmem_limit_bytes=VMEM_LIMIT)
    send_to, is_live, dst = send_blk[0, 0], send_live[0, 0], recv_dst[0, 0]

    def along_ring(value, by):
        moves = [
            (side * ring + spot, side * ring + (spot + by) % ring)
            for side in range(FAR)
            for spot in range(ring)
        ]
        return lax.ppermute(value, "blk", moves)

    def across(value):
        return lax.ppermute(value, "blk", [(i, (i + ring) % peers) for i in range(peers)])

    def product(left, right):
        return jnp.dot(left, right, preferred_element_type=F32)

    projected, outgoing = pl.pallas_call(
        project_kernel,
        out_shape=(
            jax.ShapeDtypeStruct((rows, width), BF),
            jax.ShapeDtypeStruct((parts, TILE, width), BF),
        ),
        in_specs=[smem, smem, vmem, vmem],
        out_specs=(vmem, vmem),
        compiler_params=params,
        name="project",
    )(send_to, is_live, features, weight)
    incoming = lax.all_to_all(outgoing, "dom", split_axis=0, concat_axis=0, tiled=True)
    partner = across(projected)

    wide = FAR * rows
    dense = pl.pallas_call(
        lambda *refs: spread_kernel(ring, blocks, *refs),
        out_shape=tuple(
            [jax.ShapeDtypeStruct((rows, wide), BF)] * ring
            + [jax.ShapeDtypeStruct((wide, rows), BF)] * ring
            + [jax.ShapeDtypeStruct((rows, parts * TILE), BF)]
            + [jax.ShapeDtypeStruct((parts * TILE, rows), BF)]
        ),
        in_specs=[smem] * 4 + [vmem] * 2,
        out_specs=tuple([vmem] * (2 * ring + 2)),
        compiler_params=params,
        cost_estimate=pl.CostEstimate(flops=0, bytes_accessed=24 << 20, transcendentals=0),
        name="spread",
    )(
        in_pos[0, 0].reshape(-1),
        in_count[0, 0],
        dst,
        place.reshape(1),
        in_tiles[0, 0],
        cut_tiles[0, 0],
    )
    ahead, back = dense[:ring], dense[ring : 2 * ring]
    cut_ahead, cut_back = dense[2 * ring :]

    pair = jnp.where(
        half == 0,
        jnp.concatenate([projected, partner]),
        jnp.concatenate([partner, projected]),
    )
    running = product(ahead[0], pair)
    right = left = pair
    for hop in range(1, reach):
        right, left = along_ring(right, 1), along_ring(left, -1)
        running = running + product(ahead[ring - hop], right)
        running = running + product(ahead[hop], left)
    low, high = along_ring(right[:rows], 1), along_ring(left[rows:], -1)

    chunk = parts // STEPS
    whole = lambda *shape: pl.BlockSpec(shape, lambda i: (0,) * len(shape))
    first = lambda i: jnp.minimum(i, STEPS - 1)
    second = lambda i: jnp.maximum(i - STEPS, 0)
    hidden, grad_pre, terms = pl.pallas_call(
        middle_kernel,
        grid=(2 * STEPS,),
        out_shape=(
            jax.ShapeDtypeStruct((rows, width), BF),
            jax.ShapeDtypeStruct((rows, width), BF),
            jax.ShapeDtypeStruct((parts, TILE, width), BF),
        ),
        in_specs=[
            whole(rows, width),
            whole(rows, wide),
            whole(rows, width),
            whole(rows, width),
            whole(1, width),
            whole(rows, width),
            pl.BlockSpec((rows, chunk * TILE), lambda i: (0, first(i))),
            pl.BlockSpec((chunk, TILE, width), lambda i: (first(i), 0, 0)),
            pl.BlockSpec((chunk * TILE, rows), lambda i: (second(i), 0)),
        ],
        out_specs=(
            whole(rows, width),
            whole(rows, width),
            pl.BlockSpec((chunk, TILE, width), lambda i: (second(i), 0, 0)),
        ),
        scratch_shapes=[pltpu.VMEM((rows, width), F32)],
        compiler_params=params,
        name="middle",
    )(
        running,
        ahead[reach],
        low,
        high,
        bias.reshape(1, width),
        cotangent,
        cut_ahead,
        incoming,
        cut_back,
    )
    returned = lax.all_to_all(terms, "dom", split_axis=0, concat_axis=0, tiled=True)

    farthest = product(back[reach], grad_pre).astype(BF)
    low, high = along_ring(farthest[:rows], 1), along_ring(farthest[rows:], -1)
    for hop in range(reach - 1, 0, -1):
        right = product(back[hop], grad_pre)
        left = product(back[ring - hop], grad_pre)
        if hop == reach - 1:
            right = jnp.concatenate([right[:rows] + low.astype(F32), right[rows:]])
            left = jnp.concatenate([left[:rows], left[rows:] + high.astype(F32)])
        else:
            right, left = right + from_left.astype(F32), left + from_right.astype(F32)
        from_left = along_ring(right.astype(BF), 1)
        from_right = along_ring(left.astype(BF), -1)
    both = product(back[0], grad_pre) + from_left.astype(F32) + from_right.astype(F32)
    mine = jnp.where(half == 0, both[:rows], both[rows:])
    theirs = across(jnp.where(half == 0, both[rows:], both[:rows]).astype(BF))

    grad_features = pl.pallas_call(
        last_kernel,
        grid=(STEPS,),
        out_shape=jax.ShapeDtypeStruct((rows, width), BF),
        in_specs=[
            smem,
            smem,
            whole(rows, width),
            whole(rows, width),
            whole(*weight.shape),
            pl.BlockSpec((chunk, TILE, width), lambda i: (i, 0, 0)),
        ],
        out_specs=whole(rows, width),
        scratch_shapes=[pltpu.VMEM((rows, width), F32)],
        compiler_params=params,
        name="last",
    )(send_to, is_live, mine, theirs, weight, returned)
    return (hidden, grad_features)


def solution(mesh):
    in_specs = (
        P(("dom", "blk"), None),
        P(),
        P(),
        P(("dom", "blk"), None),
        P("dom", "blk", None, None, None, None),
        P("dom", "blk", None, None),
        P("dom", "blk", None),
        P("dom", "blk", None, None, None),
        P("dom", "blk", None),
        P("dom", "blk", None),
        P("dom", "blk", None),
    )
    out_specs = (P(("dom", "blk"), None), P(("dom", "blk"), None))
    return jax.shard_map(
        on_device, mesh=mesh, in_specs=in_specs, out_specs=out_specs, check_vma=False
    )
```

time: 587 us -> 190 us (0.32)
  the two profiles are of different devices: /device:TPU:12 before, /device:TPU:2 now
where the time goes in v1:
time: 190 us; the launch traced here: 189 us
  starting transfers between devices  93.4 us (49%)
  waiting for transfers between devices  49.5 us (26%)
  Pallas kernels  19.9 us (10%)
  local copies, waits for them, and re-layouts  15.6 us (8%)
  matrix products  8.1 us (4%)
    ppermute x16, starting transfers between devices, along_ring(): return lax.ppermute(value, 'blk', moves)  62.6 us
    ppermute x16, waiting for transfers between devices, along_ring(): return lax.ppermute(value, 'blk', moves)  30.6 us
    ppermute x2, waiting for transfers between devices, across(): lax.ppermute(value, 'blk', [(i, (i + ring) % peers) for i in range(peers)])  18.9 us
    all_to_all x1, starting transfers between devices, on_device(): lax.all_to_all(terms, 'dom', split_axis=0, concat_axis=0, tiled=True)  15.9 us
    unnamed x81, local copies, waits for them, and re-layouts  15.4 us
    pallas_call x1, Pallas kernels, on_device(): pl.pallas_call(lambda *refs: spread_kernel(ring, blocks, *refs), out_shap...  11 us
    all_to_all x1, starting transfers between devices, on_device(): lax.all_to_all(outgoing, 'dom', split_axis=0, concat_axis=0, tiled=True)  9.82 us
    dot_general x15, matrix products, product(): return jnp.dot(left, right, preferred_element_type=F32)  8.1 us
  transfers between devices with their start and end apart: 20, of which 10 were waited for; matrix products, arithmetic and copies ran while one was open for 5% of the time, Pallas kernels for 6%

profile of v1, /device:TPU:2, one launch (start us, length us, event | category | flops | bytes accessed | tf_op | source)
XLA Modules:
  0.0 189.0 jit_solution(1153085381201393745)
XLA Ops:
  0.6 0.9 copy-done.24
  1.5 0.9 copy-done.26
  2.5 0.7 copy-done.32
  3.1 0.7 copy-done.34
  3.8 1.6 project.1
  5.4 1.4 copy-done.3
  6.8 9.8 %all-to-all-start = ((bf16[32,128,256]{2,1,0:T(8,128)(2,1)}), bf16[32,128,256]{2,1,0:T(8,128)(2,1)S(1)}, u32[]{:S(2)}, u32[]{:S(2)}) async-start(bf16[32,128,256]{2,1,0:T(8,128)(2,1)} %copy-done.3), calls=%async_computation | async-start | bytes 4194304 | tf_op jit(solution)/shard_map/all_to_all | solution.py:206
  16.6 3.1 %collective-permute-start = (bf16[384,256]{1,0:T(8,128)(2,1)S(1)}, bf16[384,256]{1,0:T(8,128)(2,1)S(1)}, u32[]{:S(2)}, u32[]{:S(2)}) collective-permute-start(bf16[384,256]{1,0:T(8,128)(2,1)S(1)} %get-tuple-element.26), channel_id=1, source_target_pairs={{0,8},{1,9},{2,10},{3,11},{4,12},{5,13},{6,14},{7,15},{8,0},{9,1},... | collective-permute-start | bytes 589832 | tf_op jit(solution)/shard_map/ppermute | solution.py:190
  19.7 11.8 %collective-permute-done = bf16[384,256]{1,0:T(8,128)(2,1)S(1)} collective-permute-done((bf16[384,256]{1,0:T(8,128)(2,1)S(1)}, bf16[384,256]{1,0:T(8,128)(2,1)S(1)}, u32[]{:S(2)}, u32[]{:S(2)}) %collective-permute-start) | collective-permute-done | bytes 196640 | tf_op jit(solution)/shard_map/ppermute | solution.py:190
  31.5 0.9 maximum_select_fusion
  32.4 9.4 %collective-permute-start.2 = (bf16[768,256]{1,0:T(8,128)(2,1)}, bf16[768,256]{1,0:T(8,128)(2,1)}, u32[]{:S(2)}, u32[]{:S(2)}) collective-permute-start(bf16[768,256]{1,0:T(8,128)(2,1)} %maximum_select_fusion), channel_id=1, source_target_pairs={{0,7},{1,0},{2,1},{3,2},{4,3},{5,4},{6,5},{7,6},{8,15},{9,8},{10,9... | collective-permute-start | bytes 1179656 | tf_op jit(solution)/shard_map/ppermute | solution.py:187
  41.8 1.9 %collective-permute-start.1 = (bf16[768,256]{1,0:T(8,128)(2,1)}, bf16[768,256]{1,0:T(8,128)(2,1)}, u32[]{:S(2)}, u32[]{:S(2)}) collective-permute-start(bf16[768,256]{1,0:T(8,128)(2,1)} %maximum_select_fusion), channel_id=1, source_target_pairs={{0,1},{1,2},{2,3},{3,4},{4,5},{5,6},{6,7},{7,0},{8,9},{9,10},{10,1... | collective-permute-start | bytes 1179656 | tf_op jit(solution)/shard_map/ppermute | solution.py:187
  44.0 1.6 copy-done.2
  45.5 11.0 %spread.1 = (bf16[384,768]{1,0:T(8,128)(2,1)S(1)}, bf16[384,768]{1,0:T(8,128)(2,1)S(1)}, bf16[384,768]{1,0:T(8,128)(2,1)S(1)}, bf16[384,768]{1,0:T(8,128)(2,1)S(...) custom-call(s32[64]{0:T(128)S(1)} %reshape_squeeze.3.refs_0_, ...), custom_call_target="tpu_custom_call" | custom-call | bytes 25165824 | tf_op jit(solution)/shard_map/spread/pallas_call | solution.py:210
  56.6 0.8 copy-done.22
  57.5 6.3 %collective-permute-start.4 = (bf16[768,256]{1,0:T(8,128)(2,1)}, bf16[768,256]{1,0:T(8,128)(2,1)S(1)}, u32[]{:S(2)}, u32[]{:S(2)}) collective-permute-start(bf16[768,256]{1,0:T(8,128)(2,1)} %collective-permute-done.2), channel_id=1, source_target_pairs={{0,7},{1,0},{2,1},{3,2},{4,3},{5,4},{6,5},{7,6},{8,15},{9,8},{10,9... | collective-permute-start | bytes 1179656 | tf_op jit(solution)/shard_map/ppermute | solution.py:187
  63.7 1.9 %collective-permute-start.3 = (bf16[768,256]{1,0:T(8,128)(2,1)}, bf16[768,256]{1,0:T(8,128)(2,1)S(1)}, u32[]{:S(2)}, u32[]{:S(2)}) collective-permute-start(bf16[768,256]{1,0:T(8,128)(2,1)} %collective-permute-done.1), channel_id=1, source_target_pairs={{0,1},{1,2},{2,3},{3,4},{4,5},{5,6},{6,7},{7,0},{8,9},{9,10},{10,1... | collective-permute-start | bytes 1179656 | tf_op jit(solution)/shard_map/ppermute | solution.py:187
  65.7 1.3 fusion.11
  67.0 1.3 fusion.12
  68.3 1.3 fusion.7
  69.7 5.1 %collective-permute-start.6 = (bf16[768,256]{1,0:T(8,128)(2,1)S(1)}, bf16[768,256]{1,0:T(8,128)(2,1)S(1)}, u32[]{:S(2)}, u32[]{:S(2)}) collective-permute-start(bf16[768,256]{1,0:T(8,128)(2,1)S(1)} %collective-permute-done.4), channel_id=1, source_target_pairs={{0,7},{1,0},{2,1},{3,2},{4,3},{5,4},{6,5},{7,6},{8,15},{9,8},{10,9... | collective-permute-start | bytes 1179656 | tf_op jit(solution)/shard_map/ppermute | solution.py:187
  74.9 1.9 %collective-permute-start.5 = (bf16[768,256]{1,0:T(8,128)(2,1)S(1)}, bf16[768,256]{1,0:T(8,128)(2,1)S(1)}, u32[]{:S(2)}, u32[]{:S(2)}) collective-permute-start(bf16[768,256]{1,0:T(8,128)(2,1)S(1)} %collective-permute-done.3), channel_id=1, source_target_pairs={{0,1},{1,2},{2,3},{3,4},{4,5},{5,6},{6,7},{7,0},{8,9},{9,10},{10,1... | collective-permute-start | bytes 1179656 | tf_op jit(solution)/shard_map/ppermute | solution.py:187
  76.8 0.3 fusion.13
  77.1 0.3 fusion.6
  77.5 8.4 %collective-permute-done.5 = bf16[768,256]{1,0:T(8,128)(2,1)S(1)} collective-permute-done((bf16[768,256]{1,0:T(8,128)(2,1)S(1)}, bf16[768,256]{1,0:T(8,128)(2,1)S(1)}, u32[]{:S(2)}, u32[]{:S(2)}) %collective-permute-start.5) | collective-permute-done | bytes 393248 | tf_op jit(solution)/shard_map/ppermute | solution.py:187
  85.9 1.9 %collective-permute-start.7 = (bf16[384,256]{1,0:T(8,128)(2,1)S(1)}, bf16[384,256]{1,0:T(8,128)(2,1)S(1)}, u32[]{:S(2)}, u32[]{:S(2)}) collective-permute-start(bf16[384,256]{1,0:T(8,128)(2,1)S(1)} %slice.44), channel_id=1, source_target_pairs={{0,1},{1,2},{2,3},{3,4},{4,5},{5,6},{6,7},{7,0},{8,9},{9,10},{10,1... | collective-permute-start | bytes 589832 | tf_op jit(solution)/shard_map/ppermute | solution.py:187
  87.9 5.1 %collective-permute-start.8 = (bf16[384,256]{1,0:T(8,128)(2,1)S(1)}, bf16[384,256]{1,0:T(8,128)(2,1)S(1)}, u32[]{:S(2)}, u32[]{:S(2)}) collective-permute-start(bf16[384,256]{1,0:T(8,128)(2,1)S(1)} %slice.45), channel_id=1, source_target_pairs={{0,7},{1,0},{2,1},{3,2},{4,3},{5,4},{6,5},{7,6},{8,15},{9,8},{10,9... | collective-permute-start | bytes 589832 | tf_op jit(solution)/shard_map/ppermute | solution.py:187
  93.0 0.3 fusion.14
  93.3 0.3 fusion.5.sum_ref
  93.6 1.0 collective-permute-done.7.low_ref
  94.7 0.7 copy-done.28
  95.3 0.8 collective-permute-done.8.high_ref
  96.2 0.7 copy-done.30
  96.9 1.9 copy-done
  98.8 1.9 copy-done.1
  100.6 0.9 copy-done.29
  101.6 0.9 copy-done.31
  102.5 4.9 %middle.1 = (bf16[384,256]{1,0:T(8,128)(2,1)}, bf16[384,256]{1,0:T(8,128)(2,1)S(1)}, bf16[32,128,256]{2,1,0:T(8,128)(2,1)S(1)}) custom-call(f32[384,256]{1,0:T(8,128)S(1)} %fusion.5.sum_ref, bf16[384,768]{1,0:T(8,128)(2,1)S(1)} %copy-done.7, bf16[384,256]{1,0:T(8,128)(2,1)S(1)} %copy-done.29, bf16[384,256]{1,0:T(8,128)(2,1)S(1)} %copy-done.31, ...), custom_call_target="tpu_custom_call" | custom-call | tf_op jit(solution)/shard_map/middle/pallas_call | solution.py:251
  107.4 1.3 copy-done.4
  108.7 15.9 %all-to-all-start.1 = ((bf16[32,128,256]{2,1,0:T(8,128)(2,1)}), bf16[32,128,256]{2,1,0:T(8,128)(2,1)S(1)}, u32[]{:S(2)}, u32[]{:S(2)}) async-start(bf16[32,128,256]{2,1,0:T(8,128)(2,1)} %copy-done.4), calls=%async_computation.1 | async-start | bytes 4194304 | tf_op jit(solution)/shard_map/all_to_all | solution.py:289
  124.7 0.4 convolution_convert_fusion
  125.1 1.9 %collective-permute-start.9 = (bf16[384,256]{1,0:T(8,128)(2,1)S(1)}, bf16[384,256]{1,0:T(8,128)(2,1)S(1)}, u32[]{:S(2)}, u32[]{:S(2)}) collective-permute-start(bf16[384,256]{1,0:T(8,128)(2,1)S(1)} %get-tuple-element.48), channel_id=1, source_target_pairs={{0,1},{1,2},{2,3},{3,4},{4,5},{5,6},{6,7},{7,0},{8,9},{9,10},{10,1... | collective-permute-start | bytes 589832 | tf_op jit(solution)/shard_map/ppermute | solution.py:187
  127.0 0.4 fusion.15
  127.4 5.6 %collective-permute-start.13 = (bf16[384,256]{1,0:T(8,128)(2,1)S(1)}, bf16[384,256]{1,0:T(8,128)(2,1)S(1)}, u32[]{:S(2)}, u32[]{:S(2)}) collective-permute-start(bf16[384,256]{1,0:T(8,128)(2,1)S(1)} %get-tuple-element.49), channel_id=1, source_target_pairs={{0,7},{1,0},{2,1},{3,2},{4,3},{5,4},{6,5},{7,6},{8,15},{9,8},{10,9... | collective-permute-start | bytes 589832 | tf_op jit(solution)/shard_map/ppermute | solution.py:187
  133.0 0.4 fusion.16
  133.4 2.5 %collective-permute-done.9 = bf16[384,256]{1,0:T(8,128)(2,1)S(1)} collective-permute-done((bf16[384,256]{1,0:T(8,128)(2,1)S(1)}, bf16[384,256]{1,0:T(8,128)(2,1)S(1)}, u32[]{:S(2)}, u32[]{:S(2)}) %collective-permute-start.9) | collective-permute-done | bytes 196640 | tf_op jit(solution)/shard_map/ppermute | solution.py:187
  136.0 2.1 %collective-permute-start.10 = (bf16[768,256]{1,0:T(8,128)(2,1)S(1)}, bf16[768,256]{1,0:T(8,128)(2,1)S(1)}, u32[]{:S(2)}, u32[]{:S(2)}) collective-permute-start(bf16[768,256]{1,0:T(8,128)(2,1)S(1)} %pad_maximum_fusion), channel_id=1, source_target_pairs={{0,1},{1,2},{2,3},{3,4},{4,5},{5,6},{6,7},{7,0},{8,9},{9,10},{10,1... | collective-permute-start | bytes 1179656 | tf_op jit(solution)/shard_map/ppermute | solution.py:187
  138.2 5.3 %collective-permute-start.14 = (bf16[768,256]{1,0:T(8,128)(2,1)S(1)}, bf16[768,256]{1,0:T(8,128)(2,1)S(1)}, u32[]{:S(2)}, u32[]{:S(2)}) collective-permute-start(bf16[768,256]{1,0:T(8,128)(2,1)S(1)} %pad_maximum_fusion.1), channel_id=1, source_target_pairs={{0,7},{1,0},{2,1},{3,2},{4,3},{5,4},{6,5},{7,6},{8,15},{9,8},{10,9... | collective-permute-start | bytes 1179656 | tf_op jit(solution)/shard_map/ppermute | solution.py:187
  143.4 6.4 %collective-permute-done.10 = bf16[768,256]{1,0:T(8,128)(2,1)S(1)} collective-permute-done((bf16[768,256]{1,0:T(8,128)(2,1)S(1)}, bf16[768,256]{1,0:T(8,128)(2,1)S(1)}, u32[]{:S(2)}, u32[]{:S(2)}) %collective-permute-start.10) | collective-permute-done | bytes 393248 | tf_op jit(solution)/shard_map/ppermute | solution.py:187
  149.9 0.4 fusion.2
  150.3 1.9 %collective-permute-start.11 = (bf16[768,256]{1,0:T(8,128)(2,1)S(1)}, bf16[768,256]{1,0:T(8,128)(2,1)S(1)}, u32[]{:S(2)}, u32[]{:S(2)}) collective-permute-start(bf16[768,256]{1,0:T(8,128)(2,1)S(1)} %fusion.2), channel_id=1, source_target_pairs={{0,1},{1,2},{2,3},{3,4},{4,5},{5,6},{6,7},{7,0},{8,9},{9,10},{10,1... | collective-permute-start | bytes 1179656 | tf_op jit(solution)/shard_map/ppermute | solution.py:187
  152.2 0.4 fusion.4
  152.6 5.1 %collective-permute-start.15 = (bf16[768,256]{1,0:T(8,128)(2,1)S(1)}, bf16[768,256]{1,0:T(8,128)(2,1)S(1)}, u32[]{:S(2)}, u32[]{:S(2)}) collective-permute-start(bf16[768,256]{1,0:T(8,128)(2,1)S(1)} %fusion.4), channel_id=1, source_target_pairs={{0,7},{1,0},{2,1},{3,2},{4,3},{5,4},{6,5},{7,6},{8,15},{9,8},{10,9... | collective-permute-start | bytes 1179656 | tf_op jit(solution)/shard_map/ppermute | solution.py:187
  157.7 5.4 %collective-permute-done.11 = bf16[768,256]{1,0:T(8,128)(2,1)S(1)} collective-permute-done((bf16[768,256]{1,0:T(8,128)(2,1)S(1)}, bf16[768,256]{1,0:T(8,128)(2,1)S(1)}, u32[]{:S(2)}, u32[]{:S(2)}) %collective-permute-start.11) | collective-permute-done | bytes 393248 | tf_op jit(solution)/shard_map/ppermute | solution.py:187
  163.1 0.4 fusion.1
  163.5 1.9 %collective-permute-start.12 = (bf16[768,256]{1,0:T(8,128)(2,1)S(1)}, bf16[768,256]{1,0:T(8,128)(2,1)S(1)}, u32[]{:S(2)}, u32[]{:S(2)}) collective-permute-start(bf16[768,256]{1,0:T(8,128)(2,1)S(1)} %fusion.1), channel_id=1, source_target_pairs={{0,1},{1,2},{2,3},{3,4},{4,5},{5,6},{6,7},{7,0},{8,9},{9,10},{10,1... | collective-permute-start | bytes 1179656 | tf_op jit(solution)/shard_map/ppermute | solution.py:187
  165.4 0.4 fusion.3
  165.8 5.3 %collective-permute-start.16 = (bf16[768,256]{1,0:T(8,128)(2,1)S(1)}, bf16[768,256]{1,0:T(8,128)(2,1)S(1)}, u32[]{:S(2)}, u32[]{:S(2)}) collective-permute-start(bf16[768,256]{1,0:T(8,128)(2,1)S(1)} %fusion.3), channel_id=1, source_target_pairs={{0,7},{1,0},{2,1},{3,2},{4,3},{5,4},{6,5},{7,6},{8,15},{9,8},{10,9... | collective-permute-start | bytes 1179656 | tf_op jit(solution)/shard_map/ppermute | solution.py:187
  171.1 4.3 %collective-permute-done.12 = bf16[768,256]{1,0:T(8,128)(2,1)S(1)} collective-permute-done((bf16[768,256]{1,0:T(8,128)(2,1)S(1)}, bf16[768,256]{1,0:T(8,128)(2,1)S(1)}, u32[]{:S(2)}, u32[]{:S(2)}) %collective-permute-start.12) | collective-permute-done | bytes 393248 | tf_op jit(solution)/shard_map/ppermute | solution.py:187
  175.4 1.7 collective-permute-done.16
  177.1 0.4 fusion
  177.6 1.9 %collective-permute-start.17 = (bf16[384,256]{1,0:T(8,128)(2,1)S(1)}, bf16[384,256]{1,0:T(8,128)(2,1)S(1)}, u32[]{:S(2)}, u32[]{:S(2)}) collective-permute-start(bf16[384,256]{1,0:T(8,128)(2,1)S(1)} %select_convert_fusion), channel_id=1, source_target_pairs={{0,8},{1,9},{2,10},{3,11},{4,12},{5,13},{6,14},{7,15},{8,0},{9,1},... | collective-permute-start | bytes 589832 | tf_op jit(solution)/shard_map/ppermute | solution.py:190
  179.5 7.1 %collective-permute-done.17.other_ref = bf16[384,256]{1,0:T(8,128)(2,1)S(1)} collective-permute-done((bf16[384,256]{1,0:T(8,128)(2,1)S(1)}, bf16[384,256]{1,0:T(8,128)(2,1)S(1)}, u32[]{:S(2)}, u32[]{:S(2)}) %collective-permute-start.17) | collective-permute-done | bytes 196640 | tf_op jit(solution)/shard_map/ppermute | solution.py:190
  186.6 2.4 %last.1 = bf16[384,256]{1,0:T(8,128)(2,1)} custom-call(s32[32]{0:T(128)S(1)} %bitcast.43, s32[32]{0:T(128)S(1)} %bitcast.45, f32[384,256]{1,0:T(8,128)S(1)} %slice_select_fusion.own_ref, bf16[384,256]{1,0:T(8,128)(2,1)S(1)} %collective-permute-done.17.other_ref, bf16[256,256]{1,0:T(8,128)(2,1)S(1)} %copy-done.25, ...), custom_call_target="tpu_custom_call" | custom-call | tf_op jit(solution)/shard_map/last/pallas_call | solution.py:307
  (89 shorter events, 0.7 us)
Async XLA Ops:
  0.6 0.9 copy-start.24
  1.5 0.9 copy-start.26
  2.5 0.7 copy-start.32
  3.1 0.7 copy-start.34
  5.4 1.4 copy-start.3
  6.7 37.0 %copy-start.39 = (s32[1,1,16,4]{2,3,1,0:T(4,128)S(1)}, s32[1,1,16,4]{2,3,1,0:T(4,128)}, u32[]{:S(2)}) copy-start(s32[1,1,16,4]{2,3,1,0:T(4,128)} %param.16) | copy-start | bytes 772
  6.7 37.2 %copy-start.5 = (bf16[1,1,32,128,128]{4,3,2,1,0:T(8,128)(2,1)S(1)}, bf16[1,1,32,128,128]{4,3,2,1,0:T(8,128)(2,1)}, u32[]{:S(2)}) copy-start(bf16[1,1,32,128,128]{4,3,2,1,0:T(8,128)(2,1)} %param.18) | copy-start | bytes 3145732
  6.7 37.2 %copy-start.37 = (s32[1,1,16]{2,1,0:T(1,128)S(1)}, s32[1,1,16]{2,1,0:T(1,128)}, u32[]{:S(2)}) copy-start(s32[1,1,16]{2,1,0:T(1,128)} %param.17) | copy-start | bytes 196
  6.8 37.2 %copy-start.38 = (s32[1,1,32]{2,1,0:T(1,128)S(1)}, s32[1,1,32]{2,1,0:T(1,128)}, u32[]{:S(2)}) copy-start(s32[1,1,32]{2,1,0:T(1,128)} %param.21) | copy-start | bytes 388
  6.8 90.1 %all-to-all-start = ((bf16[32,128,256]{2,1,0:T(8,128)(2,1)}), bf16[32,128,256]{2,1,0:T(8,128)(2,1)S(1)}, u32[]{:S(2)}, u32[]{:S(2)}) async-start(bf16[32,128,256]{2,1,0:T(8,128)(2,1)} %copy-done.3), calls=%async_computation | async-start | bytes 4194304 | tf_op jit(solution)/shard_map/all_to_all | solution.py:206
  16.6 14.9 %collective-permute-start = (bf16[384,256]{1,0:T(8,128)(2,1)S(1)}, bf16[384,256]{1,0:T(8,128)(2,1)S(1)}, u32[]{:S(2)}, u32[]{:S(2)}) collective-permute-start(bf16[384,256]{1,0:T(8,128)(2,1)S(1)} %get-tuple-element.26), channel_id=1, source_target_pairs={{0,8},{1,9},{2,10},{3,11},{4,12},{5,13},{6,14},{7,15},{8,0},{9,1},... | collective-permute-start | bytes 589832 | tf_op jit(solution)/shard_map/ppermute | solution.py:190
  32.4 25.0 %collective-permute-start.2 = (bf16[768,256]{1,0:T(8,128)(2,1)}, bf16[768,256]{1,0:T(8,128)(2,1)}, u32[]{:S(2)}, u32[]{:S(2)}) collective-permute-start(bf16[768,256]{1,0:T(8,128)(2,1)} %maximum_select_fusion), channel_id=1, source_target_pairs={{0,7},{1,0},{2,1},{3,2},{4,3},{5,4},{6,5},{7,6},{8,15},{9,8},{10,9... | collective-permute-start | bytes 1179656 | tf_op jit(solution)/shard_map/ppermute | solution.py:187
  41.8 21.9 %collective-permute-start.1 = (bf16[768,256]{1,0:T(8,128)(2,1)}, bf16[768,256]{1,0:T(8,128)(2,1)}, u32[]{:S(2)}, u32[]{:S(2)}) collective-permute-start(bf16[768,256]{1,0:T(8,128)(2,1)} %maximum_select_fusion), channel_id=1, source_target_pairs={{0,1},{1,2},{2,3},{3,4},{4,5},{5,6},{6,7},{7,0},{8,9},{9,10},{10,1... | collective-permute-start | bytes 1179656 | tf_op jit(solution)/shard_map/ppermute | solution.py:187
  44.0 1.6 copy-start.2
  56.6 0.8 copy-start.22
  57.4 12.2 %copy-start.6 = (bf16[384,768]{1,0:T(8,128)(2,1)}, bf16[384,768]{1,0:T(8,128)(2,1)S(1)}, u32[]{:S(2)}) copy-start(bf16[384,768]{1,0:T(8,128)(2,1)S(1)} %get-tuple-element.33.mat_ref) | copy-start | bytes 1769476
  57.4 12.3 %copy-start.8 = (bf16[768,384]{1,0:T(8,128)(2,1)}, bf16[768,384]{1,0:T(8,128)(2,1)S(1)}, u32[]{:S(2)}) copy-start(bf16[768,384]{1,0:T(8,128)(2,1)S(1)} %get-tuple-element.44) | copy-start | bytes 1769476
  57.4 12.3 %copy-start.10 = (bf16[768,384]{1,0:T(8,128)(2,1)}, bf16[768,384]{1,0:T(8,128)(2,1)S(1)}, u32[]{:S(2)}) copy-start(bf16[768,384]{1,0:T(8,128)(2,1)S(1)} %get-tuple-element.40) | copy-start | bytes 1769476
  57.4 12.3 %copy-start.12 = (bf16[768,384]{1,0:T(8,128)(2,1)}, bf16[768,384]{1,0:T(8,128)(2,1)S(1)}, u32[]{:S(2)}) copy-start(bf16[768,384]{1,0:T(8,128)(2,1)S(1)} %get-tuple-element.45) | copy-start | bytes 1769476
  57.4 12.3 %copy-start.14 = (bf16[768,384]{1,0:T(8,128)(2,1)}, bf16[768,384]{1,0:T(8,128)(2,1)S(1)}, u32[]{:S(2)}) copy-start(bf16[768,384]{1,0:T(8,128)(2,1)S(1)} %get-tuple-element.41) | copy-start | bytes 1769476
  57.4 12.3 %copy-start.16 = (bf16[768,384]{1,0:T(8,128)(2,1)}, bf16[768,384]{1,0:T(8,128)(2,1)S(1)}, u32[]{:S(2)}) copy-start(bf16[768,384]{1,0:T(8,128)(2,1)S(1)} %get-tuple-element.46) | copy-start | bytes 1769476
  57.4 12.3 %copy-start.18 = (bf16[768,384]{1,0:T(8,128)(2,1)}, bf16[768,384]{1,0:T(8,128)(2,1)S(1)}, u32[]{:S(2)}) copy-start(bf16[768,384]{1,0:T(8,128)(2,1)S(1)} %get-tuple-element.42) | copy-start | bytes 1769476
  57.4 12.3 %copy-start.20 = (bf16[768,384]{1,0:T(8,128)(2,1)}, bf16[768,384]{1,0:T(8,128)(2,1)S(1)}, u32[]{:S(2)}) copy-start(bf16[768,384]{1,0:T(8,128)(2,1)S(1)} %get-tuple-element.43) | copy-start | bytes 1769476
  57.5 12.3 %collective-permute-start.4 = (bf16[768,256]{1,0:T(8,128)(2,1)}, bf16[768,256]{1,0:T(8,128)(2,1)S(1)}, u32[]{:S(2)}, u32[]{:S(2)}) collective-permute-start(bf16[768,256]{1,0:T(8,128)(2,1)} %collective-permute-done.2), channel_id=1, source_target_pairs={{0,7},{1,0},{2,1},{3,2},{4,3},{5,4},{6,5},{7,6},{8,15},{9,8},{10,9... | collective-permute-start | bytes 1179656 | tf_op jit(solution)/shard_map/ppermute | solution.py:187
  63.7 11.1 %collective-permute-start.3 = (bf16[768,256]{1,0:T(8,128)(2,1)}, bf16[768,256]{1,0:T(8,128)(2,1)S(1)}, u32[]{:S(2)}, u32[]{:S(2)}) collective-permute-start(bf16[768,256]{1,0:T(8,128)(2,1)} %collective-permute-done.1), channel_id=1, source_target_pairs={{0,1},{1,2},{2,3},{3,4},{4,5},{5,6},{6,7},{7,0},{8,9},{9,10},{10,1... | collective-permute-start | bytes 1179656 | tf_op jit(solution)/shard_map/ppermute | solution.py:187
  69.7 18.1 %collective-permute-start.6 = (bf16[768,256]{1,0:T(8,128)(2,1)S(1)}, bf16[768,256]{1,0:T(8,128)(2,1)S(1)}, u32[]{:S(2)}, u32[]{:S(2)}) collective-permute-start(bf16[768,256]{1,0:T(8,128)(2,1)S(1)} %collective-permute-done.4), channel_id=1, source_target_pairs={{0,7},{1,0},{2,1},{3,2},{4,3},{5,4},{6,5},{7,6},{8,15},{9,8},{10,9... | collective-permute-start | bytes 1179656 | tf_op jit(solution)/shard_map/ppermute | solution.py:187
  74.9 11.0 %collective-permute-start.5 = (bf16[768,256]{1,0:T(8,128)(2,1)S(1)}, bf16[768,256]{1,0:T(8,128)(2,1)S(1)}, u32[]{:S(2)}, u32[]{:S(2)}) collective-permute-start(bf16[768,256]{1,0:T(8,128)(2,1)S(1)} %collective-permute-done.3), channel_id=1, source_target_pairs={{0,1},{1,2},{2,3},{3,4},{4,5},{5,6},{6,7},{7,0},{8,9},{9,10},{10,1... | collective-permute-start | bytes 1179656 | tf_op jit(solution)/shard_map/ppermute | solution.py:187
  77.5 19.4 %copy-start.7 = (bf16[384,768]{1,0:T(8,128)(2,1)S(1)}, bf16[384,768]{1,0:T(8,128)(2,1)}, u32[]{:S(2)}) copy-start(bf16[384,768]{1,0:T(8,128)(2,1)} %copy-done.6) | copy-start | bytes 1769476
  77.5 19.4 %copy-start.27 = (bf16[384,256]{1,0:T(8,128)(2,1)S(1)}, bf16[384,256]{1,0:T(8,128)(2,1)}, u32[]{:S(2)}) copy-start(bf16[384,256]{1,0:T(8,128)(2,1)} %cotangent_ref.1) | copy-start | bytes 589828
  77.5 19.4 %copy-start.36 = (f32[256]{0:T(256)S(1)}, f32[256]{0:T(256)}, u32[]{:S(2)}) copy-start(f32[256]{0:T(256)} %param.13) | copy-start | bytes 3076
  85.9 8.8 %collective-permute-start.7 = (bf16[384,256]{1,0:T(8,128)(2,1)S(1)}, bf16[384,256]{1,0:T(8,128)(2,1)S(1)}, u32[]{:S(2)}, u32[]{:S(2)}) collective-permute-start(bf16[384,256]{1,0:T(8,128)(2,1)S(1)} %slice.44), channel_id=1, source_target_pairs={{0,1},{1,2},{2,3},{3,4},{4,5},{5,6},{6,7},{7,0},{8,9},{9,10},{10,1... | collective-permute-start | bytes 589832 | tf_op jit(solution)/shard_map/ppermute | solution.py:187
  87.9 8.3 %collective-permute-start.8 = (bf16[384,256]{1,0:T(8,128)(2,1)S(1)}, bf16[384,256]{1,0:T(8,128)(2,1)S(1)}, u32[]{:S(2)}, u32[]{:S(2)}) collective-permute-start(bf16[384,256]{1,0:T(8,128)(2,1)S(1)} %slice.45), channel_id=1, source_target_pairs={{0,7},{1,0},{2,1},{3,2},{4,3},{5,4},{6,5},{7,6},{8,15},{9,8},{10,9... | collective-permute-start | bytes 589832 | tf_op jit(solution)/shard_map/ppermute | solution.py:187
  94.7 0.7 copy-start.28
  96.2 0.7 copy-start.30
  96.9 1.9 %copy-start = (bf16[384,4096]{1,0:T(8,128)(2,1)S(1)}, bf16[384,4096]{1,0:T(8,128)(2,1)}, u32[]{:S(2)}) copy-start(bf16[384,4096]{1,0:T(8,128)(2,1)} %get-tuple-element.34.ahead_ref) | copy-start | bytes 9437188
  98.7 1.9 copy-start.1
  100.6 0.9 copy-start.29
  101.6 0.9 copy-start.31
  107.4 1.3 copy-start.4
  108.7 16.0 %copy-start.21 = (bf16[768,384]{1,0:T(8,128)(2,1)S(1)}, bf16[768,384]{1,0:T(8,128)(2,1)}, u32[]{:S(2)}) copy-start(bf16[768,384]{1,0:T(8,128)(2,1)} %copy-done.20) | copy-start | bytes 1769476
  108.7 18.3 %copy-start.19 = (bf16[768,384]{1,0:T(8,128)(2,1)S(1)}, bf16[768,384]{1,0:T(8,128)(2,1)}, u32[]{:S(2)}) copy-start(bf16[768,384]{1,0:T(8,128)(2,1)} %copy-done.18) | copy-start | bytes 1769476
  108.7 77.9 %all-to-all-start.1 = ((bf16[32,128,256]{2,1,0:T(8,128)(2,1)}), bf16[32,128,256]{2,1,0:T(8,128)(2,1)S(1)}, u32[]{:S(2)}, u32[]{:S(2)}) async-start(bf16[32,128,256]{2,1,0:T(8,128)(2,1)} %copy-done.4), calls=%async_computation.1 | async-start | bytes 4194304 | tf_op jit(solution)/shard_map/all_to_all | solution.py:289
  124.7 8.4 %copy-start.17 = (bf16[768,384]{1,0:T(8,128)(2,1)S(1)}, bf16[768,384]{1,0:T(8,128)(2,1)}, u32[]{:S(2)}) copy-start(bf16[768,384]{1,0:T(8,128)(2,1)} %copy-done.16) | copy-start | bytes 1769476
  125.1 10.8 %collective-permute-start.9 = (bf16[384,256]{1,0:T(8,128)(2,1)S(1)}, bf16[384,256]{1,0:T(8,128)(2,1)S(1)}, u32[]{:S(2)}, u32[]{:S(2)}) collective-permute-start(bf16[384,256]{1,0:T(8,128)(2,1)S(1)} %get-tuple-element.48), channel_id=1, source_target_pairs={{0,1},{1,2},{2,3},{3,4},{4,5},{5,6},{6,7},{7,0},{8,9},{9,10},{10,1... | collective-permute-start | bytes 589832 | tf_op jit(solution)/shard_map/ppermute | solution.py:187
  127.4 10.6 %collective-permute-start.13 = (bf16[384,256]{1,0:T(8,128)(2,1)S(1)}, bf16[384,256]{1,0:T(8,128)(2,1)S(1)}, u32[]{:S(2)}, u32[]{:S(2)}) collective-permute-start(bf16[384,256]{1,0:T(8,128)(2,1)S(1)} %get-tuple-element.49), channel_id=1, source_target_pairs={{0,7},{1,0},{2,1},{3,2},{4,3},{5,4},{6,5},{7,6},{8,15},{9,8},{10,9... | collective-permute-start | bytes 589832 | tf_op jit(solution)/shard_map/ppermute | solution.py:187
  133.4 16.5 %copy-start.15 = (bf16[768,384]{1,0:T(8,128)(2,1)S(1)}, bf16[768,384]{1,0:T(8,128)(2,1)}, u32[]{:S(2)}) copy-start(bf16[768,384]{1,0:T(8,128)(2,1)} %copy-done.14) | copy-start | bytes 1769476
  135.9 16.2 %copy-start.13 = (bf16[768,384]{1,0:T(8,128)(2,1)S(1)}, bf16[768,384]{1,0:T(8,128)(2,1)}, u32[]{:S(2)}) copy-start(bf16[768,384]{1,0:T(8,128)(2,1)} %copy-done.12) | copy-start | bytes 1769476
  136.0 13.9 %collective-permute-start.10 = (bf16[768,256]{1,0:T(8,128)(2,1)S(1)}, bf16[768,256]{1,0:T(8,128)(2,1)S(1)}, u32[]{:S(2)}, u32[]{:S(2)}) collective-permute-start(bf16[768,256]{1,0:T(8,128)(2,1)S(1)} %pad_maximum_fusion), channel_id=1, source_target_pairs={{0,1},{1,2},{2,3},{3,4},{4,5},{5,6},{6,7},{7,0},{8,9},{9,10},{10,1... | collective-permute-start | bytes 1179656 | tf_op jit(solution)/shard_map/ppermute | solution.py:187
  138.1 25.0 %copy-start.11 = (bf16[768,384]{1,0:T(8,128)(2,1)S(1)}, bf16[768,384]{1,0:T(8,128)(2,1)}, u32[]{:S(2)}) copy-start(bf16[768,384]{1,0:T(8,128)(2,1)} %copy-done.10) | copy-start | bytes 1769476
  138.2 14.0 %collective-permute-start.14 = (bf16[768,256]{1,0:T(8,128)(2,1)S(1)}, bf16[768,256]{1,0:T(8,128)(2,1)S(1)}, u32[]{:S(2)}, u32[]{:S(2)}) collective-permute-start(bf16[768,256]{1,0:T(8,128)(2,1)S(1)} %pad_maximum_fusion.1), channel_id=1, source_target_pairs={{0,7},{1,0},{2,1},{3,2},{4,3},{5,4},{6,5},{7,6},{8,15},{9,8},{10,9... | collective-permute-start | bytes 1179656 | tf_op jit(solution)/shard_map/ppermute | solution.py:187
  149.9 15.5 %copy-start.9 = (bf16[768,384]{1,0:T(8,128)(2,1)S(1)}, bf16[768,384]{1,0:T(8,128)(2,1)}, u32[]{:S(2)}) copy-start(bf16[768,384]{1,0:T(8,128)(2,1)} %copy-done.8) | copy-start | bytes 1769476
  150.3 12.9 %collective-permute-start.11 = (bf16[768,256]{1,0:T(8,128)(2,1)S(1)}, bf16[768,256]{1,0:T(8,128)(2,1)S(1)}, u32[]{:S(2)}, u32[]{:S(2)}) collective-permute-start(bf16[768,256]{1,0:T(8,128)(2,1)S(1)} %fusion.2), channel_id=1, source_target_pairs={{0,1},{1,2},{2,3},{3,4},{4,5},{5,6},{6,7},{7,0},{8,9},{9,10},{10,1... | collective-permute-start | bytes 1179656 | tf_op jit(solution)/shard_map/ppermute | solution.py:187
  152.2 24.9 %copy-start.23 = (bf16[768,384]{1,0:T(8,128)(2,1)S(1)}, bf16[768,384]{1,0:T(8,128)(2,1)}, u32[]{:S(2)}) copy-start(bf16[768,384]{1,0:T(8,128)(2,1)} %copy-done.22) | copy-start | bytes 1769476
  152.6 12.8 %collective-permute-start.15 = (bf16[768,256]{1,0:T(8,128)(2,1)S(1)}, bf16[768,256]{1,0:T(8,128)(2,1)S(1)}, u32[]{:S(2)}, u32[]{:S(2)}) collective-permute-start(bf16[768,256]{1,0:T(8,128)(2,1)S(1)} %fusion.4), channel_id=1, source_target_pairs={{0,7},{1,0},{2,1},{3,2},{4,3},{5,4},{6,5},{7,6},{8,15},{9,8},{10,9... | collective-permute-start | bytes 1179656 | tf_op jit(solution)/shard_map/ppermute | solution.py:187
  163.5 11.9 %collective-permute-start.12 = (bf16[768,256]{1,0:T(8,128)(2,1)S(1)}, bf16[768,256]{1,0:T(8,128)(2,1)S(1)}, u32[]{:S(2)}, u32[]{:S(2)}) collective-permute-start(bf16[768,256]{1,0:T(8,128)(2,1)S(1)} %fusion.1), channel_id=1, source_target_pairs={{0,1},{1,2},{2,3},{3,4},{4,5},{5,6},{6,7},{7,0},{8,9},{9,10},{10,1... | collective-permute-start | bytes 1179656 | tf_op jit(solution)/shard_map/ppermute | solution.py:187
  165.8 20.8 %copy-start.25 = (bf16[256,256]{1,0:T(8,128)(2,1)S(1)}, bf16[256,256]{1,0:T(8,128)(2,1)}, u32[]{:S(2)}) copy-start(bf16[256,256]{1,0:T(8,128)(2,1)} %weight_ref.3) | copy-start | bytes 393220
  165.8 20.8 %copy-start.33 = (s32[1,1,32]{2,1,0:T(1,128)S(1)}, s32[1,1,32]{2,1,0:T(1,128)}, u32[]{:S(2)}) copy-start(s32[1,1,32]{2,1,0:T(1,128)} %param.19) | copy-start | bytes 388
  165.8 20.8 %copy-start.35 = (s32[1,1,32]{2,1,0:T(1,128)S(1)}, s32[1,1,32]{2,1,0:T(1,128)}, u32[]{:S(2)}) copy-start(s32[1,1,32]{2,1,0:T(1,128)} %param.20) | copy-start | bytes 388
  165.8 11.3 %collective-permute-start.16 = (bf16[768,256]{1,0:T(8,128)(2,1)S(1)}, bf16[768,256]{1,0:T(8,128)(2,1)S(1)}, u32[]{:S(2)}, u32[]{:S(2)}) collective-permute-start(bf16[768,256]{1,0:T(8,128)(2,1)S(1)} %fusion.3), channel_id=1, source_target_pairs={{0,7},{1,0},{2,1},{3,2},{4,3},{5,4},{6,5},{7,6},{8,15},{9,8},{10,9... | collective-permute-start | bytes 1179656 | tf_op jit(solution)/shard_map/ppermute | solution.py:187
  177.6 9.1 %collective-permute-start.17 = (bf16[384,256]{1,0:T(8,128)(2,1)S(1)}, bf16[384,256]{1,0:T(8,128)(2,1)S(1)}, u32[]{:S(2)}, u32[]{:S(2)}) collective-permute-start(bf16[384,256]{1,0:T(8,128)(2,1)S(1)} %select_convert_fusion), channel_id=1, source_target_pairs={{0,8},{1,9},{2,10},{3,11},{4,12},{5,13},{6,14},{7,15},{8,0},{9,1},... | collective-permute-start | bytes 589832 | tf_op jit(solution)/shard_map/ppermute | solution.py:190

commit v2 on v0

v2 whole, which is shorter than its diff:
```python
import jax
import jax.numpy as jnp
from jax import lax
from jax.experimental import pallas as pl
from jax.experimental.pallas import tpu as pltpu
from jax.sharding import PartitionSpec as P

BF, F32 = jnp.bfloat16, jnp.float32
TILE = 128
FAR = 2
CHUNKS = 4
VMEM_LIMIT = 16 * 1024 * 1024


def spec(space):
    return pl.BlockSpec(memory_space=space)


SMEM, VMEM, HBM = spec(pltpu.SMEM), spec(pltpu.VMEM), spec(pltpu.HBM)


def call(kernel, name, out_shape, in_specs, out_specs, scratch=(), flops=0, moved=0):
    return pl.pallas_call(
        kernel,
        out_shape=out_shape,
        in_specs=in_specs,
        out_specs=out_specs,
        scratch_shapes=scratch,
        compiler_params=pltpu.CompilerParams(vmem_limit_bytes=VMEM_LIMIT),
        cost_estimate=pl.CostEstimate(flops=flops, bytes_accessed=moved, transcendentals=0),
        name=name,
    )


def in_hbm(value):
    return pltpu.with_memory_space_constraint(value, pltpu.HBM)


def product(left, right):
    return jnp.dot(left, right, preferred_element_type=F32)


def silu_parts(preact):
    sigmoid = 1.0 / (1.0 + jnp.exp(-preact))
    return (preact * sigmoid, sigmoid * (1.0 + preact * (1.0 - sigmoid)))


def project_kernel(features_hbm, weight_hbm, projected_ref, features, weight, sems):
    copies = [
        pltpu.make_async_copy(features_hbm, features, sems.at[0]),
        pltpu.make_async_copy(weight_hbm, weight, sems.at[1]),
    ]
    for copy in copies:
        copy.start()
    for copy in copies:
        copy.wait()
    projected_ref[...] = product(features[...], weight[...]).astype(BF)


def fill_kernel(blk_ref, live_ref, projected_ref, outgoing_hbm, zeros, sems):
    zeros[...] = jnp.zeros(zeros.shape, BF)
    parts = outgoing_hbm.shape[0]

    def start(part, carried):
        @pl.when(live_ref[part] > 0)
        def _():
            row = pl.multiple_of(blk_ref[part] * TILE, TILE)
            pltpu.make_async_copy(
                projected_ref.at[pl.ds(row, TILE)], outgoing_hbm.at[part], sems.at[part]
            ).start()

        @pl.when(live_ref[part] <= 0)
        def _():
            pltpu.make_async_copy(zeros, outgoing_hbm.at[part], sems.at[part]).start()

        return carried

    def wait(part, carried):
        pltpu.make_async_copy(zeros, outgoing_hbm.at[part], sems.at[part]).wait()
        return carried

    lax.fori_loop(0, parts, start, 0)
    lax.fori_loop(0, parts, wait, 0)


def spread_kernel(ring, blocks, pos_ref, count_ref, place_ref, tiles_ref, *outs):
    rows = blocks * TILE
    place = place_ref[0]
    for offset in range(ring):
        dense = outs[offset]
        dense[...] = jnp.zeros(dense.shape, BF)
        spot = lax.rem(place + offset, ring)
        for half in range(FAR):
            source = half * ring + spot

            def put(slot, carried, dense=dense, half=half, source=source):
                position = pos_ref[source * tiles_ref.shape[1] + slot]
                target = pl.multiple_of(position // blocks * TILE, TILE)
                origin = pl.multiple_of(half * rows + position % blocks * TILE, TILE)
                dense[pl.ds(target, TILE), pl.ds(origin, TILE)] = tiles_ref[source, slot]
                return carried

            lax.fori_loop(0, count_ref[source], put, 0)


def spread_cut_kernel(dst_ref, cut_ref, dense):
    dense[...] = jnp.zeros(dense.shape, BF)

    def put(part, carried):
        target = pl.multiple_of(dst_ref[part] * TILE, TILE)
        origin = pl.multiple_of(part * TILE, TILE)
        dense[pl.ds(target, TILE), pl.ds(origin, TILE)] = cut_ref[part]
        return carried

    lax.fori_loop(0, cut_ref.shape[0], put, 0)


def middle_kernel(
    sum_ref, mat_ref, low_ref, high_ref, bias_ref, cotangent_ref, cut_ref, far_ref, hidden_ref, grad_ref
):
    rows, width = sum_ref.shape
    chunk = far_ref.shape[0] // CHUNKS
    total = (
        sum_ref[...]
        + product(mat_ref[:, :rows], low_ref[...])
        + product(mat_ref[:, rows:], high_ref[...])
    )
    for piece in range(CHUNKS):
        arrived = far_ref[pl.ds(piece * chunk, chunk)].reshape(chunk * TILE, width)
        total += product(cut_ref[:, pl.ds(piece * chunk * TILE, chunk * TILE)], arrived)
    activated, derivative = silu_parts(total + bias_ref[...])
    hidden_ref[...] = activated.astype(BF)
    grad_ref[...] = (cotangent_ref[...].astype(F32) * derivative).T.astype(BF)


def terms_kernel(grad_ref, cut_ref, terms_hbm, terms, sems):
    chunk = terms.shape[0] // CHUNKS
    copies = []
    for piece in range(CHUNKS):
        columns = pl.ds(piece * chunk * TILE, chunk * TILE)
        result = product(grad_ref[...], cut_ref[:, columns]).astype(BF)
        for slot in range(chunk):
            terms[piece * chunk + slot] = result[:, slot * TILE : (slot + 1) * TILE]
        span = pl.ds(piece * chunk, chunk)
        copies.append(pltpu.make_async_copy(terms.at[span], terms_hbm.at[span], sems.at[piece]))
        copies[-1].start()
    for copy in copies:
        copy.wait()


def gather_kernel(blk_ref, live_ref, arrived_ref, total_ref):
    total_ref[...] = jnp.zeros(total_ref.shape, F32)

    def add(part, carried):
        @pl.when(live_ref[part] > 0)
        def _():
            columns = pl.ds(pl.multiple_of(blk_ref[part] * TILE, TILE), TILE)
            total_ref[:, columns] += arrived_ref[part].astype(F32)

        return carried

    lax.fori_loop(0, arrived_ref.shape[0], add, 0)


def last_kernel(own_ref, other_ref, cut_ref, weight_ref, out_ref):
    total = own_ref[...] + other_ref[...].astype(F32) + cut_ref[...]
    out_ref[...] = lax.dot_general(
        total.T.astype(BF), weight_ref[...], (((1,), (1,)), ((), ())), preferred_element_type=F32
    ).astype(BF)


def on_device(
    features,
    weight,
    bias,
    cotangent,
    in_tiles,
    in_pos,
    in_count,
    cut_tiles,
    send_blk,
    send_live,
    recv_dst,
):
    rows, width = features.shape
    blocks = rows // TILE
    peers = lax.axis_size("blk")
    parts = lax.axis_size("dom")
    ring = peers // FAR
    reach = ring // 2
    me = lax.axis_index("blk")
    place, half = me % ring, me // ring
    wide = FAR * rows
    send_to, is_live, dst = send_blk[0, 0], send_live[0, 0], recv_dst[0, 0]
    shape = jax.ShapeDtypeStruct

    def along_ring(value, by):
        moves = [
            (side * ring + spot, side * ring + (spot + by) % ring)
            for side in range(FAR)
            for spot in range(ring)
        ]
        return lax.ppermute(value, "blk", moves)

    def across(value):
        return lax.ppermute(value, "blk", [(i, (i + ring) % peers) for i in range(peers)])

    projected = call(
        project_kernel,
        "project",
        shape((rows, width), BF),
        [HBM, HBM],
        VMEM,
        [
            pltpu.VMEM(features.shape, BF),
            pltpu.VMEM(weight.shape, BF),
            pltpu.SemaphoreType.DMA((2,)),
        ],
    )(in_hbm(features), in_hbm(weight))
    partner = across(projected)
    outgoing = call(
        fill_kernel,
        "fill",
        pltpu.HBM((parts, TILE, width), BF),
        [SMEM, SMEM, VMEM],
        HBM,
        [pltpu.VMEM((TILE, width), BF), pltpu.SemaphoreType.DMA((parts,))],
    )(send_to, is_live, projected)
    incoming = lax.all_to_all(outgoing, "dom", split_axis=0, concat_axis=0, tiled=True)

    dense = call(
        lambda *refs: spread_kernel(ring, blocks, *refs),
        "spread",
        tuple([shape((rows, wide), BF)] * ring),
        [SMEM, SMEM, SMEM, VMEM],
        tuple([VMEM] * ring),
        moved=10 << 20,
    )(in_pos[0, 0].reshape(-1), in_count[0, 0], place.reshape(1), in_tiles[0, 0])
    dense_cut = call(
        spread_cut_kernel,
        "spread_cut",
        shape((rows, parts * TILE), BF),
        [SMEM, VMEM],
        VMEM,
        moved=6 << 20,
    )(dst, cut_tiles[0, 0])

    pair = jnp.where(
        half == 0,
        jnp.concatenate([projected, partner]),
        jnp.concatenate([partner, projected]),
    )
    running = product(dense[0], pair)
    right = left = pair
    for hop in range(1, reach):
        right, left = along_ring(right, 1), along_ring(left, -1)
        running = running + product(dense[ring - hop], right)
        running = running + product(dense[hop], left)
    low, high = along_ring(right[:rows], 1), along_ring(left[rows:], -1)

    hidden, grad_pre = call(
        middle_kernel,
        "middle",
        (shape((rows, width), BF), shape((width, rows), BF)),
        [VMEM] * 8,
        (VMEM, VMEM),
    )(
        running,
        dense[reach],
        low,
        high,
        bias.reshape(1, width),
        cotangent,
        dense_cut,
        incoming,
    )

    farthest = product(grad_pre, dense[reach]).astype(BF)
    low, high = along_ring(farthest[:, :rows], 1), along_ring(farthest[:, rows:], -1)
    terms = call(
        terms_kernel,
        "terms",
        pltpu.HBM((parts, width, TILE), BF),
        [VMEM, VMEM],
        HBM,
        [pltpu.VMEM((parts, width, TILE), BF), pltpu.SemaphoreType.DMA((CHUNKS,))],
        flops=2 * rows * width * parts * TILE,
        moved=6 << 20,
    )(grad_pre, dense_cut)
    returned = lax.all_to_all(terms, "dom", split_axis=0, concat_axis=0, tiled=True)
    for hop in range(reach - 1, 0, -1):
        right = product(grad_pre, dense[hop])
        left = product(grad_pre, dense[ring - hop])
        if hop == reach - 1:
            right = jnp.concatenate([right[:, :rows] + low.astype(F32), right[:, rows:]], axis=1)
            left = jnp.concatenate([left[:, :rows], left[:, rows:] + high.astype(F32)], axis=1)
        else:
            right, left = right + from_left.astype(F32), left + from_right.astype(F32)
        from_left = along_ring(right.astype(BF), 1)
        from_right = along_ring(left.astype(BF), -1)
    both = product(grad_pre, dense[0]) + from_left.astype(F32) + from_right.astype(F32)
    own = jnp.where(half == 0, both[:, :rows], both[:, rows:])
    other = across(jnp.where(half == 0, both[:, rows:], both[:, :rows]).astype(BF))
    from_cuts = call(
        gather_kernel, "gather", shape((width, rows), F32), [SMEM, SMEM, VMEM], VMEM, moved=2 << 20
    )(send_to, is_live, returned)
    grad_features = call(
        last_kernel, "last", shape((rows, width), BF), [VMEM] * 4, VMEM
    )(own, other, from_cuts, weight)
    return (hidden, grad_features)


def solution(mesh):
    in_specs = (
        P(("dom", "blk"), None),
        P(),
        P(),
        P(("dom", "blk"), None),
        P("dom", "blk", None, None, None, None),
        P("dom", "blk", None, None),
        P("dom", "blk", None),
        P("dom", "blk", None, None, None),
        P("dom", "blk", None),
        P("dom", "blk", None),
        P("dom", "blk", None),
    )
    out_specs = (P(("dom", "blk"), None), P(("dom", "blk"), None))
    return jax.shard_map(
        on_device, mesh=mesh, in_specs=in_specs, out_specs=out_specs, check_vma=False
    )
```

time: 587 us -> 176 us (0.30)
  the two profiles are of different devices: /device:TPU:12 before, /device:TPU:2 now
where the time goes in v2:
time: 176 us; the launch traced here: 175 us
  starting transfers between devices  93.5 us (53%)
  waiting for transfers between devices  47 us (27%)
  Pallas kernels  14.4 us (8%)
  matrix products  9.13 us (5%)
  local copies, waits for them, and re-layouts  8.68 us (5%)
    ppermute x16, starting transfers between devices, along_ring(): return lax.ppermute(value, 'blk', moves)  61.7 us
    ppermute x16, waiting for transfers between devices, along_ring(): return lax.ppermute(value, 'blk', moves)  30.6 us
    ppermute x2, waiting for transfers between devices, across(): lax.ppermute(value, 'blk', [(i, (i + ring) % peers) for i in range(peers)])  16.4 us
    all_to_all x1, starting transfers between devices, on_device(): lax.all_to_all(terms, 'dom', split_axis=0, concat_axis=0, tiled=True)  15.7 us
    all_to_all x1, starting transfers between devices, on_device(): lax.all_to_all(outgoing, 'dom', split_axis=0, concat_axis=0, tiled=True)  10.4 us
    dot_general x15, matrix products, product(): return jnp.dot(left, right, preferred_element_type=F32)  9.13 us
    unnamed x67, local copies, waits for them, and re-layouts  8.48 us
    ppermute x2, starting transfers between devices, across(): lax.ppermute(value, 'blk', [(i, (i + ring) % peers) for i in range(peers)])  5.77 us
  transfers between devices with their start and end apart: 20, of which 11 were waited for; matrix products, arithmetic and copies ran while one was open for 6% of the time, Pallas kernels for 2%

profile of v2, /device:TPU:2, one launch (start us, length us, event | category | flops | bytes accessed | tf_op | source)
XLA Modules:
  0.0 174.6 jit_solution(6745892950081269054)
XLA Ops:
  0.6 1.2 project.1.projected_ref
  1.9 0.6 copy-done.25
  2.5 0.7 copy-done.27
  3.2 2.2 %fill.1 = bf16[32,128,256]{2,1,0:T(8,128)(2,1)} custom-call(s32[32]{0:T(128)S(1)} %bitcast.42, s32[32]{0:T(128)S(1)} %bitcast.44, bf16[384,256]{1,0:T(8,128)(2,1)S(1)} %project.1.projected_ref), custom_call_target="tpu_custom_call" | custom-call | tf_op jit(solution)/shard_map/fill/pallas_call | solution.py:221
  5.4 10.4 %all-to-all-start = ((bf16[32,128,256]{2,1,0:T(8,128)(2,1)}), bf16[32,128,256]{2,1,0:T(8,128)(2,1)}, u32[]{:S(2)}, u32[]{:S(2)}) async-start(bf16[32,128,256]{2,1,0:T(8,128)(2,1)} %fill.1), calls=%async_computation | async-start | bytes 4194304 | tf_op jit(solution)/shard_map/all_to_all | solution.py:229
  15.8 2.4 %collective-permute-start = (bf16[384,256]{1,0:T(8,128)(2,1)S(1)}, bf16[384,256]{1,0:T(8,128)(2,1)S(1)}, u32[]{:S(2)}, u32[]{:S(2)}) collective-permute-start(bf16[384,256]{1,0:T(8,128)(2,1)S(1)} %project.1.projected_ref), channel_id=1, source_target_pairs={{0,8},{1,9},{2,10},{3,11},{4,12},{5,13},{6,14},{7,15},{8,0},{9,1},... | collective-permute-start | bytes 589832 | tf_op jit(solution)/shard_map/ppermute | solution.py:206
  18.3 12.1 %collective-permute-done = bf16[384,256]{1,0:T(8,128)(2,1)S(1)} collective-permute-done((bf16[384,256]{1,0:T(8,128)(2,1)S(1)}, bf16[384,256]{1,0:T(8,128)(2,1)S(1)}, u32[]{:S(2)}, u32[]{:S(2)}) %collective-permute-start) | collective-permute-done | bytes 196640 | tf_op jit(solution)/shard_map/ppermute | solution.py:206
  30.5 9.3 %collective-permute-start.2 = (bf16[768,256]{1,0:T(8,128)(2,1)S(1)}, bf16[768,256]{1,0:T(8,128)(2,1)}, u32[]{:S(2)}, u32[]{:S(2)}) collective-permute-start(bf16[768,256]{1,0:T(8,128)(2,1)S(1)} %maximum_select_fusion), channel_id=1, source_target_pairs={{0,7},{1,0},{2,1},{3,2},{4,3},{5,4},{6,5},{7,6},{8,15},{9,8},{10,9... | collective-permute-start | bytes 1179656 | tf_op jit(solution)/shard_map/ppermute | solution.py:203
  39.8 1.9 %collective-permute-start.1 = (bf16[768,256]{1,0:T(8,128)(2,1)S(1)}, bf16[768,256]{1,0:T(8,128)(2,1)}, u32[]{:S(2)}, u32[]{:S(2)}) collective-permute-start(bf16[768,256]{1,0:T(8,128)(2,1)S(1)} %maximum_select_fusion), channel_id=1, source_target_pairs={{0,1},{1,2},{2,3},{3,4},{4,5},{5,6},{6,7},{7,0},{8,9},{9,10},{10,1... | collective-permute-start | bytes 1179656 | tf_op jit(solution)/shard_map/ppermute | solution.py:203
  41.9 1.2 copy-done.18
  43.2 1.1 spread_cut.1.cut_ref
  44.3 0.5 copy-done.16
  44.8 2.0 %spread.1 = (bf16[384,768]{1,0:T(8,128)(2,1)S(1)}, bf16[384,768]{1,0:T(8,128)(2,1)S(1)}, bf16[384,768]{1,0:T(8,128)(2,1)S(1)}, bf16[384,768]{1,0:T(8,128)(2,1)S(...) custom-call(s32[64]{0:T(128)S(1)} %reshape_squeeze.3.refs_0_, ...), custom_call_target="tpu_custom_call" | custom-call | bytes 10485760 | tf_op jit(solution)/shard_map/spread/pallas_call | solution.py:231
  46.8 5.0 %collective-permute-start.4 = (bf16[768,256]{1,0:T(8,128)(2,1)}, bf16[768,256]{1,0:T(8,128)(2,1)S(1)}, u32[]{:S(2)}, u32[]{:S(2)}) collective-permute-start(bf16[768,256]{1,0:T(8,128)(2,1)} %collective-permute-done.2), channel_id=1, source_target_pairs={{0,7},{1,0},{2,1},{3,2},{4,3},{5,4},{6,5},{7,6},{8,15},{9,8},{10,9... | collective-permute-start | bytes 1179656 | tf_op jit(solution)/shard_map/ppermute | solution.py:203
  51.9 1.9 %collective-permute-start.3 = (bf16[768,256]{1,0:T(8,128)(2,1)}, bf16[768,256]{1,0:T(8,128)(2,1)S(1)}, u32[]{:S(2)}, u32[]{:S(2)}) collective-permute-start(bf16[768,256]{1,0:T(8,128)(2,1)} %collective-permute-done.1), channel_id=1, source_target_pairs={{0,1},{1,2},{2,3},{3,4},{4,5},{5,6},{6,7},{7,0},{8,9},{9,10},{10,1... | collective-permute-start | bytes 1179656 | tf_op jit(solution)/shard_map/ppermute | solution.py:203
  53.8 1.3 fusion.11
  55.1 1.3 fusion.12
  56.5 0.3 fusion.7
  56.8 1.0 collective-permute-done.4
  57.8 5.5 %collective-permute-start.6 = (bf16[768,256]{1,0:T(8,128)(2,1)S(1)}, bf16[768,256]{1,0:T(8,128)(2,1)S(1)}, u32[]{:S(2)}, u32[]{:S(2)}) collective-permute-start(bf16[768,256]{1,0:T(8,128)(2,1)S(1)} %collective-permute-done.4), channel_id=1, source_target_pairs={{0,7},{1,0},{2,1},{3,2},{4,3},{5,4},{6,5},{7,6},{8,15},{9,8},{10,9... | collective-permute-start | bytes 1179656 | tf_op jit(solution)/shard_map/ppermute | solution.py:203
  63.3 1.9 %collective-permute-start.5 = (bf16[768,256]{1,0:T(8,128)(2,1)S(1)}, bf16[768,256]{1,0:T(8,128)(2,1)S(1)}, u32[]{:S(2)}, u32[]{:S(2)}) collective-permute-start(bf16[768,256]{1,0:T(8,128)(2,1)S(1)} %collective-permute-done.3), channel_id=1, source_target_pairs={{0,1},{1,2},{2,3},{3,4},{4,5},{5,6},{6,7},{7,0},{8,9},{9,10},{10,1... | collective-permute-start | bytes 1179656 | tf_op jit(solution)/shard_map/ppermute | solution.py:203
  65.3 0.3 fusion.13
  65.6 0.3 fusion.6
  65.9 8.2 %collective-permute-done.5 = bf16[768,256]{1,0:T(8,128)(2,1)S(1)} collective-permute-done((bf16[768,256]{1,0:T(8,128)(2,1)S(1)}, bf16[768,256]{1,0:T(8,128)(2,1)S(1)}, u32[]{:S(2)}, u32[]{:S(2)}) %collective-permute-start.5) | collective-permute-done | bytes 393248 | tf_op jit(solution)/shard_map/ppermute | solution.py:203
  74.2 1.9 %collective-permute-start.7 = (bf16[384,256]{1,0:T(8,128)(2,1)S(1)}, bf16[384,256]{1,0:T(8,128)(2,1)S(1)}, u32[]{:S(2)}, u32[]{:S(2)}) collective-permute-start(bf16[384,256]{1,0:T(8,128)(2,1)S(1)} %slice.44), channel_id=1, source_target_pairs={{0,1},{1,2},{2,3},{3,4},{4,5},{5,6},{6,7},{7,0},{8,9},{9,10},{10,1... | collective-permute-start | bytes 589832 | tf_op jit(solution)/shard_map/ppermute | solution.py:203
  76.2 5.1 %collective-permute-start.8 = (bf16[384,256]{1,0:T(8,128)(2,1)S(1)}, bf16[384,256]{1,0:T(8,128)(2,1)S(1)}, u32[]{:S(2)}, u32[]{:S(2)}) collective-permute-start(bf16[384,256]{1,0:T(8,128)(2,1)S(1)} %slice.45), channel_id=1, source_target_pairs={{0,7},{1,0},{2,1},{3,2},{4,3},{5,4},{6,5},{7,6},{8,15},{9,8},{10,9... | collective-permute-start | bytes 589832 | tf_op jit(solution)/shard_map/ppermute | solution.py:203
  81.3 0.3 fusion.14
  81.7 1.1 fusion.5.sum_ref
  82.8 0.2 collective-permute-done.7.low_ref
  83.0 0.7 copy-done.21
  83.7 0.8 collective-permute-done.8.high_ref
  84.5 0.7 copy-done.23
  85.2 1.1 copy-done.13
  86.2 1.0 copy-done.17
  87.2 0.9 copy-done.22
  88.2 0.9 copy-done.24
  89.1 3.5 %middle.1 = (bf16[384,256]{1,0:T(8,128)(2,1)}, bf16[256,384]{1,0:T(8,128)(2,1)S(1)}) custom-call(f32[384,256]{1,0:T(8,128)S(1)} %copy-done.17, bf16[384,768]{1,0:T(8,128)(2,1)S(1)} %copy-done.13, bf16[384,256]{1,0:T(8,128)(2,1)S(1)} %copy-done.22, bf16[384,256]{1,0:T(8,128)(2,1)S(1)} %copy-done.24, f32[1,256]{1,0:T(1,128)S(1)} %bitcast.46, ...), custom_call_target="tpu_custom_call" | custom-call | tf_op jit(solution)/shard_map/middle/pallas_call | solution.py:261
  92.6 2.1 %terms.1 = bf16[32,256,128]{2,1,0:T(8,128)(2,1)} custom-call(bf16[256,384]{1,0:T(8,128)(2,1)S(1)} %get-tuple-element.21.grad_ref, bf16[384,4096]{1,0:T(8,128)(2,1)S(1)} %spread_cut.1.cut_ref), custom_call_target="tpu_custom_call" | custom-call | flops 805306368 | bytes 6291456 | tf_op jit(solution)/shard_map/terms/pallas_call | solution.py:280
  94.7 15.7 %all-to-all-start.1 = ((bf16[32,256,128]{2,1,0:T(8,128)(2,1)}), bf16[32,256,128]{2,1,0:T(8,128)(2,1)S(1)}, u32[]{:S(2)}, u32[]{:S(2)}) async-start(bf16[32,256,128]{2,1,0:T(8,128)(2,1)} %terms.1), calls=%async_computation.1 | async-start | bytes 4194304 | tf_op jit(solution)/shard_map/all_to_all | solution.py:290
  110.4 1.5 convolution_convert_fusion
  112.0 1.9 %collective-permute-start.9 = (bf16[256,384]{1,0:T(8,128)(2,1)S(1)}, bf16[256,384]{1,0:T(8,128)(2,1)S(1)}, u32[]{:S(2)}, u32[]{:S(2)}) collective-permute-start(bf16[256,384]{1,0:T(8,128)(2,1)S(1)} %get-tuple-element.22), channel_id=1, source_target_pairs={{0,1},{1,2},{2,3},{3,4},{4,5},{5,6},{6,7},{7,0},{8,9},{9,10},{10,1... | collective-permute-start | bytes 589832 | tf_op jit(solution)/shard_map/ppermute | solution.py:203
  114.0 0.4 fusion.15
  114.4 5.6 %collective-permute-start.13 = (bf16[256,384]{1,0:T(8,128)(2,1)S(1)}, bf16[256,384]{1,0:T(8,128)(2,1)S(1)}, u32[]{:S(2)}, u32[]{:S(2)}) collective-permute-start(bf16[256,384]{1,0:T(8,128)(2,1)S(1)} %get-tuple-element.23), channel_id=1, source_target_pairs={{0,7},{1,0},{2,1},{3,2},{4,3},{5,4},{6,5},{7,6},{8,15},{9,8},{10,9... | collective-permute-start | bytes 589832 | tf_op jit(solution)/shard_map/ppermute | solution.py:203
  120.0 0.4 fusion.16
  120.4 2.4 %collective-permute-done.9 = bf16[256,384]{1,0:T(8,128)(2,1)S(1)} collective-permute-done((bf16[256,384]{1,0:T(8,128)(2,1)S(1)}, bf16[256,384]{1,0:T(8,128)(2,1)S(1)}, u32[]{:S(2)}, u32[]{:S(2)}) %collective-permute-start.9) | collective-permute-done | bytes 196640 | tf_op jit(solution)/shard_map/ppermute | solution.py:203
  122.9 2.1 %collective-permute-start.10 = (bf16[256,768]{1,0:T(8,128)(2,1)S(1)}, bf16[256,768]{1,0:T(8,128)(2,1)S(1)}, u32[]{:S(2)}, u32[]{:S(2)}) collective-permute-start(bf16[256,768]{1,0:T(8,128)(2,1)S(1)} %pad_maximum_fusion), channel_id=1, source_target_pairs={{0,1},{1,2},{2,3},{3,4},{4,5},{5,6},{6,7},{7,0},{8,9},{9,10},{10,1... | collective-permute-start | bytes 1179656 | tf_op jit(solution)/shard_map/ppermute | solution.py:203
  125.1 5.3 %collective-permute-start.14 = (bf16[256,768]{1,0:T(8,128)(2,1)S(1)}, bf16[256,768]{1,0:T(8,128)(2,1)S(1)}, u32[]{:S(2)}, u32[]{:S(2)}) collective-permute-start(bf16[256,768]{1,0:T(8,128)(2,1)S(1)} %pad_maximum_fusion.1), channel_id=1, source_target_pairs={{0,7},{1,0},{2,1},{3,2},{4,3},{5,4},{6,5},{7,6},{8,15},{9,8},{10,9... | collective-permute-start | bytes 1179656 | tf_op jit(solution)/shard_map/ppermute | solution.py:203
  130.4 6.4 %collective-permute-done.10 = bf16[256,768]{1,0:T(8,128)(2,1)S(1)} collective-permute-done((bf16[256,768]{1,0:T(8,128)(2,1)S(1)}, bf16[256,768]{1,0:T(8,128)(2,1)S(1)}, u32[]{:S(2)}, u32[]{:S(2)}) %collective-permute-start.10) | collective-permute-done | bytes 393248 | tf_op jit(solution)/shard_map/ppermute | solution.py:203
  136.8 0.4 fusion.2
  137.2 2.1 %collective-permute-start.11 = (bf16[256,768]{1,0:T(8,128)(2,1)S(1)}, bf16[256,768]{1,0:T(8,128)(2,1)S(1)}, u32[]{:S(2)}, u32[]{:S(2)}) collective-permute-start(bf16[256,768]{1,0:T(8,128)(2,1)S(1)} %fusion.2), channel_id=1, source_target_pairs={{0,1},{1,2},{2,3},{3,4},{4,5},{5,6},{6,7},{7,0},{8,9},{9,10},{10,1... | collective-permute-start | bytes 1179656 | tf_op jit(solution)/shard_map/ppermute | solution.py:203
  139.3 0.4 fusion.4
  139.7 5.1 %collective-permute-start.15 = (bf16[256,768]{1,0:T(8,128)(2,1)S(1)}, bf16[256,768]{1,0:T(8,128)(2,1)S(1)}, u32[]{:S(2)}, u32[]{:S(2)}) collective-permute-start(bf16[256,768]{1,0:T(8,128)(2,1)S(1)} %fusion.4), channel_id=1, source_target_pairs={{0,7},{1,0},{2,1},{3,2},{4,3},{5,4},{6,5},{7,6},{8,15},{9,8},{10,9... | collective-permute-start | bytes 1179656 | tf_op jit(solution)/shard_map/ppermute | solution.py:203
  144.8 5.4 %collective-permute-done.11 = bf16[256,768]{1,0:T(8,128)(2,1)S(1)} collective-permute-done((bf16[256,768]{1,0:T(8,128)(2,1)S(1)}, bf16[256,768]{1,0:T(8,128)(2,1)S(1)}, u32[]{:S(2)}, u32[]{:S(2)}) %collective-permute-start.11) | collective-permute-done | bytes 393248 | tf_op jit(solution)/shard_map/ppermute | solution.py:203
  150.2 0.4 fusion.1
  150.6 1.9 %collective-permute-start.12 = (bf16[256,768]{1,0:T(8,128)(2,1)S(1)}, bf16[256,768]{1,0:T(8,128)(2,1)S(1)}, u32[]{:S(2)}, u32[]{:S(2)}) collective-permute-start(bf16[256,768]{1,0:T(8,128)(2,1)S(1)} %fusion.1), channel_id=1, source_target_pairs={{0,1},{1,2},{2,3},{3,4},{4,5},{5,6},{6,7},{7,0},{8,9},{9,10},{10,1... | collective-permute-start | bytes 1179656 | tf_op jit(solution)/shard_map/ppermute | solution.py:203
  152.5 0.4 fusion.3
  152.9 5.1 %collective-permute-start.16 = (bf16[256,768]{1,0:T(8,128)(2,1)S(1)}, bf16[256,768]{1,0:T(8,128)(2,1)S(1)}, u32[]{:S(2)}, u32[]{:S(2)}) collective-permute-start(bf16[256,768]{1,0:T(8,128)(2,1)S(1)} %fusion.3), channel_id=1, source_target_pairs={{0,7},{1,0},{2,1},{3,2},{4,3},{5,4},{6,5},{7,6},{8,15},{9,8},{10,9... | collective-permute-start | bytes 1179656 | tf_op jit(solution)/shard_map/ppermute | solution.py:203
  158.1 4.4 %collective-permute-done.12 = bf16[256,768]{1,0:T(8,128)(2,1)S(1)} collective-permute-done((bf16[256,768]{1,0:T(8,128)(2,1)S(1)}, bf16[256,768]{1,0:T(8,128)(2,1)S(1)}, u32[]{:S(2)}, u32[]{:S(2)}) %collective-permute-start.12) | collective-permute-done | bytes 393248 | tf_op jit(solution)/shard_map/ppermute | solution.py:203
  162.5 1.6 collective-permute-done.16
  164.1 0.4 fusion
  164.6 3.3 %collective-permute-start.17 = (bf16[256,384]{1,0:T(8,128)(2,1)S(1)}, bf16[256,384]{1,0:T(8,128)(2,1)S(1)}, u32[]{:S(2)}, u32[]{:S(2)}) collective-permute-start(bf16[256,384]{1,0:T(8,128)(2,1)S(1)} %select_convert_fusion), channel_id=1, source_target_pairs={{0,8},{1,9},{2,10},{3,11},{4,12},{5,13},{6,14},{7,15},{8,0},{9,1},... | collective-permute-start | bytes 589832 | tf_op jit(solution)/shard_map/ppermute | solution.py:206
  168.0 1.3 gather.1.cut_ref
  169.3 4.3 %collective-permute-done.17.other_ref = bf16[256,384]{1,0:T(8,128)(2,1)S(1)} collective-permute-done((bf16[256,384]{1,0:T(8,128)(2,1)S(1)}, bf16[256,384]{1,0:T(8,128)(2,1)S(1)}, u32[]{:S(2)}, u32[]{:S(2)}) %collective-permute-start.17) | collective-permute-done | bytes 196640 | tf_op jit(solution)/shard_map/ppermute | solution.py:206
  173.6 1.0 last.1
  (79 shorter events, 0.8 us)
Async XLA Ops:
  1.9 0.7 copy-start.25
  2.5 0.7 copy-start.27
  5.4 36.3 %copy-start.32 = (s32[1,1,16,4]{2,3,1,0:T(4,128)S(1)}, s32[1,1,16,4]{2,3,1,0:T(4,128)}, u32[]{:S(2)}) copy-start(s32[1,1,16,4]{2,3,1,0:T(4,128)} %param.16) | copy-start | bytes 772
  5.4 36.5 %copy-start.30 = (s32[1,1,32]{2,1,0:T(1,128)S(1)}, s32[1,1,32]{2,1,0:T(1,128)}, u32[]{:S(2)}) copy-start(s32[1,1,32]{2,1,0:T(1,128)} %param.21) | copy-start | bytes 388
  5.4 79.7 %all-to-all-start = ((bf16[32,128,256]{2,1,0:T(8,128)(2,1)}), bf16[32,128,256]{2,1,0:T(8,128)(2,1)}, u32[]{:S(2)}, u32[]{:S(2)}) async-start(bf16[32,128,256]{2,1,0:T(8,128)(2,1)} %fill.1), calls=%async_computation | async-start | bytes 4194304 | tf_op jit(solution)/shard_map/all_to_all | solution.py:229
  15.8 14.5 %collective-permute-start = (bf16[384,256]{1,0:T(8,128)(2,1)S(1)}, bf16[384,256]{1,0:T(8,128)(2,1)S(1)}, u32[]{:S(2)}, u32[]{:S(2)}) collective-permute-start(bf16[384,256]{1,0:T(8,128)(2,1)S(1)} %project.1.projected_ref), channel_id=1, source_target_pairs={{0,8},{1,9},{2,10},{3,11},{4,12},{5,13},{6,14},{7,15},{8,0},{9,1},... | collective-permute-start | bytes 589832 | tf_op jit(solution)/shard_map/ppermute | solution.py:206
  30.5 16.3 %collective-permute-start.2 = (bf16[768,256]{1,0:T(8,128)(2,1)S(1)}, bf16[768,256]{1,0:T(8,128)(2,1)}, u32[]{:S(2)}, u32[]{:S(2)}) collective-permute-start(bf16[768,256]{1,0:T(8,128)(2,1)S(1)} %maximum_select_fusion), channel_id=1, source_target_pairs={{0,7},{1,0},{2,1},{3,2},{4,3},{5,4},{6,5},{7,6},{8,15},{9,8},{10,9... | collective-permute-start | bytes 1179656 | tf_op jit(solution)/shard_map/ppermute | solution.py:203
  39.8 12.1 %collective-permute-start.1 = (bf16[768,256]{1,0:T(8,128)(2,1)S(1)}, bf16[768,256]{1,0:T(8,128)(2,1)}, u32[]{:S(2)}, u32[]{:S(2)}) collective-permute-start(bf16[768,256]{1,0:T(8,128)(2,1)S(1)} %maximum_select_fusion), channel_id=1, source_target_pairs={{0,1},{1,2},{2,3},{3,4},{4,5},{5,6},{6,7},{7,0},{8,9},{9,10},{10,1... | collective-permute-start | bytes 1179656 | tf_op jit(solution)/shard_map/ppermute | solution.py:203
  41.9 1.2 copy-start.18
  43.2 1.6 copy-start.16
  43.2 1.6 copy-start.31
  46.7 10.1 %copy-start = (bf16[384,768]{1,0:T(8,128)(2,1)}, bf16[384,768]{1,0:T(8,128)(2,1)S(1)}, u32[]{:S(2)}) copy-start(bf16[384,768]{1,0:T(8,128)(2,1)S(1)} %get-tuple-element.13) | copy-start | bytes 1769476
  46.8 10.1 %copy-start.2 = (bf16[384,768]{1,0:T(8,128)(2,1)}, bf16[384,768]{1,0:T(8,128)(2,1)S(1)}, u32[]{:S(2)}) copy-start(bf16[384,768]{1,0:T(8,128)(2,1)S(1)} %get-tuple-element.14) | copy-start | bytes 1769476
  46.8 10.1 %copy-start.12 = (bf16[384,768]{1,0:T(8,128)(2,1)}, bf16[384,768]{1,0:T(8,128)(2,1)S(1)}, u32[]{:S(2)}) copy-start(bf16[384,768]{1,0:T(8,128)(2,1)S(1)} %get-tuple-element.19.mat_ref) | copy-start | bytes 1769476
  46.8 10.1 %copy-start.14 = (bf16[384,768]{1,0:T(8,128)(2,1)}, bf16[384,768]{1,0:T(8,128)(2,1)S(1)}, u32[]{:S(2)}) copy-start(bf16[384,768]{1,0:T(8,128)(2,1)S(1)} %get-tuple-element.12) | copy-start | bytes 1769476
  46.8 18.5 %copy-start.6 = (bf16[384,768]{1,0:T(8,128)(2,1)}, bf16[384,768]{1,0:T(8,128)(2,1)S(1)}, u32[]{:S(2)}) copy-start(bf16[384,768]{1,0:T(8,128)(2,1)S(1)} %get-tuple-element.16) | copy-start | bytes 1769476
  46.8 18.8 %copy-start.4 = (bf16[384,768]{1,0:T(8,128)(2,1)}, bf16[384,768]{1,0:T(8,128)(2,1)S(1)}, u32[]{:S(2)}) copy-start(bf16[384,768]{1,0:T(8,128)(2,1)S(1)} %get-tuple-element.15) | copy-start | bytes 1769476
  46.8 34.5 %copy-start.10 = (bf16[384,768]{1,0:T(8,128)(2,1)}, bf16[384,768]{1,0:T(8,128)(2,1)S(1)}, u32[]{:S(2)}) copy-start(bf16[384,768]{1,0:T(8,128)(2,1)S(1)} %get-tuple-element.18) | copy-start | bytes 1769476
  46.8 34.8 %copy-start.8 = (bf16[384,768]{1,0:T(8,128)(2,1)}, bf16[384,768]{1,0:T(8,128)(2,1)S(1)}, u32[]{:S(2)}) copy-start(bf16[384,768]{1,0:T(8,128)(2,1)S(1)} %get-tuple-element.17) | copy-start | bytes 1769476
  46.8 11.0 %collective-permute-start.4 = (bf16[768,256]{1,0:T(8,128)(2,1)}, bf16[768,256]{1,0:T(8,128)(2,1)S(1)}, u32[]{:S(2)}, u32[]{:S(2)}) collective-permute-start(bf16[768,256]{1,0:T(8,128)(2,1)} %collective-permute-done.2), channel_id=1, source_target_pairs={{0,7},{1,0},{2,1},{3,2},{4,3},{5,4},{6,5},{7,6},{8,15},{9,8},{10,9... | collective-permute-start | bytes 1179656 | tf_op jit(solution)/shard_map/ppermute | solution.py:203
  51.9 11.4 %collective-permute-start.3 = (bf16[768,256]{1,0:T(8,128)(2,1)}, bf16[768,256]{1,0:T(8,128)(2,1)S(1)}, u32[]{:S(2)}, u32[]{:S(2)}) collective-permute-start(bf16[768,256]{1,0:T(8,128)(2,1)} %collective-permute-done.1), channel_id=1, source_target_pairs={{0,1},{1,2},{2,3},{3,4},{4,5},{5,6},{6,7},{7,0},{8,9},{9,10},{10,1... | collective-permute-start | bytes 1179656 | tf_op jit(solution)/shard_map/ppermute | solution.py:203
  57.8 18.3 %collective-permute-start.6 = (bf16[768,256]{1,0:T(8,128)(2,1)S(1)}, bf16[768,256]{1,0:T(8,128)(2,1)S(1)}, u32[]{:S(2)}, u32[]{:S(2)}) collective-permute-start(bf16[768,256]{1,0:T(8,128)(2,1)S(1)} %collective-permute-done.4), channel_id=1, source_target_pairs={{0,7},{1,0},{2,1},{3,2},{4,3},{5,4},{6,5},{7,6},{8,15},{9,8},{10,9... | collective-permute-start | bytes 1179656 | tf_op jit(solution)/shard_map/ppermute | solution.py:203
  63.3 10.9 %collective-permute-start.5 = (bf16[768,256]{1,0:T(8,128)(2,1)S(1)}, bf16[768,256]{1,0:T(8,128)(2,1)S(1)}, u32[]{:S(2)}, u32[]{:S(2)}) collective-permute-start(bf16[768,256]{1,0:T(8,128)(2,1)S(1)} %collective-permute-done.3), channel_id=1, source_target_pairs={{0,1},{1,2},{2,3},{3,4},{4,5},{5,6},{6,7},{7,0},{8,9},{9,10},{10,1... | collective-permute-start | bytes 1179656 | tf_op jit(solution)/shard_map/ppermute | solution.py:203
  65.9 19.2 %copy-start.20 = (bf16[384,256]{1,0:T(8,128)(2,1)S(1)}, bf16[384,256]{1,0:T(8,128)(2,1)}, u32[]{:S(2)}) copy-start(bf16[384,256]{1,0:T(8,128)(2,1)} %cotangent_ref.1) | copy-start | bytes 589828
  65.9 19.2 %copy-start.29 = (f32[256]{0:T(256)S(1)}, f32[256]{0:T(256)}, u32[]{:S(2)}) copy-start(f32[256]{0:T(256)} %param.13) | copy-start | bytes 3076
  74.2 8.8 %collective-permute-start.7 = (bf16[384,256]{1,0:T(8,128)(2,1)S(1)}, bf16[384,256]{1,0:T(8,128)(2,1)S(1)}, u32[]{:S(2)}, u32[]{:S(2)}) collective-permute-start(bf16[384,256]{1,0:T(8,128)(2,1)S(1)} %slice.44), channel_id=1, source_target_pairs={{0,1},{1,2},{2,3},{3,4},{4,5},{5,6},{6,7},{7,0},{8,9},{9,10},{10,1... | collective-permute-start | bytes 589832 | tf_op jit(solution)/shard_map/ppermute | solution.py:203
  76.2 8.3 %collective-permute-start.8 = (bf16[384,256]{1,0:T(8,128)(2,1)S(1)}, bf16[384,256]{1,0:T(8,128)(2,1)S(1)}, u32[]{:S(2)}, u32[]{:S(2)}) collective-permute-start(bf16[384,256]{1,0:T(8,128)(2,1)S(1)} %slice.45), channel_id=1, source_target_pairs={{0,7},{1,0},{2,1},{3,2},{4,3},{5,4},{6,5},{7,6},{8,15},{9,8},{10,9... | collective-permute-start | bytes 589832 | tf_op jit(solution)/shard_map/ppermute | solution.py:203
  83.0 0.7 copy-start.21
  84.5 0.7 copy-start.23
  85.2 1.1 copy-start.13
  86.2 1.0 copy-start.17
  87.2 0.9 copy-start.22
  88.2 0.9 copy-start.24
  94.7 73.2 %all-to-all-start.1 = ((bf16[32,256,128]{2,1,0:T(8,128)(2,1)}), bf16[32,256,128]{2,1,0:T(8,128)(2,1)S(1)}, u32[]{:S(2)}, u32[]{:S(2)}) async-start(bf16[32,256,128]{2,1,0:T(8,128)(2,1)} %terms.1), calls=%async_computation.1 | async-start | bytes 4194304 | tf_op jit(solution)/shard_map/all_to_all | solution.py:290
  110.4 3.5 %copy-start.11 = (bf16[384,768]{1,0:T(8,128)(2,1)S(1)}, bf16[384,768]{1,0:T(8,128)(2,1)}, u32[]{:S(2)}) copy-start(bf16[384,768]{1,0:T(8,128)(2,1)} %copy-done.10) | copy-start | bytes 1769476
  110.4 9.5 %copy-start.9 = (bf16[384,768]{1,0:T(8,128)(2,1)S(1)}, bf16[384,768]{1,0:T(8,128)(2,1)}, u32[]{:S(2)}) copy-start(bf16[384,768]{1,0:T(8,128)(2,1)} %copy-done.8) | copy-start | bytes 1769476
  112.0 10.8 %collective-permute-start.9 = (bf16[256,384]{1,0:T(8,128)(2,1)S(1)}, bf16[256,384]{1,0:T(8,128)(2,1)S(1)}, u32[]{:S(2)}, u32[]{:S(2)}) collective-permute-start(bf16[256,384]{1,0:T(8,128)(2,1)S(1)} %get-tuple-element.22), channel_id=1, source_target_pairs={{0,1},{1,2},{2,3},{3,4},{4,5},{5,6},{6,7},{7,0},{8,9},{9,10},{10,1... | collective-permute-start | bytes 589832 | tf_op jit(solution)/shard_map/ppermute | solution.py:203
  114.4 10.6 %collective-permute-start.13 = (bf16[256,384]{1,0:T(8,128)(2,1)S(1)}, bf16[256,384]{1,0:T(8,128)(2,1)S(1)}, u32[]{:S(2)}, u32[]{:S(2)}) collective-permute-start(bf16[256,384]{1,0:T(8,128)(2,1)S(1)} %get-tuple-element.23), channel_id=1, source_target_pairs={{0,7},{1,0},{2,1},{3,2},{4,3},{5,4},{6,5},{7,6},{8,15},{9,8},{10,9... | collective-permute-start | bytes 589832 | tf_op jit(solution)/shard_map/ppermute | solution.py:203
  120.3 16.5 %copy-start.7 = (bf16[384,768]{1,0:T(8,128)(2,1)S(1)}, bf16[384,768]{1,0:T(8,128)(2,1)}, u32[]{:S(2)}) copy-start(bf16[384,768]{1,0:T(8,128)(2,1)} %copy-done.6) | copy-start | bytes 1769476
  122.9 16.4 %copy-start.5 = (bf16[384,768]{1,0:T(8,128)(2,1)S(1)}, bf16[384,768]{1,0:T(8,128)(2,1)}, u32[]{:S(2)}) copy-start(bf16[384,768]{1,0:T(8,128)(2,1)} %copy-done.4) | copy-start | bytes 1769476
  122.9 13.9 %collective-permute-start.10 = (bf16[256,768]{1,0:T(8,128)(2,1)S(1)}, bf16[256,768]{1,0:T(8,128)(2,1)S(1)}, u32[]{:S(2)}, u32[]{:S(2)}) collective-permute-start(bf16[256,768]{1,0:T(8,128)(2,1)S(1)} %pad_maximum_fusion), channel_id=1, source_target_pairs={{0,1},{1,2},{2,3},{3,4},{4,5},{5,6},{6,7},{7,0},{8,9},{9,10},{10,1... | collective-permute-start | bytes 1179656 | tf_op jit(solution)/shard_map/ppermute | solution.py:203
  125.0 25.2 %copy-start.3 = (bf16[384,768]{1,0:T(8,128)(2,1)S(1)}, bf16[384,768]{1,0:T(8,128)(2,1)}, u32[]{:S(2)}) copy-start(bf16[384,768]{1,0:T(8,128)(2,1)} %copy-done.2) | copy-start | bytes 1769476
  125.1 27.4 %copy-start.1 = (bf16[384,768]{1,0:T(8,128)(2,1)S(1)}, bf16[384,768]{1,0:T(8,128)(2,1)}, u32[]{:S(2)}) copy-start(bf16[384,768]{1,0:T(8,128)(2,1)} %copy-done) | copy-start | bytes 1769476
  125.1 14.2 %collective-permute-start.14 = (bf16[256,768]{1,0:T(8,128)(2,1)S(1)}, bf16[256,768]{1,0:T(8,128)(2,1)S(1)}, u32[]{:S(2)}, u32[]{:S(2)}) collective-permute-start(bf16[256,768]{1,0:T(8,128)(2,1)S(1)} %pad_maximum_fusion.1), channel_id=1, source_target_pairs={{0,7},{1,0},{2,1},{3,2},{4,3},{5,4},{6,5},{7,6},{8,15},{9,8},{10,9... | collective-permute-start | bytes 1179656 | tf_op jit(solution)/shard_map/ppermute | solution.py:203
  137.2 26.9 %copy-start.15 = (bf16[384,768]{1,0:T(8,128)(2,1)S(1)}, bf16[384,768]{1,0:T(8,128)(2,1)}, u32[]{:S(2)}) copy-start(bf16[384,768]{1,0:T(8,128)(2,1)} %copy-done.14) | copy-start | bytes 1769476
  137.2 13.0 %collective-permute-start.11 = (bf16[256,768]{1,0:T(8,128)(2,1)S(1)}, bf16[256,768]{1,0:T(8,128)(2,1)S(1)}, u32[]{:S(2)}, u32[]{:S(2)}) collective-permute-start(bf16[256,768]{1,0:T(8,128)(2,1)S(1)} %fusion.2), channel_id=1, source_target_pairs={{0,1},{1,2},{2,3},{3,4},{4,5},{5,6},{6,7},{7,0},{8,9},{9,10},{10,1... | collective-permute-start | bytes 1179656 | tf_op jit(solution)/shard_map/ppermute | solution.py:203
  139.7 12.8 %collective-permute-start.15 = (bf16[256,768]{1,0:T(8,128)(2,1)S(1)}, bf16[256,768]{1,0:T(8,128)(2,1)S(1)}, u32[]{:S(2)}, u32[]{:S(2)}) collective-permute-start(bf16[256,768]{1,0:T(8,128)(2,1)S(1)} %fusion.4), channel_id=1, source_target_pairs={{0,7},{1,0},{2,1},{3,2},{4,3},{5,4},{6,5},{7,6},{8,15},{9,8},{10,9... | collective-permute-start | bytes 1179656 | tf_op jit(solution)/shard_map/ppermute | solution.py:203
  150.6 11.9 %collective-permute-start.12 = (bf16[256,768]{1,0:T(8,128)(2,1)S(1)}, bf16[256,768]{1,0:T(8,128)(2,1)S(1)}, u32[]{:S(2)}, u32[]{:S(2)}) collective-permute-start(bf16[256,768]{1,0:T(8,128)(2,1)S(1)} %fusion.1), channel_id=1, source_target_pairs={{0,1},{1,2},{2,3},{3,4},{4,5},{5,6},{6,7},{7,0},{8,9},{9,10},{10,1... | collective-permute-start | bytes 1179656 | tf_op jit(solution)/shard_map/ppermute | solution.py:203
  152.9 15.0 %copy-start.26 = (s32[1,1,32]{2,1,0:T(1,128)S(1)}, s32[1,1,32]{2,1,0:T(1,128)}, u32[]{:S(2)}) copy-start(s32[1,1,32]{2,1,0:T(1,128)} %param.19) | copy-start | bytes 388
  152.9 15.0 %copy-start.28 = (s32[1,1,32]{2,1,0:T(1,128)S(1)}, s32[1,1,32]{2,1,0:T(1,128)}, u32[]{:S(2)}) copy-start(s32[1,1,32]{2,1,0:T(1,128)} %param.20) | copy-start | bytes 388
  152.9 11.2 %collective-permute-start.16 = (bf16[256,768]{1,0:T(8,128)(2,1)S(1)}, bf16[256,768]{1,0:T(8,128)(2,1)S(1)}, u32[]{:S(2)}, u32[]{:S(2)}) collective-permute-start(bf16[256,768]{1,0:T(8,128)(2,1)S(1)} %fusion.3), channel_id=1, source_target_pairs={{0,7},{1,0},{2,1},{3,2},{4,3},{5,4},{6,5},{7,6},{8,15},{9,8},{10,9... | collective-permute-start | bytes 1179656 | tf_op jit(solution)/shard_map/ppermute | solution.py:203
  164.5 9.1 %copy-start.19 = (bf16[256,256]{1,0:T(8,128)(2,1)S(1)}, bf16[256,256]{1,0:T(8,128)(2,1)}, u32[]{:S(2)}) copy-start(bf16[256,256]{1,0:T(8,128)(2,1)} %weight_ref.1) | copy-start | bytes 393220
  164.6 9.1 %collective-permute-start.17 = (bf16[256,384]{1,0:T(8,128)(2,1)S(1)}, bf16[256,384]{1,0:T(8,128)(2,1)S(1)}, u32[]{:S(2)}, u32[]{:S(2)}) collective-permute-start(bf16[256,384]{1,0:T(8,128)(2,1)S(1)} %select_convert_fusion), channel_id=1, source_target_pairs={{0,8},{1,9},{2,10},{3,11},{4,12},{5,13},{6,14},{7,15},{8,0},{9,1},... | collective-permute-start | bytes 589832 | tf_op jit(solution)/shard_map/ppermute | solution.py:206

commit v3 on v2

--- a/solution.py
+++ b/solution.py
@@ -10,6 +10,8 @@
 FAR = 2
 CHUNKS = 4
 VMEM_LIMIT = 16 * 1024 * 1024
+PAIR_COST = 100_000_000_000
+CLOSE_COST = 27_800_000_000
 
 
 def spec(space):
@@ -103,48 +105,86 @@
             lax.fori_loop(0, count_ref[source], put, 0)
 
 
-def spread_cut_kernel(dst_ref, cut_ref, dense):
+def spread_cut_kernel(dst_ref, cut_ref, dense_hbm, dense, sem):
+    chunks, _, columns = dense.shape
+    chunk = columns // TILE
     dense[...] = jnp.zeros(dense.shape, BF)
 
     def put(part, carried):
         target = pl.multiple_of(dst_ref[part] * TILE, TILE)
-        origin = pl.multiple_of(part * TILE, TILE)
-        dense[pl.ds(target, TILE), pl.ds(origin, TILE)] = cut_ref[part]
+        origin = pl.multiple_of(lax.rem(part, chunk) * TILE, TILE)
+        dense[lax.div(part, chunk), pl.ds(target, TILE), pl.ds(origin, TILE)] = cut_ref[part]
         return carried
 
-    lax.fori_loop(0, cut_ref.shape[0], put, 0)
+    lax.fori_loop(0, chunks * chunk, put, 0)
+    copy = pltpu.make_async_copy(dense, dense_hbm, sem)
+    copy.start()
+    copy.wait()
+
+
+def pair_kernel(half_ref, own_ref, other_ref, pair_ref):
+    rows = own_ref.shape[0]
+    place = pl.multiple_of(half_ref[0] * rows, TILE)
+    pair_ref[pl.ds(place, rows)] = own_ref[...]
+    pair_ref[pl.ds(pl.multiple_of(rows - place, TILE), rows)] = other_ref[...]
 
 
 def middle_kernel(
-    sum_ref, mat_ref, low_ref, high_ref, bias_ref, cotangent_ref, cut_ref, far_ref, hidden_ref, grad_ref
+    sum_hbm,
+    cotangent_hbm,
+    bias_ref,
+    mat_hbm,
+    cut_hbm,
+    far_hbm,
+    hidden_ref,
+    grad_ref,
+    low_ref,
+    high_ref,
+    terms_hbm,
+    total,
+    cotangent,
+    mat,
+    cut,
+    far,
+    terms,
+    sems,
 ):
-    rows, width = sum_ref.shape
-    chunk = far_ref.shape[0] // CHUNKS
-    total = (
-        sum_ref[...]
-        + product(mat_ref[:, :rows], low_ref[...])
-        + product(mat_ref[:, rows:], high_ref[...])
-    )
-    for piece in range(CHUNKS):
-        arrived = far_ref[pl.ds(piece * chunk, chunk)].reshape(chunk * TILE, width)
-        total += product(cut_ref[:, pl.ds(piece * chunk * TILE, chunk * TILE)], arrived)
-    activated, derivative = silu_parts(total + bias_ref[...])
+    rows, width = total.shape
+    chunks = cut.shape[0]
+    chunk = far.shape[0] // chunks
+    move = lambda source, target, place: pltpu.make_async_copy(source, target, sems.at[place])
+    copies = [move(sum_hbm, total, 2 * chunks)]
+    for piece in range(chunks):
+        span = pl.ds(piece * chunk, chunk)
+        copies.append(move(cut_hbm.at[piece], cut.at[piece], piece))
+        copies.append(move(far_hbm.at[span], far.at[span], chunks + piece))
+    copies.append(move(cotangent_hbm, cotangent, 2 * chunks + 1))
+    copies.append(move(mat_hbm, mat, 2 * chunks + 2))
+    for copy in copies:
+        copy.start()
+    copies[0].wait()
+    for piece in range(chunks):
+        copies[1 + 2 * piece].wait()
+        copies[2 + 2 * piece].wait()
+        arrived = far[pl.ds(piece * chunk, chunk)].reshape(chunk * TILE, width)
+        total[...] += product(cut[piece], arrived)
+    activated, derivative = silu_parts(total[...] + bias_ref[...])
     hidden_ref[...] = activated.astype(BF)
-    grad_ref[...] = (cotangent_ref[...].astype(F32) * derivative).T.astype(BF)
-
-
-def terms_kernel(grad_ref, cut_ref, terms_hbm, terms, sems):
-    chunk = terms.shape[0] // CHUNKS
-    copies = []
-    for piece in range(CHUNKS):
-        columns = pl.ds(piece * chunk * TILE, chunk * TILE)
-        result = product(grad_ref[...], cut_ref[:, columns]).astype(BF)
+    copies[-2].wait()
+    grad = (cotangent[...].astype(F32) * derivative).T.astype(BF)
+    grad_ref[...] = grad
+    copies[-1].wait()
+    low_ref[...] = product(grad, mat[:, :rows]).astype(BF)
+    high_ref[...] = product(grad, mat[:, rows:]).astype(BF)
+    stores = []
+    for piece in range(chunks):
+        result = product(grad, cut[piece]).astype(BF)
         for slot in range(chunk):
             terms[piece * chunk + slot] = result[:, slot * TILE : (slot + 1) * TILE]
         span = pl.ds(piece * chunk, chunk)
-        copies.append(pltpu.make_async_copy(terms.at[span], terms_hbm.at[span], sems.at[piece]))
-        copies[-1].start()
-    for copy in copies:
+        stores.append(move(terms.at[span], terms_hbm.at[span], 2 * chunks + 3 + piece))
+        stores[-1].start()
+    for copy in stores:
         copy.wait()
 
 
@@ -160,6 +200,29 @@
         return carried
 
     lax.fori_loop(0, arrived_ref.shape[0], add, 0)
+
+
+def hop_kernel(at, grad_ref, mat_ref, arrived_ref, out_ref):
+    wide, held = out_ref.shape[1], arrived_ref.shape[1]
+    for low, high in ((0, at), (at, at + held), (at + held, wide)):
+        if low < high:
+            term = product(grad_ref[...], mat_ref[:, low:high])
+            if low == at:
+                term += arrived_ref[...].astype(F32)
+            out_ref[:, low:high] = term.astype(BF)
+
+
+def close_kernel(half_ref, grad_ref, mat_ref, left_ref, right_ref, own_ref, other_ref):
+    rows = grad_ref.shape[1]
+    mine = pl.ds(pl.multiple_of(half_ref[0] * rows, TILE), rows)
+    theirs = pl.ds(pl.multiple_of((1 - half_ref[0]) * rows, TILE), rows)
+
+    def total(columns):
+        arrived = left_ref[:, columns].astype(F32) + right_ref[:, columns].astype(F32)
+        return product(grad_ref[...], mat_ref[:, columns]) + arrived
+
+    other_ref[...] = total(theirs).astype(BF)
+    own_ref[...] = total(mine)
 
 
 def last_kernel(own_ref, other_ref, cut_ref, weight_ref, out_ref):
@@ -239,17 +302,19 @@
     dense_cut = call(
         spread_cut_kernel,
         "spread_cut",
-        shape((rows, parts * TILE), BF),
+        pltpu.HBM((CHUNKS, rows, parts // CHUNKS * TILE), BF),
         [SMEM, VMEM],
-        VMEM,
+        HBM,
+        [
+            pltpu.VMEM((CHUNKS, rows, parts // CHUNKS * TILE), BF),
+            pltpu.SemaphoreType.DMA,
+        ],
         moved=6 << 20,
     )(dst, cut_tiles[0, 0])
 
-    pair = jnp.where(
-        half == 0,
-        jnp.concatenate([projected, partner]),
-        jnp.concatenate([partner, projected]),
-    )
+    pair = call(
+        pair_kernel, "pair", shape((wide, width), BF), [SMEM, VMEM, VMEM], VMEM, flops=PAIR_COST
+    )(half.reshape(1), projected, partner)
     running = product(dense[0], pair)
     right = left = pair
     for hop in range(1, reach):
@@ -258,49 +323,56 @@
         running = running + product(dense[hop], left)
     low, high = along_ring(right[:rows], 1), along_ring(left[rows:], -1)
 
-    hidden, grad_pre = call(
+    running = running + product(dense[reach][:, :rows], low)
+    running = running + product(dense[reach][:, rows:], high)
+
+    hidden, grad_pre, low, high, terms = call(
         middle_kernel,
         "middle",
-        (shape((rows, width), BF), shape((width, rows), BF)),
-        [VMEM] * 8,
-        (VMEM, VMEM),
+        (shape((rows, width), BF),)
+        + (shape((width, rows), BF),) * 3
+        + (pltpu.HBM((parts, width, TILE), BF),),
+        [HBM, HBM, VMEM, HBM, HBM, HBM],
+        (VMEM,) * 4 + (HBM,),
+        [
+            pltpu.VMEM((rows, width), F32),
+            pltpu.VMEM((rows, width), BF),
+            pltpu.VMEM((rows, wide), BF),
+            pltpu.VMEM(dense_cut.shape, BF),
+            pltpu.VMEM((parts, TILE, width), BF),
+            pltpu.VMEM((parts, width, TILE), BF),
+            pltpu.SemaphoreType.DMA((3 * CHUNKS + 3,)),
+        ],
     )(
-        running,
-        dense[reach],
-        low,
-        high,
+        in_hbm(running),
+        in_hbm(cotangent),
         bias.reshape(1, width),
-        cotangent,
-        dense_cut,
-        incoming,
+        in_hbm(dense[reach]),
+        in_hbm(dense_cut),
+        in_hbm(incoming),
     )
 
-    farthest = product(grad_pre, dense[reach]).astype(BF)
-    low, high = along_ring(farthest[:, :rows], 1), along_ring(farthest[:, rows:], -1)
-    terms = call(
-        terms_kernel,
-        "terms",
-        pltpu.HBM((parts, width, TILE), BF),
-        [VMEM, VMEM],
-        HBM,
-        [pltpu.VMEM((parts, width, TILE), BF), pltpu.SemaphoreType.DMA((CHUNKS,))],
-        flops=2 * rows * width * parts * TILE,
-        moved=6 << 20,
-    )(grad_pre, dense_cut)
+    def add_on(mat, arrived, at):
+        return call(
+            lambda *refs: hop_kernel(at, *refs), "hop", shape((width, wide), BF), [VMEM] * 3, VMEM
+        )(grad_pre, mat, arrived)
+
+    low, high = along_ring(low, 1), along_ring(high, -1)
     returned = lax.all_to_all(terms, "dom", split_axis=0, concat_axis=0, tiled=True)
     for hop in range(reach - 1, 0, -1):
-        right = product(grad_pre, dense[hop])
-        left = product(grad_pre, dense[ring - hop])
-        if hop == reach - 1:
-            right = jnp.concatenate([right[:, :rows] + low.astype(F32), right[:, rows:]], axis=1)
-            left = jnp.concatenate([left[:, :rows], left[:, rows:] + high.astype(F32)], axis=1)
-        else:
-            right, left = right + from_left.astype(F32), left + from_right.astype(F32)
-        from_left = along_ring(right.astype(BF), 1)
-        from_right = along_ring(left.astype(BF), -1)
-    both = product(grad_pre, dense[0]) + from_left.astype(F32) + from_right.astype(F32)
-    own = jnp.where(half == 0, both[:, :rows], both[:, rows:])
-    other = across(jnp.where(half == 0, both[:, rows:], both[:, :rows]).astype(BF))
+        first = hop == reach - 1
+        right = add_on(dense[hop], low if first else from_left, 0)
+        left = add_on(dense[ring - hop], high if first else from_right, rows if first else 0)
+        from_left, from_right = along_ring(right, 1), along_ring(left, -1)
+    own, other = call(
+        close_kernel,
+        "close",
+        (shape((width, rows), F32), shape((width, rows), BF)),
+        [SMEM] + [VMEM] * 4,
+        (VMEM, VMEM),
+        flops=CLOSE_COST,
+    )(half.reshape(1), grad_pre, dense[0], from_left, from_right)
+    other = across(other)
     from_cuts = call(
         gather_kernel, "gather", shape((width, rows), F32), [SMEM, SMEM, VMEM], VMEM, moved=2 << 20
     )(send_to, is_live, returned)

time: 176 us -> 166 us (0.943)
  Pallas kernels: 14.4 us -> 22.3 us
  matrix products: 9.13 us -> 3.51 us
  local copies, waits for them, and re-layouts: 8.68 us -> 3.77 us
  starting transfers between devices: 93.5 us -> 88.9 us
    ppermute x2, waiting for transfers between devices: 16.4 us -> 4.43 us  [across(): lax.ppermute(value, 'blk', [(i, (i + ring) % peers) for i in range(peers)])]
    ppermute x16, waiting for transfers between devices: 30.6 us -> 40.8 us  [along_ring(): return lax.ppermute(value, 'blk', moves)]
    pallas_call x3 -> x10, Pallas kernels: 6.7 us -> 14.8 us  [the longest x1 7.49 us: on_device(): call(middle_kernel, 'middle', (shape((rows, width), BF),) + (shape((width...]
    all_to_all x1, starting transfers between devices: 15.7 us -> 8.32 us  [on_device(): lax.all_to_all(terms, 'dom', split_axis=0, concat_axis=0, tiled=True)]
    dot_general x15 -> x9, matrix products: 9.13 us -> 3.51 us  [product(): return jnp.dot(left, right, preferred_element_type=F32)]
    unnamed x67 -> x45, local copies, waits for them, and re-layouts: 8.48 us -> 3.66 us
    ppermute x16, starting transfers between devices: 61.7 us -> 64.4 us  [along_ring(): return lax.ppermute(value, 'blk', moves)]
  transfers between devices with their start and end apart: 20 -> 20, of which waited for: 11 -> 12; matrix products, arithmetic and copies ran while one was open for 6% -> 2% of each run, Pallas kernels for 2% -> 8%
where the time goes in v3:
time: 166 us; the launch traced here: 165 us
  starting transfers between devices  88.9 us (54%)
  waiting for transfers between devices  45.3 us (27%)
  Pallas kernels  22.3 us (13%)
  local copies, waits for them, and re-layouts  3.77 us (2%)
  matrix products  3.51 us (2%)
    ppermute x16, starting transfers between devices, along_ring(): return lax.ppermute(value, 'blk', moves)  64.4 us
    ppermute x16, waiting for transfers between devices, along_ring(): return lax.ppermute(value, 'blk', moves)  40.8 us
    all_to_all x1, starting transfers between devices, on_device(): lax.all_to_all(outgoing, 'dom', split_axis=0, concat_axis=0, tiled=True)  8.79 us
    all_to_all x1, starting transfers between devices, on_device(): lax.all_to_all(terms, 'dom', split_axis=0, concat_axis=0, tiled=True)  8.32 us
    pallas_call x1, Pallas kernels, on_device(): call(middle_kernel, 'middle', (shape((rows, width), BF),) + (shape((width...  7.49 us
    ppermute x2, starting transfers between devices, across(): lax.ppermute(value, 'blk', [(i, (i + ring) % peers) for i in range(peers)])  7.48 us
    ppermute x2, waiting for transfers between devices, across(): lax.ppermute(value, 'blk', [(i, (i + ring) % peers) for i in range(peers)])  4.43 us
    pallas_call x6, Pallas kernels, add_on(): call(lambda *refs: hop_kernel(at, *refs), 'hop', shape((width, wide), BF)...  4.15 us
  transfers between devices with their start and end apart: 20, of which 12 were waited for; matrix products, arithmetic and copies ran while one was open for 2% of the time, Pallas kernels for 8%

profile of v3, /device:TPU:2, one launch (start us, length us, event | category | flops | bytes accessed | tf_op | source)
XLA Modules:
  0.0 165.1 jit_solution(9573903772926239004)
XLA Ops:
  0.6 1.2 project.1.own_ref.projected_ref
  1.9 4.0 %collective-permute-start = (bf16[384,256]{1,0:T(8,128)(2,1)S(1)}, bf16[384,256]{1,0:T(8,128)(2,1)S(1)}, u32[]{:S(2)}, u32[]{:S(2)}) collective-permute-start(bf16[384,256]{1,0:T(8,128)(2,1)S(1)} %project.1.own_ref.projected_ref), channel_id=1, source_target_pairs={{0,8},{1,9},{2,10},{3,11},{4,12},{5,13},{6,14},{7,15},{8,0},{9,1},... | collective-permute-start | bytes 589832 | tf_op jit(solution)/shard_map/ppermute | solution.py:269
  5.9 0.6 copy-done.14
  6.6 0.7 copy-done.16
  7.2 2.2 %fill.1 = bf16[32,128,256]{2,1,0:T(8,128)(2,1)} custom-call(s32[32]{0:T(128)S(1)} %bitcast.29, s32[32]{0:T(128)S(1)} %bitcast.31, bf16[384,256]{1,0:T(8,128)(2,1)S(1)} %project.1.own_ref.projected_ref), custom_call_target="tpu_custom_call" | custom-call | tf_op jit(solution)/shard_map/fill/pallas_call | solution.py:284
  9.4 8.8 %all-to-all-start = ((bf16[32,128,256]{2,1,0:T(8,128)(2,1)}), bf16[32,128,256]{2,1,0:T(8,128)(2,1)}, u32[]{:S(2)}, u32[]{:S(2)}) async-start(bf16[32,128,256]{2,1,0:T(8,128)(2,1)} %fill.1), calls=%async_computation | async-start | bytes 4194304 | tf_op jit(solution)/shard_map/all_to_all | solution.py:292
  18.2 0.0 copy-start.21
  18.3 0.0 copy-start.10
  18.3 11.1 %collective-permute-start.2 = (bf16[768,256]{1,0:T(8,128)(2,1)S(1)}, bf16[768,256]{1,0:T(8,128)(2,1)S(1)}, u32[]{:S(2)}, u32[]{:S(2)}) collective-permute-start(bf16[768,256]{1,0:T(8,128)(2,1)S(1)} %pair.1), channel_id=1, source_target_pairs={{0,7},{1,0},{2,1},{3,2},{4,3},{5,4},{6,5},{7,6},{8,15},{9,8},{10,9... | collective-permute-start | bytes 1179656 | tf_op jit(solution)/shard_map/ppermute | solution.py:266
  29.4 1.9 %collective-permute-start.1 = (bf16[768,256]{1,0:T(8,128)(2,1)S(1)}, bf16[768,256]{1,0:T(8,128)(2,1)S(1)}, u32[]{:S(2)}, u32[]{:S(2)}) collective-permute-start(bf16[768,256]{1,0:T(8,128)(2,1)S(1)} %pair.1), channel_id=1, source_target_pairs={{0,1},{1,2},{2,3},{3,4},{4,5},{5,6},{6,7},{7,0},{8,9},{9,10},{10,1... | collective-permute-start | bytes 1179656 | tf_op jit(solution)/shard_map/ppermute | solution.py:266
  31.4 0.1 copy.14
  31.4 0.1 reshape_squeeze.3.refs_0_
  31.6 0.0 copy-start.9
  31.6 2.8 %spread_cut.1.cut_hbm = bf16[4,384,1024]{2,1,0:T(8,128)(2,1)} custom-call(s32[32]{0:T(128)S(1)} %bitcast.34, bf16[32,128,128]{2,1,0:T(8,128)(2,1)S(1)} %bitcast.28), custom_call_target="tpu_custom_call" | custom-call | bytes 6291456 | tf_op jit(solution)/shard_map/spread_cut/pallas_call | solution.py:302
  34.4 1.8 %spread.1 = (bf16[384,768]{1,0:T(8,128)(2,1)S(1)}, bf16[384,768]{1,0:T(8,128)(2,1)S(1)}, bf16[384,768]{1,0:T(8,128)(2,1)S(1)}, bf16[384,768]{1,0:T(8,128)(2,1)S(...) custom-call(s32[64]{0:T(128)S(1)} %reshape_squeeze.3.refs_0_, ...), custom_call_target="tpu_custom_call" | custom-call | bytes 10485760 | tf_op jit(solution)/shard_map/spread/pallas_call | solution.py:294
  36.3 1.8 %collective-permute-done.2 = bf16[768,256]{1,0:T(8,128)(2,1)S(1)} collective-permute-done((bf16[768,256]{1,0:T(8,128)(2,1)S(1)}, bf16[768,256]{1,0:T(8,128)(2,1)S(1)}, u32[]{:S(2)}, u32[]{:S(2)}) %collective-permute-start.2) | collective-permute-done | bytes 393248 | tf_op jit(solution)/shard_map/ppermute | solution.py:266
  38.1 5.6 %collective-permute-start.4 = (bf16[768,256]{1,0:T(8,128)(2,1)S(1)}, bf16[768,256]{1,0:T(8,128)(2,1)S(1)}, u32[]{:S(2)}, u32[]{:S(2)}) collective-permute-start(bf16[768,256]{1,0:T(8,128)(2,1)S(1)} %collective-permute-done.2), channel_id=1, source_target_pairs={{0,7},{1,0},{2,1},{3,2},{4,3},{5,4},{6,5},{7,6},{8,15},{9,8},{10,9... | collective-permute-start | bytes 1179656 | tf_op jit(solution)/shard_map/ppermute | solution.py:266
  43.7 1.9 %collective-permute-start.3 = (bf16[768,256]{1,0:T(8,128)(2,1)S(1)}, bf16[768,256]{1,0:T(8,128)(2,1)S(1)}, u32[]{:S(2)}, u32[]{:S(2)}) collective-permute-start(bf16[768,256]{1,0:T(8,128)(2,1)S(1)} %collective-permute-done.1), channel_id=1, source_target_pairs={{0,1},{1,2},{2,3},{3,4},{4,5},{5,6},{6,7},{7,0},{8,9},{9,10},{10,1... | collective-permute-start | bytes 1179656 | tf_op jit(solution)/shard_map/ppermute | solution.py:266
  45.6 0.3 fusion.10
  45.9 0.3 fusion.9
  46.3 0.3 fusion.4
  46.6 10.3 %collective-permute-done.3 = bf16[768,256]{1,0:T(8,128)(2,1)S(1)} collective-permute-done((bf16[768,256]{1,0:T(8,128)(2,1)S(1)}, bf16[768,256]{1,0:T(8,128)(2,1)S(1)}, u32[]{:S(2)}, u32[]{:S(2)}) %collective-permute-start.3) | collective-permute-done | bytes 393248 | tf_op jit(solution)/shard_map/ppermute | solution.py:266
  57.0 1.9 %collective-permute-start.5 = (bf16[768,256]{1,0:T(8,128)(2,1)S(1)}, bf16[768,256]{1,0:T(8,128)(2,1)S(1)}, u32[]{:S(2)}, u32[]{:S(2)}) collective-permute-start(bf16[768,256]{1,0:T(8,128)(2,1)S(1)} %collective-permute-done.3), channel_id=1, source_target_pairs={{0,1},{1,2},{2,3},{3,4},{4,5},{5,6},{6,7},{7,0},{8,9},{9,10},{10,1... | collective-permute-start | bytes 1179656 | tf_op jit(solution)/shard_map/ppermute | solution.py:266
  58.9 5.1 %collective-permute-start.6 = (bf16[768,256]{1,0:T(8,128)(2,1)S(1)}, bf16[768,256]{1,0:T(8,128)(2,1)S(1)}, u32[]{:S(2)}, u32[]{:S(2)}) collective-permute-start(bf16[768,256]{1,0:T(8,128)(2,1)S(1)} %collective-permute-done.4), channel_id=1, source_target_pairs={{0,7},{1,0},{2,1},{3,2},{4,3},{5,4},{6,5},{7,6},{8,15},{9,8},{10,9... | collective-permute-start | bytes 1179656 | tf_op jit(solution)/shard_map/ppermute | solution.py:266
  64.0 0.3 fusion.11
  64.4 0.3 fusion.3
  64.7 4.7 %collective-permute-done.5 = bf16[768,256]{1,0:T(8,128)(2,1)S(1)} collective-permute-done((bf16[768,256]{1,0:T(8,128)(2,1)S(1)}, bf16[768,256]{1,0:T(8,128)(2,1)S(1)}, u32[]{:S(2)}, u32[]{:S(2)}) %collective-permute-start.5) | collective-permute-done | bytes 393248 | tf_op jit(solution)/shard_map/ppermute | solution.py:266
  69.4 1.9 %collective-permute-start.7 = (bf16[384,256]{1,0:T(8,128)(2,1)S(1)}, bf16[384,256]{1,0:T(8,128)(2,1)S(1)}, u32[]{:S(2)}, u32[]{:S(2)}) collective-permute-start(bf16[384,256]{1,0:T(8,128)(2,1)S(1)} %slice.16), channel_id=1, source_target_pairs={{0,1},{1,2},{2,3},{3,4},{4,5},{5,6},{6,7},{7,0},{8,9},{9,10},{10,1... | collective-permute-start | bytes 589832 | tf_op jit(solution)/shard_map/ppermute | solution.py:266
  71.4 5.1 %collective-permute-start.8 = (bf16[384,256]{1,0:T(8,128)(2,1)S(1)}, bf16[384,256]{1,0:T(8,128)(2,1)S(1)}, u32[]{:S(2)}, u32[]{:S(2)}) collective-permute-start(bf16[384,256]{1,0:T(8,128)(2,1)S(1)} %slice.17), channel_id=1, source_target_pairs={{0,7},{1,0},{2,1},{3,2},{4,3},{5,4},{6,5},{7,6},{8,15},{9,8},{10,9... | collective-permute-start | bytes 589832 | tf_op jit(solution)/shard_map/ppermute | solution.py:266
  76.5 0.3 fusion.12
  76.9 1.3 collective-permute-done.7
  78.2 0.3 fusion.7
  78.5 1.2 collective-permute-done.8
  79.7 0.3 fusion.5
  80.0 1.1 fusion.2.sum_hbm
  81.0 7.5 %middle.1 = (bf16[384,256]{1,0:T(8,128)(2,1)}, bf16[256,384]{1,0:T(8,128)(2,1)S(1)}, bf16[256,384]{1,0:T(8,128)(2,1)}, bf16[256,384]{1,0:T(8,128)(2,1)}, bf16[32,256,128]{2,1,0:T(8,128)(2,1)}) custom-call(f32[384,256]{1,0:T(8,128)} %fusion.2.sum_hbm, bf16[384,256]{1,0:T(8,128)(2,1)} %cotangent_hbm.1, f32[1,256]{1,0:T(1,128)S(1)} %bitcast.33, ...), custom_call_target="tpu_custom_call" | custom-call | tf_op jit(solution)/shard_map/middle/pallas_call | solution.py:329
  88.5 5.6 %collective-permute-start.13 = (bf16[256,384]{1,0:T(8,128)(2,1)}, bf16[256,384]{1,0:T(8,128)(2,1)}, u32[]{:S(2)}, u32[]{:S(2)}) collective-permute-start(bf16[256,384]{1,0:T(8,128)(2,1)} %get-tuple-element.28), channel_id=1, source_target_pairs={{0,7},{1,0},{2,1},{3,2},{4,3},{5,4},{6,5},{7,6},{8,15},{9,8},{10,9... | collective-permute-start | bytes 589832 | tf_op jit(solution)/shard_map/ppermute | solution.py:266
  94.1 1.9 %collective-permute-start.9 = (bf16[256,384]{1,0:T(8,128)(2,1)}, bf16[256,384]{1,0:T(8,128)(2,1)}, u32[]{:S(2)}, u32[]{:S(2)}) collective-permute-start(bf16[256,384]{1,0:T(8,128)(2,1)} %get-tuple-element.27), channel_id=1, source_target_pairs={{0,1},{1,2},{2,3},{3,4},{4,5},{5,6},{6,7},{7,0},{8,9},{9,10},{10,1... | collective-permute-start | bytes 589832 | tf_op jit(solution)/shard_map/ppermute | solution.py:266
  96.1 8.3 %all-to-all-start.1 = ((bf16[32,256,128]{2,1,0:T(8,128)(2,1)}), bf16[32,256,128]{2,1,0:T(8,128)(2,1)S(1)}, u32[]{:S(2)}, u32[]{:S(2)}) async-start(bf16[32,256,128]{2,1,0:T(8,128)(2,1)} %get-tuple-element.31), calls=%async_computation.1 | async-start | bytes 4194304 | tf_op jit(solution)/shard_map/all_to_all | solution.py:361
  104.4 1.1 copy-done.8
  105.5 1.4 hop.9
  106.9 5.1 %collective-permute-start.14 = (bf16[256,768]{1,0:T(8,128)(2,1)S(1)}, bf16[256,768]{1,0:T(8,128)(2,1)S(1)}, u32[]{:S(2)}, u32[]{:S(2)}) collective-permute-start(bf16[256,768]{1,0:T(8,128)(2,1)S(1)} %hop.9), channel_id=1, source_target_pairs={{0,7},{1,0},{2,1},{3,2},{4,3},{5,4},{6,5},{7,6},{8,15},{9,8},{10,9... | collective-permute-start | bytes 1179656 | tf_op jit(solution)/shard_map/ppermute | solution.py:266
  112.1 1.1 copy-done.6
  113.1 1.3 hop.6
  114.5 1.9 %collective-permute-start.10 = (bf16[256,768]{1,0:T(8,128)(2,1)S(1)}, bf16[256,768]{1,0:T(8,128)(2,1)S(1)}, u32[]{:S(2)}, u32[]{:S(2)}) collective-permute-start(bf16[256,768]{1,0:T(8,128)(2,1)S(1)} %hop.6), channel_id=1, source_target_pairs={{0,1},{1,2},{2,3},{3,4},{4,5},{5,6},{6,7},{7,0},{8,9},{9,10},{10,1... | collective-permute-start | bytes 1179656 | tf_op jit(solution)/shard_map/ppermute | solution.py:266
  116.4 4.3 %collective-permute-done.14.refs_2_ = bf16[256,768]{1,0:T(8,128)(2,1)S(1)} collective-permute-done((bf16[256,768]{1,0:T(8,128)(2,1)S(1)}, bf16[256,768]{1,0:T(8,128)(2,1)S(1)}, u32[]{:S(2)}, u32[]{:S(2)}) %collective-permute-start.14) | collective-permute-done | bytes 393248 | tf_op jit(solution)/shard_map/ppermute | solution.py:266
  120.7 0.4 hop.10
  121.1 5.7 %collective-permute-start.15 = (bf16[256,768]{1,0:T(8,128)(2,1)S(1)}, bf16[256,768]{1,0:T(8,128)(2,1)S(1)}, u32[]{:S(2)}, u32[]{:S(2)}) collective-permute-start(bf16[256,768]{1,0:T(8,128)(2,1)S(1)} %hop.10), channel_id=1, source_target_pairs={{0,7},{1,0},{2,1},{3,2},{4,3},{5,4},{6,5},{7,6},{8,15},{9,8},{10,9... | collective-permute-start | bytes 1179656 | tf_op jit(solution)/shard_map/ppermute | solution.py:266
  126.9 1.6 collective-permute-done.10.refs_2_
  128.5 0.4 hop.7
  128.8 1.9 %collective-permute-start.11 = (bf16[256,768]{1,0:T(8,128)(2,1)S(1)}, bf16[256,768]{1,0:T(8,128)(2,1)S(1)}, u32[]{:S(2)}, u32[]{:S(2)}) collective-permute-start(bf16[256,768]{1,0:T(8,128)(2,1)S(1)} %hop.7), channel_id=1, source_target_pairs={{0,1},{1,2},{2,3},{3,4},{4,5},{5,6},{6,7},{7,0},{8,9},{9,10},{10,1... | collective-permute-start | bytes 1179656 | tf_op jit(solution)/shard_map/ppermute | solution.py:266
  130.8 3.9 %collective-permute-done.15.refs_2_ = bf16[256,768]{1,0:T(8,128)(2,1)S(1)} collective-permute-done((bf16[256,768]{1,0:T(8,128)(2,1)S(1)}, bf16[256,768]{1,0:T(8,128)(2,1)S(1)}, u32[]{:S(2)}, u32[]{:S(2)}) %collective-permute-start.15) | collective-permute-done | bytes 393248 | tf_op jit(solution)/shard_map/ppermute | solution.py:266
  134.7 0.4 hop.11
  135.1 5.6 %collective-permute-start.16 = (bf16[256,768]{1,0:T(8,128)(2,1)S(1)}, bf16[256,768]{1,0:T(8,128)(2,1)S(1)}, u32[]{:S(2)}, u32[]{:S(2)}) collective-permute-start(bf16[256,768]{1,0:T(8,128)(2,1)S(1)} %hop.11), channel_id=1, source_target_pairs={{0,7},{1,0},{2,1},{3,2},{4,3},{5,4},{6,5},{7,6},{8,15},{9,8},{10,9... | collective-permute-start | bytes 1179656 | tf_op jit(solution)/shard_map/ppermute | solution.py:266
  140.7 1.3 collective-permute-done.11.refs_2_
  142.0 0.4 hop.8
  142.3 1.9 %collective-permute-start.12 = (bf16[256,768]{1,0:T(8,128)(2,1)S(1)}, bf16[256,768]{1,0:T(8,128)(2,1)S(1)}, u32[]{:S(2)}, u32[]{:S(2)}) collective-permute-start(bf16[256,768]{1,0:T(8,128)(2,1)S(1)} %hop.8), channel_id=1, source_target_pairs={{0,1},{1,2},{2,3},{3,4},{4,5},{5,6},{6,7},{7,0},{8,9},{9,10},{10,1... | collective-permute-start | bytes 1179656 | tf_op jit(solution)/shard_map/ppermute | solution.py:266
  144.3 3.3 %collective-permute-done.16.right_ref = bf16[256,768]{1,0:T(8,128)(2,1)S(1)} collective-permute-done((bf16[256,768]{1,0:T(8,128)(2,1)S(1)}, bf16[256,768]{1,0:T(8,128)(2,1)S(1)}, u32[]{:S(2)}, u32[]{:S(2)}) %collective-permute-start.16) | collective-permute-done | bytes 393248 | tf_op jit(solution)/shard_map/ppermute | solution.py:266
  147.6 7.0 %collective-permute-done.12.left_ref = bf16[256,768]{1,0:T(8,128)(2,1)S(1)} collective-permute-done((bf16[256,768]{1,0:T(8,128)(2,1)S(1)}, bf16[256,768]{1,0:T(8,128)(2,1)S(1)}, u32[]{:S(2)}, u32[]{:S(2)}) %collective-permute-start.12) | collective-permute-done | bytes 393248 | tf_op jit(solution)/shard_map/ppermute | solution.py:266
  154.6 0.4 close.1
  155.0 3.4 %collective-permute-start.17 = (bf16[256,384]{1,0:T(8,128)(2,1)S(1)}, bf16[256,384]{1,0:T(8,128)(2,1)S(1)}, u32[]{:S(2)}, u32[]{:S(2)}) collective-permute-start(bf16[256,384]{1,0:T(8,128)(2,1)S(1)} %get-tuple-element.30), channel_id=1, source_target_pairs={{0,8},{1,9},{2,10},{3,11},{4,12},{5,13},{6,14},{7,15},{8,0},{9,1},... | collective-permute-start | bytes 589832 | tf_op jit(solution)/shard_map/ppermute | solution.py:269
  158.5 1.3 gather.1.cut_ref
  159.7 4.4 %collective-permute-done.17.other_ref = bf16[256,384]{1,0:T(8,128)(2,1)S(1)} collective-permute-done((bf16[256,384]{1,0:T(8,128)(2,1)S(1)}, bf16[256,384]{1,0:T(8,128)(2,1)S(1)}, u32[]{:S(2)}, u32[]{:S(2)}) %collective-permute-start.17) | collective-permute-done | bytes 196640 | tf_op jit(solution)/shard_map/ppermute | solution.py:269
  164.2 1.0 last.1
  (48 shorter events, 0.2 us)
Async XLA Ops:
  1.9 16.4 %collective-permute-start = (bf16[384,256]{1,0:T(8,128)(2,1)S(1)}, bf16[384,256]{1,0:T(8,128)(2,1)S(1)}, u32[]{:S(2)}, u32[]{:S(2)}) collective-permute-start(bf16[384,256]{1,0:T(8,128)(2,1)S(1)} %project.1.own_ref.projected_ref), channel_id=1, source_target_pairs={{0,8},{1,9},{2,10},{3,11},{4,12},{5,13},{6,14},{7,15},{8,0},{9,1},... | collective-permute-start | bytes 589832 | tf_op jit(solution)/shard_map/ppermute | solution.py:269
  5.9 0.7 copy-start.14
  6.6 0.7 copy-start.16
  9.4 71.6 %all-to-all-start = ((bf16[32,128,256]{2,1,0:T(8,128)(2,1)}), bf16[32,128,256]{2,1,0:T(8,128)(2,1)}, u32[]{:S(2)}, u32[]{:S(2)}) async-start(bf16[32,128,256]{2,1,0:T(8,128)(2,1)} %fill.1), calls=%async_computation | async-start | bytes 4194304 | tf_op jit(solution)/shard_map/all_to_all | solution.py:292
  18.2 13.1 %copy-start.21 = (s32[1,1,16,4]{2,3,1,0:T(4,128)S(1)}, s32[1,1,16,4]{2,3,1,0:T(4,128)}, u32[]{:S(2)}) copy-start(s32[1,1,16,4]{2,3,1,0:T(4,128)} %param.16) | copy-start | bytes 772
  18.3 13.3 %copy-start.10 = (bf16[1,1,32,128,128]{4,3,2,1,0:T(8,128)(2,1)S(1)}, bf16[1,1,32,128,128]{4,3,2,1,0:T(8,128)(2,1)}, u32[]{:S(2)}) copy-start(bf16[1,1,32,128,128]{4,3,2,1,0:T(8,128)(2,1)} %param.18) | copy-start | bytes 3145732
  18.3 13.3 %copy-start.19 = (s32[1,1,32]{2,1,0:T(1,128)S(1)}, s32[1,1,32]{2,1,0:T(1,128)}, u32[]{:S(2)}) copy-start(s32[1,1,32]{2,1,0:T(1,128)} %param.21) | copy-start | bytes 388
  18.3 19.8 %collective-permute-start.2 = (bf16[768,256]{1,0:T(8,128)(2,1)S(1)}, bf16[768,256]{1,0:T(8,128)(2,1)S(1)}, u32[]{:S(2)}, u32[]{:S(2)}) collective-permute-start(bf16[768,256]{1,0:T(8,128)(2,1)S(1)} %pair.1), channel_id=1, source_target_pairs={{0,7},{1,0},{2,1},{3,2},{4,3},{5,4},{6,5},{7,6},{8,15},{9,8},{10,9... | collective-permute-start | bytes 1179656 | tf_op jit(solution)/shard_map/ppermute | solution.py:266
  29.4 14.3 %collective-permute-start.1 = (bf16[768,256]{1,0:T(8,128)(2,1)S(1)}, bf16[768,256]{1,0:T(8,128)(2,1)S(1)}, u32[]{:S(2)}, u32[]{:S(2)}) collective-permute-start(bf16[768,256]{1,0:T(8,128)(2,1)S(1)} %pair.1), channel_id=1, source_target_pairs={{0,1},{1,2},{2,3},{3,4},{4,5},{5,6},{6,7},{7,0},{8,9},{9,10},{10,1... | collective-permute-start | bytes 1179656 | tf_op jit(solution)/shard_map/ppermute | solution.py:266
  31.6 2.8 %copy-start.9 = (bf16[1,1,16,4,128,128]{5,4,3,2,1,0:T(8,128)(2,1)S(1)}, bf16[1,1,16,4,128,128]{5,4,3,2,1,0:T(8,128)(2,1)}, u32[]{:S(2)}) copy-start(bf16[1,1,16,4,128,128]{5,4,3,2,1,0:T(8,128)(2,1)} %param.15) | copy-start | bytes 6291460
  31.6 2.8 %copy-start.20 = (s32[1,1,16]{2,1,0:T(1,128)S(1)}, s32[1,1,16]{2,1,0:T(1,128)}, u32[]{:S(2)}) copy-start(s32[1,1,16]{2,1,0:T(1,128)} %param.17) | copy-start | bytes 196
  36.2 10.4 %copy-start.11 = (bf16[384,768]{1,0:T(8,128)(2,1)}, bf16[384,768]{1,0:T(8,128)(2,1)S(1)}, u32[]{:S(2)}) copy-start(bf16[384,768]{1,0:T(8,128)(2,1)S(1)} %get-tuple-element.17.mat_ref) | copy-start | bytes 1769476
  36.2 27.8 %copy-start = (bf16[384,768]{1,0:T(8,128)(2,1)}, bf16[384,768]{1,0:T(8,128)(2,1)S(1)}, u32[]{:S(2)}) copy-start(bf16[384,768]{1,0:T(8,128)(2,1)S(1)} %get-tuple-element.21.refs_1_) | copy-start | bytes 1769476
  36.2 28.1 %copy-start.2 = (bf16[384,768]{1,0:T(8,128)(2,1)}, bf16[384,768]{1,0:T(8,128)(2,1)S(1)}, u32[]{:S(2)}) copy-start(bf16[384,768]{1,0:T(8,128)(2,1)S(1)} %get-tuple-element.20.refs_1_) | copy-start | bytes 1769476
  36.2 40.3 %copy-start.5 = (bf16[384,768]{1,0:T(8,128)(2,1)}, bf16[384,768]{1,0:T(8,128)(2,1)S(1)}, u32[]{:S(2)}) copy-start(bf16[384,768]{1,0:T(8,128)(2,1)S(1)} %get-tuple-element.23.refs_1_) | copy-start | bytes 1769476
  36.3 43.4 %copy-start.4 = (bf16[384,768]{1,0:T(8,128)(2,1)}, bf16[384,768]{1,0:T(8,128)(2,1)S(1)}, u32[]{:S(2)}) copy-start(bf16[384,768]{1,0:T(8,128)(2,1)S(1)} %get-tuple-element.24.mat_hbm) | copy-start | bytes 1769476
  36.3 43.7 %copy-start.7 = (bf16[384,768]{1,0:T(8,128)(2,1)}, bf16[384,768]{1,0:T(8,128)(2,1)S(1)}, u32[]{:S(2)}) copy-start(bf16[384,768]{1,0:T(8,128)(2,1)S(1)} %get-tuple-element.22.refs_1_) | copy-start | bytes 1769476
  38.1 20.8 %collective-permute-start.4 = (bf16[768,256]{1,0:T(8,128)(2,1)S(1)}, bf16[768,256]{1,0:T(8,128)(2,1)S(1)}, u32[]{:S(2)}, u32[]{:S(2)}) collective-permute-start(bf16[768,256]{1,0:T(8,128)(2,1)S(1)} %collective-permute-done.2), channel_id=1, source_target_pairs={{0,7},{1,0},{2,1},{3,2},{4,3},{5,4},{6,5},{7,6},{8,15},{9,8},{10,9... | collective-permute-start | bytes 1179656 | tf_op jit(solution)/shard_map/ppermute | solution.py:266
  43.7 13.3 %collective-permute-start.3 = (bf16[768,256]{1,0:T(8,128)(2,1)S(1)}, bf16[768,256]{1,0:T(8,128)(2,1)S(1)}, u32[]{:S(2)}, u32[]{:S(2)}) collective-permute-start(bf16[768,256]{1,0:T(8,128)(2,1)S(1)} %collective-permute-done.1), channel_id=1, source_target_pairs={{0,1},{1,2},{2,3},{3,4},{4,5},{5,6},{6,7},{7,0},{8,9},{9,10},{10,1... | collective-permute-start | bytes 1179656 | tf_op jit(solution)/shard_map/ppermute | solution.py:266
  57.0 12.4 %collective-permute-start.5 = (bf16[768,256]{1,0:T(8,128)(2,1)S(1)}, bf16[768,256]{1,0:T(8,128)(2,1)S(1)}, u32[]{:S(2)}, u32[]{:S(2)}) collective-permute-start(bf16[768,256]{1,0:T(8,128)(2,1)S(1)} %collective-permute-done.3), channel_id=1, source_target_pairs={{0,1},{1,2},{2,3},{3,4},{4,5},{5,6},{6,7},{7,0},{8,9},{9,10},{10,1... | collective-permute-start | bytes 1179656 | tf_op jit(solution)/shard_map/ppermute | solution.py:266
  58.9 12.5 %collective-permute-start.6 = (bf16[768,256]{1,0:T(8,128)(2,1)S(1)}, bf16[768,256]{1,0:T(8,128)(2,1)S(1)}, u32[]{:S(2)}, u32[]{:S(2)}) collective-permute-start(bf16[768,256]{1,0:T(8,128)(2,1)S(1)} %collective-permute-done.4), channel_id=1, source_target_pairs={{0,7},{1,0},{2,1},{3,2},{4,3},{5,4},{6,5},{7,6},{8,15},{9,8},{10,9... | collective-permute-start | bytes 1179656 | tf_op jit(solution)/shard_map/ppermute | solution.py:266
  69.4 8.8 %collective-permute-start.7 = (bf16[384,256]{1,0:T(8,128)(2,1)S(1)}, bf16[384,256]{1,0:T(8,128)(2,1)S(1)}, u32[]{:S(2)}, u32[]{:S(2)}) collective-permute-start(bf16[384,256]{1,0:T(8,128)(2,1)S(1)} %slice.16), channel_id=1, source_target_pairs={{0,1},{1,2},{2,3},{3,4},{4,5},{5,6},{6,7},{7,0},{8,9},{9,10},{10,1... | collective-permute-start | bytes 589832 | tf_op jit(solution)/shard_map/ppermute | solution.py:266
  71.4 8.3 %collective-permute-start.8 = (bf16[384,256]{1,0:T(8,128)(2,1)S(1)}, bf16[384,256]{1,0:T(8,128)(2,1)S(1)}, u32[]{:S(2)}, u32[]{:S(2)}) collective-permute-start(bf16[384,256]{1,0:T(8,128)(2,1)S(1)} %slice.17), channel_id=1, source_target_pairs={{0,7},{1,0},{2,1},{3,2},{4,3},{5,4},{6,5},{7,6},{8,15},{9,8},{10,9... | collective-permute-start | bytes 589832 | tf_op jit(solution)/shard_map/ppermute | solution.py:266
  78.4 2.6 %copy-start.18 = (f32[256]{0:T(256)S(1)}, f32[256]{0:T(256)}, u32[]{:S(2)}) copy-start(f32[256]{0:T(256)} %param.13) | copy-start | bytes 3076
  88.5 15.9 %collective-permute-start.13 = (bf16[256,384]{1,0:T(8,128)(2,1)}, bf16[256,384]{1,0:T(8,128)(2,1)}, u32[]{:S(2)}, u32[]{:S(2)}) collective-permute-start(bf16[256,384]{1,0:T(8,128)(2,1)} %get-tuple-element.28), channel_id=1, source_target_pairs={{0,7},{1,0},{2,1},{3,2},{4,3},{5,4},{6,5},{7,6},{8,15},{9,8},{10,9... | collective-permute-start | bytes 589832 | tf_op jit(solution)/shard_map/ppermute | solution.py:266
  94.1 17.9 %collective-permute-start.9 = (bf16[256,384]{1,0:T(8,128)(2,1)}, bf16[256,384]{1,0:T(8,128)(2,1)}, u32[]{:S(2)}, u32[]{:S(2)}) collective-permute-start(bf16[256,384]{1,0:T(8,128)(2,1)} %get-tuple-element.27), channel_id=1, source_target_pairs={{0,1},{1,2},{2,3},{3,4},{4,5},{5,6},{6,7},{7,0},{8,9},{9,10},{10,1... | collective-permute-start | bytes 589832 | tf_op jit(solution)/shard_map/ppermute | solution.py:266
  96.1 62.3 %all-to-all-start.1 = ((bf16[32,256,128]{2,1,0:T(8,128)(2,1)}), bf16[32,256,128]{2,1,0:T(8,128)(2,1)S(1)}, u32[]{:S(2)}, u32[]{:S(2)}) async-start(bf16[32,256,128]{2,1,0:T(8,128)(2,1)} %get-tuple-element.31), calls=%async_computation.1 | async-start | bytes 4194304 | tf_op jit(solution)/shard_map/all_to_all | solution.py:361
  104.4 16.3 %copy-start.3 = (bf16[384,768]{1,0:T(8,128)(2,1)S(1)}, bf16[384,768]{1,0:T(8,128)(2,1)}, u32[]{:S(2)}) copy-start(bf16[384,768]{1,0:T(8,128)(2,1)} %copy-done.2) | copy-start | bytes 1769476
  104.4 1.1 copy-start.8
  105.5 22.9 %copy-start.1 = (bf16[384,768]{1,0:T(8,128)(2,1)S(1)}, bf16[384,768]{1,0:T(8,128)(2,1)}, u32[]{:S(2)}) copy-start(bf16[384,768]{1,0:T(8,128)(2,1)} %copy-done) | copy-start | bytes 1769476
  106.9 13.8 %collective-permute-start.14 = (bf16[256,768]{1,0:T(8,128)(2,1)S(1)}, bf16[256,768]{1,0:T(8,128)(2,1)S(1)}, u32[]{:S(2)}, u32[]{:S(2)}) collective-permute-start(bf16[256,768]{1,0:T(8,128)(2,1)S(1)} %hop.9), channel_id=1, source_target_pairs={{0,7},{1,0},{2,1},{3,2},{4,3},{5,4},{6,5},{7,6},{8,15},{9,8},{10,9... | collective-permute-start | bytes 1179656 | tf_op jit(solution)/shard_map/ppermute | solution.py:266
  112.1 1.1 copy-start.6
  114.5 14.0 %collective-permute-start.10 = (bf16[256,768]{1,0:T(8,128)(2,1)S(1)}, bf16[256,768]{1,0:T(8,128)(2,1)S(1)}, u32[]{:S(2)}, u32[]{:S(2)}) collective-permute-start(bf16[256,768]{1,0:T(8,128)(2,1)S(1)} %hop.6), channel_id=1, source_target_pairs={{0,1},{1,2},{2,3},{3,4},{4,5},{5,6},{6,7},{7,0},{8,9},{9,10},{10,1... | collective-permute-start | bytes 1179656 | tf_op jit(solution)/shard_map/ppermute | solution.py:266
  121.1 33.4 %copy-start.12 = (bf16[384,768]{1,0:T(8,128)(2,1)S(1)}, bf16[384,768]{1,0:T(8,128)(2,1)}, u32[]{:S(2)}) copy-start(bf16[384,768]{1,0:T(8,128)(2,1)} %copy-done.11) | copy-start | bytes 1769476
  121.1 13.6 %collective-permute-start.15 = (bf16[256,768]{1,0:T(8,128)(2,1)S(1)}, bf16[256,768]{1,0:T(8,128)(2,1)S(1)}, u32[]{:S(2)}, u32[]{:S(2)}) collective-permute-start(bf16[256,768]{1,0:T(8,128)(2,1)S(1)} %hop.10), channel_id=1, source_target_pairs={{0,7},{1,0},{2,1},{3,2},{4,3},{5,4},{6,5},{7,6},{8,15},{9,8},{10,9... | collective-permute-start | bytes 1179656 | tf_op jit(solution)/shard_map/ppermute | solution.py:266
  128.8 13.1 %collective-permute-start.11 = (bf16[256,768]{1,0:T(8,128)(2,1)S(1)}, bf16[256,768]{1,0:T(8,128)(2,1)S(1)}, u32[]{:S(2)}, u32[]{:S(2)}) collective-permute-start(bf16[256,768]{1,0:T(8,128)(2,1)S(1)} %hop.7), channel_id=1, source_target_pairs={{0,1},{1,2},{2,3},{3,4},{4,5},{5,6},{6,7},{7,0},{8,9},{9,10},{10,1... | collective-permute-start | bytes 1179656 | tf_op jit(solution)/shard_map/ppermute | solution.py:266
  135.1 12.5 %collective-permute-start.16 = (bf16[256,768]{1,0:T(8,128)(2,1)S(1)}, bf16[256,768]{1,0:T(8,128)(2,1)S(1)}, u32[]{:S(2)}, u32[]{:S(2)}) collective-permute-start(bf16[256,768]{1,0:T(8,128)(2,1)S(1)} %hop.11), channel_id=1, source_target_pairs={{0,7},{1,0},{2,1},{3,2},{4,3},{5,4},{6,5},{7,6},{8,15},{9,8},{10,9... | collective-permute-start | bytes 1179656 | tf_op jit(solution)/shard_map/ppermute | solution.py:266
  142.3 16.1 %copy-start.15 = (s32[1,1,32]{2,1,0:T(1,128)S(1)}, s32[1,1,32]{2,1,0:T(1,128)}, u32[]{:S(2)}) copy-start(s32[1,1,32]{2,1,0:T(1,128)} %param.19) | copy-start | bytes 388
  142.3 16.1 %copy-start.17 = (s32[1,1,32]{2,1,0:T(1,128)S(1)}, s32[1,1,32]{2,1,0:T(1,128)}, u32[]{:S(2)}) copy-start(s32[1,1,32]{2,1,0:T(1,128)} %param.20) | copy-start | bytes 388
  142.3 12.2 %collective-permute-start.12 = (bf16[256,768]{1,0:T(8,128)(2,1)S(1)}, bf16[256,768]{1,0:T(8,128)(2,1)S(1)}, u32[]{:S(2)}, u32[]{:S(2)}) collective-permute-start(bf16[256,768]{1,0:T(8,128)(2,1)S(1)} %hop.8), channel_id=1, source_target_pairs={{0,1},{1,2},{2,3},{3,4},{4,5},{5,6},{6,7},{7,0},{8,9},{9,10},{10,1... | collective-permute-start | bytes 1179656 | tf_op jit(solution)/shard_map/ppermute | solution.py:266
  155.0 9.2 %copy-start.13 = (bf16[256,256]{1,0:T(8,128)(2,1)S(1)}, bf16[256,256]{1,0:T(8,128)(2,1)}, u32[]{:S(2)}) copy-start(bf16[256,256]{1,0:T(8,128)(2,1)} %weight_ref.1) | copy-start | bytes 393220
  155.0 9.2 %collective-permute-start.17 = (bf16[256,384]{1,0:T(8,128)(2,1)S(1)}, bf16[256,384]{1,0:T(8,128)(2,1)S(1)}, u32[]{:S(2)}, u32[]{:S(2)}) collective-permute-start(bf16[256,384]{1,0:T(8,128)(2,1)S(1)} %get-tuple-element.30), channel_id=1, source_target_pairs={{0,8},{1,9},{2,10},{3,11},{4,12},{5,13},{6,14},{7,15},{8,0},{9,1},... | collective-permute-start | bytes 589832 | tf_op jit(solution)/shard_map/ppermute | solution.py:269

commit v4 on v3

--- a/solution.py
+++ b/solution.py
@@ -11,7 +11,8 @@
 CHUNKS = 4
 VMEM_LIMIT = 16 * 1024 * 1024
 PAIR_COST = 100_000_000_000
-CLOSE_COST = 27_800_000_000
+TERMS_COST = 1_600_000_000
+CLOSE_COST = 30_500_000_000
 
 
 def spec(space):
@@ -129,24 +130,37 @@
     pair_ref[pl.ds(pl.multiple_of(rows - place, TILE), rows)] = other_ref[...]
 
 
+def tail_kernel(sum_ref, mat_a, from_a, mat_b, from_b, mat_c, from_c, out_hbm, total, sem):
+    total[...] = (
+        sum_ref[...]
+        + product(mat_a[...], from_a[...])
+        + product(mat_b[...], from_b[...])
+        + product(mat_c[...], from_c[...])
+    )
+    copy = pltpu.make_async_copy(total, out_hbm, sem)
+    copy.start()
+    copy.wait()
+
+
 def middle_kernel(
     sum_hbm,
     cotangent_hbm,
     bias_ref,
-    mat_hbm,
+    right_hbm,
+    left_hbm,
+    across_hbm,
     cut_hbm,
     far_hbm,
     hidden_ref,
     grad_ref,
-    low_ref,
-    high_ref,
-    terms_hbm,
+    right_ref,
+    left_ref,
+    across_ref,
     total,
     cotangent,
-    mat,
+    mats,
     cut,
     far,
-    terms,
     sems,
 ):
     rows, width = total.shape
@@ -159,7 +173,8 @@
         copies.append(move(cut_hbm.at[piece], cut.at[piece], piece))
         copies.append(move(far_hbm.at[span], far.at[span], chunks + piece))
     copies.append(move(cotangent_hbm, cotangent, 2 * chunks + 1))
-    copies.append(move(mat_hbm, mat, 2 * chunks + 2))
+    for place, mat in enumerate((right_hbm, left_hbm, across_hbm)):
+        copies.append(move(mat, mats.at[place], 2 * chunks + 2 + place))
     for copy in copies:
         copy.start()
     copies[0].wait()
@@ -170,19 +185,33 @@
         total[...] += product(cut[piece], arrived)
     activated, derivative = silu_parts(total[...] + bias_ref[...])
     hidden_ref[...] = activated.astype(BF)
-    copies[-2].wait()
+    copies[-4].wait()
     grad = (cotangent[...].astype(F32) * derivative).T.astype(BF)
     grad_ref[...] = grad
-    copies[-1].wait()
-    low_ref[...] = product(grad, mat[:, :rows]).astype(BF)
-    high_ref[...] = product(grad, mat[:, rows:]).astype(BF)
+    for place, out_ref in enumerate((right_ref, left_ref, across_ref)):
+        copies[place - 3].wait()
+        out_ref[...] = product(grad, mats[place]).astype(BF)
+
+
+def terms_kernel(grad_ref, cut_hbm, terms_hbm, cut, terms, sems):
+    chunks = cut.shape[0]
+    chunk = terms.shape[0] // chunks
+    loads = [
+        pltpu.make_async_copy(cut_hbm.at[piece], cut.at[piece], sems.at[piece])
+        for piece in range(chunks)
+    ]
     stores = []
+    for copy in loads:
+        copy.start()
     for piece in range(chunks):
-        result = product(grad, cut[piece]).astype(BF)
+        loads[piece].wait()
+        result = product(grad_ref[...], cut[piece]).astype(BF)
         for slot in range(chunk):
             terms[piece * chunk + slot] = result[:, slot * TILE : (slot + 1) * TILE]
         span = pl.ds(piece * chunk, chunk)
-        stores.append(move(terms.at[span], terms_hbm.at[span], 2 * chunks + 3 + piece))
+        stores.append(
+            pltpu.make_async_copy(terms.at[span], terms_hbm.at[span], sems.at[chunks + piece])
+        )
         stores[-1].start()
     for copy in stores:
         copy.wait()
@@ -202,23 +231,21 @@
     lax.fori_loop(0, arrived_ref.shape[0], add, 0)
 
 
-def hop_kernel(at, grad_ref, mat_ref, arrived_ref, out_ref):
-    wide, held = out_ref.shape[1], arrived_ref.shape[1]
-    for low, high in ((0, at), (at, at + held), (at + held, wide)):
-        if low < high:
-            term = product(grad_ref[...], mat_ref[:, low:high])
-            if low == at:
-                term += arrived_ref[...].astype(F32)
-            out_ref[:, low:high] = term.astype(BF)
-
-
-def close_kernel(half_ref, grad_ref, mat_ref, left_ref, right_ref, own_ref, other_ref):
+def hop_kernel(grad_ref, mat_ref, arrived_ref, out_ref):
+    term = product(grad_ref[...], mat_ref[...]) + arrived_ref[...].astype(F32)
+    out_ref[...] = term.astype(BF)
+
+
+def close_kernel(
+    half_ref, grad_ref, mat_ref, left_ref, right_ref, across_ref, own_ref, other_ref
+):
     rows = grad_ref.shape[1]
     mine = pl.ds(pl.multiple_of(half_ref[0] * rows, TILE), rows)
     theirs = pl.ds(pl.multiple_of((1 - half_ref[0]) * rows, TILE), rows)
 
     def total(columns):
         arrived = left_ref[:, columns].astype(F32) + right_ref[:, columns].astype(F32)
+        arrived += across_ref[:, columns].astype(F32)
         return product(grad_ref[...], mat_ref[:, columns]) + arrived
 
     other_ref[...] = total(theirs).astype(BF)
@@ -317,61 +344,78 @@
     )(half.reshape(1), projected, partner)
     running = product(dense[0], pair)
     right = left = pair
+    across_ring = along_ring(pair, reach)
     for hop in range(1, reach):
         right, left = along_ring(right, 1), along_ring(left, -1)
-        running = running + product(dense[ring - hop], right)
-        running = running + product(dense[hop], left)
-    low, high = along_ring(right[:rows], 1), along_ring(left[rows:], -1)
-
-    running = running + product(dense[reach][:, :rows], low)
-    running = running + product(dense[reach][:, rows:], high)
-
-    hidden, grad_pre, low, high, terms = call(
+        if hop < reach - 1:
+            running = running + product(dense[ring - hop], right)
+            running = running + product(dense[hop], left)
+    running = call(
+        tail_kernel,
+        "tail",
+        pltpu.HBM((rows, width), F32),
+        [VMEM] * 7,
+        HBM,
+        [pltpu.VMEM((rows, width), F32), pltpu.SemaphoreType.DMA],
+    )(running, dense[reach + 1], right, dense[reach - 1], left, dense[reach], across_ring)
+
+    hidden, grad_pre, right, left, across_ring = call(
         middle_kernel,
         "middle",
-        (shape((rows, width), BF),)
-        + (shape((width, rows), BF),) * 3
-        + (pltpu.HBM((parts, width, TILE), BF),),
-        [HBM, HBM, VMEM, HBM, HBM, HBM],
-        (VMEM,) * 4 + (HBM,),
+        (shape((rows, width), BF), shape((width, rows), BF)) + (shape((width, wide), BF),) * 3,
+        [HBM, HBM, VMEM] + [HBM] * 5,
+        (VMEM,) * 5,
         [
             pltpu.VMEM((rows, width), F32),
             pltpu.VMEM((rows, width), BF),
-            pltpu.VMEM((rows, wide), BF),
+            pltpu.VMEM((3, rows, wide), BF),
             pltpu.VMEM(dense_cut.shape, BF),
             pltpu.VMEM((parts, TILE, width), BF),
-            pltpu.VMEM((parts, width, TILE), BF),
-            pltpu.SemaphoreType.DMA((3 * CHUNKS + 3,)),
+            pltpu.SemaphoreType.DMA((2 * CHUNKS + 5,)),
         ],
     )(
         in_hbm(running),
         in_hbm(cotangent),
         bias.reshape(1, width),
+        in_hbm(dense[reach - 1]),
+        in_hbm(dense[reach + 1]),
         in_hbm(dense[reach]),
         in_hbm(dense_cut),
         in_hbm(incoming),
     )
 
-    def add_on(mat, arrived, at):
-        return call(
-            lambda *refs: hop_kernel(at, *refs), "hop", shape((width, wide), BF), [VMEM] * 3, VMEM
-        )(grad_pre, mat, arrived)
-
-    low, high = along_ring(low, 1), along_ring(high, -1)
+    def add_on(mat, arrived):
+        return call(hop_kernel, "hop", shape((width, wide), BF), [VMEM] * 3, VMEM)(
+            grad_pre, mat, arrived
+        )
+
+    right, left = along_ring(right, 1), along_ring(left, -1)
+    across_ring = along_ring(across_ring, reach)
+    terms = call(
+        terms_kernel,
+        "terms",
+        pltpu.HBM((parts, width, TILE), BF),
+        [VMEM, HBM],
+        HBM,
+        [
+            pltpu.VMEM(dense_cut.shape, BF),
+            pltpu.VMEM((parts, width, TILE), BF),
+            pltpu.SemaphoreType.DMA((2 * CHUNKS,)),
+        ],
+        flops=TERMS_COST,
+    )(grad_pre, in_hbm(dense_cut))
     returned = lax.all_to_all(terms, "dom", split_axis=0, concat_axis=0, tiled=True)
-    for hop in range(reach - 1, 0, -1):
-        first = hop == reach - 1
-        right = add_on(dense[hop], low if first else from_left, 0)
-        left = add_on(dense[ring - hop], high if first else from_right, rows if first else 0)
-        from_left, from_right = along_ring(right, 1), along_ring(left, -1)
+    for hop in range(reach - 2, 0, -1):
+        right = along_ring(add_on(dense[hop], right), 1)
+        left = along_ring(add_on(dense[ring - hop], left), -1)
     own, other = call(
         close_kernel,
         "close",
         (shape((width, rows), F32), shape((width, rows), BF)),
-        [SMEM] + [VMEM] * 4,
+        [SMEM] + [VMEM] * 5,
         (VMEM, VMEM),
         flops=CLOSE_COST,
-    )(half.reshape(1), grad_pre, dense[0], from_left, from_right)
+    )(half.reshape(1), grad_pre, dense[0], right, left, across_ring)
     other = across(other)
     from_cuts = call(
         gather_kernel, "gather", shape((width, rows), F32), [SMEM, SMEM, VMEM], VMEM, moved=2 << 20

time: 166 us -> 179 us (1.078)
  the two profiles are of different devices: /device:TPU:2 before, /device:TPU:1 now
where the time goes in v4:
time: 179 us; the launch traced here: 178 us
  starting transfers between devices  82.5 us (46%)
  waiting for transfers between devices  58.5 us (33%)
  Pallas kernels  25.7 us (14%)
  local copies, waits for them, and re-layouts  5.74 us (3%)
  matrix products  4.6 us (3%)
    ppermute x14, waiting for transfers between devices, along_ring(): return lax.ppermute(value, 'blk', moves)  53.9 us
    ppermute x14, starting transfers between devices, along_ring(): return lax.ppermute(value, 'blk', moves)  52 us
    all_to_all x1, starting transfers between devices, on_device(): lax.all_to_all(terms, 'dom', split_axis=0, concat_axis=0, tiled=True)  14.7 us
    all_to_all x1, starting transfers between devices, on_device(): lax.all_to_all(outgoing, 'dom', split_axis=0, concat_axis=0, tiled=True)  8.25 us
    ppermute x2, starting transfers between devices, across(): lax.ppermute(value, 'blk', [(i, (i + ring) % peers) for i in range(peers)])  7.53 us
    unnamed x47, local copies, waits for them, and re-layouts  5.65 us
    pallas_call x1, Pallas kernels, on_device(): call(middle_kernel, 'middle', (shape((rows, width), BF), shape((width, ro...  5.61 us
    ppermute x2, waiting for transfers between devices, across(): lax.ppermute(value, 'blk', [(i, (i + ring) % peers) for i in range(peers)])  4.63 us
  transfers between devices with their start and end apart: 18, of which 9 were waited for; matrix products, arithmetic and copies ran while one was open for 3% of the time, Pallas kernels for 10%

profile of v4, /device:TPU:1, one launch (start us, length us, event | category | flops | bytes accessed | tf_op | source)
XLA Modules:
  0.0 178.4 jit_solution(12031352621254495321)
XLA Ops:
  0.6 1.2 project.1.own_ref.projected_ref
  1.9 5.5 %collective-permute-start = (bf16[384,256]{1,0:T(8,128)(2,1)S(1)}, bf16[384,256]{1,0:T(8,128)(2,1)S(1)}, u32[]{:S(2)}, u32[]{:S(2)}) collective-permute-start(bf16[384,256]{1,0:T(8,128)(2,1)S(1)} %project.1.own_ref.projected_ref), channel_id=1, source_target_pairs={{0,8},{1,9},{2,10},{3,11},{4,12},{5,13},{6,14},{7,15},{8,0},{9,1},... | collective-permute-start | bytes 589832 | tf_op jit(solution)/shard_map/ppermute | solution.py:296
  7.4 0.0 copy-start.12
  7.4 0.6 copy-done.12
  8.0 0.7 copy-done.14
  8.7 2.2 %fill.1 = bf16[32,128,256]{2,1,0:T(8,128)(2,1)} custom-call(s32[32]{0:T(128)S(1)} %bitcast.23, s32[32]{0:T(128)S(1)} %bitcast.25, bf16[384,256]{1,0:T(8,128)(2,1)S(1)} %project.1.own_ref.projected_ref), custom_call_target="tpu_custom_call" | custom-call | tf_op jit(solution)/shard_map/fill/pallas_call | solution.py:311
  10.8 8.3 %all-to-all-start = ((bf16[32,128,256]{2,1,0:T(8,128)(2,1)}), bf16[32,128,256]{2,1,0:T(8,128)(2,1)S(1)}, u32[]{:S(2)}, u32[]{:S(2)}) async-start(bf16[32,128,256]{2,1,0:T(8,128)(2,1)} %fill.1), calls=%async_computation | async-start | bytes 4194304 | tf_op jit(solution)/shard_map/all_to_all | solution.py:319
  19.1 0.0 copy-start.22
  19.2 0.0 copy-start.8
  19.2 0.0 copy-start.17
  19.2 0.8 pair.1
  20.0 10.7 %collective-permute-start.2 = (bf16[768,256]{1,0:T(8,128)(2,1)}, bf16[768,256]{1,0:T(8,128)(2,1)}, u32[]{:S(2)}, u32[]{:S(2)}) collective-permute-start(bf16[768,256]{1,0:T(8,128)(2,1)} %pair.1), channel_id=1, source_target_pairs={{0,7},{1,0},{2,1},{3,2},{4,3},{5,4},{6,5},{7,6},{8,15},{9,8},{10,9... | collective-permute-start | bytes 1179656 | tf_op jit(solution)/shard_map/ppermute | solution.py:293
  30.6 1.9 %collective-permute-start.1 = (bf16[768,256]{1,0:T(8,128)(2,1)}, bf16[768,256]{1,0:T(8,128)(2,1)}, u32[]{:S(2)}, u32[]{:S(2)}) collective-permute-start(bf16[768,256]{1,0:T(8,128)(2,1)} %pair.1), channel_id=1, source_target_pairs={{0,1},{1,2},{2,3},{3,4},{4,5},{5,6},{6,7},{7,0},{8,9},{9,10},{10,1... | collective-permute-start | bytes 1179656 | tf_op jit(solution)/shard_map/ppermute | solution.py:293
  32.6 0.1 copy.14
  32.7 0.1 reshape_squeeze.3.refs_0_
  32.8 0.0 copy-start.7
  32.8 0.0 copy-start.18
  32.8 2.8 %spread_cut.1.cut_hbm = bf16[4,384,1024]{2,1,0:T(8,128)(2,1)} custom-call(s32[32]{0:T(128)S(1)} %bitcast.28, bf16[32,128,128]{2,1,0:T(8,128)(2,1)S(1)} %bitcast.22), custom_call_target="tpu_custom_call" | custom-call | bytes 6291456 | tf_op jit(solution)/shard_map/spread_cut/pallas_call | solution.py:329
  35.6 1.7 spread.1
  37.4 3.3 %collective-permute-start.7 = (bf16[768,256]{1,0:T(8,128)(2,1)}, bf16[768,256]{1,0:T(8,128)(2,1)S(1)}, u32[]{:S(2)}, u32[]{:S(2)}) collective-permute-start(bf16[768,256]{1,0:T(8,128)(2,1)} %pair.1), channel_id=1, source_target_pairs={{0,4},{1,5},{2,6},{3,7},{4,0},{5,1},{6,2},{7,3},{8,12},{9,13},{10,... | collective-permute-start | bytes 1179656 | tf_op jit(solution)/shard_map/ppermute | solution.py:293
  40.7 3.8 %collective-permute-start.4 = (bf16[768,256]{1,0:T(8,128)(2,1)}, bf16[768,256]{1,0:T(8,128)(2,1)S(1)}, u32[]{:S(2)}, u32[]{:S(2)}) collective-permute-start(bf16[768,256]{1,0:T(8,128)(2,1)} %collective-permute-done.2), channel_id=1, source_target_pairs={{0,7},{1,0},{2,1},{3,2},{4,3},{5,4},{6,5},{7,6},{8,15},{9,8},{10,9... | collective-permute-start | bytes 1179656 | tf_op jit(solution)/shard_map/ppermute | solution.py:293
  44.5 14.5 %collective-permute-done.1 = bf16[768,256]{1,0:T(8,128)(2,1)} collective-permute-done((bf16[768,256]{1,0:T(8,128)(2,1)}, bf16[768,256]{1,0:T(8,128)(2,1)}, u32[]{:S(2)}, u32[]{:S(2)}) %collective-permute-start.1) | collective-permute-done | bytes 393248 | tf_op jit(solution)/shard_map/ppermute | solution.py:293
  59.1 1.9 %collective-permute-start.3 = (bf16[768,256]{1,0:T(8,128)(2,1)}, bf16[768,256]{1,0:T(8,128)(2,1)S(1)}, u32[]{:S(2)}, u32[]{:S(2)}) collective-permute-start(bf16[768,256]{1,0:T(8,128)(2,1)} %collective-permute-done.1), channel_id=1, source_target_pairs={{0,1},{1,2},{2,3},{3,4},{4,5},{5,6},{6,7},{7,0},{8,9},{9,10},{10,1... | collective-permute-start | bytes 1179656 | tf_op jit(solution)/shard_map/ppermute | solution.py:293
  61.0 1.3 fusion.2
  62.3 1.3 fusion.3
  63.6 1.3 fusion.1
  65.0 5.4 %collective-permute-done.3 = bf16[768,256]{1,0:T(8,128)(2,1)S(1)} collective-permute-done((bf16[768,256]{1,0:T(8,128)(2,1)}, bf16[768,256]{1,0:T(8,128)(2,1)S(1)}, u32[]{:S(2)}, u32[]{:S(2)}) %collective-permute-start.3) | collective-permute-done | bytes 393248 | tf_op jit(solution)/shard_map/ppermute | solution.py:293
  70.4 1.9 %collective-permute-start.5 = (bf16[768,256]{1,0:T(8,128)(2,1)S(1)}, bf16[768,256]{1,0:T(8,128)(2,1)S(1)}, u32[]{:S(2)}, u32[]{:S(2)}) collective-permute-start(bf16[768,256]{1,0:T(8,128)(2,1)S(1)} %collective-permute-done.3), channel_id=1, source_target_pairs={{0,1},{1,2},{2,3},{3,4},{4,5},{5,6},{6,7},{7,0},{8,9},{9,10},{10,1... | collective-permute-start | bytes 1179656 | tf_op jit(solution)/shard_map/ppermute | solution.py:293
  72.3 4.6 %collective-permute-start.6 = (bf16[768,256]{1,0:T(8,128)(2,1)S(1)}, bf16[768,256]{1,0:T(8,128)(2,1)S(1)}, u32[]{:S(2)}, u32[]{:S(2)}) collective-permute-start(bf16[768,256]{1,0:T(8,128)(2,1)S(1)} %collective-permute-done.4), channel_id=1, source_target_pairs={{0,7},{1,0},{2,1},{3,2},{4,3},{5,4},{6,5},{7,6},{8,15},{9,8},{10,9... | collective-permute-start | bytes 1179656 | tf_op jit(solution)/shard_map/ppermute | solution.py:293
  76.9 0.3 fusion.4
  77.2 0.3 fusion.sum_ref
  77.6 0.0 copy-start.16
  77.6 3.0 %collective-permute-done.5.from_a = bf16[768,256]{1,0:T(8,128)(2,1)S(1)} collective-permute-done((bf16[768,256]{1,0:T(8,128)(2,1)S(1)}, bf16[768,256]{1,0:T(8,128)(2,1)S(1)}, u32[]{:S(2)}, u32[]{:S(2)}) %collective-permute-start.5) | collective-permute-done | bytes 393248 | tf_op jit(solution)/shard_map/ppermute | solution.py:293
  80.6 1.0 collective-permute-done.6.from_b
  81.6 1.4 tail.1.sum_hbm
  83.0 1.3 copy-done.21
  84.4 5.6 %middle.1 = (bf16[384,256]{1,0:T(8,128)(2,1)}, bf16[256,384]{1,0:T(8,128)(2,1)S(1)}, bf16[256,768]{1,0:T(8,128)(2,1)}, bf16[256,768]{1,0:T(8,128)(2,1)}, bf16[256,768]{1,0:T(8,128)(2,1)S(1)}) custom-call(f32[384,256]{1,0:T(8,128)} %tail.1.sum_hbm, bf16[384,256]{1,0:T(8,128)(2,1)} %cotangent_hbm.1, f32[1,256]{1,0:T(1,128)S(1)} %bitcast.27, ...), custom_call_target="tpu_custom_call" | custom-call | tf_op jit(solution)/shard_map/middle/pallas_call | solution.py:362
  90.0 0.7 copy-done.19
  90.7 5.0 %collective-permute-start.11 = (bf16[256,768]{1,0:T(8,128)(2,1)}, bf16[256,768]{1,0:T(8,128)(2,1)}, u32[]{:S(2)}, u32[]{:S(2)}) collective-permute-start(bf16[256,768]{1,0:T(8,128)(2,1)} %get-tuple-element.28), channel_id=1, source_target_pairs={{0,7},{1,0},{2,1},{3,2},{4,3},{5,4},{6,5},{7,6},{8,15},{9,8},{10,9... | collective-permute-start | bytes 1179656 | tf_op jit(solution)/shard_map/ppermute | solution.py:293
  95.7 1.9 %collective-permute-start.8 = (bf16[256,768]{1,0:T(8,128)(2,1)}, bf16[256,768]{1,0:T(8,128)(2,1)}, u32[]{:S(2)}, u32[]{:S(2)}) collective-permute-start(bf16[256,768]{1,0:T(8,128)(2,1)} %get-tuple-element.27), channel_id=1, source_target_pairs={{0,1},{1,2},{2,3},{3,4},{4,5},{5,6},{6,7},{7,0},{8,9},{9,10},{10,1... | collective-permute-start | bytes 1179656 | tf_op jit(solution)/shard_map/ppermute | solution.py:293
  97.7 3.8 %terms.1 = bf16[32,256,128]{2,1,0:T(8,128)(2,1)} custom-call(bf16[256,384]{1,0:T(8,128)(2,1)S(1)} %get-tuple-element.26.grad_ref, bf16[4,384,1024]{2,1,0:T(8,128)(2,1)} %spread_cut.1.cut_hbm), custom_call_target="tpu_custom_call" | custom-call | flops 1600000000 | tf_op jit(solution)/shard_map/terms/pallas_call | solution.py:394
  101.5 14.7 %all-to-all-start.1 = ((bf16[32,256,128]{2,1,0:T(8,128)(2,1)}), bf16[32,256,128]{2,1,0:T(8,128)(2,1)S(1)}, u32[]{:S(2)}, u32[]{:S(2)}) async-start(bf16[32,256,128]{2,1,0:T(8,128)(2,1)} %terms.1), calls=%async_computation.1 | async-start | bytes 4194304 | tf_op jit(solution)/shard_map/all_to_all | solution.py:407
  116.2 1.1 copy-done.3
  117.3 1.4 hop.6
  118.8 4.8 %collective-permute-start.12 = (bf16[256,768]{1,0:T(8,128)(2,1)S(1)}, bf16[256,768]{1,0:T(8,128)(2,1)S(1)}, u32[]{:S(2)}, u32[]{:S(2)}) collective-permute-start(bf16[256,768]{1,0:T(8,128)(2,1)S(1)} %hop.6), channel_id=1, source_target_pairs={{0,7},{1,0},{2,1},{3,2},{4,3},{5,4},{6,5},{7,6},{8,15},{9,8},{10,9... | collective-permute-start | bytes 1179656 | tf_op jit(solution)/shard_map/ppermute | solution.py:293
  123.6 1.1 copy-done.1
  124.7 1.4 hop.4
  126.1 1.9 %collective-permute-start.9 = (bf16[256,768]{1,0:T(8,128)(2,1)S(1)}, bf16[256,768]{1,0:T(8,128)(2,1)S(1)}, u32[]{:S(2)}, u32[]{:S(2)}) collective-permute-start(bf16[256,768]{1,0:T(8,128)(2,1)S(1)} %hop.4), channel_id=1, source_target_pairs={{0,1},{1,2},{2,3},{3,4},{4,5},{5,6},{6,7},{7,0},{8,9},{9,10},{10,1... | collective-permute-start | bytes 1179656 | tf_op jit(solution)/shard_map/ppermute | solution.py:293
  128.0 2.8 %collective-permute-start.14 = (bf16[256,768]{1,0:T(8,128)(2,1)S(1)}, bf16[256,768]{1,0:T(8,128)(2,1)S(1)}, u32[]{:S(2)}, u32[]{:S(2)}) collective-permute-start(bf16[256,768]{1,0:T(8,128)(2,1)S(1)} %copy-done.20), channel_id=1, source_target_pairs={{0,4},{1,5},{2,6},{3,7},{4,0},{5,1},{6,2},{7,3},{8,12},{9,13},{10,... | collective-permute-start | bytes 1179656 | tf_op jit(solution)/shard_map/ppermute | solution.py:293
  130.8 9.5 %collective-permute-done.12.arrived_ref = bf16[256,768]{1,0:T(8,128)(2,1)S(1)} collective-permute-done((bf16[256,768]{1,0:T(8,128)(2,1)S(1)}, bf16[256,768]{1,0:T(8,128)(2,1)S(1)}, u32[]{:S(2)}, u32[]{:S(2)}) %collective-permute-start.12) | collective-permute-done | bytes 393248 | tf_op jit(solution)/shard_map/ppermute | solution.py:293
  140.4 0.4 hop.7
  140.8 5.5 %collective-permute-start.13 = (bf16[256,768]{1,0:T(8,128)(2,1)S(1)}, bf16[256,768]{1,0:T(8,128)(2,1)S(1)}, u32[]{:S(2)}, u32[]{:S(2)}) collective-permute-start(bf16[256,768]{1,0:T(8,128)(2,1)S(1)} %hop.7), channel_id=1, source_target_pairs={{0,7},{1,0},{2,1},{3,2},{4,3},{5,4},{6,5},{7,6},{8,15},{9,8},{10,9... | collective-permute-start | bytes 1179656 | tf_op jit(solution)/shard_map/ppermute | solution.py:293
  146.2 9.9 %collective-permute-done.9.arrived_ref = bf16[256,768]{1,0:T(8,128)(2,1)S(1)} collective-permute-done((bf16[256,768]{1,0:T(8,128)(2,1)S(1)}, bf16[256,768]{1,0:T(8,128)(2,1)S(1)}, u32[]{:S(2)}, u32[]{:S(2)}) %collective-permute-start.9) | collective-permute-done | bytes 393248 | tf_op jit(solution)/shard_map/ppermute | solution.py:293
  156.2 0.4 hop.5
  156.5 0.0 copy-start.13
  156.6 0.0 copy-start.15
  156.6 1.9 %collective-permute-start.10 = (bf16[256,768]{1,0:T(8,128)(2,1)S(1)}, bf16[256,768]{1,0:T(8,128)(2,1)S(1)}, u32[]{:S(2)}, u32[]{:S(2)}) collective-permute-start(bf16[256,768]{1,0:T(8,128)(2,1)S(1)} %hop.5), channel_id=1, source_target_pairs={{0,1},{1,2},{2,3},{3,4},{4,5},{5,6},{6,7},{7,0},{8,9},{9,10},{10,1... | collective-permute-start | bytes 1179656 | tf_op jit(solution)/shard_map/ppermute | solution.py:293
  158.5 1.5 collective-permute-done.13.right_ref
  160.0 8.9 %collective-permute-done.10.left_ref = bf16[256,768]{1,0:T(8,128)(2,1)S(1)} collective-permute-done((bf16[256,768]{1,0:T(8,128)(2,1)S(1)}, bf16[256,768]{1,0:T(8,128)(2,1)S(1)}, u32[]{:S(2)}, u32[]{:S(2)}) %collective-permute-start.10) | collective-permute-done | bytes 393248 | tf_op jit(solution)/shard_map/ppermute | solution.py:293
  168.9 0.4 close.1
  169.3 2.1 %collective-permute-start.15 = (bf16[256,384]{1,0:T(8,128)(2,1)S(1)}, bf16[256,384]{1,0:T(8,128)(2,1)S(1)}, u32[]{:S(2)}, u32[]{:S(2)}) collective-permute-start(bf16[256,384]{1,0:T(8,128)(2,1)S(1)} %get-tuple-element.31), channel_id=1, source_target_pairs={{0,8},{1,9},{2,10},{3,11},{4,12},{5,13},{6,14},{7,15},{8,0},{9,1},... | collective-permute-start | bytes 589832 | tf_op jit(solution)/shard_map/ppermute | solution.py:296
  171.4 1.3 gather.1.cut_ref
  172.8 4.6 %collective-permute-done.15.other_ref = bf16[256,384]{1,0:T(8,128)(2,1)S(1)} collective-permute-done((bf16[256,384]{1,0:T(8,128)(2,1)S(1)}, bf16[256,384]{1,0:T(8,128)(2,1)S(1)}, u32[]{:S(2)}, u32[]{:S(2)}) %collective-permute-start.15) | collective-permute-done | bytes 196640 | tf_op jit(solution)/shard_map/ppermute | solution.py:296
  177.4 1.0 last.1
  (40 shorter events, 0.1 us)
Async XLA Ops:
  1.9 17.3 %collective-permute-start = (bf16[384,256]{1,0:T(8,128)(2,1)S(1)}, bf16[384,256]{1,0:T(8,128)(2,1)S(1)}, u32[]{:S(2)}, u32[]{:S(2)}) collective-permute-start(bf16[384,256]{1,0:T(8,128)(2,1)S(1)} %project.1.own_ref.projected_ref), channel_id=1, source_target_pairs={{0,8},{1,9},{2,10},{3,11},{4,12},{5,13},{6,14},{7,15},{8,0},{9,1},... | collective-permute-start | bytes 589832 | tf_op jit(solution)/shard_map/ppermute | solution.py:296
  7.4 0.7 copy-start.12
  8.0 0.7 copy-start.14
  10.8 72.2 %all-to-all-start = ((bf16[32,128,256]{2,1,0:T(8,128)(2,1)}), bf16[32,128,256]{2,1,0:T(8,128)(2,1)S(1)}, u32[]{:S(2)}, u32[]{:S(2)}) async-start(bf16[32,128,256]{2,1,0:T(8,128)(2,1)} %fill.1), calls=%async_computation | async-start | bytes 4194304 | tf_op jit(solution)/shard_map/all_to_all | solution.py:319
  19.1 13.4 %copy-start.22 = (s32[1,1,16,4]{2,3,1,0:T(4,128)S(1)}, s32[1,1,16,4]{2,3,1,0:T(4,128)}, u32[]{:S(2)}) copy-start(s32[1,1,16,4]{2,3,1,0:T(4,128)} %param.16) | copy-start | bytes 772
  19.2 13.6 %copy-start.8 = (bf16[1,1,32,128,128]{4,3,2,1,0:T(8,128)(2,1)S(1)}, bf16[1,1,32,128,128]{4,3,2,1,0:T(8,128)(2,1)}, u32[]{:S(2)}) copy-start(bf16[1,1,32,128,128]{4,3,2,1,0:T(8,128)(2,1)} %param.18) | copy-start | bytes 3145732
  19.2 13.6 %copy-start.17 = (s32[1,1,32]{2,1,0:T(1,128)S(1)}, s32[1,1,32]{2,1,0:T(1,128)}, u32[]{:S(2)}) copy-start(s32[1,1,32]{2,1,0:T(1,128)} %param.21) | copy-start | bytes 388
  20.0 20.7 %collective-permute-start.2 = (bf16[768,256]{1,0:T(8,128)(2,1)}, bf16[768,256]{1,0:T(8,128)(2,1)}, u32[]{:S(2)}, u32[]{:S(2)}) collective-permute-start(bf16[768,256]{1,0:T(8,128)(2,1)} %pair.1), channel_id=1, source_target_pairs={{0,7},{1,0},{2,1},{3,2},{4,3},{5,4},{6,5},{7,6},{8,15},{9,8},{10,9... | collective-permute-start | bytes 1179656 | tf_op jit(solution)/shard_map/ppermute | solution.py:293
  30.6 28.4 %collective-permute-start.1 = (bf16[768,256]{1,0:T(8,128)(2,1)}, bf16[768,256]{1,0:T(8,128)(2,1)}, u32[]{:S(2)}, u32[]{:S(2)}) collective-permute-start(bf16[768,256]{1,0:T(8,128)(2,1)} %pair.1), channel_id=1, source_target_pairs={{0,1},{1,2},{2,3},{3,4},{4,5},{5,6},{6,7},{7,0},{8,9},{9,10},{10,1... | collective-permute-start | bytes 1179656 | tf_op jit(solution)/shard_map/ppermute | solution.py:293
  32.8 2.8 %copy-start.7 = (bf16[1,1,16,4,128,128]{5,4,3,2,1,0:T(8,128)(2,1)S(1)}, bf16[1,1,16,4,128,128]{5,4,3,2,1,0:T(8,128)(2,1)}, u32[]{:S(2)}) copy-start(bf16[1,1,16,4,128,128]{5,4,3,2,1,0:T(8,128)(2,1)} %param.15) | copy-start | bytes 6291460
  32.8 2.8 %copy-start.18 = (s32[1,1,16]{2,1,0:T(1,128)S(1)}, s32[1,1,16]{2,1,0:T(1,128)}, u32[]{:S(2)}) copy-start(s32[1,1,16]{2,1,0:T(1,128)} %param.17) | copy-start | bytes 196
  37.3 27.6 %copy-start.9 = (bf16[384,768]{1,0:T(8,128)(2,1)}, bf16[384,768]{1,0:T(8,128)(2,1)S(1)}, u32[]{:S(2)}) copy-start(bf16[384,768]{1,0:T(8,128)(2,1)S(1)} %get-tuple-element.17.mat_ref) | copy-start | bytes 1769476
  37.3 39.6 %copy-start = (bf16[384,768]{1,0:T(8,128)(2,1)}, bf16[384,768]{1,0:T(8,128)(2,1)S(1)}, u32[]{:S(2)}) copy-start(bf16[384,768]{1,0:T(8,128)(2,1)S(1)} %get-tuple-element.21.mat_ref) | copy-start | bytes 1769476
  37.3 39.9 %copy-start.2 = (bf16[384,768]{1,0:T(8,128)(2,1)}, bf16[384,768]{1,0:T(8,128)(2,1)S(1)}, u32[]{:S(2)}) copy-start(bf16[384,768]{1,0:T(8,128)(2,1)S(1)} %get-tuple-element.20.mat_ref) | copy-start | bytes 1769476
  37.3 44.2 %copy-start.4 = (bf16[384,768]{1,0:T(8,128)(2,1)}, bf16[384,768]{1,0:T(8,128)(2,1)S(1)}, u32[]{:S(2)}) copy-start(bf16[384,768]{1,0:T(8,128)(2,1)S(1)} %get-tuple-element.23.mat_b.right_hbm) | copy-start | bytes 1769476
  37.4 44.2 %copy-start.5 = (bf16[384,768]{1,0:T(8,128)(2,1)}, bf16[384,768]{1,0:T(8,128)(2,1)S(1)}, u32[]{:S(2)}) copy-start(bf16[384,768]{1,0:T(8,128)(2,1)S(1)} %get-tuple-element.24.mat_c.across_hbm) | copy-start | bytes 1769476
  37.4 44.2 %copy-start.6 = (bf16[384,768]{1,0:T(8,128)(2,1)}, bf16[384,768]{1,0:T(8,128)(2,1)S(1)}, u32[]{:S(2)}) copy-start(bf16[384,768]{1,0:T(8,128)(2,1)S(1)} %get-tuple-element.22.mat_a.left_hbm) | copy-start | bytes 1769476
  37.4 40.2 %collective-permute-start.7 = (bf16[768,256]{1,0:T(8,128)(2,1)}, bf16[768,256]{1,0:T(8,128)(2,1)S(1)}, u32[]{:S(2)}, u32[]{:S(2)}) collective-permute-start(bf16[768,256]{1,0:T(8,128)(2,1)} %pair.1), channel_id=1, source_target_pairs={{0,4},{1,5},{2,6},{3,7},{4,0},{5,1},{6,2},{7,3},{8,12},{9,13},{10,... | collective-permute-start | bytes 1179656 | tf_op jit(solution)/shard_map/ppermute | solution.py:293
  40.7 31.6 %collective-permute-start.4 = (bf16[768,256]{1,0:T(8,128)(2,1)}, bf16[768,256]{1,0:T(8,128)(2,1)S(1)}, u32[]{:S(2)}, u32[]{:S(2)}) collective-permute-start(bf16[768,256]{1,0:T(8,128)(2,1)} %collective-permute-done.2), channel_id=1, source_target_pairs={{0,7},{1,0},{2,1},{3,2},{4,3},{5,4},{6,5},{7,6},{8,15},{9,8},{10,9... | collective-permute-start | bytes 1179656 | tf_op jit(solution)/shard_map/ppermute | solution.py:293
  59.1 11.3 %collective-permute-start.3 = (bf16[768,256]{1,0:T(8,128)(2,1)}, bf16[768,256]{1,0:T(8,128)(2,1)S(1)}, u32[]{:S(2)}, u32[]{:S(2)}) collective-permute-start(bf16[768,256]{1,0:T(8,128)(2,1)} %collective-permute-done.1), channel_id=1, source_target_pairs={{0,1},{1,2},{2,3},{3,4},{4,5},{5,6},{6,7},{7,0},{8,9},{9,10},{10,1... | collective-permute-start | bytes 1179656 | tf_op jit(solution)/shard_map/ppermute | solution.py:293
  70.4 10.2 %collective-permute-start.5 = (bf16[768,256]{1,0:T(8,128)(2,1)S(1)}, bf16[768,256]{1,0:T(8,128)(2,1)S(1)}, u32[]{:S(2)}, u32[]{:S(2)}) collective-permute-start(bf16[768,256]{1,0:T(8,128)(2,1)S(1)} %collective-permute-done.3), channel_id=1, source_target_pairs={{0,1},{1,2},{2,3},{3,4},{4,5},{5,6},{6,7},{7,0},{8,9},{9,10},{10,1... | collective-permute-start | bytes 1179656 | tf_op jit(solution)/shard_map/ppermute | solution.py:293
  72.3 9.3 %collective-permute-start.6 = (bf16[768,256]{1,0:T(8,128)(2,1)S(1)}, bf16[768,256]{1,0:T(8,128)(2,1)S(1)}, u32[]{:S(2)}, u32[]{:S(2)}) collective-permute-start(bf16[768,256]{1,0:T(8,128)(2,1)S(1)} %collective-permute-done.4), channel_id=1, source_target_pairs={{0,7},{1,0},{2,1},{3,2},{4,3},{5,4},{6,5},{7,6},{8,15},{9,8},{10,9... | collective-permute-start | bytes 1179656 | tf_op jit(solution)/shard_map/ppermute | solution.py:293
  77.6 6.8 %copy-start.16 = (f32[256]{0:T(256)S(1)}, f32[256]{0:T(256)}, u32[]{:S(2)}) copy-start(f32[256]{0:T(256)} %param.13) | copy-start | bytes 3076
  83.0 1.3 copy-start.21
  90.0 0.7 copy-start.19
  90.7 25.5 %collective-permute-start.11 = (bf16[256,768]{1,0:T(8,128)(2,1)}, bf16[256,768]{1,0:T(8,128)(2,1)}, u32[]{:S(2)}, u32[]{:S(2)}) collective-permute-start(bf16[256,768]{1,0:T(8,128)(2,1)} %get-tuple-element.28), channel_id=1, source_target_pairs={{0,7},{1,0},{2,1},{3,2},{4,3},{5,4},{6,5},{7,6},{8,15},{9,8},{10,9... | collective-permute-start | bytes 1179656 | tf_op jit(solution)/shard_map/ppermute | solution.py:293
  95.7 27.9 %collective-permute-start.8 = (bf16[256,768]{1,0:T(8,128)(2,1)}, bf16[256,768]{1,0:T(8,128)(2,1)}, u32[]{:S(2)}, u32[]{:S(2)}) collective-permute-start(bf16[256,768]{1,0:T(8,128)(2,1)} %get-tuple-element.27), channel_id=1, source_target_pairs={{0,1},{1,2},{2,3},{3,4},{4,5},{5,6},{6,7},{7,0},{8,9},{9,10},{10,1... | collective-permute-start | bytes 1179656 | tf_op jit(solution)/shard_map/ppermute | solution.py:293
  101.5 69.9 %all-to-all-start.1 = ((bf16[32,256,128]{2,1,0:T(8,128)(2,1)}), bf16[32,256,128]{2,1,0:T(8,128)(2,1)S(1)}, u32[]{:S(2)}, u32[]{:S(2)}) async-start(bf16[32,256,128]{2,1,0:T(8,128)(2,1)} %terms.1), calls=%async_computation.1 | async-start | bytes 4194304 | tf_op jit(solution)/shard_map/all_to_all | solution.py:407
  116.2 1.1 copy-start.3
  117.3 10.7 %copy-start.20 = (bf16[256,768]{1,0:T(8,128)(2,1)S(1)}, bf16[256,768]{1,0:T(8,128)(2,1)}, u32[]{:S(2)}) copy-start(bf16[256,768]{1,0:T(8,128)(2,1)} %copy-done.19) | copy-start | bytes 1179652
  117.3 51.6 %copy-start.10 = (bf16[384,768]{1,0:T(8,128)(2,1)S(1)}, bf16[384,768]{1,0:T(8,128)(2,1)}, u32[]{:S(2)}) copy-start(bf16[384,768]{1,0:T(8,128)(2,1)} %copy-done.9) | copy-start | bytes 1769476
  118.8 21.6 %collective-permute-start.12 = (bf16[256,768]{1,0:T(8,128)(2,1)S(1)}, bf16[256,768]{1,0:T(8,128)(2,1)S(1)}, u32[]{:S(2)}, u32[]{:S(2)}) collective-permute-start(bf16[256,768]{1,0:T(8,128)(2,1)S(1)} %hop.6), channel_id=1, source_target_pairs={{0,7},{1,0},{2,1},{3,2},{4,3},{5,4},{6,5},{7,6},{8,15},{9,8},{10,9... | collective-permute-start | bytes 1179656 | tf_op jit(solution)/shard_map/ppermute | solution.py:293
  123.6 1.1 copy-start.1
  126.1 30.1 %collective-permute-start.9 = (bf16[256,768]{1,0:T(8,128)(2,1)S(1)}, bf16[256,768]{1,0:T(8,128)(2,1)S(1)}, u32[]{:S(2)}, u32[]{:S(2)}) collective-permute-start(bf16[256,768]{1,0:T(8,128)(2,1)S(1)} %hop.4), channel_id=1, source_target_pairs={{0,1},{1,2},{2,3},{3,4},{4,5},{5,6},{6,7},{7,0},{8,9},{9,10},{10,1... | collective-permute-start | bytes 1179656 | tf_op jit(solution)/shard_map/ppermute | solution.py:293
  128.0 30.5 %collective-permute-start.14 = (bf16[256,768]{1,0:T(8,128)(2,1)S(1)}, bf16[256,768]{1,0:T(8,128)(2,1)S(1)}, u32[]{:S(2)}, u32[]{:S(2)}) collective-permute-start(bf16[256,768]{1,0:T(8,128)(2,1)S(1)} %copy-done.20), channel_id=1, source_target_pairs={{0,4},{1,5},{2,6},{3,7},{4,0},{5,1},{6,2},{7,3},{8,12},{9,13},{10,... | collective-permute-start | bytes 1179656 | tf_op jit(solution)/shard_map/ppermute | solution.py:293
  140.8 19.3 %collective-permute-start.13 = (bf16[256,768]{1,0:T(8,128)(2,1)S(1)}, bf16[256,768]{1,0:T(8,128)(2,1)S(1)}, u32[]{:S(2)}, u32[]{:S(2)}) collective-permute-start(bf16[256,768]{1,0:T(8,128)(2,1)S(1)} %hop.7), channel_id=1, source_target_pairs={{0,7},{1,0},{2,1},{3,2},{4,3},{5,4},{6,5},{7,6},{8,15},{9,8},{10,9... | collective-permute-start | bytes 1179656 | tf_op jit(solution)/shard_map/ppermute | solution.py:293
  156.5 14.9 %copy-start.13 = (s32[1,1,32]{2,1,0:T(1,128)S(1)}, s32[1,1,32]{2,1,0:T(1,128)}, u32[]{:S(2)}) copy-start(s32[1,1,32]{2,1,0:T(1,128)} %param.19) | copy-start | bytes 388
  156.6 14.9 %copy-start.15 = (s32[1,1,32]{2,1,0:T(1,128)S(1)}, s32[1,1,32]{2,1,0:T(1,128)}, u32[]{:S(2)}) copy-start(s32[1,1,32]{2,1,0:T(1,128)} %param.20) | copy-start | bytes 388
  156.6 12.3 %collective-permute-start.10 = (bf16[256,768]{1,0:T(8,128)(2,1)S(1)}, bf16[256,768]{1,0:T(8,128)(2,1)S(1)}, u32[]{:S(2)}, u32[]{:S(2)}) collective-permute-start(bf16[256,768]{1,0:T(8,128)(2,1)S(1)} %hop.5), channel_id=1, source_target_pairs={{0,1},{1,2},{2,3},{3,4},{4,5},{5,6},{6,7},{7,0},{8,9},{9,10},{10,1... | collective-permute-start | bytes 1179656 | tf_op jit(solution)/shard_map/ppermute | solution.py:293
  169.3 8.1 %copy-start.11 = (bf16[256,256]{1,0:T(8,128)(2,1)S(1)}, bf16[256,256]{1,0:T(8,128)(2,1)}, u32[]{:S(2)}) copy-start(bf16[256,256]{1,0:T(8,128)(2,1)} %weight_ref.1) | copy-start | bytes 393220
  169.3 8.1 %collective-permute-start.15 = (bf16[256,384]{1,0:T(8,128)(2,1)S(1)}, bf16[256,384]{1,0:T(8,128)(2,1)S(1)}, u32[]{:S(2)}, u32[]{:S(2)}) collective-permute-start(bf16[256,384]{1,0:T(8,128)(2,1)S(1)} %get-tuple-element.31), channel_id=1, source_target_pairs={{0,8},{1,9},{2,10},{3,11},{4,12},{5,13},{6,14},{7,15},{8,0},{9,1},... | collective-permute-start | bytes 589832 | tf_op jit(solution)/shard_map/ppermute | solution.py:296

commit v5 on v3

--- a/solution.py
+++ b/solution.py
@@ -11,7 +11,8 @@
 CHUNKS = 4
 VMEM_LIMIT = 16 * 1024 * 1024
 PAIR_COST = 100_000_000_000
-CLOSE_COST = 27_800_000_000
+CLOSE_COST = 26_500_000_000
+CUT_COST = 2_000_000_000
 
 
 def spec(space):
@@ -129,60 +130,73 @@
     pair_ref[pl.ds(pl.multiple_of(rows - place, TILE), rows)] = other_ref[...]
 
 
+def cut_sum_kernel(cut_hbm, far_hbm, total_ref, cut, far, sems):
+    chunks = cut.shape[0]
+    chunk = far.shape[0] // chunks
+    width = far.shape[2]
+    copies = []
+    for piece in range(chunks):
+        span = pl.ds(piece * chunk, chunk)
+        copies.append(
+            (
+                pltpu.make_async_copy(cut_hbm.at[piece], cut.at[piece], sems.at[piece]),
+                pltpu.make_async_copy(far_hbm.at[span], far.at[span], sems.at[chunks + piece]),
+            )
+        )
+    for pair in copies:
+        for copy in pair:
+            copy.start()
+    for piece in range(chunks):
+        for copy in copies[piece]:
+            copy.wait()
+        arrived = far[pl.ds(piece * chunk, chunk)].reshape(chunk * TILE, width)
+        term = product(cut[piece], arrived)
+        total_ref[...] = term if piece == 0 else total_ref[...] + term
+
+
 def middle_kernel(
-    sum_hbm,
-    cotangent_hbm,
+    sum_ref,
+    cut_sum_ref,
+    last_ref,
     bias_ref,
-    mat_hbm,
+    cotangent_ref,
+    far_mat_ref,
+    near_mat_ref,
     cut_hbm,
-    far_hbm,
     hidden_ref,
     grad_ref,
-    low_ref,
-    high_ref,
+    left_ref,
+    right_ref,
     terms_hbm,
-    total,
-    cotangent,
-    mat,
     cut,
-    far,
     terms,
     sems,
 ):
-    rows, width = total.shape
     chunks = cut.shape[0]
-    chunk = far.shape[0] // chunks
-    move = lambda source, target, place: pltpu.make_async_copy(source, target, sems.at[place])
-    copies = [move(sum_hbm, total, 2 * chunks)]
-    for piece in range(chunks):
-        span = pl.ds(piece * chunk, chunk)
-        copies.append(move(cut_hbm.at[piece], cut.at[piece], piece))
-        copies.append(move(far_hbm.at[span], far.at[span], chunks + piece))
-    copies.append(move(cotangent_hbm, cotangent, 2 * chunks + 1))
-    copies.append(move(mat_hbm, mat, 2 * chunks + 2))
-    for copy in copies:
+    chunk = terms.shape[0] // chunks
+    loads = [
+        pltpu.make_async_copy(cut_hbm.at[piece], cut.at[piece], sems.at[piece])
+        for piece in range(chunks)
+    ]
+    for copy in loads:
         copy.start()
-    copies[0].wait()
-    for piece in range(chunks):
-        copies[1 + 2 * piece].wait()
-        copies[2 + 2 * piece].wait()
-        arrived = far[pl.ds(piece * chunk, chunk)].reshape(chunk * TILE, width)
-        total[...] += product(cut[piece], arrived)
-    activated, derivative = silu_parts(total[...] + bias_ref[...])
+    total = sum_ref[...] + cut_sum_ref[...] + product(far_mat_ref[...], last_ref[...])
+    activated, derivative = silu_parts(total + bias_ref[...])
     hidden_ref[...] = activated.astype(BF)
-    copies[-2].wait()
-    grad = (cotangent[...].astype(F32) * derivative).T.astype(BF)
+    grad = (cotangent_ref[...].astype(F32) * derivative).T.astype(BF)
     grad_ref[...] = grad
-    copies[-1].wait()
-    low_ref[...] = product(grad, mat[:, :rows]).astype(BF)
-    high_ref[...] = product(grad, mat[:, rows:]).astype(BF)
+    left_ref[...] = product(grad, far_mat_ref[...]).astype(BF)
+    right_ref[...] = product(grad, near_mat_ref[...]).astype(BF)
     stores = []
     for piece in range(chunks):
+        loads[piece].wait()
         result = product(grad, cut[piece]).astype(BF)
         for slot in range(chunk):
             terms[piece * chunk + slot] = result[:, slot * TILE : (slot + 1) * TILE]
         span = pl.ds(piece * chunk, chunk)
-        stores.append(move(terms.at[span], terms_hbm.at[span], 2 * chunks + 3 + piece))
+        stores.append(
+            pltpu.make_async_copy(terms.at[span], terms_hbm.at[span], sems.at[chunks + piece])
+        )
         stores[-1].start()
     for copy in stores:
         copy.wait()
@@ -202,14 +216,9 @@
     lax.fori_loop(0, arrived_ref.shape[0], add, 0)
 
 
-def hop_kernel(at, grad_ref, mat_ref, arrived_ref, out_ref):
-    wide, held = out_ref.shape[1], arrived_ref.shape[1]
-    for low, high in ((0, at), (at, at + held), (at + held, wide)):
-        if low < high:
-            term = product(grad_ref[...], mat_ref[:, low:high])
-            if low == at:
-                term += arrived_ref[...].astype(F32)
-            out_ref[:, low:high] = term.astype(BF)
+def hop_kernel(grad_ref, mat_ref, arrived_ref, out_ref):
+    term = product(grad_ref[...], mat_ref[...]) + arrived_ref[...].astype(F32)
+    out_ref[...] = term.astype(BF)
 
 
 def close_kernel(half_ref, grad_ref, mat_ref, left_ref, right_ref, own_ref, other_ref):
@@ -318,52 +327,59 @@
     running = product(dense[0], pair)
     right = left = pair
     for hop in range(1, reach):
-        right, left = along_ring(right, 1), along_ring(left, -1)
+        left, right = along_ring(left, -1), along_ring(right, 1)
+        running = running + product(dense[hop], left)
         running = running + product(dense[ring - hop], right)
-        running = running + product(dense[hop], left)
-    low, high = along_ring(right[:rows], 1), along_ring(left[rows:], -1)
-
-    running = running + product(dense[reach][:, :rows], low)
-    running = running + product(dense[reach][:, rows:], high)
-
-    hidden, grad_pre, low, high, terms = call(
+    left = along_ring(left, -1)
+    cut_sum = call(
+        cut_sum_kernel,
+        "cut_sum",
+        shape((rows, width), F32),
+        [HBM, HBM],
+        VMEM,
+        [
+            pltpu.VMEM(dense_cut.shape, BF),
+            pltpu.VMEM((parts, TILE, width), BF),
+            pltpu.SemaphoreType.DMA((2 * CHUNKS,)),
+        ],
+        flops=CUT_COST,
+    )(in_hbm(dense_cut), in_hbm(incoming))
+
+    hidden, grad_pre, left, right, terms = call(
         middle_kernel,
         "middle",
-        (shape((rows, width), BF),)
-        + (shape((width, rows), BF),) * 3
+        (shape((rows, width), BF), shape((width, rows), BF))
+        + (shape((width, wide), BF),) * 2
         + (pltpu.HBM((parts, width, TILE), BF),),
-        [HBM, HBM, VMEM, HBM, HBM, HBM],
+        [VMEM] * 7 + [HBM],
         (VMEM,) * 4 + (HBM,),
         [
-            pltpu.VMEM((rows, width), F32),
-            pltpu.VMEM((rows, width), BF),
-            pltpu.VMEM((rows, wide), BF),
             pltpu.VMEM(dense_cut.shape, BF),
-            pltpu.VMEM((parts, TILE, width), BF),
             pltpu.VMEM((parts, width, TILE), BF),
-            pltpu.SemaphoreType.DMA((3 * CHUNKS + 3,)),
+            pltpu.SemaphoreType.DMA((2 * CHUNKS,)),
         ],
     )(
-        in_hbm(running),
-        in_hbm(cotangent),
+        running,
+        cut_sum,
+        left,
         bias.reshape(1, width),
-        in_hbm(dense[reach]),
+        cotangent,
+        dense[reach],
+        dense[reach - 1],
         in_hbm(dense_cut),
-        in_hbm(incoming),
     )
 
-    def add_on(mat, arrived, at):
-        return call(
-            lambda *refs: hop_kernel(at, *refs), "hop", shape((width, wide), BF), [VMEM] * 3, VMEM
-        )(grad_pre, mat, arrived)
-
-    low, high = along_ring(low, 1), along_ring(high, -1)
+    def add_on(mat, arrived):
+        return call(hop_kernel, "hop", shape((width, wide), BF), [VMEM] * 3, VMEM)(
+            grad_pre, mat, arrived
+        )
+
+    left, right = along_ring(left, -1), along_ring(right, 1)
     returned = lax.all_to_all(terms, "dom", split_axis=0, concat_axis=0, tiled=True)
     for hop in range(reach - 1, 0, -1):
-        first = hop == reach - 1
-        right = add_on(dense[hop], low if first else from_left, 0)
-        left = add_on(dense[ring - hop], high if first else from_right, rows if first else 0)
-        from_left, from_right = along_ring(right, 1), along_ring(left, -1)
+        left = along_ring(add_on(dense[ring - hop], left), -1)
+        if hop > 1:
+            right = along_ring(add_on(dense[hop - 1], right), 1)
     own, other = call(
         close_kernel,
         "close",
@@ -371,7 +387,7 @@
         [SMEM] + [VMEM] * 4,
         (VMEM, VMEM),
         flops=CLOSE_COST,
-    )(half.reshape(1), grad_pre, dense[0], from_left, from_right)
+    )(half.reshape(1), grad_pre, dense[0], right, left)
     other = across(other)
     from_cuts = call(
         gather_kernel, "gather", shape((width, rows), F32), [SMEM, SMEM, VMEM], VMEM, moved=2 << 20

time: 166 us -> 155 us (0.934)
  the two profiles are of different devices: /device:TPU:2 before, /device:TPU:1 now
where the time goes in v5:
time: 155 us; the launch traced here: 152 us
  starting transfers between devices  85.8 us (55%)
  waiting for transfers between devices  33.6 us (22%)
  Pallas kernels  21.9 us (14%)
  matrix products  5.25 us (3%)
  local copies, waits for them, and re-layouts  4.42 us (3%)
    ppermute x14, starting transfers between devices, along_ring(): return lax.ppermute(value, 'blk', moves)  57.2 us
    ppermute x14, waiting for transfers between devices, along_ring(): return lax.ppermute(value, 'blk', moves)  29.2 us
    all_to_all x1, starting transfers between devices, on_device(): lax.all_to_all(terms, 'dom', split_axis=0, concat_axis=0, tiled=True)  11.1 us
    ppermute x2, starting transfers between devices, across(): lax.ppermute(value, 'blk', [(i, (i + ring) % peers) for i in range(peers)])  9.25 us
    all_to_all x1, starting transfers between devices, on_device(): lax.all_to_all(outgoing, 'dom', split_axis=0, concat_axis=0, tiled=True)  8.31 us
    pallas_call x1, Pallas kernels, on_device(): call(middle_kernel, 'middle', (shape((rows, width), BF), shape((width, ro...  5.28 us
    dot_general x7, matrix products, product(): return jnp.dot(left, right, preferred_element_type=F32)  5.25 us
    unnamed x43, local copies, waits for them, and re-layouts  4.33 us
  transfers between devices with their start and end apart: 18, of which 10 were waited for; matrix products, arithmetic and copies ran while one was open for 4% of the time, Pallas kernels for 9%

profile of v5, /device:TPU:1, one launch (start us, length us, event | category | flops | bytes accessed | tf_op | source)
XLA Modules:
  0.0 152.2 jit_solution(2746911570783043748)
XLA Ops:
  0.6 1.2 project.1.own_ref.projected_ref
  1.9 5.5 %collective-permute-start = (bf16[384,256]{1,0:T(8,128)(2,1)S(1)}, bf16[384,256]{1,0:T(8,128)(2,1)S(1)}, u32[]{:S(2)}, u32[]{:S(2)}) collective-permute-start(bf16[384,256]{1,0:T(8,128)(2,1)S(1)} %project.1.own_ref.projected_ref), channel_id=1, source_target_pairs={{0,8},{1,9},{2,10},{3,11},{4,12},{5,13},{6,14},{7,15},{8,0},{9,1},... | collective-permute-start | bytes 589832 | tf_op jit(solution)/shard_map/ppermute | solution.py:278
  7.4 0.0 copy-start.12
  7.4 0.6 copy-done.12
  8.0 0.7 copy-done.14
  8.7 2.2 %fill.1 = bf16[32,128,256]{2,1,0:T(8,128)(2,1)} custom-call(s32[32]{0:T(128)S(1)} %bitcast.27, s32[32]{0:T(128)S(1)} %bitcast.29, bf16[384,256]{1,0:T(8,128)(2,1)S(1)} %project.1.own_ref.projected_ref), custom_call_target="tpu_custom_call" | custom-call | tf_op jit(solution)/shard_map/fill/pallas_call | solution.py:293
  10.8 8.3 %all-to-all-start = ((bf16[32,128,256]{2,1,0:T(8,128)(2,1)}), bf16[32,128,256]{2,1,0:T(8,128)(2,1)}, u32[]{:S(2)}, u32[]{:S(2)}) async-start(bf16[32,128,256]{2,1,0:T(8,128)(2,1)} %fill.1), calls=%async_computation | async-start | bytes 4194304 | tf_op jit(solution)/shard_map/all_to_all | solution.py:301
  19.2 0.0 copy-start.20
  19.2 0.0 copy-start.7
  19.2 0.0 copy-start.17
  19.3 4.1 %collective-permute-start.2 = (bf16[768,256]{1,0:T(8,128)(2,1)S(1)}, bf16[768,256]{1,0:T(8,128)(2,1)}, u32[]{:S(2)}, u32[]{:S(2)}) collective-permute-start(bf16[768,256]{1,0:T(8,128)(2,1)S(1)} %pair.1), channel_id=1, source_target_pairs={{0,1},{1,2},{2,3},{3,4},{4,5},{5,6},{6,7},{7,0},{8,9},{9,10},{10,1... | collective-permute-start | bytes 1179656 | tf_op jit(solution)/shard_map/ppermute | solution.py:275
  23.4 8.6 %collective-permute-start.1 = (bf16[768,256]{1,0:T(8,128)(2,1)S(1)}, bf16[768,256]{1,0:T(8,128)(2,1)}, u32[]{:S(2)}, u32[]{:S(2)}) collective-permute-start(bf16[768,256]{1,0:T(8,128)(2,1)S(1)} %pair.1), channel_id=1, source_target_pairs={{0,7},{1,0},{2,1},{3,2},{4,3},{5,4},{6,5},{7,6},{8,15},{9,8},{10,9... | collective-permute-start | bytes 1179656 | tf_op jit(solution)/shard_map/ppermute | solution.py:275
  32.0 0.1 copy.14
  32.1 0.1 reshape_squeeze.3.refs_0_
  32.2 0.0 copy-start.6
  32.2 0.0 copy-start.18
  32.2 2.8 %spread_cut.1.cut_hbm = bf16[4,384,1024]{2,1,0:T(8,128)(2,1)} custom-call(s32[32]{0:T(128)S(1)} %bitcast.32, bf16[32,128,128]{2,1,0:T(8,128)(2,1)S(1)} %bitcast.26), custom_call_target="tpu_custom_call" | custom-call | bytes 6291456 | tf_op jit(solution)/shard_map/spread_cut/pallas_call | solution.py:311
  35.0 1.6 %spread.1 = (bf16[384,768]{1,0:T(8,128)(2,1)S(1)}, bf16[384,768]{1,0:T(8,128)(2,1)S(1)}, bf16[384,768]{1,0:T(8,128)(2,1)S(1)}, bf16[384,768]{1,0:T(8,128)(2,1)S(...) custom-call(s32[64]{0:T(128)S(1)} %reshape_squeeze.3.refs_0_, ...), custom_call_target="tpu_custom_call" | custom-call | bytes 10485760 | tf_op jit(solution)/shard_map/spread/pallas_call | solution.py:303
  36.7 2.8 %collective-permute-done.2 = bf16[768,256]{1,0:T(8,128)(2,1)} collective-permute-done((bf16[768,256]{1,0:T(8,128)(2,1)S(1)}, bf16[768,256]{1,0:T(8,128)(2,1)}, u32[]{:S(2)}, u32[]{:S(2)}) %collective-permute-start.2) | collective-permute-done | bytes 393248 | tf_op jit(solution)/shard_map/ppermute | solution.py:275
  39.4 1.9 %collective-permute-start.4 = (bf16[768,256]{1,0:T(8,128)(2,1)}, bf16[768,256]{1,0:T(8,128)(2,1)S(1)}, u32[]{:S(2)}, u32[]{:S(2)}) collective-permute-start(bf16[768,256]{1,0:T(8,128)(2,1)} %collective-permute-done.2), channel_id=1, source_target_pairs={{0,1},{1,2},{2,3},{3,4},{4,5},{5,6},{6,7},{7,0},{8,9},{9,10},{10,1... | collective-permute-start | bytes 1179656 | tf_op jit(solution)/shard_map/ppermute | solution.py:275
  41.3 4.6 %collective-permute-start.3 = (bf16[768,256]{1,0:T(8,128)(2,1)}, bf16[768,256]{1,0:T(8,128)(2,1)S(1)}, u32[]{:S(2)}, u32[]{:S(2)}) collective-permute-start(bf16[768,256]{1,0:T(8,128)(2,1)} %collective-permute-done.1), channel_id=1, source_target_pairs={{0,7},{1,0},{2,1},{3,2},{4,3},{5,4},{6,5},{7,6},{8,15},{9,8},{10,9... | collective-permute-start | bytes 1179656 | tf_op jit(solution)/shard_map/ppermute | solution.py:275
  45.9 1.3 fusion.3
  47.3 1.3 fusion.4
  48.6 0.3 fusion.2
  48.9 3.6 %collective-permute-done.4 = bf16[768,256]{1,0:T(8,128)(2,1)S(1)} collective-permute-done((bf16[768,256]{1,0:T(8,128)(2,1)}, bf16[768,256]{1,0:T(8,128)(2,1)S(1)}, u32[]{:S(2)}, u32[]{:S(2)}) %collective-permute-start.4) | collective-permute-done | bytes 393248 | tf_op jit(solution)/shard_map/ppermute | solution.py:275
  52.5 1.9 %collective-permute-start.6 = (bf16[768,256]{1,0:T(8,128)(2,1)S(1)}, bf16[768,256]{1,0:T(8,128)(2,1)S(1)}, u32[]{:S(2)}, u32[]{:S(2)}) collective-permute-start(bf16[768,256]{1,0:T(8,128)(2,1)S(1)} %collective-permute-done.4), channel_id=1, source_target_pairs={{0,1},{1,2},{2,3},{3,4},{4,5},{5,6},{6,7},{7,0},{8,9},{9,10},{10,1... | collective-permute-start | bytes 1179656 | tf_op jit(solution)/shard_map/ppermute | solution.py:275
  54.5 4.6 %collective-permute-start.5 = (bf16[768,256]{1,0:T(8,128)(2,1)S(1)}, bf16[768,256]{1,0:T(8,128)(2,1)}, u32[]{:S(2)}, u32[]{:S(2)}) collective-permute-start(bf16[768,256]{1,0:T(8,128)(2,1)S(1)} %collective-permute-done.3), channel_id=1, source_target_pairs={{0,7},{1,0},{2,1},{3,2},{4,3},{5,4},{6,5},{7,6},{8,15},{9,8},{10,9... | collective-permute-start | bytes 1179656 | tf_op jit(solution)/shard_map/ppermute | solution.py:275
  59.1 0.3 fusion.5
  59.4 0.3 fusion.1
  59.7 5.7 %collective-permute-done.5 = bf16[768,256]{1,0:T(8,128)(2,1)} collective-permute-done((bf16[768,256]{1,0:T(8,128)(2,1)S(1)}, bf16[768,256]{1,0:T(8,128)(2,1)}, u32[]{:S(2)}, u32[]{:S(2)}) %collective-permute-start.5) | collective-permute-done | bytes 393248 | tf_op jit(solution)/shard_map/ppermute | solution.py:275
  65.4 5.4 %collective-permute-start.7 = (bf16[768,256]{1,0:T(8,128)(2,1)}, bf16[768,256]{1,0:T(8,128)(2,1)S(1)}, u32[]{:S(2)}, u32[]{:S(2)}) collective-permute-start(bf16[768,256]{1,0:T(8,128)(2,1)} %collective-permute-done.5), channel_id=1, source_target_pairs={{0,7},{1,0},{2,1},{3,2},{4,3},{5,4},{6,5},{7,6},{8,15},{9,8},{10,9... | collective-permute-start | bytes 1179656 | tf_op jit(solution)/shard_map/ppermute | solution.py:275
  70.9 0.3 fusion.6
  71.2 1.3 fusion.sum_ref
  72.5 0.0 copy-start.16
  72.6 0.0 copy-start.11
  72.6 3.4 %cut_sum.1.cut_sum_ref = f32[384,256]{1,0:T(8,128)S(1)} custom-call(bf16[4,384,1024]{2,1,0:T(8,128)(2,1)} %spread_cut.1.cut_hbm, bf16[32,128,256]{2,1,0:T(8,128)(2,1)} %all-to-all-done.far_hbm), custom_call_target="tpu_custom_call" | custom-call | flops 2000000000 | tf_op jit(solution)/shard_map/cut_sum/pallas_call | solution.py:334
  76.0 0.7 collective-permute-done.7.last_ref
  76.7 5.3 %middle.1 = (bf16[384,256]{1,0:T(8,128)(2,1)}, bf16[256,384]{1,0:T(8,128)(2,1)S(1)}, bf16[256,768]{1,0:T(8,128)(2,1)}, bf16[256,768]{1,0:T(8,128)(2,1)S(1)}, bf16[32,256,128]{2,1,0:T(8,128)(2,1)}) custom-call(f32[384,256]{1,0:T(8,128)S(1)} %fusion.sum_ref, f32[384,256]{1,0:T(8,128)S(1)} %cut_sum.1.cut_sum_ref, ...), custom_call_target="tpu_custom_call" | custom-call | tf_op jit(solution)/shard_map/middle/pallas_call | solution.py:348
  82.0 0.7 copy-done.19
  82.7 6.0 %collective-permute-start.11 = (bf16[256,768]{1,0:T(8,128)(2,1)}, bf16[256,768]{1,0:T(8,128)(2,1)}, u32[]{:S(2)}, u32[]{:S(2)}) collective-permute-start(bf16[256,768]{1,0:T(8,128)(2,1)} %get-tuple-element.28), channel_id=1, source_target_pairs={{0,7},{1,0},{2,1},{3,2},{4,3},{5,4},{6,5},{7,6},{8,15},{9,8},{10,9... | collective-permute-start | bytes 1179656 | tf_op jit(solution)/shard_map/ppermute | solution.py:275
  88.7 11.1 %all-to-all-start.1 = ((bf16[32,256,128]{2,1,0:T(8,128)(2,1)}), bf16[32,256,128]{2,1,0:T(8,128)(2,1)S(1)}, u32[]{:S(2)}, u32[]{:S(2)}) async-start(bf16[32,256,128]{2,1,0:T(8,128)(2,1)} %get-tuple-element.31), calls=%async_computation.1 | async-start | bytes 4194304 | tf_op jit(solution)/shard_map/all_to_all | solution.py:378
  99.8 2.1 %collective-permute-start.8 = (bf16[256,768]{1,0:T(8,128)(2,1)}, bf16[256,768]{1,0:T(8,128)(2,1)S(1)}, u32[]{:S(2)}, u32[]{:S(2)}) collective-permute-start(bf16[256,768]{1,0:T(8,128)(2,1)} %copy-done.19), channel_id=1, source_target_pairs={{0,1},{1,2},{2,3},{3,4},{4,5},{5,6},{6,7},{7,0},{8,9},{9,10},{10,1... | collective-permute-start | bytes 1179656 | tf_op jit(solution)/shard_map/ppermute | solution.py:275
  101.9 1.1 copy-done.5
  103.0 1.4 hop.7
  104.3 4.6 %collective-permute-start.12 = (bf16[256,768]{1,0:T(8,128)(2,1)S(1)}, bf16[256,768]{1,0:T(8,128)(2,1)S(1)}, u32[]{:S(2)}, u32[]{:S(2)}) collective-permute-start(bf16[256,768]{1,0:T(8,128)(2,1)S(1)} %hop.7), channel_id=1, source_target_pairs={{0,7},{1,0},{2,1},{3,2},{4,3},{5,4},{6,5},{7,6},{8,15},{9,8},{10,9... | collective-permute-start | bytes 1179656 | tf_op jit(solution)/shard_map/ppermute | solution.py:275
  108.9 4.8 %collective-permute-done.8.arrived_ref = bf16[256,768]{1,0:T(8,128)(2,1)S(1)} collective-permute-done((bf16[256,768]{1,0:T(8,128)(2,1)}, bf16[256,768]{1,0:T(8,128)(2,1)S(1)}, u32[]{:S(2)}, u32[]{:S(2)}) %collective-permute-start.8) | collective-permute-done | bytes 393248 | tf_op jit(solution)/shard_map/ppermute | solution.py:275
  113.7 1.1 copy-done.3
  114.8 0.4 hop.5
  115.2 2.1 %collective-permute-start.9 = (bf16[256,768]{1,0:T(8,128)(2,1)S(1)}, bf16[256,768]{1,0:T(8,128)(2,1)S(1)}, u32[]{:S(2)}, u32[]{:S(2)}) collective-permute-start(bf16[256,768]{1,0:T(8,128)(2,1)S(1)} %hop.5), channel_id=1, source_target_pairs={{0,1},{1,2},{2,3},{3,4},{4,5},{5,6},{6,7},{7,0},{8,9},{9,10},{10,1... | collective-permute-start | bytes 1179656 | tf_op jit(solution)/shard_map/ppermute | solution.py:275
  117.3 0.4 hop.8
  117.6 4.9 %collective-permute-start.13 = (bf16[256,768]{1,0:T(8,128)(2,1)S(1)}, bf16[256,768]{1,0:T(8,128)(2,1)S(1)}, u32[]{:S(2)}, u32[]{:S(2)}) collective-permute-start(bf16[256,768]{1,0:T(8,128)(2,1)S(1)} %hop.8), channel_id=1, source_target_pairs={{0,7},{1,0},{2,1},{3,2},{4,3},{5,4},{6,5},{7,6},{8,15},{9,8},{10,9... | collective-permute-start | bytes 1179656 | tf_op jit(solution)/shard_map/ppermute | solution.py:275
  122.5 5.4 %collective-permute-done.9.arrived_ref = bf16[256,768]{1,0:T(8,128)(2,1)S(1)} collective-permute-done((bf16[256,768]{1,0:T(8,128)(2,1)S(1)}, bf16[256,768]{1,0:T(8,128)(2,1)S(1)}, u32[]{:S(2)}, u32[]{:S(2)}) %collective-permute-start.9) | collective-permute-done | bytes 393248 | tf_op jit(solution)/shard_map/ppermute | solution.py:275
  128.0 0.4 hop.6
  128.4 1.9 %collective-permute-start.10 = (bf16[256,768]{1,0:T(8,128)(2,1)S(1)}, bf16[256,768]{1,0:T(8,128)(2,1)S(1)}, u32[]{:S(2)}, u32[]{:S(2)}) collective-permute-start(bf16[256,768]{1,0:T(8,128)(2,1)S(1)} %hop.6), channel_id=1, source_target_pairs={{0,1},{1,2},{2,3},{3,4},{4,5},{5,6},{6,7},{7,0},{8,9},{9,10},{10,1... | collective-permute-start | bytes 1179656 | tf_op jit(solution)/shard_map/ppermute | solution.py:275
  130.3 0.4 hop.9
  130.7 4.6 %collective-permute-start.14 = (bf16[256,768]{1,0:T(8,128)(2,1)S(1)}, bf16[256,768]{1,0:T(8,128)(2,1)S(1)}, u32[]{:S(2)}, u32[]{:S(2)}) collective-permute-start(bf16[256,768]{1,0:T(8,128)(2,1)S(1)} %hop.9), channel_id=1, source_target_pairs={{0,7},{1,0},{2,1},{3,2},{4,3},{5,4},{6,5},{7,6},{8,15},{9,8},{10,9... | collective-permute-start | bytes 1179656 | tf_op jit(solution)/shard_map/ppermute | solution.py:275
  135.3 4.8 %collective-permute-done.10.left_ref = bf16[256,768]{1,0:T(8,128)(2,1)S(1)} collective-permute-done((bf16[256,768]{1,0:T(8,128)(2,1)S(1)}, bf16[256,768]{1,0:T(8,128)(2,1)S(1)}, u32[]{:S(2)}, u32[]{:S(2)}) %collective-permute-start.10) | collective-permute-done | bytes 393248 | tf_op jit(solution)/shard_map/ppermute | solution.py:275
  140.1 1.3 collective-permute-done.14.right_ref
  141.4 0.4 close.1
  141.8 3.8 %collective-permute-start.15 = (bf16[256,384]{1,0:T(8,128)(2,1)S(1)}, bf16[256,384]{1,0:T(8,128)(2,1)S(1)}, u32[]{:S(2)}, u32[]{:S(2)}) collective-permute-start(bf16[256,384]{1,0:T(8,128)(2,1)S(1)} %get-tuple-element.30), channel_id=1, source_target_pairs={{0,8},{1,9},{2,10},{3,11},{4,12},{5,13},{6,14},{7,15},{8,0},{9,1},... | collective-permute-start | bytes 589832 | tf_op jit(solution)/shard_map/ppermute | solution.py:278
  145.6 3.6 %all-to-all-done.1.arrived_ref = bf16[32,256,128]{2,1,0:T(8,128)(2,1)S(1)} async-done(((bf16[32,256,128]{2,1,0:T(8,128)(2,1)}), bf16[32,256,128]{2,1,0:T(8,128)(2,1)S(1)}, u32[]{:S(2)}, u32[]{:S(2)}) %all-to-all-start.1) | async-done | bytes 2097184 | tf_op jit(solution)/shard_map/all_to_all | solution.py:378
  149.2 1.3 gather.1.cut_ref
  150.5 0.8 collective-permute-done.15.other_ref
  151.3 0.9 last.1
  (38 shorter events, 0.1 us)
Async XLA Ops:
  1.9 17.3 %collective-permute-start = (bf16[384,256]{1,0:T(8,128)(2,1)S(1)}, bf16[384,256]{1,0:T(8,128)(2,1)S(1)}, u32[]{:S(2)}, u32[]{:S(2)}) collective-permute-start(bf16[384,256]{1,0:T(8,128)(2,1)S(1)} %project.1.own_ref.projected_ref), channel_id=1, source_target_pairs={{0,8},{1,9},{2,10},{3,11},{4,12},{5,13},{6,14},{7,15},{8,0},{9,1},... | collective-permute-start | bytes 589832 | tf_op jit(solution)/shard_map/ppermute | solution.py:278
  7.4 0.7 copy-start.12
  8.0 0.7 copy-start.14
  10.8 61.7 %all-to-all-start = ((bf16[32,128,256]{2,1,0:T(8,128)(2,1)}), bf16[32,128,256]{2,1,0:T(8,128)(2,1)}, u32[]{:S(2)}, u32[]{:S(2)}) async-start(bf16[32,128,256]{2,1,0:T(8,128)(2,1)} %fill.1), calls=%async_computation | async-start | bytes 4194304 | tf_op jit(solution)/shard_map/all_to_all | solution.py:301
  19.2 12.8 %copy-start.20 = (s32[1,1,16,4]{2,3,1,0:T(4,128)S(1)}, s32[1,1,16,4]{2,3,1,0:T(4,128)}, u32[]{:S(2)}) copy-start(s32[1,1,16,4]{2,3,1,0:T(4,128)} %param.16) | copy-start | bytes 772
  19.2 13.0 %copy-start.7 = (bf16[1,1,32,128,128]{4,3,2,1,0:T(8,128)(2,1)S(1)}, bf16[1,1,32,128,128]{4,3,2,1,0:T(8,128)(2,1)}, u32[]{:S(2)}) copy-start(bf16[1,1,32,128,128]{4,3,2,1,0:T(8,128)(2,1)} %param.18) | copy-start | bytes 3145732
  19.2 13.0 %copy-start.17 = (s32[1,1,32]{2,1,0:T(1,128)S(1)}, s32[1,1,32]{2,1,0:T(1,128)}, u32[]{:S(2)}) copy-start(s32[1,1,32]{2,1,0:T(1,128)} %param.21) | copy-start | bytes 388
  19.3 20.2 %collective-permute-start.2 = (bf16[768,256]{1,0:T(8,128)(2,1)S(1)}, bf16[768,256]{1,0:T(8,128)(2,1)}, u32[]{:S(2)}, u32[]{:S(2)}) collective-permute-start(bf16[768,256]{1,0:T(8,128)(2,1)S(1)} %pair.1), channel_id=1, source_target_pairs={{0,1},{1,2},{2,3},{3,4},{4,5},{5,6},{6,7},{7,0},{8,9},{9,10},{10,1... | collective-permute-start | bytes 1179656 | tf_op jit(solution)/shard_map/ppermute | solution.py:275
  23.4 17.9 %collective-permute-start.1 = (bf16[768,256]{1,0:T(8,128)(2,1)S(1)}, bf16[768,256]{1,0:T(8,128)(2,1)}, u32[]{:S(2)}, u32[]{:S(2)}) collective-permute-start(bf16[768,256]{1,0:T(8,128)(2,1)S(1)} %pair.1), channel_id=1, source_target_pairs={{0,7},{1,0},{2,1},{3,2},{4,3},{5,4},{6,5},{7,6},{8,15},{9,8},{10,9... | collective-permute-start | bytes 1179656 | tf_op jit(solution)/shard_map/ppermute | solution.py:275
  32.2 2.8 %copy-start.6 = (bf16[1,1,16,4,128,128]{5,4,3,2,1,0:T(8,128)(2,1)S(1)}, bf16[1,1,16,4,128,128]{5,4,3,2,1,0:T(8,128)(2,1)}, u32[]{:S(2)}) copy-start(bf16[1,1,16,4,128,128]{5,4,3,2,1,0:T(8,128)(2,1)} %param.15) | copy-start | bytes 6291460
  32.2 2.8 %copy-start.18 = (s32[1,1,16]{2,1,0:T(1,128)S(1)}, s32[1,1,16]{2,1,0:T(1,128)}, u32[]{:S(2)}) copy-start(s32[1,1,16]{2,1,0:T(1,128)} %param.17) | copy-start | bytes 196
  36.6 12.3 %copy-start.8 = (bf16[384,768]{1,0:T(8,128)(2,1)}, bf16[384,768]{1,0:T(8,128)(2,1)S(1)}, u32[]{:S(2)}) copy-start(bf16[384,768]{1,0:T(8,128)(2,1)S(1)} %get-tuple-element.17.mat_ref) | copy-start | bytes 1769476
  36.6 22.4 %copy-start = (bf16[384,768]{1,0:T(8,128)(2,1)}, bf16[384,768]{1,0:T(8,128)(2,1)S(1)}, u32[]{:S(2)}) copy-start(bf16[384,768]{1,0:T(8,128)(2,1)S(1)} %get-tuple-element.21.mat_ref) | copy-start | bytes 1769476
  36.6 22.7 %copy-start.2 = (bf16[384,768]{1,0:T(8,128)(2,1)}, bf16[384,768]{1,0:T(8,128)(2,1)S(1)}, u32[]{:S(2)}) copy-start(bf16[384,768]{1,0:T(8,128)(2,1)S(1)} %get-tuple-element.20.mat_ref) | copy-start | bytes 1769476
  36.7 34.2 %copy-start.4 = (bf16[384,768]{1,0:T(8,128)(2,1)}, bf16[384,768]{1,0:T(8,128)(2,1)S(1)}, u32[]{:S(2)}) copy-start(bf16[384,768]{1,0:T(8,128)(2,1)S(1)} %get-tuple-element.23.mat_ref) | copy-start | bytes 1769476
  39.4 13.1 %collective-permute-start.4 = (bf16[768,256]{1,0:T(8,128)(2,1)}, bf16[768,256]{1,0:T(8,128)(2,1)S(1)}, u32[]{:S(2)}, u32[]{:S(2)}) collective-permute-start(bf16[768,256]{1,0:T(8,128)(2,1)} %collective-permute-done.2), channel_id=1, source_target_pairs={{0,1},{1,2},{2,3},{3,4},{4,5},{5,6},{6,7},{7,0},{8,9},{9,10},{10,1... | collective-permute-start | bytes 1179656 | tf_op jit(solution)/shard_map/ppermute | solution.py:275
  41.3 13.1 %collective-permute-start.3 = (bf16[768,256]{1,0:T(8,128)(2,1)}, bf16[768,256]{1,0:T(8,128)(2,1)S(1)}, u32[]{:S(2)}, u32[]{:S(2)}) collective-permute-start(bf16[768,256]{1,0:T(8,128)(2,1)} %collective-permute-done.1), channel_id=1, source_target_pairs={{0,7},{1,0},{2,1},{3,2},{4,3},{5,4},{6,5},{7,6},{8,15},{9,8},{10,9... | collective-permute-start | bytes 1179656 | tf_op jit(solution)/shard_map/ppermute | solution.py:275
  52.5 18.3 %collective-permute-start.6 = (bf16[768,256]{1,0:T(8,128)(2,1)S(1)}, bf16[768,256]{1,0:T(8,128)(2,1)S(1)}, u32[]{:S(2)}, u32[]{:S(2)}) collective-permute-start(bf16[768,256]{1,0:T(8,128)(2,1)S(1)} %collective-permute-done.4), channel_id=1, source_target_pairs={{0,1},{1,2},{2,3},{3,4},{4,5},{5,6},{6,7},{7,0},{8,9},{9,10},{10,1... | collective-permute-start | bytes 1179656 | tf_op jit(solution)/shard_map/ppermute | solution.py:275
  54.5 11.0 %collective-permute-start.5 = (bf16[768,256]{1,0:T(8,128)(2,1)S(1)}, bf16[768,256]{1,0:T(8,128)(2,1)}, u32[]{:S(2)}, u32[]{:S(2)}) collective-permute-start(bf16[768,256]{1,0:T(8,128)(2,1)S(1)} %collective-permute-done.3), channel_id=1, source_target_pairs={{0,7},{1,0},{2,1},{3,2},{4,3},{5,4},{6,5},{7,6},{8,15},{9,8},{10,9... | collective-permute-start | bytes 1179656 | tf_op jit(solution)/shard_map/ppermute | solution.py:275
  65.4 11.2 %collective-permute-start.7 = (bf16[768,256]{1,0:T(8,128)(2,1)}, bf16[768,256]{1,0:T(8,128)(2,1)S(1)}, u32[]{:S(2)}, u32[]{:S(2)}) collective-permute-start(bf16[768,256]{1,0:T(8,128)(2,1)} %collective-permute-done.5), channel_id=1, source_target_pairs={{0,7},{1,0},{2,1},{3,2},{4,3},{5,4},{6,5},{7,6},{8,15},{9,8},{10,9... | collective-permute-start | bytes 1179656 | tf_op jit(solution)/shard_map/ppermute | solution.py:275
  72.5 4.1 %copy-start.16 = (f32[256]{0:T(256)S(1)}, f32[256]{0:T(256)}, u32[]{:S(2)}) copy-start(f32[256]{0:T(256)} %param.13) | copy-start | bytes 3076
  72.6 4.1 %copy-start.11 = (bf16[384,256]{1,0:T(8,128)(2,1)S(1)}, bf16[384,256]{1,0:T(8,128)(2,1)}, u32[]{:S(2)}) copy-start(bf16[384,256]{1,0:T(8,128)(2,1)} %cotangent_ref.1) | copy-start | bytes 589828
  81.9 0.7 copy-start.19
  82.7 19.2 %collective-permute-start.11 = (bf16[256,768]{1,0:T(8,128)(2,1)}, bf16[256,768]{1,0:T(8,128)(2,1)}, u32[]{:S(2)}, u32[]{:S(2)}) collective-permute-start(bf16[256,768]{1,0:T(8,128)(2,1)} %get-tuple-element.28), channel_id=1, source_target_pairs={{0,7},{1,0},{2,1},{3,2},{4,3},{5,4},{6,5},{7,6},{8,15},{9,8},{10,9... | collective-permute-start | bytes 1179656 | tf_op jit(solution)/shard_map/ppermute | solution.py:275
  88.7 60.5 %all-to-all-start.1 = ((bf16[32,256,128]{2,1,0:T(8,128)(2,1)}), bf16[32,256,128]{2,1,0:T(8,128)(2,1)S(1)}, u32[]{:S(2)}, u32[]{:S(2)}) async-start(bf16[32,256,128]{2,1,0:T(8,128)(2,1)} %get-tuple-element.31), calls=%async_computation.1 | async-start | bytes 4194304 | tf_op jit(solution)/shard_map/all_to_all | solution.py:378
  99.8 17.5 %copy-start.1 = (bf16[384,768]{1,0:T(8,128)(2,1)S(1)}, bf16[384,768]{1,0:T(8,128)(2,1)}, u32[]{:S(2)}) copy-start(bf16[384,768]{1,0:T(8,128)(2,1)} %copy-done) | copy-start | bytes 1769476
  99.8 13.9 %collective-permute-start.8 = (bf16[256,768]{1,0:T(8,128)(2,1)}, bf16[256,768]{1,0:T(8,128)(2,1)S(1)}, u32[]{:S(2)}, u32[]{:S(2)}) collective-permute-start(bf16[256,768]{1,0:T(8,128)(2,1)} %copy-done.19), channel_id=1, source_target_pairs={{0,1},{1,2},{2,3},{3,4},{4,5},{5,6},{6,7},{7,0},{8,9},{9,10},{10,1... | collective-permute-start | bytes 1179656 | tf_op jit(solution)/shard_map/ppermute | solution.py:275
  101.9 1.1 copy-start.5
  104.3 12.9 %collective-permute-start.12 = (bf16[256,768]{1,0:T(8,128)(2,1)S(1)}, bf16[256,768]{1,0:T(8,128)(2,1)S(1)}, u32[]{:S(2)}, u32[]{:S(2)}) collective-permute-start(bf16[256,768]{1,0:T(8,128)(2,1)S(1)} %hop.7), channel_id=1, source_target_pairs={{0,7},{1,0},{2,1},{3,2},{4,3},{5,4},{6,5},{7,6},{8,15},{9,8},{10,9... | collective-permute-start | bytes 1179656 | tf_op jit(solution)/shard_map/ppermute | solution.py:275
  113.7 1.1 copy-start.3
  115.2 26.2 %copy-start.9 = (bf16[384,768]{1,0:T(8,128)(2,1)S(1)}, bf16[384,768]{1,0:T(8,128)(2,1)}, u32[]{:S(2)}) copy-start(bf16[384,768]{1,0:T(8,128)(2,1)} %copy-done.8) | copy-start | bytes 1769476
  115.2 12.8 %collective-permute-start.9 = (bf16[256,768]{1,0:T(8,128)(2,1)S(1)}, bf16[256,768]{1,0:T(8,128)(2,1)S(1)}, u32[]{:S(2)}, u32[]{:S(2)}) collective-permute-start(bf16[256,768]{1,0:T(8,128)(2,1)S(1)} %hop.5), channel_id=1, source_target_pairs={{0,1},{1,2},{2,3},{3,4},{4,5},{5,6},{6,7},{7,0},{8,9},{9,10},{10,1... | collective-permute-start | bytes 1179656 | tf_op jit(solution)/shard_map/ppermute | solution.py:275
  117.6 12.6 %collective-permute-start.13 = (bf16[256,768]{1,0:T(8,128)(2,1)S(1)}, bf16[256,768]{1,0:T(8,128)(2,1)S(1)}, u32[]{:S(2)}, u32[]{:S(2)}) collective-permute-start(bf16[256,768]{1,0:T(8,128)(2,1)S(1)} %hop.8), channel_id=1, source_target_pairs={{0,7},{1,0},{2,1},{3,2},{4,3},{5,4},{6,5},{7,6},{8,15},{9,8},{10,9... | collective-permute-start | bytes 1179656 | tf_op jit(solution)/shard_map/ppermute | solution.py:275
  128.4 11.7 %collective-permute-start.10 = (bf16[256,768]{1,0:T(8,128)(2,1)S(1)}, bf16[256,768]{1,0:T(8,128)(2,1)S(1)}, u32[]{:S(2)}, u32[]{:S(2)}) collective-permute-start(bf16[256,768]{1,0:T(8,128)(2,1)S(1)} %hop.6), channel_id=1, source_target_pairs={{0,1},{1,2},{2,3},{3,4},{4,5},{5,6},{6,7},{7,0},{8,9},{9,10},{10,1... | collective-permute-start | bytes 1179656 | tf_op jit(solution)/shard_map/ppermute | solution.py:275
  130.7 18.5 %copy-start.13 = (s32[1,1,32]{2,1,0:T(1,128)S(1)}, s32[1,1,32]{2,1,0:T(1,128)}, u32[]{:S(2)}) copy-start(s32[1,1,32]{2,1,0:T(1,128)} %param.19) | copy-start | bytes 388
  130.7 18.5 %copy-start.15 = (s32[1,1,32]{2,1,0:T(1,128)S(1)}, s32[1,1,32]{2,1,0:T(1,128)}, u32[]{:S(2)}) copy-start(s32[1,1,32]{2,1,0:T(1,128)} %param.20) | copy-start | bytes 388
  130.7 10.7 %collective-permute-start.14 = (bf16[256,768]{1,0:T(8,128)(2,1)S(1)}, bf16[256,768]{1,0:T(8,128)(2,1)S(1)}, u32[]{:S(2)}, u32[]{:S(2)}) collective-permute-start(bf16[256,768]{1,0:T(8,128)(2,1)S(1)} %hop.9), channel_id=1, source_target_pairs={{0,7},{1,0},{2,1},{3,2},{4,3},{5,4},{6,5},{7,6},{8,15},{9,8},{10,9... | collective-permute-start | bytes 1179656 | tf_op jit(solution)/shard_map/ppermute | solution.py:275
  141.8 9.5 %copy-start.10 = (bf16[256,256]{1,0:T(8,128)(2,1)S(1)}, bf16[256,256]{1,0:T(8,128)(2,1)}, u32[]{:S(2)}) copy-start(bf16[256,256]{1,0:T(8,128)(2,1)} %weight_ref.1) | copy-start | bytes 393220
  141.8 9.5 %collective-permute-start.15 = (bf16[256,384]{1,0:T(8,128)(2,1)S(1)}, bf16[256,384]{1,0:T(8,128)(2,1)S(1)}, u32[]{:S(2)}, u32[]{:S(2)}) collective-permute-start(bf16[256,384]{1,0:T(8,128)(2,1)S(1)} %get-tuple-element.30), channel_id=1, source_target_pairs={{0,8},{1,9},{2,10},{3,11},{4,12},{5,13},{6,14},{7,15},{8,0},{9,1},... | collective-permute-start | bytes 589832 | tf_op jit(solution)/shard_map/ppermute | solution.py:278

commit v6 on v5

--- a/solution.py
+++ b/solution.py
@@ -8,7 +8,7 @@
 BF, F32 = jnp.bfloat16, jnp.float32
 TILE = 128
 FAR = 2
-CHUNKS = 4
+CHUNKS = 8
 VMEM_LIMIT = 16 * 1024 * 1024
 PAIR_COST = 100_000_000_000
 CLOSE_COST = 26_500_000_000
@@ -60,9 +60,19 @@
     projected_ref[...] = product(features[...], weight[...]).astype(BF)
 
 
-def fill_kernel(blk_ref, live_ref, projected_ref, outgoing_hbm, zeros, sems):
+def fill_kernel(
+    blk_hbm, live_hbm, projected_ref, outgoing_hbm, blk_ref, live_ref, zeros, load_sems, sems
+):
+    parts = outgoing_hbm.shape[0]
+    loads = [
+        pltpu.make_async_copy(blk_hbm, blk_ref, load_sems.at[0]),
+        pltpu.make_async_copy(live_hbm, live_ref, load_sems.at[1]),
+    ]
+    for copy in loads:
+        copy.start()
     zeros[...] = jnp.zeros(zeros.shape, BF)
-    parts = outgoing_hbm.shape[0]
+    for copy in loads:
+        copy.wait()
 
     def start(part, carried):
         @pl.when(live_ref[part] > 0)
@@ -165,9 +175,10 @@
     cut_hbm,
     hidden_ref,
     grad_ref,
-    left_ref,
-    right_ref,
+    left_hbm,
+    right_hbm,
     terms_hbm,
+    messages,
     cut,
     terms,
     sems,
@@ -185,9 +196,15 @@
     hidden_ref[...] = activated.astype(BF)
     grad = (cotangent_ref[...].astype(F32) * derivative).T.astype(BF)
     grad_ref[...] = grad
-    left_ref[...] = product(grad, far_mat_ref[...]).astype(BF)
-    right_ref[...] = product(grad, near_mat_ref[...]).astype(BF)
     stores = []
+    for place, (mat_ref, out_hbm) in enumerate(
+        ((far_mat_ref, left_hbm), (near_mat_ref, right_hbm))
+    ):
+        messages[place] = product(grad, mat_ref[...]).astype(BF)
+        stores.append(
+            pltpu.make_async_copy(messages.at[place], out_hbm, sems.at[2 * chunks + place])
+        )
+        stores[-1].start()
     for piece in range(chunks):
         loads[piece].wait()
         result = product(grad, cut[piece]).astype(BF)
@@ -263,6 +280,7 @@
     me = lax.axis_index("blk")
     place, half = me % ring, me // ring
     wide = FAR * rows
+    chunks = min(CHUNKS, parts)
     send_to, is_live, dst = send_blk[0, 0], send_live[0, 0], recv_dst[0, 0]
     shape = jax.ShapeDtypeStruct
 
@@ -294,10 +312,16 @@
         fill_kernel,
         "fill",
         pltpu.HBM((parts, TILE, width), BF),
-        [SMEM, SMEM, VMEM],
+        [HBM, HBM, VMEM],
         HBM,
-        [pltpu.VMEM((TILE, width), BF), pltpu.SemaphoreType.DMA((parts,))],
-    )(send_to, is_live, projected)
+        [
+            pltpu.SMEM((parts,), jnp.int32),
+            pltpu.SMEM((parts,), jnp.int32),
+            pltpu.VMEM((TILE, width), BF),
+            pltpu.SemaphoreType.DMA((2,)),
+            pltpu.SemaphoreType.DMA((parts,)),
+        ],
+    )(in_hbm(send_to), in_hbm(is_live), projected)
     incoming = lax.all_to_all(outgoing, "dom", split_axis=0, concat_axis=0, tiled=True)
 
     dense = call(
@@ -311,11 +335,11 @@
     dense_cut = call(
         spread_cut_kernel,
         "spread_cut",
-        pltpu.HBM((CHUNKS, rows, parts // CHUNKS * TILE), BF),
+        pltpu.HBM((chunks, rows, parts // chunks * TILE), BF),
         [SMEM, VMEM],
         HBM,
         [
-            pltpu.VMEM((CHUNKS, rows, parts // CHUNKS * TILE), BF),
+            pltpu.VMEM((chunks, rows, parts // chunks * TILE), BF),
             pltpu.SemaphoreType.DMA,
         ],
         moved=6 << 20,
@@ -327,9 +351,9 @@
     running = product(dense[0], pair)
     right = left = pair
     for hop in range(1, reach):
-        left, right = along_ring(left, -1), along_ring(right, 1)
+        right, left = along_ring(right, 1), along_ring(left, -1)
+        running = running + product(dense[ring - hop], right)
         running = running + product(dense[hop], left)
-        running = running + product(dense[ring - hop], right)
     left = along_ring(left, -1)
     cut_sum = call(
         cut_sum_kernel,
@@ -340,7 +364,7 @@
         [
             pltpu.VMEM(dense_cut.shape, BF),
             pltpu.VMEM((parts, TILE, width), BF),
-            pltpu.SemaphoreType.DMA((2 * CHUNKS,)),
+            pltpu.SemaphoreType.DMA((2 * chunks,)),
         ],
         flops=CUT_COST,
     )(in_hbm(dense_cut), in_hbm(incoming))
@@ -349,14 +373,15 @@
         middle_kernel,
         "middle",
         (shape((rows, width), BF), shape((width, rows), BF))
-        + (shape((width, wide), BF),) * 2
+        + (pltpu.HBM((width, wide), BF),) * 2
         + (pltpu.HBM((parts, width, TILE), BF),),
         [VMEM] * 7 + [HBM],
-        (VMEM,) * 4 + (HBM,),
+        (VMEM,) * 2 + (HBM,) * 3,
         [
+            pltpu.VMEM((2, width, wide), BF),
             pltpu.VMEM(dense_cut.shape, BF),
             pltpu.VMEM((parts, width, TILE), BF),
-            pltpu.SemaphoreType.DMA((2 * CHUNKS,)),
+            pltpu.SemaphoreType.DMA((2 * chunks + 2,)),
         ],
     )(
         running,

time: 155 us -> 150 us (0.968)
  waiting for transfers between devices: 33.6 us -> 29 us
  local copies, waits for them, and re-layouts: 4.42 us -> 2.38 us
  starting transfers between devices: 85.8 us -> 87.5 us
    ppermute x14, waiting for transfers between devices: 29.2 us -> 24.6 us  [along_ring(): return lax.ppermute(value, 'blk', moves)]
    ppermute x14, starting transfers between devices: 57.2 us -> 61.3 us  [along_ring(): return lax.ppermute(value, 'blk', moves)]
    all_to_all x1, starting transfers between devices: 11.1 us -> 8.61 us  [on_device(): lax.all_to_all(terms, 'dom', split_axis=0, concat_axis=0, tiled=True)]
    unnamed x43 -> x37, local copies, waits for them, and re-layouts: 4.33 us -> 2.29 us
  transfers between devices with their start and end apart: 18 -> 18, of which waited for: 10 -> 10; matrix products, arithmetic and copies ran while one was open for 4% -> 4% of each run, Pallas kernels for 9% -> 10%
where the time goes in v6:
time: 150 us; the launch traced here: 148 us
  starting transfers between devices  87.5 us (58%)
  waiting for transfers between devices  29 us (19%)
  Pallas kernels  22.5 us (15%)
  matrix products  5.26 us (4%)
  local copies, waits for them, and re-layouts  2.38 us (2%)
    ppermute x14, starting transfers between devices, along_ring(): return lax.ppermute(value, 'blk', moves)  61.3 us
    ppermute x14, waiting for transfers between devices, along_ring(): return lax.ppermute(value, 'blk', moves)  24.6 us
    ppermute x2, starting transfers between devices, across(): lax.ppermute(value, 'blk', [(i, (i + ring) % peers) for i in range(peers)])  9.24 us
    all_to_all x1, starting transfers between devices, on_device(): lax.all_to_all(terms, 'dom', split_axis=0, concat_axis=0, tiled=True)  8.61 us
    all_to_all x1, starting transfers between devices, on_device(): lax.all_to_all(outgoing, 'dom', split_axis=0, concat_axis=0, tiled=True)  8.3 us
    dot_general x7, matrix products, product(): return jnp.dot(left, right, preferred_element_type=F32)  5.26 us
    pallas_call x1, Pallas kernels, on_device(): call(middle_kernel, 'middle', (shape((rows, width), BF), shape((width, ro...  5.23 us
    all_to_all x1, waiting for transfers between devices, on_device(): lax.all_to_all(terms, 'dom', split_axis=0, concat_axis=0, tiled=True)  3.64 us
  transfers between devices with their start and end apart: 18, of which 10 were waited for; matrix products, arithmetic and copies ran while one was open for 4% of the time, Pallas kernels for 10%

profile of v6, /device:TPU:1, one launch (start us, length us, event | category | flops | bytes accessed | tf_op | source)
XLA Modules:
  0.0 147.8 jit_solution(17793002318926291592)
XLA Ops:
  0.6 1.2 project.1.own_ref.projected_ref
  1.9 5.5 %collective-permute-start = (bf16[384,256]{1,0:T(8,128)(2,1)S(1)}, bf16[384,256]{1,0:T(8,128)(2,1)S(1)}, u32[]{:S(2)}, u32[]{:S(2)}) collective-permute-start(bf16[384,256]{1,0:T(8,128)(2,1)S(1)} %project.1.own_ref.projected_ref), channel_id=1, source_target_pairs={{0,8},{1,9},{2,10},{3,11},{4,12},{5,13},{6,14},{7,15},{8,0},{9,1},... | collective-permute-start | bytes 589832 | tf_op jit(solution)/shard_map/ppermute | solution.py:296
  7.4 2.3 %fill.1 = bf16[32,128,256]{2,1,0:T(8,128)(2,1)} custom-call(s32[32]{0:T(128)} %bitcast.27, s32[32]{0:T(128)} %bitcast.29, bf16[384,256]{1,0:T(8,128)(2,1)S(1)} %project.1.own_ref.projected_ref), custom_call_target="tpu_custom_call" | custom-call | tf_op jit(solution)/shard_map/fill/pallas_call | solution.py:311
  9.7 8.3 %all-to-all-start = ((bf16[32,128,256]{2,1,0:T(8,128)(2,1)}), bf16[32,128,256]{2,1,0:T(8,128)(2,1)}, u32[]{:S(2)}, u32[]{:S(2)}) async-start(bf16[32,128,256]{2,1,0:T(8,128)(2,1)} %fill.1), calls=%async_computation | async-start | bytes 4194304 | tf_op jit(solution)/shard_map/all_to_all | solution.py:325
  18.0 0.0 collective-permute-done.other_ref
  18.0 0.0 copy-start.17
  18.0 0.0 copy-start.7
  18.0 0.0 copy-start.15
  18.1 10.8 %collective-permute-start.2 = (bf16[768,256]{1,0:T(8,128)(2,1)S(1)}, bf16[768,256]{1,0:T(8,128)(2,1)}, u32[]{:S(2)}, u32[]{:S(2)}) collective-permute-start(bf16[768,256]{1,0:T(8,128)(2,1)S(1)} %pair.1), channel_id=1, source_target_pairs={{0,7},{1,0},{2,1},{3,2},{4,3},{5,4},{6,5},{7,6},{8,15},{9,8},{10,9... | collective-permute-start | bytes 1179656 | tf_op jit(solution)/shard_map/ppermute | solution.py:293
  28.9 1.9 %collective-permute-start.1 = (bf16[768,256]{1,0:T(8,128)(2,1)S(1)}, bf16[768,256]{1,0:T(8,128)(2,1)}, u32[]{:S(2)}, u32[]{:S(2)}) collective-permute-start(bf16[768,256]{1,0:T(8,128)(2,1)S(1)} %pair.1), channel_id=1, source_target_pairs={{0,1},{1,2},{2,3},{3,4},{4,5},{5,6},{6,7},{7,0},{8,9},{9,10},{10,1... | collective-permute-start | bytes 1179656 | tf_op jit(solution)/shard_map/ppermute | solution.py:293
  30.8 0.1 copy.14
  30.9 0.1 reshape_squeeze.3.refs_0_
  31.0 0.0 copy-start.6
  31.0 0.0 copy-start.16
  31.1 2.8 %spread_cut.1.cut_hbm = bf16[8,384,512]{2,1,0:T(8,128)(2,1)} custom-call(s32[32]{0:T(128)S(1)} %bitcast.32, bf16[32,128,128]{2,1,0:T(8,128)(2,1)S(1)} %bitcast.26), custom_call_target="tpu_custom_call" | custom-call | bytes 6291456 | tf_op jit(solution)/shard_map/spread_cut/pallas_call | solution.py:335
  33.8 2.1 %spread.1 = (bf16[384,768]{1,0:T(8,128)(2,1)S(1)}, bf16[384,768]{1,0:T(8,128)(2,1)S(1)}, bf16[384,768]{1,0:T(8,128)(2,1)S(1)}, bf16[384,768]{1,0:T(8,128)(2,1)S(...) custom-call(s32[64]{0:T(128)S(1)} %reshape_squeeze.3.refs_0_, ...), custom_call_target="tpu_custom_call" | custom-call | bytes 10485760 | tf_op jit(solution)/shard_map/spread/pallas_call | solution.py:327
  36.0 1.1 collective-permute-done.2
  37.1 5.4 %collective-permute-start.4 = (bf16[768,256]{1,0:T(8,128)(2,1)}, bf16[768,256]{1,0:T(8,128)(2,1)S(1)}, u32[]{:S(2)}, u32[]{:S(2)}) collective-permute-start(bf16[768,256]{1,0:T(8,128)(2,1)} %collective-permute-done.2), channel_id=1, source_target_pairs={{0,7},{1,0},{2,1},{3,2},{4,3},{5,4},{6,5},{7,6},{8,15},{9,8},{10,9... | collective-permute-start | bytes 1179656 | tf_op jit(solution)/shard_map/ppermute | solution.py:293
  42.5 1.9 %collective-permute-start.3 = (bf16[768,256]{1,0:T(8,128)(2,1)}, bf16[768,256]{1,0:T(8,128)(2,1)S(1)}, u32[]{:S(2)}, u32[]{:S(2)}) collective-permute-start(bf16[768,256]{1,0:T(8,128)(2,1)} %collective-permute-done.1), channel_id=1, source_target_pairs={{0,1},{1,2},{2,3},{3,4},{4,5},{5,6},{6,7},{7,0},{8,9},{9,10},{10,1... | collective-permute-start | bytes 1179656 | tf_op jit(solution)/shard_map/ppermute | solution.py:293
  44.4 1.3 fusion.3
  45.7 1.3 fusion.4
  47.1 0.3 fusion.2
  47.4 2.6 %collective-permute-done.4 = bf16[768,256]{1,0:T(8,128)(2,1)S(1)} collective-permute-done((bf16[768,256]{1,0:T(8,128)(2,1)}, bf16[768,256]{1,0:T(8,128)(2,1)S(1)}, u32[]{:S(2)}, u32[]{:S(2)}) %collective-permute-start.4) | collective-permute-done | bytes 393248 | tf_op jit(solution)/shard_map/ppermute | solution.py:293
  50.0 5.3 %collective-permute-start.6 = (bf16[768,256]{1,0:T(8,128)(2,1)S(1)}, bf16[768,256]{1,0:T(8,128)(2,1)}, u32[]{:S(2)}, u32[]{:S(2)}) collective-permute-start(bf16[768,256]{1,0:T(8,128)(2,1)S(1)} %collective-permute-done.4), channel_id=1, source_target_pairs={{0,7},{1,0},{2,1},{3,2},{4,3},{5,4},{6,5},{7,6},{8,15},{9,8},{10,9... | collective-permute-start | bytes 1179656 | tf_op jit(solution)/shard_map/ppermute | solution.py:293
  55.3 1.9 %collective-permute-start.5 = (bf16[768,256]{1,0:T(8,128)(2,1)S(1)}, bf16[768,256]{1,0:T(8,128)(2,1)S(1)}, u32[]{:S(2)}, u32[]{:S(2)}) collective-permute-start(bf16[768,256]{1,0:T(8,128)(2,1)S(1)} %collective-permute-done.3), channel_id=1, source_target_pairs={{0,1},{1,2},{2,3},{3,4},{4,5},{5,6},{6,7},{7,0},{8,9},{9,10},{10,1... | collective-permute-start | bytes 1179656 | tf_op jit(solution)/shard_map/ppermute | solution.py:293
  57.3 0.3 fusion.5
  57.6 0.3 fusion.1
  57.9 3.8 %collective-permute-done.6 = bf16[768,256]{1,0:T(8,128)(2,1)} collective-permute-done((bf16[768,256]{1,0:T(8,128)(2,1)S(1)}, bf16[768,256]{1,0:T(8,128)(2,1)}, u32[]{:S(2)}, u32[]{:S(2)}) %collective-permute-start.6) | collective-permute-done | bytes 393248 | tf_op jit(solution)/shard_map/ppermute | solution.py:293
  61.7 5.4 %collective-permute-start.7 = (bf16[768,256]{1,0:T(8,128)(2,1)}, bf16[768,256]{1,0:T(8,128)(2,1)S(1)}, u32[]{:S(2)}, u32[]{:S(2)}) collective-permute-start(bf16[768,256]{1,0:T(8,128)(2,1)} %collective-permute-done.6), channel_id=1, source_target_pairs={{0,7},{1,0},{2,1},{3,2},{4,3},{5,4},{6,5},{7,6},{8,15},{9,8},{10,9... | collective-permute-start | bytes 1179656 | tf_op jit(solution)/shard_map/ppermute | solution.py:293
  67.1 1.3 fusion.6
  68.5 0.3 fusion.sum_ref
  68.8 0.0 copy-start.14
  68.8 0.0 copy-start.11
  68.9 3.4 %cut_sum.1.cut_sum_ref = f32[384,256]{1,0:T(8,128)S(1)} custom-call(bf16[8,384,512]{2,1,0:T(8,128)(2,1)} %spread_cut.1.cut_hbm, bf16[32,128,256]{2,1,0:T(8,128)(2,1)} %all-to-all-done.far_hbm), custom_call_target="tpu_custom_call" | custom-call | flops 2000000000 | tf_op jit(solution)/shard_map/cut_sum/pallas_call | solution.py:358
  72.2 0.7 collective-permute-done.7.last_ref
  72.9 5.2 %middle.1 = (bf16[384,256]{1,0:T(8,128)(2,1)}, bf16[256,384]{1,0:T(8,128)(2,1)S(1)}, bf16[256,768]{1,0:T(8,128)(2,1)}, bf16[256,768]{1,0:T(8,128)(2,1)}, bf16[32,256,128]{2,1,0:T(8,128)(2,1)}) custom-call(f32[384,256]{1,0:T(8,128)S(1)} %fusion.sum_ref, f32[384,256]{1,0:T(8,128)S(1)} %cut_sum.1.cut_sum_ref, ...), custom_call_target="tpu_custom_call" | custom-call | tf_op jit(solution)/shard_map/middle/pallas_call | solution.py:372
  78.2 8.6 %collective-permute-start.11 = (bf16[256,768]{1,0:T(8,128)(2,1)}, bf16[256,768]{1,0:T(8,128)(2,1)}, u32[]{:S(2)}, u32[]{:S(2)}) collective-permute-start(bf16[256,768]{1,0:T(8,128)(2,1)} %get-tuple-element.28), channel_id=1, source_target_pairs={{0,7},{1,0},{2,1},{3,2},{4,3},{5,4},{6,5},{7,6},{8,15},{9,8},{10,9... | collective-permute-start | bytes 1179656 | tf_op jit(solution)/shard_map/ppermute | solution.py:293
  86.8 8.6 %all-to-all-start.1 = ((bf16[32,256,128]{2,1,0:T(8,128)(2,1)}), bf16[32,256,128]{2,1,0:T(8,128)(2,1)S(1)}, u32[]{:S(2)}, u32[]{:S(2)}) async-start(bf16[32,256,128]{2,1,0:T(8,128)(2,1)} %get-tuple-element.31), calls=%async_computation.1 | async-start | bytes 4194304 | tf_op jit(solution)/shard_map/all_to_all | solution.py:403
  95.4 2.1 %collective-permute-start.8 = (bf16[256,768]{1,0:T(8,128)(2,1)}, bf16[256,768]{1,0:T(8,128)(2,1)S(1)}, u32[]{:S(2)}, u32[]{:S(2)}) collective-permute-start(bf16[256,768]{1,0:T(8,128)(2,1)} %get-tuple-element.27), channel_id=1, source_target_pairs={{0,1},{1,2},{2,3},{3,4},{4,5},{5,6},{6,7},{7,0},{8,9},{9,10},{10,1... | collective-permute-start | bytes 1179656 | tf_op jit(solution)/shard_map/ppermute | solution.py:293
  97.5 1.1 copy-done.5
  98.5 1.4 hop.7
  99.9 4.6 %collective-permute-start.12 = (bf16[256,768]{1,0:T(8,128)(2,1)S(1)}, bf16[256,768]{1,0:T(8,128)(2,1)S(1)}, u32[]{:S(2)}, u32[]{:S(2)}) collective-permute-start(bf16[256,768]{1,0:T(8,128)(2,1)S(1)} %hop.7), channel_id=1, source_target_pairs={{0,7},{1,0},{2,1},{3,2},{4,3},{5,4},{6,5},{7,6},{8,15},{9,8},{10,9... | collective-permute-start | bytes 1179656 | tf_op jit(solution)/shard_map/ppermute | solution.py:293
  104.5 4.8 %collective-permute-done.8.arrived_ref = bf16[256,768]{1,0:T(8,128)(2,1)S(1)} collective-permute-done((bf16[256,768]{1,0:T(8,128)(2,1)}, bf16[256,768]{1,0:T(8,128)(2,1)S(1)}, u32[]{:S(2)}, u32[]{:S(2)}) %collective-permute-start.8) | collective-permute-done | bytes 393248 | tf_op jit(solution)/shard_map/ppermute | solution.py:293
  109.3 1.1 copy-done.3
  110.4 0.4 hop.5
  110.8 2.1 %collective-permute-start.9 = (bf16[256,768]{1,0:T(8,128)(2,1)S(1)}, bf16[256,768]{1,0:T(8,128)(2,1)S(1)}, u32[]{:S(2)}, u32[]{:S(2)}) collective-permute-start(bf16[256,768]{1,0:T(8,128)(2,1)S(1)} %hop.5), channel_id=1, source_target_pairs={{0,1},{1,2},{2,3},{3,4},{4,5},{5,6},{6,7},{7,0},{8,9},{9,10},{10,1... | collective-permute-start | bytes 1179656 | tf_op jit(solution)/shard_map/ppermute | solution.py:293
  112.8 0.4 hop.8
  113.2 4.9 %collective-permute-start.13 = (bf16[256,768]{1,0:T(8,128)(2,1)S(1)}, bf16[256,768]{1,0:T(8,128)(2,1)S(1)}, u32[]{:S(2)}, u32[]{:S(2)}) collective-permute-start(bf16[256,768]{1,0:T(8,128)(2,1)S(1)} %hop.8), channel_id=1, source_target_pairs={{0,7},{1,0},{2,1},{3,2},{4,3},{5,4},{6,5},{7,6},{8,15},{9,8},{10,9... | collective-permute-start | bytes 1179656 | tf_op jit(solution)/shard_map/ppermute | solution.py:293
  118.1 5.4 %collective-permute-done.9.arrived_ref = bf16[256,768]{1,0:T(8,128)(2,1)S(1)} collective-permute-done((bf16[256,768]{1,0:T(8,128)(2,1)S(1)}, bf16[256,768]{1,0:T(8,128)(2,1)S(1)}, u32[]{:S(2)}, u32[]{:S(2)}) %collective-permute-start.9) | collective-permute-done | bytes 393248 | tf_op jit(solution)/shard_map/ppermute | solution.py:293
  123.6 0.4 hop.6
  123.9 1.9 %collective-permute-start.10 = (bf16[256,768]{1,0:T(8,128)(2,1)S(1)}, bf16[256,768]{1,0:T(8,128)(2,1)S(1)}, u32[]{:S(2)}, u32[]{:S(2)}) collective-permute-start(bf16[256,768]{1,0:T(8,128)(2,1)S(1)} %hop.6), channel_id=1, source_target_pairs={{0,1},{1,2},{2,3},{3,4},{4,5},{5,6},{6,7},{7,0},{8,9},{9,10},{10,1... | collective-permute-start | bytes 1179656 | tf_op jit(solution)/shard_map/ppermute | solution.py:293
  125.9 0.4 hop.9
  126.2 0.0 copy-start.12
  126.3 0.0 copy-start.13
  126.3 4.6 %collective-permute-start.14 = (bf16[256,768]{1,0:T(8,128)(2,1)S(1)}, bf16[256,768]{1,0:T(8,128)(2,1)S(1)}, u32[]{:S(2)}, u32[]{:S(2)}) collective-permute-start(bf16[256,768]{1,0:T(8,128)(2,1)S(1)} %hop.9), channel_id=1, source_target_pairs={{0,7},{1,0},{2,1},{3,2},{4,3},{5,4},{6,5},{7,6},{8,15},{9,8},{10,9... | collective-permute-start | bytes 1179656 | tf_op jit(solution)/shard_map/ppermute | solution.py:293
  130.9 4.8 %collective-permute-done.10.left_ref = bf16[256,768]{1,0:T(8,128)(2,1)S(1)} collective-permute-done((bf16[256,768]{1,0:T(8,128)(2,1)S(1)}, bf16[256,768]{1,0:T(8,128)(2,1)S(1)}, u32[]{:S(2)}, u32[]{:S(2)}) %collective-permute-start.10) | collective-permute-done | bytes 393248 | tf_op jit(solution)/shard_map/ppermute | solution.py:293
  135.7 1.3 collective-permute-done.14.right_ref
  137.0 0.4 close.1
  137.4 0.0 copy-start.10
  137.4 3.8 %collective-permute-start.15 = (bf16[256,384]{1,0:T(8,128)(2,1)S(1)}, bf16[256,384]{1,0:T(8,128)(2,1)S(1)}, u32[]{:S(2)}, u32[]{:S(2)}) collective-permute-start(bf16[256,384]{1,0:T(8,128)(2,1)S(1)} %get-tuple-element.30), channel_id=1, source_target_pairs={{0,8},{1,9},{2,10},{3,11},{4,12},{5,13},{6,14},{7,15},{8,0},{9,1},... | collective-permute-start | bytes 589832 | tf_op jit(solution)/shard_map/ppermute | solution.py:296
  141.1 3.6 %all-to-all-done.1.arrived_ref = bf16[32,256,128]{2,1,0:T(8,128)(2,1)S(1)} async-done(((bf16[32,256,128]{2,1,0:T(8,128)(2,1)}), bf16[32,256,128]{2,1,0:T(8,128)(2,1)S(1)}, u32[]{:S(2)}, u32[]{:S(2)}) %all-to-all-start.1) | async-done | bytes 2097184 | tf_op jit(solution)/shard_map/all_to_all | solution.py:403
  144.8 1.3 gather.1.cut_ref
  146.1 0.7 collective-permute-done.15.other_ref
  146.9 0.9 last.1
  (32 shorter events, 0.1 us)
Async XLA Ops:
  1.9 16.1 %collective-permute-start = (bf16[384,256]{1,0:T(8,128)(2,1)S(1)}, bf16[384,256]{1,0:T(8,128)(2,1)S(1)}, u32[]{:S(2)}, u32[]{:S(2)}) collective-permute-start(bf16[384,256]{1,0:T(8,128)(2,1)S(1)} %project.1.own_ref.projected_ref), channel_id=1, source_target_pairs={{0,8},{1,9},{2,10},{3,11},{4,12},{5,13},{6,14},{7,15},{8,0},{9,1},... | collective-permute-start | bytes 589832 | tf_op jit(solution)/shard_map/ppermute | solution.py:296
  9.7 59.2 %all-to-all-start = ((bf16[32,128,256]{2,1,0:T(8,128)(2,1)}), bf16[32,128,256]{2,1,0:T(8,128)(2,1)}, u32[]{:S(2)}, u32[]{:S(2)}) async-start(bf16[32,128,256]{2,1,0:T(8,128)(2,1)} %fill.1), calls=%async_computation | async-start | bytes 4194304 | tf_op jit(solution)/shard_map/all_to_all | solution.py:325
  18.0 12.8 %copy-start.17 = (s32[1,1,16,4]{2,3,1,0:T(4,128)S(1)}, s32[1,1,16,4]{2,3,1,0:T(4,128)}, u32[]{:S(2)}) copy-start(s32[1,1,16,4]{2,3,1,0:T(4,128)} %param.16) | copy-start | bytes 772
  18.0 13.0 %copy-start.7 = (bf16[1,1,32,128,128]{4,3,2,1,0:T(8,128)(2,1)S(1)}, bf16[1,1,32,128,128]{4,3,2,1,0:T(8,128)(2,1)}, u32[]{:S(2)}) copy-start(bf16[1,1,32,128,128]{4,3,2,1,0:T(8,128)(2,1)} %param.18) | copy-start | bytes 3145732
  18.0 13.0 %copy-start.15 = (s32[1,1,32]{2,1,0:T(1,128)S(1)}, s32[1,1,32]{2,1,0:T(1,128)}, u32[]{:S(2)}) copy-start(s32[1,1,32]{2,1,0:T(1,128)} %param.21) | copy-start | bytes 388
  18.1 19.0 %collective-permute-start.2 = (bf16[768,256]{1,0:T(8,128)(2,1)S(1)}, bf16[768,256]{1,0:T(8,128)(2,1)}, u32[]{:S(2)}, u32[]{:S(2)}) collective-permute-start(bf16[768,256]{1,0:T(8,128)(2,1)S(1)} %pair.1), channel_id=1, source_target_pairs={{0,7},{1,0},{2,1},{3,2},{4,3},{5,4},{6,5},{7,6},{8,15},{9,8},{10,9... | collective-permute-start | bytes 1179656 | tf_op jit(solution)/shard_map/ppermute | solution.py:293
  28.9 13.6 %collective-permute-start.1 = (bf16[768,256]{1,0:T(8,128)(2,1)S(1)}, bf16[768,256]{1,0:T(8,128)(2,1)}, u32[]{:S(2)}, u32[]{:S(2)}) collective-permute-start(bf16[768,256]{1,0:T(8,128)(2,1)S(1)} %pair.1), channel_id=1, source_target_pairs={{0,1},{1,2},{2,3},{3,4},{4,5},{5,6},{6,7},{7,0},{8,9},{9,10},{10,1... | collective-permute-start | bytes 1179656 | tf_op jit(solution)/shard_map/ppermute | solution.py:293
  31.0 2.8 %copy-start.6 = (bf16[1,1,16,4,128,128]{5,4,3,2,1,0:T(8,128)(2,1)S(1)}, bf16[1,1,16,4,128,128]{5,4,3,2,1,0:T(8,128)(2,1)}, u32[]{:S(2)}) copy-start(bf16[1,1,16,4,128,128]{5,4,3,2,1,0:T(8,128)(2,1)} %param.15) | copy-start | bytes 6291460
  31.0 2.8 %copy-start.16 = (s32[1,1,16]{2,1,0:T(1,128)S(1)}, s32[1,1,16]{2,1,0:T(1,128)}, u32[]{:S(2)}) copy-start(s32[1,1,16]{2,1,0:T(1,128)} %param.17) | copy-start | bytes 196
  35.9 11.5 %copy-start.8 = (bf16[384,768]{1,0:T(8,128)(2,1)}, bf16[384,768]{1,0:T(8,128)(2,1)S(1)}, u32[]{:S(2)}) copy-start(bf16[384,768]{1,0:T(8,128)(2,1)S(1)} %get-tuple-element.17.mat_ref) | copy-start | bytes 1769476
  35.9 21.3 %copy-start.2 = (bf16[384,768]{1,0:T(8,128)(2,1)}, bf16[384,768]{1,0:T(8,128)(2,1)S(1)}, u32[]{:S(2)}) copy-start(bf16[384,768]{1,0:T(8,128)(2,1)S(1)} %get-tuple-element.21.mat_ref) | copy-start | bytes 1769476
  35.9 21.7 %copy-start = (bf16[384,768]{1,0:T(8,128)(2,1)}, bf16[384,768]{1,0:T(8,128)(2,1)S(1)}, u32[]{:S(2)}) copy-start(bf16[384,768]{1,0:T(8,128)(2,1)S(1)} %get-tuple-element.20.mat_ref) | copy-start | bytes 1769476
  35.9 32.5 %copy-start.4 = (bf16[384,768]{1,0:T(8,128)(2,1)}, bf16[384,768]{1,0:T(8,128)(2,1)S(1)}, u32[]{:S(2)}) copy-start(bf16[384,768]{1,0:T(8,128)(2,1)S(1)} %get-tuple-element.22.mat_ref) | copy-start | bytes 1769476
  37.1 13.0 %collective-permute-start.4 = (bf16[768,256]{1,0:T(8,128)(2,1)}, bf16[768,256]{1,0:T(8,128)(2,1)S(1)}, u32[]{:S(2)}, u32[]{:S(2)}) collective-permute-start(bf16[768,256]{1,0:T(8,128)(2,1)} %collective-permute-done.2), channel_id=1, source_target_pairs={{0,7},{1,0},{2,1},{3,2},{4,3},{5,4},{6,5},{7,6},{8,15},{9,8},{10,9... | collective-permute-start | bytes 1179656 | tf_op jit(solution)/shard_map/ppermute | solution.py:293
  42.5 12.8 %collective-permute-start.3 = (bf16[768,256]{1,0:T(8,128)(2,1)}, bf16[768,256]{1,0:T(8,128)(2,1)S(1)}, u32[]{:S(2)}, u32[]{:S(2)}) collective-permute-start(bf16[768,256]{1,0:T(8,128)(2,1)} %collective-permute-done.1), channel_id=1, source_target_pairs={{0,1},{1,2},{2,3},{3,4},{4,5},{5,6},{6,7},{7,0},{8,9},{9,10},{10,1... | collective-permute-start | bytes 1179656 | tf_op jit(solution)/shard_map/ppermute | solution.py:293
  50.0 11.7 %collective-permute-start.6 = (bf16[768,256]{1,0:T(8,128)(2,1)S(1)}, bf16[768,256]{1,0:T(8,128)(2,1)}, u32[]{:S(2)}, u32[]{:S(2)}) collective-permute-start(bf16[768,256]{1,0:T(8,128)(2,1)S(1)} %collective-permute-done.4), channel_id=1, source_target_pairs={{0,7},{1,0},{2,1},{3,2},{4,3},{5,4},{6,5},{7,6},{8,15},{9,8},{10,9... | collective-permute-start | bytes 1179656 | tf_op jit(solution)/shard_map/ppermute | solution.py:293
  55.3 13.1 %collective-permute-start.5 = (bf16[768,256]{1,0:T(8,128)(2,1)S(1)}, bf16[768,256]{1,0:T(8,128)(2,1)S(1)}, u32[]{:S(2)}, u32[]{:S(2)}) collective-permute-start(bf16[768,256]{1,0:T(8,128)(2,1)S(1)} %collective-permute-done.3), channel_id=1, source_target_pairs={{0,1},{1,2},{2,3},{3,4},{4,5},{5,6},{6,7},{7,0},{8,9},{9,10},{10,1... | collective-permute-start | bytes 1179656 | tf_op jit(solution)/shard_map/ppermute | solution.py:293
  61.7 11.2 %collective-permute-start.7 = (bf16[768,256]{1,0:T(8,128)(2,1)}, bf16[768,256]{1,0:T(8,128)(2,1)S(1)}, u32[]{:S(2)}, u32[]{:S(2)}) collective-permute-start(bf16[768,256]{1,0:T(8,128)(2,1)} %collective-permute-done.6), channel_id=1, source_target_pairs={{0,7},{1,0},{2,1},{3,2},{4,3},{5,4},{6,5},{7,6},{8,15},{9,8},{10,9... | collective-permute-start | bytes 1179656 | tf_op jit(solution)/shard_map/ppermute | solution.py:293
  68.8 4.1 %copy-start.14 = (f32[256]{0:T(256)S(1)}, f32[256]{0:T(256)}, u32[]{:S(2)}) copy-start(f32[256]{0:T(256)} %param.13) | copy-start | bytes 3076
  68.8 4.1 %copy-start.11 = (bf16[384,256]{1,0:T(8,128)(2,1)S(1)}, bf16[384,256]{1,0:T(8,128)(2,1)}, u32[]{:S(2)}) copy-start(bf16[384,256]{1,0:T(8,128)(2,1)} %cotangent_ref.1) | copy-start | bytes 589828
  78.2 19.3 %collective-permute-start.11 = (bf16[256,768]{1,0:T(8,128)(2,1)}, bf16[256,768]{1,0:T(8,128)(2,1)}, u32[]{:S(2)}, u32[]{:S(2)}) collective-permute-start(bf16[256,768]{1,0:T(8,128)(2,1)} %get-tuple-element.28), channel_id=1, source_target_pairs={{0,7},{1,0},{2,1},{3,2},{4,3},{5,4},{6,5},{7,6},{8,15},{9,8},{10,9... | collective-permute-start | bytes 1179656 | tf_op jit(solution)/shard_map/ppermute | solution.py:293
  86.8 58.0 %all-to-all-start.1 = ((bf16[32,256,128]{2,1,0:T(8,128)(2,1)}), bf16[32,256,128]{2,1,0:T(8,128)(2,1)S(1)}, u32[]{:S(2)}, u32[]{:S(2)}) async-start(bf16[32,256,128]{2,1,0:T(8,128)(2,1)} %get-tuple-element.31), calls=%async_computation.1 | async-start | bytes 4194304 | tf_op jit(solution)/shard_map/all_to_all | solution.py:403
  95.4 17.5 %copy-start.1 = (bf16[384,768]{1,0:T(8,128)(2,1)S(1)}, bf16[384,768]{1,0:T(8,128)(2,1)}, u32[]{:S(2)}) copy-start(bf16[384,768]{1,0:T(8,128)(2,1)} %copy-done) | copy-start | bytes 1769476
  95.4 13.9 %collective-permute-start.8 = (bf16[256,768]{1,0:T(8,128)(2,1)}, bf16[256,768]{1,0:T(8,128)(2,1)S(1)}, u32[]{:S(2)}, u32[]{:S(2)}) collective-permute-start(bf16[256,768]{1,0:T(8,128)(2,1)} %get-tuple-element.27), channel_id=1, source_target_pairs={{0,1},{1,2},{2,3},{3,4},{4,5},{5,6},{6,7},{7,0},{8,9},{9,10},{10,1... | collective-permute-start | bytes 1179656 | tf_op jit(solution)/shard_map/ppermute | solution.py:293
  97.5 1.1 copy-start.5
  99.9 12.9 %collective-permute-start.12 = (bf16[256,768]{1,0:T(8,128)(2,1)S(1)}, bf16[256,768]{1,0:T(8,128)(2,1)S(1)}, u32[]{:S(2)}, u32[]{:S(2)}) collective-permute-start(bf16[256,768]{1,0:T(8,128)(2,1)S(1)} %hop.7), channel_id=1, source_target_pairs={{0,7},{1,0},{2,1},{3,2},{4,3},{5,4},{6,5},{7,6},{8,15},{9,8},{10,9... | collective-permute-start | bytes 1179656 | tf_op jit(solution)/shard_map/ppermute | solution.py:293
  109.3 1.1 copy-start.3
  110.8 26.2 %copy-start.9 = (bf16[384,768]{1,0:T(8,128)(2,1)S(1)}, bf16[384,768]{1,0:T(8,128)(2,1)}, u32[]{:S(2)}) copy-start(bf16[384,768]{1,0:T(8,128)(2,1)} %copy-done.8) | copy-start | bytes 1769476
  110.8 12.8 %collective-permute-start.9 = (bf16[256,768]{1,0:T(8,128)(2,1)S(1)}, bf16[256,768]{1,0:T(8,128)(2,1)S(1)}, u32[]{:S(2)}, u32[]{:S(2)}) collective-permute-start(bf16[256,768]{1,0:T(8,128)(2,1)S(1)} %hop.5), channel_id=1, source_target_pairs={{0,1},{1,2},{2,3},{3,4},{4,5},{5,6},{6,7},{7,0},{8,9},{9,10},{10,1... | collective-permute-start | bytes 1179656 | tf_op jit(solution)/shard_map/ppermute | solution.py:293
  113.2 12.6 %collective-permute-start.13 = (bf16[256,768]{1,0:T(8,128)(2,1)S(1)}, bf16[256,768]{1,0:T(8,128)(2,1)S(1)}, u32[]{:S(2)}, u32[]{:S(2)}) collective-permute-start(bf16[256,768]{1,0:T(8,128)(2,1)S(1)} %hop.8), channel_id=1, source_target_pairs={{0,7},{1,0},{2,1},{3,2},{4,3},{5,4},{6,5},{7,6},{8,15},{9,8},{10,9... | collective-permute-start | bytes 1179656 | tf_op jit(solution)/shard_map/ppermute | solution.py:293
  123.9 11.7 %collective-permute-start.10 = (bf16[256,768]{1,0:T(8,128)(2,1)S(1)}, bf16[256,768]{1,0:T(8,128)(2,1)S(1)}, u32[]{:S(2)}, u32[]{:S(2)}) collective-permute-start(bf16[256,768]{1,0:T(8,128)(2,1)S(1)} %hop.6), channel_id=1, source_target_pairs={{0,1},{1,2},{2,3},{3,4},{4,5},{5,6},{6,7},{7,0},{8,9},{9,10},{10,1... | collective-permute-start | bytes 1179656 | tf_op jit(solution)/shard_map/ppermute | solution.py:293
  126.2 18.5 %copy-start.12 = (s32[1,1,32]{2,1,0:T(1,128)S(1)}, s32[1,1,32]{2,1,0:T(1,128)}, u32[]{:S(2)}) copy-start(s32[1,1,32]{2,1,0:T(1,128)} %param.19) | copy-start | bytes 388
  126.3 18.5 %copy-start.13 = (s32[1,1,32]{2,1,0:T(1,128)S(1)}, s32[1,1,32]{2,1,0:T(1,128)}, u32[]{:S(2)}) copy-start(s32[1,1,32]{2,1,0:T(1,128)} %param.20) | copy-start | bytes 388
  126.3 10.7 %collective-permute-start.14 = (bf16[256,768]{1,0:T(8,128)(2,1)S(1)}, bf16[256,768]{1,0:T(8,128)(2,1)S(1)}, u32[]{:S(2)}, u32[]{:S(2)}) collective-permute-start(bf16[256,768]{1,0:T(8,128)(2,1)S(1)} %hop.9), channel_id=1, source_target_pairs={{0,7},{1,0},{2,1},{3,2},{4,3},{5,4},{6,5},{7,6},{8,15},{9,8},{10,9... | collective-permute-start | bytes 1179656 | tf_op jit(solution)/shard_map/ppermute | solution.py:293
  137.4 9.5 %copy-start.10 = (bf16[256,256]{1,0:T(8,128)(2,1)S(1)}, bf16[256,256]{1,0:T(8,128)(2,1)}, u32[]{:S(2)}) copy-start(bf16[256,256]{1,0:T(8,128)(2,1)} %weight_ref.1) | copy-start | bytes 393220
  137.4 9.5 %collective-permute-start.15 = (bf16[256,384]{1,0:T(8,128)(2,1)S(1)}, bf16[256,384]{1,0:T(8,128)(2,1)S(1)}, u32[]{:S(2)}, u32[]{:S(2)}) collective-permute-start(bf16[256,384]{1,0:T(8,128)(2,1)S(1)} %get-tuple-element.30), channel_id=1, source_target_pairs={{0,8},{1,9},{2,10},{3,11},{4,12},{5,13},{6,14},{7,15},{8,0},{9,1},... | collective-permute-start | bytes 589832 | tf_op jit(solution)/shard_map/ppermute | solution.py:296

commit v7 on v6

--- a/solution.py
+++ b/solution.py
@@ -98,11 +98,11 @@
 
 def spread_kernel(ring, blocks, pos_ref, count_ref, place_ref, tiles_ref, *outs):
     rows = blocks * TILE
-    place = place_ref[0]
+    place, mirrored = place_ref[0], place_ref[1]
     for offset in range(ring):
         dense = outs[offset]
         dense[...] = jnp.zeros(dense.shape, BF)
-        spot = lax.rem(place + offset, ring)
+        spot = lax.rem(place + jnp.where(mirrored > 0, ring - offset, offset), ring)
         for half in range(FAR):
             source = half * ring + spot
 
@@ -173,11 +173,13 @@
     far_mat_ref,
     near_mat_ref,
     cut_hbm,
-    hidden_ref,
-    grad_ref,
+    hidden_hbm,
+    grad_hbm,
     left_hbm,
     right_hbm,
     terms_hbm,
+    hidden,
+    gradient,
     messages,
     cut,
     terms,
@@ -193,10 +195,15 @@
         copy.start()
     total = sum_ref[...] + cut_sum_ref[...] + product(far_mat_ref[...], last_ref[...])
     activated, derivative = silu_parts(total + bias_ref[...])
-    hidden_ref[...] = activated.astype(BF)
+    hidden[...] = activated.astype(BF)
     grad = (cotangent_ref[...].astype(F32) * derivative).T.astype(BF)
-    grad_ref[...] = grad
-    stores = []
+    gradient[...] = grad
+    stores = [
+        pltpu.make_async_copy(hidden, hidden_hbm, sems.at[2 * chunks + 2]),
+        pltpu.make_async_copy(gradient, grad_hbm, sems.at[2 * chunks + 3]),
+    ]
+    for copy in stores:
+        copy.start()
     for place, (mat_ref, out_hbm) in enumerate(
         ((far_mat_ref, left_hbm), (near_mat_ref, right_hbm))
     ):
@@ -284,13 +291,16 @@
     send_to, is_live, dst = send_blk[0, 0], send_live[0, 0], recv_dst[0, 0]
     shape = jax.ShapeDtypeStruct
 
+    mirrored = lax.axis_index("dom") % 2
+
     def along_ring(value, by):
         moves = [
-            (side * ring + spot, side * ring + (spot + by) % ring)
-            for side in range(FAR)
+            (first + spot, first + (spot + (by if part % 2 == 0 else -by)) % ring)
+            for part in range(parts)
+            for first in range(part * peers, (part + 1) * peers, ring)
             for spot in range(ring)
         ]
-        return lax.ppermute(value, "blk", moves)
+        return lax.ppermute(value, ("dom", "blk"), moves)
 
     def across(value):
         return lax.ppermute(value, "blk", [(i, (i + ring) % peers) for i in range(peers)])
@@ -331,7 +341,7 @@
         [SMEM, SMEM, SMEM, VMEM],
         tuple([VMEM] * ring),
         moved=10 << 20,
-    )(in_pos[0, 0].reshape(-1), in_count[0, 0], place.reshape(1), in_tiles[0, 0])
+    )(in_pos[0, 0].reshape(-1), in_count[0, 0], jnp.stack([place, mirrored]), in_tiles[0, 0])
     dense_cut = call(
         spread_cut_kernel,
         "spread_cut",
@@ -372,16 +382,18 @@
     hidden, grad_pre, left, right, terms = call(
         middle_kernel,
         "middle",
-        (shape((rows, width), BF), shape((width, rows), BF))
+        (pltpu.HBM((rows, width), BF), pltpu.HBM((width, rows), BF))
         + (pltpu.HBM((width, wide), BF),) * 2
         + (pltpu.HBM((parts, width, TILE), BF),),
         [VMEM] * 7 + [HBM],
-        (VMEM,) * 2 + (HBM,) * 3,
+        (HBM,) * 5,
         [
+            pltpu.VMEM((rows, width), BF),
+            pltpu.VMEM((width, rows), BF),
             pltpu.VMEM((2, width, wide), BF),
             pltpu.VMEM(dense_cut.shape, BF),
             pltpu.VMEM((parts, width, TILE), BF),
-            pltpu.SemaphoreType.DMA((2 * chunks + 2,)),
+            pltpu.SemaphoreType.DMA((2 * chunks + 4,)),
         ],
     )(
         running,

time: 150 us -> 154 us (1.027)
  waiting for transfers between devices: 29 us -> 39.9 us
  starting transfers between devices: 87.5 us -> 83.6 us
  matrix products: 5.26 us -> 3.25 us
    ppermute x14, starting transfers between devices: 61.3 us -> 48.6 us  [along_ring(): return lax.ppermute(value, ('dom', 'blk'), moves)]
    all_to_all x1, starting transfers between devices: 8.61 us -> 17.4 us  [on_device(): lax.all_to_all(terms, 'dom', split_axis=0, concat_axis=0, tiled=True)]
    ppermute x14, waiting for transfers between devices: 24.6 us -> 33.2 us  [along_ring(): return lax.ppermute(value, ('dom', 'blk'), moves)]
    ppermute x2, waiting for transfers between devices: 0.75 us -> 3.45 us  [across(): lax.ppermute(value, 'blk', [(i, (i + ring) % peers) for i in range(peers)])]
    dot_general x7, matrix products: 5.26 us -> 3.25 us  [product(): return jnp.dot(left, right, preferred_element_type=F32)]
  transfers between devices with their start and end apart: 18 -> 18, of which waited for: 10 -> 13; matrix products, arithmetic and copies ran while one was open for 4% -> 2% of each run, Pallas kernels for 10% -> 10%
where the time goes in v7:
time: 154 us; the launch traced here: 153 us
  starting transfers between devices  83.6 us (54%)
  waiting for transfers between devices  39.9 us (26%)
  Pallas kernels  22.5 us (15%)
  matrix products  3.25 us (2%)
  local copies, waits for them, and re-layouts  2.39 us (2%)
    ppermute x14, starting transfers between devices, along_ring(): return lax.ppermute(value, ('dom', 'blk'), moves)  48.6 us
    ppermute x14, waiting for transfers between devices, along_ring(): return lax.ppermute(value, ('dom', 'blk'), moves)  33.2 us
    all_to_all x1, starting transfers between devices, on_device(): lax.all_to_all(terms, 'dom', split_axis=0, concat_axis=0, tiled=True)  17.4 us
    ppermute x2, starting transfers between devices, across(): lax.ppermute(value, 'blk', [(i, (i + ring) % peers) for i in range(peers)])  9.26 us
    all_to_all x1, starting transfers between devices, on_device(): lax.all_to_all(outgoing, 'dom', split_axis=0, concat_axis=0, tiled=True)  8.3 us
    pallas_call x1, Pallas kernels, on_device(): call(middle_kernel, 'middle', (pltpu.HBM((rows, width), BF), pltpu.HBM((w...  5.53 us
    ppermute x2, waiting for transfers between devices, across(): lax.ppermute(value, 'blk', [(i, (i + ring) % peers) for i in range(peers)])  3.45 us
    pallas_call x1, Pallas kernels, on_device(): call(cut_sum_kernel, 'cut_sum', shape((rows, width), F32), [HBM, HBM], VM...  3.34 us
  transfers between devices with their start and end apart: 18, of which 13 were waited for; matrix products, arithmetic and copies ran while one was open for 2% of the time, Pallas kernels for 10%

profile of v7, /device:TPU:1, one launch (start us, length us, event | category | flops | bytes accessed | tf_op | source)
XLA Modules:
  0.0 152.9 jit_solution(2684104490813709561)
XLA Ops:
  0.6 1.2 project.1.own_ref.projected_ref
  1.9 5.5 %collective-permute-start = (bf16[384,256]{1,0:T(8,128)(2,1)S(1)}, bf16[384,256]{1,0:T(8,128)(2,1)S(1)}, u32[]{:S(2)}, u32[]{:S(2)}) collective-permute-start(bf16[384,256]{1,0:T(8,128)(2,1)S(1)} %project.1.own_ref.projected_ref), channel_id=1, source_target_pairs={{0,8},{1,9},{2,10},{3,11},{4,12},{5,13},{6,14},{7,15},{8,0},{9,1},... | collective-permute-start | bytes 589832 | tf_op jit(solution)/shard_map/ppermute | solution.py:306
  7.4 2.3 %fill.1 = bf16[32,128,256]{2,1,0:T(8,128)(2,1)} custom-call(s32[32]{0:T(128)} %bitcast.28, s32[32]{0:T(128)} %bitcast.30, bf16[384,256]{1,0:T(8,128)(2,1)S(1)} %project.1.own_ref.projected_ref), custom_call_target="tpu_custom_call" | custom-call | tf_op jit(solution)/shard_map/fill/pallas_call | solution.py:321
  9.7 8.3 %all-to-all-start = ((bf16[32,128,256]{2,1,0:T(8,128)(2,1)}), bf16[32,128,256]{2,1,0:T(8,128)(2,1)}, u32[]{:S(2)}, u32[]{:S(2)}) async-start(bf16[32,128,256]{2,1,0:T(8,128)(2,1)} %fill.1), calls=%async_computation | async-start | bytes 4194304 | tf_op jit(solution)/shard_map/all_to_all | solution.py:335
  18.0 0.0 copy-start.18
  18.0 0.0 copy-start.8
  18.0 0.0 copy-start.16
  18.1 4.1 %collective-permute-start.2 = (bf16[768,256]{1,0:T(8,128)(2,1)S(1)}, bf16[768,256]{1,0:T(8,128)(2,1)S(1)}, u32[]{:S(2)}, u32[]{:S(2)}) collective-permute-start(bf16[768,256]{1,0:T(8,128)(2,1)S(1)} %pair.1), channel_id=1, source_target_pairs={{0,7},{1,0},{2,1},{3,2},{4,3},{5,4},{6,5},{7,6},{8,15},{9,8},{10,9... | collective-permute-start | bytes 1179656 | tf_op jit(solution)/shard_map/ppermute | solution.py:303
  22.2 8.6 %collective-permute-start.1 = (bf16[768,256]{1,0:T(8,128)(2,1)S(1)}, bf16[768,256]{1,0:T(8,128)(2,1)S(1)}, u32[]{:S(2)}, u32[]{:S(2)}) collective-permute-start(bf16[768,256]{1,0:T(8,128)(2,1)S(1)} %pair.1), channel_id=1, source_target_pairs={{0,1},{1,2},{2,3},{3,4},{4,5},{5,6},{6,7},{7,0},{8,9},{9,10},{10,1... | collective-permute-start | bytes 1179656 | tf_op jit(solution)/shard_map/ppermute | solution.py:303
  30.8 0.1 copy.14
  30.9 0.1 reshape_squeeze.3.refs_0_
  31.1 0.0 copy-start.7
  31.1 2.8 %spread_cut.1.cut_hbm = bf16[8,384,512]{2,1,0:T(8,128)(2,1)} custom-call(s32[32]{0:T(128)S(1)} %bitcast.33, bf16[32,128,128]{2,1,0:T(8,128)(2,1)S(1)} %bitcast.27), custom_call_target="tpu_custom_call" | custom-call | bytes 6291456 | tf_op jit(solution)/shard_map/spread_cut/pallas_call | solution.py:345
  33.8 0.1 pad_add_fusion.refs_2_
  33.9 1.8 %spread.1 = (bf16[384,768]{1,0:T(8,128)(2,1)S(1)}, bf16[384,768]{1,0:T(8,128)(2,1)S(1)}, bf16[384,768]{1,0:T(8,128)(2,1)S(1)}, bf16[384,768]{1,0:T(8,128)(2,1)S(...) custom-call(s32[64]{0:T(128)S(1)} %reshape_squeeze.3.refs_0_, ...), custom_call_target="tpu_custom_call" | custom-call | bytes 10485760 | tf_op jit(solution)/shard_map/spread/pallas_call | solution.py:337
  35.8 1.9 %collective-permute-start.4 = (bf16[768,256]{1,0:T(8,128)(2,1)S(1)}, bf16[768,256]{1,0:T(8,128)(2,1)S(1)}, u32[]{:S(2)}, u32[]{:S(2)}) collective-permute-start(bf16[768,256]{1,0:T(8,128)(2,1)S(1)} %collective-permute-done.2), channel_id=1, source_target_pairs={{0,7},{1,0},{2,1},{3,2},{4,3},{5,4},{6,5},{7,6},{8,15},{9,8},{10,9... | collective-permute-start | bytes 1179656 | tf_op jit(solution)/shard_map/ppermute | solution.py:303
  37.7 0.9 collective-permute-done.1
  38.6 5.3 %collective-permute-start.3 = (bf16[768,256]{1,0:T(8,128)(2,1)S(1)}, bf16[768,256]{1,0:T(8,128)(2,1)S(1)}, u32[]{:S(2)}, u32[]{:S(2)}) collective-permute-start(bf16[768,256]{1,0:T(8,128)(2,1)S(1)} %collective-permute-done.1), channel_id=1, source_target_pairs={{0,1},{1,2},{2,3},{3,4},{4,5},{5,6},{6,7},{7,0},{8,9},{9,10},{10,1... | collective-permute-start | bytes 1179656 | tf_op jit(solution)/shard_map/ppermute | solution.py:303
  43.8 0.3 fusion.3
  44.2 0.3 fusion.4
  44.5 0.3 fusion.2
  44.8 1.1 collective-permute-done.4
  45.9 1.9 %collective-permute-start.6 = (bf16[768,256]{1,0:T(8,128)(2,1)S(1)}, bf16[768,256]{1,0:T(8,128)(2,1)}, u32[]{:S(2)}, u32[]{:S(2)}) collective-permute-start(bf16[768,256]{1,0:T(8,128)(2,1)S(1)} %collective-permute-done.4), channel_id=1, source_target_pairs={{0,7},{1,0},{2,1},{3,2},{4,3},{5,4},{6,5},{7,6},{8,15},{9,8},{10,9... | collective-permute-start | bytes 1179656 | tf_op jit(solution)/shard_map/ppermute | solution.py:303
  47.8 4.7 %collective-permute-done.3 = bf16[768,256]{1,0:T(8,128)(2,1)S(1)} collective-permute-done((bf16[768,256]{1,0:T(8,128)(2,1)S(1)}, bf16[768,256]{1,0:T(8,128)(2,1)S(1)}, u32[]{:S(2)}, u32[]{:S(2)}) %collective-permute-start.3) | collective-permute-done | bytes 393248 | tf_op jit(solution)/shard_map/ppermute | solution.py:303
  52.5 5.4 %collective-permute-start.5 = (bf16[768,256]{1,0:T(8,128)(2,1)S(1)}, bf16[768,256]{1,0:T(8,128)(2,1)S(1)}, u32[]{:S(2)}, u32[]{:S(2)}) collective-permute-start(bf16[768,256]{1,0:T(8,128)(2,1)S(1)} %collective-permute-done.3), channel_id=1, source_target_pairs={{0,1},{1,2},{2,3},{3,4},{4,5},{5,6},{6,7},{7,0},{8,9},{9,10},{10,1... | collective-permute-start | bytes 1179656 | tf_op jit(solution)/shard_map/ppermute | solution.py:303
  57.9 0.3 fusion.5
  58.2 0.3 fusion.1
  58.6 1.9 %collective-permute-start.7 = (bf16[768,256]{1,0:T(8,128)(2,1)}, bf16[768,256]{1,0:T(8,128)(2,1)S(1)}, u32[]{:S(2)}, u32[]{:S(2)}) collective-permute-start(bf16[768,256]{1,0:T(8,128)(2,1)} %collective-permute-done.6), channel_id=1, source_target_pairs={{0,7},{1,0},{2,1},{3,2},{4,3},{5,4},{6,5},{7,6},{8,15},{9,8},{10,9... | collective-permute-start | bytes 1179656 | tf_op jit(solution)/shard_map/ppermute | solution.py:303
  60.5 1.3 fusion.6
  61.8 4.6 %collective-permute-done.5 = bf16[768,256]{1,0:T(8,128)(2,1)S(1)} collective-permute-done((bf16[768,256]{1,0:T(8,128)(2,1)S(1)}, bf16[768,256]{1,0:T(8,128)(2,1)S(1)}, u32[]{:S(2)}, u32[]{:S(2)}) %collective-permute-start.5) | collective-permute-done | bytes 393248 | tf_op jit(solution)/shard_map/ppermute | solution.py:303
  66.4 0.3 fusion.sum_ref
  66.8 0.0 copy-start.15
  66.8 0.7 all-to-all-done.far_hbm
  67.4 3.3 %cut_sum.1.cut_sum_ref = f32[384,256]{1,0:T(8,128)S(1)} custom-call(bf16[8,384,512]{2,1,0:T(8,128)(2,1)} %spread_cut.1.cut_hbm, bf16[32,128,256]{2,1,0:T(8,128)(2,1)} %all-to-all-done.far_hbm), custom_call_target="tpu_custom_call" | custom-call | flops 2000000000 | tf_op jit(solution)/shard_map/cut_sum/pallas_call | solution.py:368
  70.8 2.0 %collective-permute-done.7.last_ref = bf16[768,256]{1,0:T(8,128)(2,1)S(1)} collective-permute-done((bf16[768,256]{1,0:T(8,128)(2,1)}, bf16[768,256]{1,0:T(8,128)(2,1)S(1)}, u32[]{:S(2)}, u32[]{:S(2)}) %collective-permute-start.7) | collective-permute-done | bytes 393248 | tf_op jit(solution)/shard_map/ppermute | solution.py:303
  72.7 5.5 %middle.1 = (bf16[384,256]{1,0:T(8,128)(2,1)}, bf16[256,384]{1,0:T(8,128)(2,1)}, bf16[256,768]{1,0:T(8,128)(2,1)}, bf16[256,768]{1,0:T(8,128)(2,1)}, bf16[32,256,128]{2,1,0:T(8,128)(2,1)}) custom-call(f32[384,256]{1,0:T(8,128)S(1)} %fusion.sum_ref, f32[384,256]{1,0:T(8,128)S(1)} %cut_sum.1.cut_sum_ref, bf16[768,256]{1,0:T(8,128)(2,1)S(1)} %collective-permute-done.7.last_ref, ...), custom_call_target="tpu_custom_call" | custom-call | tf_op jit(solution)/shard_map/middle/pallas_call | solution.py:382
  78.3 2.1 %collective-permute-start.11 = (bf16[256,768]{1,0:T(8,128)(2,1)}, bf16[256,768]{1,0:T(8,128)(2,1)}, u32[]{:S(2)}, u32[]{:S(2)}) collective-permute-start(bf16[256,768]{1,0:T(8,128)(2,1)} %get-tuple-element.28), channel_id=1, source_target_pairs={{0,7},{1,0},{2,1},{3,2},{4,3},{5,4},{6,5},{7,6},{8,15},{9,8},{10,9... | collective-permute-start | bytes 1179656 | tf_op jit(solution)/shard_map/ppermute | solution.py:303
  80.4 0.0 copy-start
  80.4 17.4 %all-to-all-start.1 = ((bf16[32,256,128]{2,1,0:T(8,128)(2,1)}), bf16[32,256,128]{2,1,0:T(8,128)(2,1)S(1)}, u32[]{:S(2)}, u32[]{:S(2)}) async-start(bf16[32,256,128]{2,1,0:T(8,128)(2,1)} %get-tuple-element.31), calls=%async_computation.1 | async-start | bytes 4194304 | tf_op jit(solution)/shard_map/all_to_all | solution.py:415
  97.8 2.1 %collective-permute-start.8 = (bf16[256,768]{1,0:T(8,128)(2,1)}, bf16[256,768]{1,0:T(8,128)(2,1)S(1)}, u32[]{:S(2)}, u32[]{:S(2)}) collective-permute-start(bf16[256,768]{1,0:T(8,128)(2,1)} %get-tuple-element.27), channel_id=1, source_target_pairs={{0,1},{1,2},{2,3},{3,4},{4,5},{5,6},{6,7},{7,0},{8,9},{9,10},{10,1... | collective-permute-start | bytes 1179656 | tf_op jit(solution)/shard_map/ppermute | solution.py:303
  99.9 1.1 copy-done.6
  100.9 1.4 hop.7
  102.3 3.4 %collective-permute-start.12 = (bf16[256,768]{1,0:T(8,128)(2,1)S(1)}, bf16[256,768]{1,0:T(8,128)(2,1)S(1)}, u32[]{:S(2)}, u32[]{:S(2)}) collective-permute-start(bf16[256,768]{1,0:T(8,128)(2,1)S(1)} %hop.7), channel_id=1, source_target_pairs={{0,7},{1,0},{2,1},{3,2},{4,3},{5,4},{6,5},{7,6},{8,15},{9,8},{10,9... | collective-permute-start | bytes 1179656 | tf_op jit(solution)/shard_map/ppermute | solution.py:303
  105.7 1.3 collective-permute-done.8.arrived_ref
  106.9 1.1 copy-done.4
  108.0 0.4 hop.5
  108.4 3.3 %collective-permute-start.9 = (bf16[256,768]{1,0:T(8,128)(2,1)S(1)}, bf16[256,768]{1,0:T(8,128)(2,1)S(1)}, u32[]{:S(2)}, u32[]{:S(2)}) collective-permute-start(bf16[256,768]{1,0:T(8,128)(2,1)S(1)} %hop.5), channel_id=1, source_target_pairs={{0,1},{1,2},{2,3},{3,4},{4,5},{5,6},{6,7},{7,0},{8,9},{9,10},{10,1... | collective-permute-start | bytes 1179656 | tf_op jit(solution)/shard_map/ppermute | solution.py:303
  111.6 1.2 collective-permute-done.12.arrived_ref
  112.9 0.4 hop.8
  113.3 1.9 %collective-permute-start.13 = (bf16[256,768]{1,0:T(8,128)(2,1)S(1)}, bf16[256,768]{1,0:T(8,128)(2,1)S(1)}, u32[]{:S(2)}, u32[]{:S(2)}) collective-permute-start(bf16[256,768]{1,0:T(8,128)(2,1)S(1)} %hop.8), channel_id=1, source_target_pairs={{0,7},{1,0},{2,1},{3,2},{4,3},{5,4},{6,5},{7,6},{8,15},{9,8},{10,9... | collective-permute-start | bytes 1179656 | tf_op jit(solution)/shard_map/ppermute | solution.py:303
  115.2 2.0 %collective-permute-done.9.arrived_ref = bf16[256,768]{1,0:T(8,128)(2,1)S(1)} collective-permute-done((bf16[256,768]{1,0:T(8,128)(2,1)S(1)}, bf16[256,768]{1,0:T(8,128)(2,1)S(1)}, u32[]{:S(2)}, u32[]{:S(2)}) %collective-permute-start.9) | collective-permute-done | bytes 393248 | tf_op jit(solution)/shard_map/ppermute | solution.py:303
  117.2 0.4 hop.6
  117.6 4.9 %collective-permute-start.10 = (bf16[256,768]{1,0:T(8,128)(2,1)S(1)}, bf16[256,768]{1,0:T(8,128)(2,1)S(1)}, u32[]{:S(2)}, u32[]{:S(2)}) collective-permute-start(bf16[256,768]{1,0:T(8,128)(2,1)S(1)} %hop.6), channel_id=1, source_target_pairs={{0,1},{1,2},{2,3},{3,4},{4,5},{5,6},{6,7},{7,0},{8,9},{9,10},{10,1... | collective-permute-start | bytes 1179656 | tf_op jit(solution)/shard_map/ppermute | solution.py:303
  122.5 3.7 %collective-permute-done.13.arrived_ref = bf16[256,768]{1,0:T(8,128)(2,1)S(1)} collective-permute-done((bf16[256,768]{1,0:T(8,128)(2,1)S(1)}, bf16[256,768]{1,0:T(8,128)(2,1)S(1)}, u32[]{:S(2)}, u32[]{:S(2)}) %collective-permute-start.13) | collective-permute-done | bytes 393248 | tf_op jit(solution)/shard_map/ppermute | solution.py:303
  126.2 0.4 hop.9
  126.6 1.9 %collective-permute-start.14 = (bf16[256,768]{1,0:T(8,128)(2,1)S(1)}, bf16[256,768]{1,0:T(8,128)(2,1)S(1)}, u32[]{:S(2)}, u32[]{:S(2)}) collective-permute-start(bf16[256,768]{1,0:T(8,128)(2,1)S(1)} %hop.9), channel_id=1, source_target_pairs={{0,7},{1,0},{2,1},{3,2},{4,3},{5,4},{6,5},{7,6},{8,15},{9,8},{10,9... | collective-permute-start | bytes 1179656 | tf_op jit(solution)/shard_map/ppermute | solution.py:303
  128.5 11.8 %collective-permute-done.14.right_ref = bf16[256,768]{1,0:T(8,128)(2,1)S(1)} collective-permute-done((bf16[256,768]{1,0:T(8,128)(2,1)S(1)}, bf16[256,768]{1,0:T(8,128)(2,1)S(1)}, u32[]{:S(2)}, u32[]{:S(2)}) %collective-permute-start.14) | collective-permute-done | bytes 393248 | tf_op jit(solution)/shard_map/ppermute | solution.py:303
  140.3 0.4 close.1
  140.7 0.0 copy-start.11
  140.7 3.8 %collective-permute-start.15 = (bf16[256,384]{1,0:T(8,128)(2,1)S(1)}, bf16[256,384]{1,0:T(8,128)(2,1)S(1)}, u32[]{:S(2)}, u32[]{:S(2)}) collective-permute-start(bf16[256,384]{1,0:T(8,128)(2,1)S(1)} %get-tuple-element.30), channel_id=1, source_target_pairs={{0,8},{1,9},{2,10},{3,11},{4,12},{5,13},{6,14},{7,15},{8,0},{9,1},... | collective-permute-start | bytes 589832 | tf_op jit(solution)/shard_map/ppermute | solution.py:306
  144.5 2.7 %all-to-all-done.1.arrived_ref = bf16[32,256,128]{2,1,0:T(8,128)(2,1)S(1)} async-done(((bf16[32,256,128]{2,1,0:T(8,128)(2,1)}), bf16[32,256,128]{2,1,0:T(8,128)(2,1)S(1)}, u32[]{:S(2)}, u32[]{:S(2)}) %all-to-all-start.1) | async-done | bytes 2097184 | tf_op jit(solution)/shard_map/all_to_all | solution.py:415
  147.2 1.3 gather.1.cut_ref
  148.5 3.4 %collective-permute-done.15.other_ref = bf16[256,384]{1,0:T(8,128)(2,1)S(1)} collective-permute-done((bf16[256,384]{1,0:T(8,128)(2,1)S(1)}, bf16[256,384]{1,0:T(8,128)(2,1)S(1)}, u32[]{:S(2)}, u32[]{:S(2)}) %collective-permute-start.15) | collective-permute-done | bytes 196640 | tf_op jit(solution)/shard_map/ppermute | solution.py:306
  151.9 1.0 last.1
  (35 shorter events, 0.1 us)
Async XLA Ops:
  1.9 16.1 %collective-permute-start = (bf16[384,256]{1,0:T(8,128)(2,1)S(1)}, bf16[384,256]{1,0:T(8,128)(2,1)S(1)}, u32[]{:S(2)}, u32[]{:S(2)}) collective-permute-start(bf16[384,256]{1,0:T(8,128)(2,1)S(1)} %project.1.own_ref.projected_ref), channel_id=1, source_target_pairs={{0,8},{1,9},{2,10},{3,11},{4,12},{5,13},{6,14},{7,15},{8,0},{9,1},... | collective-permute-start | bytes 589832 | tf_op jit(solution)/shard_map/ppermute | solution.py:306
  9.7 57.8 %all-to-all-start = ((bf16[32,128,256]{2,1,0:T(8,128)(2,1)}), bf16[32,128,256]{2,1,0:T(8,128)(2,1)}, u32[]{:S(2)}, u32[]{:S(2)}) async-start(bf16[32,128,256]{2,1,0:T(8,128)(2,1)} %fill.1), calls=%async_computation | async-start | bytes 4194304 | tf_op jit(solution)/shard_map/all_to_all | solution.py:335
  18.0 12.8 %copy-start.18 = (s32[1,1,16,4]{2,3,1,0:T(4,128)S(1)}, s32[1,1,16,4]{2,3,1,0:T(4,128)}, u32[]{:S(2)}) copy-start(s32[1,1,16,4]{2,3,1,0:T(4,128)} %param.16) | copy-start | bytes 772
  18.0 13.0 %copy-start.8 = (bf16[1,1,32,128,128]{4,3,2,1,0:T(8,128)(2,1)S(1)}, bf16[1,1,32,128,128]{4,3,2,1,0:T(8,128)(2,1)}, u32[]{:S(2)}) copy-start(bf16[1,1,32,128,128]{4,3,2,1,0:T(8,128)(2,1)} %param.18) | copy-start | bytes 3145732
  18.0 13.0 %copy-start.16 = (s32[1,1,32]{2,1,0:T(1,128)S(1)}, s32[1,1,32]{2,1,0:T(1,128)}, u32[]{:S(2)}) copy-start(s32[1,1,32]{2,1,0:T(1,128)} %param.21) | copy-start | bytes 388
  18.1 17.7 %collective-permute-start.2 = (bf16[768,256]{1,0:T(8,128)(2,1)S(1)}, bf16[768,256]{1,0:T(8,128)(2,1)S(1)}, u32[]{:S(2)}, u32[]{:S(2)}) collective-permute-start(bf16[768,256]{1,0:T(8,128)(2,1)S(1)} %pair.1), channel_id=1, source_target_pairs={{0,7},{1,0},{2,1},{3,2},{4,3},{5,4},{6,5},{7,6},{8,15},{9,8},{10,9... | collective-permute-start | bytes 1179656 | tf_op jit(solution)/shard_map/ppermute | solution.py:303
  22.2 16.3 %collective-permute-start.1 = (bf16[768,256]{1,0:T(8,128)(2,1)S(1)}, bf16[768,256]{1,0:T(8,128)(2,1)S(1)}, u32[]{:S(2)}, u32[]{:S(2)}) collective-permute-start(bf16[768,256]{1,0:T(8,128)(2,1)S(1)} %pair.1), channel_id=1, source_target_pairs={{0,1},{1,2},{2,3},{3,4},{4,5},{5,6},{6,7},{7,0},{8,9},{9,10},{10,1... | collective-permute-start | bytes 1179656 | tf_op jit(solution)/shard_map/ppermute | solution.py:303
  31.1 2.9 %copy-start.7 = (bf16[1,1,16,4,128,128]{5,4,3,2,1,0:T(8,128)(2,1)S(1)}, bf16[1,1,16,4,128,128]{5,4,3,2,1,0:T(8,128)(2,1)}, u32[]{:S(2)}) copy-start(bf16[1,1,16,4,128,128]{5,4,3,2,1,0:T(8,128)(2,1)} %param.15) | copy-start | bytes 6291460
  31.1 2.9 %copy-start.17 = (s32[1,1,16]{2,1,0:T(1,128)S(1)}, s32[1,1,16]{2,1,0:T(1,128)}, u32[]{:S(2)}) copy-start(s32[1,1,16]{2,1,0:T(1,128)} %param.17) | copy-start | bytes 196
  35.7 9.1 %copy-start.9 = (bf16[384,768]{1,0:T(8,128)(2,1)}, bf16[384,768]{1,0:T(8,128)(2,1)S(1)}, u32[]{:S(2)}) copy-start(bf16[384,768]{1,0:T(8,128)(2,1)S(1)} %get-tuple-element.17.mat_ref) | copy-start | bytes 1769476
  35.7 22.2 %copy-start.3 = (bf16[384,768]{1,0:T(8,128)(2,1)}, bf16[384,768]{1,0:T(8,128)(2,1)S(1)}, u32[]{:S(2)}) copy-start(bf16[384,768]{1,0:T(8,128)(2,1)S(1)} %get-tuple-element.21.mat_ref) | copy-start | bytes 1769476
  35.7 22.5 %copy-start.1 = (bf16[384,768]{1,0:T(8,128)(2,1)}, bf16[384,768]{1,0:T(8,128)(2,1)S(1)}, u32[]{:S(2)}) copy-start(bf16[384,768]{1,0:T(8,128)(2,1)S(1)} %get-tuple-element.20.mat_ref) | copy-start | bytes 1769476
  35.7 30.7 %copy-start.5 = (bf16[384,768]{1,0:T(8,128)(2,1)}, bf16[384,768]{1,0:T(8,128)(2,1)S(1)}, u32[]{:S(2)}) copy-start(bf16[384,768]{1,0:T(8,128)(2,1)S(1)} %get-tuple-element.22.mat_ref) | copy-start | bytes 1769476
  35.8 10.1 %collective-permute-start.4 = (bf16[768,256]{1,0:T(8,128)(2,1)S(1)}, bf16[768,256]{1,0:T(8,128)(2,1)S(1)}, u32[]{:S(2)}, u32[]{:S(2)}) collective-permute-start(bf16[768,256]{1,0:T(8,128)(2,1)S(1)} %collective-permute-done.2), channel_id=1, source_target_pairs={{0,7},{1,0},{2,1},{3,2},{4,3},{5,4},{6,5},{7,6},{8,15},{9,8},{10,9... | collective-permute-start | bytes 1179656 | tf_op jit(solution)/shard_map/ppermute | solution.py:303
  38.6 13.9 %collective-permute-start.3 = (bf16[768,256]{1,0:T(8,128)(2,1)S(1)}, bf16[768,256]{1,0:T(8,128)(2,1)S(1)}, u32[]{:S(2)}, u32[]{:S(2)}) collective-permute-start(bf16[768,256]{1,0:T(8,128)(2,1)S(1)} %collective-permute-done.1), channel_id=1, source_target_pairs={{0,1},{1,2},{2,3},{3,4},{4,5},{5,6},{6,7},{7,0},{8,9},{9,10},{10,1... | collective-permute-start | bytes 1179656 | tf_op jit(solution)/shard_map/ppermute | solution.py:303
  45.9 12.7 %collective-permute-start.6 = (bf16[768,256]{1,0:T(8,128)(2,1)S(1)}, bf16[768,256]{1,0:T(8,128)(2,1)}, u32[]{:S(2)}, u32[]{:S(2)}) collective-permute-start(bf16[768,256]{1,0:T(8,128)(2,1)S(1)} %collective-permute-done.4), channel_id=1, source_target_pairs={{0,7},{1,0},{2,1},{3,2},{4,3},{5,4},{6,5},{7,6},{8,15},{9,8},{10,9... | collective-permute-start | bytes 1179656 | tf_op jit(solution)/shard_map/ppermute | solution.py:303
  52.5 13.9 %collective-permute-start.5 = (bf16[768,256]{1,0:T(8,128)(2,1)S(1)}, bf16[768,256]{1,0:T(8,128)(2,1)S(1)}, u32[]{:S(2)}, u32[]{:S(2)}) collective-permute-start(bf16[768,256]{1,0:T(8,128)(2,1)S(1)} %collective-permute-done.3), channel_id=1, source_target_pairs={{0,1},{1,2},{2,3},{3,4},{4,5},{5,6},{6,7},{7,0},{8,9},{9,10},{10,1... | collective-permute-start | bytes 1179656 | tf_op jit(solution)/shard_map/ppermute | solution.py:303
  58.6 14.2 %collective-permute-start.7 = (bf16[768,256]{1,0:T(8,128)(2,1)}, bf16[768,256]{1,0:T(8,128)(2,1)S(1)}, u32[]{:S(2)}, u32[]{:S(2)}) collective-permute-start(bf16[768,256]{1,0:T(8,128)(2,1)} %collective-permute-done.6), channel_id=1, source_target_pairs={{0,7},{1,0},{2,1},{3,2},{4,3},{5,4},{6,5},{7,6},{8,15},{9,8},{10,9... | collective-permute-start | bytes 1179656 | tf_op jit(solution)/shard_map/ppermute | solution.py:303
  66.7 6.0 %copy-start.12 = (bf16[384,256]{1,0:T(8,128)(2,1)S(1)}, bf16[384,256]{1,0:T(8,128)(2,1)}, u32[]{:S(2)}) copy-start(bf16[384,256]{1,0:T(8,128)(2,1)} %cotangent_ref.1) | copy-start | bytes 589828
  66.8 6.0 %copy-start.15 = (f32[256]{0:T(256)S(1)}, f32[256]{0:T(256)}, u32[]{:S(2)}) copy-start(f32[256]{0:T(256)} %param.13) | copy-start | bytes 3076
  78.3 21.6 %collective-permute-start.11 = (bf16[256,768]{1,0:T(8,128)(2,1)}, bf16[256,768]{1,0:T(8,128)(2,1)}, u32[]{:S(2)}, u32[]{:S(2)}) collective-permute-start(bf16[256,768]{1,0:T(8,128)(2,1)} %get-tuple-element.28), channel_id=1, source_target_pairs={{0,7},{1,0},{2,1},{3,2},{4,3},{5,4},{6,5},{7,6},{8,15},{9,8},{10,9... | collective-permute-start | bytes 1179656 | tf_op jit(solution)/shard_map/ppermute | solution.py:303
  80.4 19.5 %copy-start = (bf16[256,384]{1,0:T(8,128)(2,1)S(1)}, bf16[256,384]{1,0:T(8,128)(2,1)}, u32[]{:S(2)}) copy-start(bf16[256,384]{1,0:T(8,128)(2,1)} %get-tuple-element.26.grad_ref) | copy-start | bytes 589828
  80.4 66.8 %all-to-all-start.1 = ((bf16[32,256,128]{2,1,0:T(8,128)(2,1)}), bf16[32,256,128]{2,1,0:T(8,128)(2,1)S(1)}, u32[]{:S(2)}, u32[]{:S(2)}) async-start(bf16[32,256,128]{2,1,0:T(8,128)(2,1)} %get-tuple-element.31), calls=%async_computation.1 | async-start | bytes 4194304 | tf_op jit(solution)/shard_map/all_to_all | solution.py:415
  97.8 15.1 %copy-start.2 = (bf16[384,768]{1,0:T(8,128)(2,1)S(1)}, bf16[384,768]{1,0:T(8,128)(2,1)}, u32[]{:S(2)}) copy-start(bf16[384,768]{1,0:T(8,128)(2,1)} %copy-done.1) | copy-start | bytes 1769476
  97.8 9.2 %collective-permute-start.8 = (bf16[256,768]{1,0:T(8,128)(2,1)}, bf16[256,768]{1,0:T(8,128)(2,1)S(1)}, u32[]{:S(2)}, u32[]{:S(2)}) collective-permute-start(bf16[256,768]{1,0:T(8,128)(2,1)} %get-tuple-element.27), channel_id=1, source_target_pairs={{0,1},{1,2},{2,3},{3,4},{4,5},{5,6},{6,7},{7,0},{8,9},{9,10},{10,1... | collective-permute-start | bytes 1179656 | tf_op jit(solution)/shard_map/ppermute | solution.py:303
  99.9 1.1 copy-start.6
  102.3 10.6 %collective-permute-start.12 = (bf16[256,768]{1,0:T(8,128)(2,1)S(1)}, bf16[256,768]{1,0:T(8,128)(2,1)S(1)}, u32[]{:S(2)}, u32[]{:S(2)}) collective-permute-start(bf16[256,768]{1,0:T(8,128)(2,1)S(1)} %hop.7), channel_id=1, source_target_pairs={{0,7},{1,0},{2,1},{3,2},{4,3},{5,4},{6,5},{7,6},{8,15},{9,8},{10,9... | collective-permute-start | bytes 1179656 | tf_op jit(solution)/shard_map/ppermute | solution.py:303
  106.9 1.1 copy-start.4
  108.4 31.9 %copy-start.10 = (bf16[384,768]{1,0:T(8,128)(2,1)S(1)}, bf16[384,768]{1,0:T(8,128)(2,1)}, u32[]{:S(2)}) copy-start(bf16[384,768]{1,0:T(8,128)(2,1)} %copy-done.9) | copy-start | bytes 1769476
  108.4 8.8 %collective-permute-start.9 = (bf16[256,768]{1,0:T(8,128)(2,1)S(1)}, bf16[256,768]{1,0:T(8,128)(2,1)S(1)}, u32[]{:S(2)}, u32[]{:S(2)}) collective-permute-start(bf16[256,768]{1,0:T(8,128)(2,1)S(1)} %hop.5), channel_id=1, source_target_pairs={{0,1},{1,2},{2,3},{3,4},{4,5},{5,6},{6,7},{7,0},{8,9},{9,10},{10,1... | collective-permute-start | bytes 1179656 | tf_op jit(solution)/shard_map/ppermute | solution.py:303
  113.3 12.9 %collective-permute-start.13 = (bf16[256,768]{1,0:T(8,128)(2,1)S(1)}, bf16[256,768]{1,0:T(8,128)(2,1)S(1)}, u32[]{:S(2)}, u32[]{:S(2)}) collective-permute-start(bf16[256,768]{1,0:T(8,128)(2,1)S(1)} %hop.8), channel_id=1, source_target_pairs={{0,7},{1,0},{2,1},{3,2},{4,3},{5,4},{6,5},{7,6},{8,15},{9,8},{10,9... | collective-permute-start | bytes 1179656 | tf_op jit(solution)/shard_map/ppermute | solution.py:303
  117.6 10.9 %collective-permute-start.10 = (bf16[256,768]{1,0:T(8,128)(2,1)S(1)}, bf16[256,768]{1,0:T(8,128)(2,1)S(1)}, u32[]{:S(2)}, u32[]{:S(2)}) collective-permute-start(bf16[256,768]{1,0:T(8,128)(2,1)S(1)} %hop.6), channel_id=1, source_target_pairs={{0,1},{1,2},{2,3},{3,4},{4,5},{5,6},{6,7},{7,0},{8,9},{9,10},{10,1... | collective-permute-start | bytes 1179656 | tf_op jit(solution)/shard_map/ppermute | solution.py:303
  126.6 20.6 %copy-start.13 = (s32[1,1,32]{2,1,0:T(1,128)S(1)}, s32[1,1,32]{2,1,0:T(1,128)}, u32[]{:S(2)}) copy-start(s32[1,1,32]{2,1,0:T(1,128)} %param.19) | copy-start | bytes 388
  126.6 20.6 %copy-start.14 = (s32[1,1,32]{2,1,0:T(1,128)S(1)}, s32[1,1,32]{2,1,0:T(1,128)}, u32[]{:S(2)}) copy-start(s32[1,1,32]{2,1,0:T(1,128)} %param.20) | copy-start | bytes 388
  126.6 13.7 %collective-permute-start.14 = (bf16[256,768]{1,0:T(8,128)(2,1)S(1)}, bf16[256,768]{1,0:T(8,128)(2,1)S(1)}, u32[]{:S(2)}, u32[]{:S(2)}) collective-permute-start(bf16[256,768]{1,0:T(8,128)(2,1)S(1)} %hop.9), channel_id=1, source_target_pairs={{0,7},{1,0},{2,1},{3,2},{4,3},{5,4},{6,5},{7,6},{8,15},{9,8},{10,9... | collective-permute-start | bytes 1179656 | tf_op jit(solution)/shard_map/ppermute | solution.py:303
  140.7 11.3 %copy-start.11 = (bf16[256,256]{1,0:T(8,128)(2,1)S(1)}, bf16[256,256]{1,0:T(8,128)(2,1)}, u32[]{:S(2)}) copy-start(bf16[256,256]{1,0:T(8,128)(2,1)} %weight_ref.1) | copy-start | bytes 393220
  140.7 11.2 %collective-permute-start.15 = (bf16[256,384]{1,0:T(8,128)(2,1)S(1)}, bf16[256,384]{1,0:T(8,128)(2,1)S(1)}, u32[]{:S(2)}, u32[]{:S(2)}) collective-permute-start(bf16[256,384]{1,0:T(8,128)(2,1)S(1)} %get-tuple-element.30), channel_id=1, source_target_pairs={{0,8},{1,9},{2,10},{3,11},{4,12},{5,13},{6,14},{7,15},{8,0},{9,1},... | collective-permute-start | bytes 589832 | tf_op jit(solution)/shard_map/ppermute | solution.py:306

commit v8 on v6

--- a/solution.py
+++ b/solution.py
@@ -10,7 +10,6 @@
 FAR = 2
 CHUNKS = 8
 VMEM_LIMIT = 16 * 1024 * 1024
-PAIR_COST = 100_000_000_000
 CLOSE_COST = 26_500_000_000
 CUT_COST = 2_000_000_000
 
@@ -98,13 +97,13 @@
 
 def spread_kernel(ring, blocks, pos_ref, count_ref, place_ref, tiles_ref, *outs):
     rows = blocks * TILE
-    place = place_ref[0]
+    place, mine = place_ref[0], place_ref[1]
     for offset in range(ring):
         dense = outs[offset]
         dense[...] = jnp.zeros(dense.shape, BF)
         spot = lax.rem(place + offset, ring)
         for half in range(FAR):
-            source = half * ring + spot
+            source = (mine if half == 0 else 1 - mine) * ring + spot
 
             def put(slot, carried, dense=dense, half=half, source=source):
                 position = pos_ref[source * tiles_ref.shape[1] + slot]
@@ -131,13 +130,6 @@
     copy = pltpu.make_async_copy(dense, dense_hbm, sem)
     copy.start()
     copy.wait()
-
-
-def pair_kernel(half_ref, own_ref, other_ref, pair_ref):
-    rows = own_ref.shape[0]
-    place = pl.multiple_of(half_ref[0] * rows, TILE)
-    pair_ref[pl.ds(place, rows)] = own_ref[...]
-    pair_ref[pl.ds(pl.multiple_of(rows - place, TILE), rows)] = other_ref[...]
 
 
 def cut_sum_kernel(cut_hbm, far_hbm, total_ref, cut, far, sems):
@@ -167,7 +159,8 @@
 def middle_kernel(
     sum_ref,
     cut_sum_ref,
-    last_ref,
+    own_hbm,
+    other_hbm,
     bias_ref,
     cotangent_ref,
     far_mat_ref,
@@ -178,6 +171,7 @@
     left_hbm,
     right_hbm,
     terms_hbm,
+    arrived,
     messages,
     cut,
     terms,
@@ -185,13 +179,24 @@
 ):
     chunks = cut.shape[0]
     chunk = terms.shape[0] // chunks
+    last = [
+        pltpu.make_async_copy(source, arrived.at[place], sems.at[2 * chunks + 2 + place])
+        for place, source in enumerate((own_hbm, other_hbm))
+    ]
+    for copy in last:
+        copy.start()
     loads = [
         pltpu.make_async_copy(cut_hbm.at[piece], cut.at[piece], sems.at[piece])
         for piece in range(chunks)
     ]
     for copy in loads:
         copy.start()
-    total = sum_ref[...] + cut_sum_ref[...] + product(far_mat_ref[...], last_ref[...])
+    rows = sum_ref.shape[0]
+    total = sum_ref[...] + cut_sum_ref[...]
+    for place, copy in enumerate(last):
+        copy.wait()
+        columns = pl.ds(place * rows, rows)
+        total += product(far_mat_ref[:, columns], arrived[place])
     activated, derivative = silu_parts(total + bias_ref[...])
     hidden_ref[...] = activated.astype(BF)
     grad = (cotangent_ref[...].astype(F32) * derivative).T.astype(BF)
@@ -238,17 +243,15 @@
     out_ref[...] = term.astype(BF)
 
 
-def close_kernel(half_ref, grad_ref, mat_ref, left_ref, right_ref, own_ref, other_ref):
+def close_kernel(grad_ref, mat_ref, left_ref, right_ref, own_ref, other_ref):
     rows = grad_ref.shape[1]
-    mine = pl.ds(pl.multiple_of(half_ref[0] * rows, TILE), rows)
-    theirs = pl.ds(pl.multiple_of((1 - half_ref[0]) * rows, TILE), rows)
 
     def total(columns):
         arrived = left_ref[:, columns].astype(F32) + right_ref[:, columns].astype(F32)
         return product(grad_ref[...], mat_ref[:, columns]) + arrived
 
-    other_ref[...] = total(theirs).astype(BF)
-    own_ref[...] = total(mine)
+    other_ref[...] = total(slice(rows, None)).astype(BF)
+    own_ref[...] = total(slice(0, rows))
 
 
 def last_kernel(own_ref, other_ref, cut_ref, weight_ref, out_ref):
@@ -331,7 +334,7 @@
         [SMEM, SMEM, SMEM, VMEM],
         tuple([VMEM] * ring),
         moved=10 << 20,
-    )(in_pos[0, 0].reshape(-1), in_count[0, 0], place.reshape(1), in_tiles[0, 0])
+    )(in_pos[0, 0].reshape(-1), in_count[0, 0], jnp.stack([place, half]), in_tiles[0, 0])
     dense_cut = call(
         spread_cut_kernel,
         "spread_cut",
@@ -345,16 +348,16 @@
         moved=6 << 20,
     )(dst, cut_tiles[0, 0])
 
-    pair = call(
-        pair_kernel, "pair", shape((wide, width), BF), [SMEM, VMEM, VMEM], VMEM, flops=PAIR_COST
-    )(half.reshape(1), projected, partner)
-    running = product(dense[0], pair)
-    right = left = pair
-    for hop in range(1, reach):
-        right, left = along_ring(right, 1), along_ring(left, -1)
-        running = running + product(dense[ring - hop], right)
-        running = running + product(dense[hop], left)
-    left = along_ring(left, -1)
+    running = jnp.zeros((rows, width), F32)
+    last = []
+    for source, columns in ((projected, slice(0, rows)), (partner, slice(rows, wide))):
+        running = running + product(dense[0][:, columns], source)
+        right = left = source
+        for hop in range(1, reach):
+            right, left = along_ring(right, 1), along_ring(left, -1)
+            running = running + product(dense[ring - hop][:, columns], right)
+            running = running + product(dense[hop][:, columns], left)
+        last.append(in_hbm(along_ring(left, -1)))
     cut_sum = call(
         cut_sum_kernel,
         "cut_sum",
@@ -375,18 +378,19 @@
         (shape((rows, width), BF), shape((width, rows), BF))
         + (pltpu.HBM((width, wide), BF),) * 2
         + (pltpu.HBM((parts, width, TILE), BF),),
-        [VMEM] * 7 + [HBM],
+        [VMEM] * 2 + [HBM] * 2 + [VMEM] * 4 + [HBM],
         (VMEM,) * 2 + (HBM,) * 3,
         [
+            pltpu.VMEM((2, rows, width), BF),
             pltpu.VMEM((2, width, wide), BF),
             pltpu.VMEM(dense_cut.shape, BF),
             pltpu.VMEM((parts, width, TILE), BF),
-            pltpu.SemaphoreType.DMA((2 * chunks + 2,)),
+            pltpu.SemaphoreType.DMA((2 * chunks + 4,)),
         ],
     )(
         running,
         cut_sum,
-        left,
+        *last,
         bias.reshape(1, width),
         cotangent,
         dense[reach],
@@ -409,10 +413,10 @@
         close_kernel,
         "close",
         (shape((width, rows), F32), shape((width, rows), BF)),
-        [SMEM] + [VMEM] * 4,
+        [VMEM] * 4,
         (VMEM, VMEM),
         flops=CLOSE_COST,
-    )(half.reshape(1), grad_pre, dense[0], right, left)
+    )(grad_pre, dense[0], right, left)
     other = across(other)
     from_cuts = call(
         gather_kernel, "gather", shape((width, rows), F32), [SMEM, SMEM, VMEM], VMEM, moved=2 << 20

time: 150 us -> 163 us (1.087)
  starting transfers between devices: 87.5 us -> 104 us
  waiting for transfers between devices: 29 us -> 21 us
  matrix products: 5.26 us -> 7.27 us
    ppermute x14 -> x21, starting transfers between devices: 61.3 us -> 76 us  [along_ring(): return lax.ppermute(value, 'blk', moves)]
    ppermute x14 -> x21, waiting for transfers between devices: 24.6 us -> 16.5 us  [along_ring(): return lax.ppermute(value, 'blk', moves)]
    all_to_all x1, starting transfers between devices: 8.3 us -> 11.4 us  [on_device(): lax.all_to_all(outgoing, 'dom', split_axis=0, concat_axis=0, tiled=True)]
    ppermute x2, starting transfers between devices: 9.24 us -> 6.29 us  [across(): lax.ppermute(value, 'blk', [(i, (i + ring) % peers) for i in range(peers)])]
    all_to_all x1, starting transfers between devices: 8.61 us -> 10.7 us  [on_device(): lax.all_to_all(terms, 'dom', split_axis=0, concat_axis=0, tiled=True)]
    dot_general x7 -> x14, matrix products: 5.26 us -> 7.27 us  [product(): return jnp.dot(left, right, preferred_element_type=F32)]
  transfers between devices with their start and end apart: 18 -> 25, of which waited for: 10 -> 6; matrix products, arithmetic and copies ran while one was open for 4% -> 5% of each run, Pallas kernels for 10% -> 8%
where the time goes in v8:
time: 163 us; the launch traced here: 161 us
  starting transfers between devices  104 us (64%)
  Pallas kernels  23.6 us (14%)
  waiting for transfers between devices  21 us (13%)
  matrix products  7.27 us (4%)
  local copies, waits for them, and re-layouts  3.03 us (2%)
    ppermute x21, starting transfers between devices, along_ring(): return lax.ppermute(value, 'blk', moves)  76 us
    ppermute x21, waiting for transfers between devices, along_ring(): return lax.ppermute(value, 'blk', moves)  16.5 us
    all_to_all x1, starting transfers between devices, on_device(): lax.all_to_all(outgoing, 'dom', split_axis=0, concat_axis=0, tiled=True)  11.4 us
    all_to_all x1, starting transfers between devices, on_device(): lax.all_to_all(terms, 'dom', split_axis=0, concat_axis=0, tiled=True)  10.7 us
    dot_general x14, matrix products, product(): return jnp.dot(left, right, preferred_element_type=F32)  7.27 us
    ppermute x2, starting transfers between devices, across(): lax.ppermute(value, 'blk', [(i, (i + ring) % peers) for i in range(peers)])  6.29 us
    pallas_call x1, Pallas kernels, on_device(): call(middle_kernel, 'middle', (shape((rows, width), BF), shape((width, ro...  6.27 us
    all_to_all x1, waiting for transfers between devices, on_device(): lax.all_to_all(terms, 'dom', split_axis=0, concat_axis=0, tiled=True)  4.01 us
  transfers between devices with their start and end apart: 25, of which 6 were waited for; matrix products, arithmetic and copies ran while one was open for 5% of the time, Pallas kernels for 8%

profile of v8, /device:TPU:1, one launch (start us, length us, event | category | flops | bytes accessed | tf_op | source)
XLA Modules:
  0.0 160.7 jit_solution(13178002641747932988)
XLA Ops:
  0.6 1.2 project.1.projected_ref
  1.9 2.3 %fill.1 = bf16[32,128,256]{2,1,0:T(8,128)(2,1)} custom-call(s32[32]{0:T(128)} %bitcast.27, s32[32]{0:T(128)} %bitcast.29, bf16[384,256]{1,0:T(8,128)(2,1)S(1)} %project.1.projected_ref), custom_call_target="tpu_custom_call" | custom-call | tf_op jit(solution)/shard_map/fill/pallas_call | solution.py:314
  4.2 11.4 %all-to-all-start = ((bf16[32,128,256]{2,1,0:T(8,128)(2,1)}), bf16[32,128,256]{2,1,0:T(8,128)(2,1)}, u32[]{:S(2)}, u32[]{:S(2)}) async-start(bf16[32,128,256]{2,1,0:T(8,128)(2,1)} %fill.1), calls=%async_computation | async-start | bytes 4194304 | tf_op jit(solution)/shard_map/all_to_all | solution.py:328
  15.6 2.9 %collective-permute-start.6 = (bf16[384,256]{1,0:T(8,128)(2,1)S(1)}, bf16[384,256]{1,0:T(8,128)(2,1)}, u32[]{:S(2)}, u32[]{:S(2)}) collective-permute-start(bf16[384,256]{1,0:T(8,128)(2,1)S(1)} %project.1.projected_ref), channel_id=1, source_target_pairs={{0,8},{1,9},{2,10},{3,11},{4,12},{5,13},{6,14},{7,15},{8,0},{9,1},... | collective-permute-start | bytes 589832 | tf_op jit(solution)/shard_map/ppermute | solution.py:299
  18.5 10.7 %collective-permute-start.1 = (bf16[384,256]{1,0:T(8,128)(2,1)S(1)}, bf16[384,256]{1,0:T(8,128)(2,1)}, u32[]{:S(2)}, u32[]{:S(2)}) collective-permute-start(bf16[384,256]{1,0:T(8,128)(2,1)S(1)} %project.1.projected_ref), channel_id=1, source_target_pairs={{0,7},{1,0},{2,1},{3,2},{4,3},{5,4},{6,5},{7,6},{8,15},{9,8},{10,9... | collective-permute-start | bytes 589832 | tf_op jit(solution)/shard_map/ppermute | solution.py:296
  29.1 1.9 %collective-permute-start = (bf16[384,256]{1,0:T(8,128)(2,1)S(1)}, bf16[384,256]{1,0:T(8,128)(2,1)S(1)}, u32[]{:S(2)}, u32[]{:S(2)}) collective-permute-start(bf16[384,256]{1,0:T(8,128)(2,1)S(1)} %project.1.projected_ref), channel_id=1, source_target_pairs={{0,1},{1,2},{2,3},{3,4},{4,5},{5,6},{6,7},{7,0},{8,9},{9,10},{10,1... | collective-permute-start | bytes 589832 | tf_op jit(solution)/shard_map/ppermute | solution.py:296
  31.1 0.1 copy.14
  31.2 0.1 reshape_squeeze.3.refs_0_
  31.3 2.8 %spread_cut.1.cut_hbm = bf16[8,384,512]{2,1,0:T(8,128)(2,1)} custom-call(s32[32]{0:T(128)S(1)} %bitcast.32, bf16[32,128,128]{2,1,0:T(8,128)(2,1)S(1)} %bitcast.26), custom_call_target="tpu_custom_call" | custom-call | bytes 6291456 | tf_op jit(solution)/shard_map/spread_cut/pallas_call | solution.py:338
  34.2 2.1 %spread.1 = (bf16[384,768]{1,0:T(8,128)(2,1)S(1)}, bf16[384,768]{1,0:T(8,128)(2,1)S(1)}, bf16[384,768]{1,0:T(8,128)(2,1)S(1)}, bf16[384,768]{1,0:T(8,128)(2,1)S(...) custom-call(s32[64]{0:T(128)S(1)} %reshape_squeeze.3.refs_0_, ...), custom_call_target="tpu_custom_call" | custom-call | bytes 10485760 | tf_op jit(solution)/shard_map/spread/pallas_call | solution.py:330
  36.4 0.3 fusion.25
  36.6 4.5 %collective-permute-start.8 = (bf16[384,256]{1,0:T(8,128)(2,1)}, bf16[384,256]{1,0:T(8,128)(2,1)S(1)}, u32[]{:S(2)}, u32[]{:S(2)}) collective-permute-start(bf16[384,256]{1,0:T(8,128)(2,1)} %collective-permute-done.6), channel_id=1, source_target_pairs={{0,7},{1,0},{2,1},{3,2},{4,3},{5,4},{6,5},{7,6},{8,15},{9,8},{10,9... | collective-permute-start | bytes 589832 | tf_op jit(solution)/shard_map/ppermute | solution.py:296
  41.1 1.9 %collective-permute-start.7 = (bf16[384,256]{1,0:T(8,128)(2,1)}, bf16[384,256]{1,0:T(8,128)(2,1)S(1)}, u32[]{:S(2)}, u32[]{:S(2)}) collective-permute-start(bf16[384,256]{1,0:T(8,128)(2,1)} %collective-permute-done.6), channel_id=1, source_target_pairs={{0,1},{1,2},{2,3},{3,4},{4,5},{5,6},{6,7},{7,0},{8,9},{9,10},{10,1... | collective-permute-start | bytes 589832 | tf_op jit(solution)/shard_map/ppermute | solution.py:296
  43.1 4.6 %collective-permute-start.3 = (bf16[384,256]{1,0:T(8,128)(2,1)}, bf16[384,256]{1,0:T(8,128)(2,1)S(1)}, u32[]{:S(2)}, u32[]{:S(2)}) collective-permute-start(bf16[384,256]{1,0:T(8,128)(2,1)} %collective-permute-done.1), channel_id=1, source_target_pairs={{0,7},{1,0},{2,1},{3,2},{4,3},{5,4},{6,5},{7,6},{8,15},{9,8},{10,9... | collective-permute-start | bytes 589832 | tf_op jit(solution)/shard_map/ppermute | solution.py:296
  47.7 1.9 %collective-permute-start.2 = (bf16[384,256]{1,0:T(8,128)(2,1)S(1)}, bf16[384,256]{1,0:T(8,128)(2,1)S(1)}, u32[]{:S(2)}, u32[]{:S(2)}) collective-permute-start(bf16[384,256]{1,0:T(8,128)(2,1)S(1)} %collective-permute-done), channel_id=1, source_target_pairs={{0,1},{1,2},{2,3},{3,4},{4,5},{5,6},{6,7},{7,0},{8,9},{9,10},{10,1... | collective-permute-start | bytes 589832 | tf_op jit(solution)/shard_map/ppermute | solution.py:296
  49.6 0.3 convolution_add_fusion.6
  49.8 1.2 convolution_add_fusion.5
  51.0 1.2 fusion.15
  52.2 4.6 %collective-permute-start.10 = (bf16[384,256]{1,0:T(8,128)(2,1)S(1)}, bf16[384,256]{1,0:T(8,128)(2,1)S(1)}, u32[]{:S(2)}, u32[]{:S(2)}) collective-permute-start(bf16[384,256]{1,0:T(8,128)(2,1)S(1)} %collective-permute-done.8), channel_id=1, source_target_pairs={{0,7},{1,0},{2,1},{3,2},{4,3},{5,4},{6,5},{7,6},{8,15},{9,8},{10,9... | collective-permute-start | bytes 589832 | tf_op jit(solution)/shard_map/ppermute | solution.py:296
  56.8 1.9 %collective-permute-start.9 = (bf16[384,256]{1,0:T(8,128)(2,1)S(1)}, bf16[384,256]{1,0:T(8,128)(2,1)S(1)}, u32[]{:S(2)}, u32[]{:S(2)}) collective-permute-start(bf16[384,256]{1,0:T(8,128)(2,1)S(1)} %collective-permute-done.7), channel_id=1, source_target_pairs={{0,1},{1,2},{2,3},{3,4},{4,5},{5,6},{6,7},{7,0},{8,9},{9,10},{10,1... | collective-permute-start | bytes 589832 | tf_op jit(solution)/shard_map/ppermute | solution.py:296
  58.8 4.6 %collective-permute-start.5 = (bf16[384,256]{1,0:T(8,128)(2,1)S(1)}, bf16[384,256]{1,0:T(8,128)(2,1)}, u32[]{:S(2)}, u32[]{:S(2)}) collective-permute-start(bf16[384,256]{1,0:T(8,128)(2,1)S(1)} %collective-permute-done.3), channel_id=1, source_target_pairs={{0,7},{1,0},{2,1},{3,2},{4,3},{5,4},{6,5},{7,6},{8,15},{9,8},{10,9... | collective-permute-start | bytes 589832 | tf_op jit(solution)/shard_map/ppermute | solution.py:296
  63.4 1.9 %collective-permute-start.4 = (bf16[384,256]{1,0:T(8,128)(2,1)S(1)}, bf16[384,256]{1,0:T(8,128)(2,1)S(1)}, u32[]{:S(2)}, u32[]{:S(2)}) collective-permute-start(bf16[384,256]{1,0:T(8,128)(2,1)S(1)} %collective-permute-done.2), channel_id=1, source_target_pairs={{0,1},{1,2},{2,3},{3,4},{4,5},{5,6},{6,7},{7,0},{8,9},{9,10},{10,1... | collective-permute-start | bytes 589832 | tf_op jit(solution)/shard_map/ppermute | solution.py:296
  65.3 0.3 fusion.20
  65.5 0.3 fusion
  65.8 0.3 fusion.12
  66.1 4.6 %collective-permute-start.12 = (bf16[384,256]{1,0:T(8,128)(2,1)S(1)}, bf16[384,256]{1,0:T(8,128)(2,1)}, u32[]{:S(2)}, u32[]{:S(2)}) collective-permute-start(bf16[384,256]{1,0:T(8,128)(2,1)S(1)} %collective-permute-done.10), channel_id=1, source_target_pairs={{0,7},{1,0},{2,1},{3,2},{4,3},{5,4},{6,5},{7,6},{8,15},{9,8},{10,9... | collective-permute-start | bytes 589832 | tf_op jit(solution)/shard_map/ppermute | solution.py:296
  70.7 1.9 %collective-permute-start.11 = (bf16[384,256]{1,0:T(8,128)(2,1)S(1)}, bf16[384,256]{1,0:T(8,128)(2,1)S(1)}, u32[]{:S(2)}, u32[]{:S(2)}) collective-permute-start(bf16[384,256]{1,0:T(8,128)(2,1)S(1)} %collective-permute-done.9), channel_id=1, source_target_pairs={{0,1},{1,2},{2,3},{3,4},{4,5},{5,6},{6,7},{7,0},{8,9},{9,10},{10,1... | collective-permute-start | bytes 589832 | tf_op jit(solution)/shard_map/ppermute | solution.py:296
  72.6 4.6 %collective-permute-start.13 = (bf16[384,256]{1,0:T(8,128)(2,1)}, bf16[384,256]{1,0:T(8,128)(2,1)S(1)}, u32[]{:S(2)}, u32[]{:S(2)}) collective-permute-start(bf16[384,256]{1,0:T(8,128)(2,1)} %collective-permute-done.5), channel_id=1, source_target_pairs={{0,7},{1,0},{2,1},{3,2},{4,3},{5,4},{6,5},{7,6},{8,15},{9,8},{10,9... | collective-permute-start | bytes 589832 | tf_op jit(solution)/shard_map/ppermute | solution.py:296
  77.2 0.3 fusion.9
  77.5 1.2 fusion.17
  78.7 0.3 fusion.2
  78.9 0.3 fusion.3
  79.2 0.3 fusion.4
  79.5 1.9 %collective-permute-start.14 = (bf16[384,256]{1,0:T(8,128)(2,1)}, bf16[384,256]{1,0:T(8,128)(2,1)}, u32[]{:S(2)}, u32[]{:S(2)}) collective-permute-start(bf16[384,256]{1,0:T(8,128)(2,1)} %collective-permute-done.12), channel_id=1, source_target_pairs={{0,7},{1,0},{2,1},{3,2},{4,3},{5,4},{6,5},{7,6},{8,15},{9,8},{10,9... | collective-permute-start | bytes 589832 | tf_op jit(solution)/shard_map/ppermute | solution.py:296
  81.4 1.2 fusion.6
  82.6 0.3 fusion.5.sum_ref
  82.9 3.4 %cut_sum.1.cut_sum_ref = f32[384,256]{1,0:T(8,128)S(1)} custom-call(bf16[8,384,512]{2,1,0:T(8,128)(2,1)} %spread_cut.1.cut_hbm, bf16[32,128,256]{2,1,0:T(8,128)(2,1)} %all-to-all-done.far_hbm), custom_call_target="tpu_custom_call" | custom-call | flops 2000000000 | tf_op jit(solution)/shard_map/cut_sum/pallas_call | solution.py:361
  86.3 0.6 copy-done.17
  87.0 6.3 %middle.1 = (bf16[384,256]{1,0:T(8,128)(2,1)}, bf16[256,384]{1,0:T(8,128)(2,1)S(1)}, bf16[256,768]{1,0:T(8,128)(2,1)}, bf16[256,768]{1,0:T(8,128)(2,1)}, bf16[32,256,128]{2,1,0:T(8,128)(2,1)}) custom-call(f32[384,256]{1,0:T(8,128)S(1)} %fusion.5.sum_ref, f32[384,256]{1,0:T(8,128)S(1)} %cut_sum.1.cut_sum_ref, bf16[384,256]{1,0:T(8,128)(2,1)} %copy-done.17, ...), custom_call_target="tpu_custom_call" | custom-call | tf_op jit(solution)/shard_map/middle/pallas_call | solution.py:375
  93.3 4.5 %collective-permute-start.18 = (bf16[256,768]{1,0:T(8,128)(2,1)}, bf16[256,768]{1,0:T(8,128)(2,1)}, u32[]{:S(2)}, u32[]{:S(2)}) collective-permute-start(bf16[256,768]{1,0:T(8,128)(2,1)} %get-tuple-element.28), channel_id=1, source_target_pairs={{0,7},{1,0},{2,1},{3,2},{4,3},{5,4},{6,5},{7,6},{8,15},{9,8},{10,9... | collective-permute-start | bytes 1179656 | tf_op jit(solution)/shard_map/ppermute | solution.py:296
  97.8 10.7 %all-to-all-start.1 = ((bf16[32,256,128]{2,1,0:T(8,128)(2,1)}), bf16[32,256,128]{2,1,0:T(8,128)(2,1)S(1)}, u32[]{:S(2)}, u32[]{:S(2)}) async-start(bf16[32,256,128]{2,1,0:T(8,128)(2,1)} %get-tuple-element.31), calls=%async_computation.1 | async-start | bytes 4194304 | tf_op jit(solution)/shard_map/all_to_all | solution.py:407
  108.4 2.6 %collective-permute-start.15 = (bf16[256,768]{1,0:T(8,128)(2,1)}, bf16[256,768]{1,0:T(8,128)(2,1)S(1)}, u32[]{:S(2)}, u32[]{:S(2)}) collective-permute-start(bf16[256,768]{1,0:T(8,128)(2,1)} %get-tuple-element.27), channel_id=1, source_target_pairs={{0,1},{1,2},{2,3},{3,4},{4,5},{5,6},{6,7},{7,0},{8,9},{9,10},{10,1... | collective-permute-start | bytes 1179656 | tf_op jit(solution)/shard_map/ppermute | solution.py:296
  111.0 1.1 copy-done.5
  112.1 1.4 hop.7
  113.4 4.1 %collective-permute-start.19 = (bf16[256,768]{1,0:T(8,128)(2,1)S(1)}, bf16[256,768]{1,0:T(8,128)(2,1)S(1)}, u32[]{:S(2)}, u32[]{:S(2)}) collective-permute-start(bf16[256,768]{1,0:T(8,128)(2,1)S(1)} %hop.7), channel_id=1, source_target_pairs={{0,7},{1,0},{2,1},{3,2},{4,3},{5,4},{6,5},{7,6},{8,15},{9,8},{10,9... | collective-permute-start | bytes 1179656 | tf_op jit(solution)/shard_map/ppermute | solution.py:296
  117.5 4.8 %collective-permute-done.15.arrived_ref = bf16[256,768]{1,0:T(8,128)(2,1)S(1)} collective-permute-done((bf16[256,768]{1,0:T(8,128)(2,1)}, bf16[256,768]{1,0:T(8,128)(2,1)S(1)}, u32[]{:S(2)}, u32[]{:S(2)}) %collective-permute-start.15) | collective-permute-done | bytes 393248 | tf_op jit(solution)/shard_map/ppermute | solution.py:296
  122.4 1.1 copy-done.3
  123.4 0.4 hop.5
  123.8 2.1 %collective-permute-start.16 = (bf16[256,768]{1,0:T(8,128)(2,1)S(1)}, bf16[256,768]{1,0:T(8,128)(2,1)S(1)}, u32[]{:S(2)}, u32[]{:S(2)}) collective-permute-start(bf16[256,768]{1,0:T(8,128)(2,1)S(1)} %hop.5), channel_id=1, source_target_pairs={{0,1},{1,2},{2,3},{3,4},{4,5},{5,6},{6,7},{7,0},{8,9},{9,10},{10,1... | collective-permute-start | bytes 1179656 | tf_op jit(solution)/shard_map/ppermute | solution.py:296
  125.9 0.4 hop.8
  126.3 4.9 %collective-permute-start.20 = (bf16[256,768]{1,0:T(8,128)(2,1)S(1)}, bf16[256,768]{1,0:T(8,128)(2,1)S(1)}, u32[]{:S(2)}, u32[]{:S(2)}) collective-permute-start(bf16[256,768]{1,0:T(8,128)(2,1)S(1)} %hop.8), channel_id=1, source_target_pairs={{0,7},{1,0},{2,1},{3,2},{4,3},{5,4},{6,5},{7,6},{8,15},{9,8},{10,9... | collective-permute-start | bytes 1179656 | tf_op jit(solution)/shard_map/ppermute | solution.py:296
  131.2 5.4 %collective-permute-done.16.arrived_ref = bf16[256,768]{1,0:T(8,128)(2,1)S(1)} collective-permute-done((bf16[256,768]{1,0:T(8,128)(2,1)S(1)}, bf16[256,768]{1,0:T(8,128)(2,1)S(1)}, u32[]{:S(2)}, u32[]{:S(2)}) %collective-permute-start.16) | collective-permute-done | bytes 393248 | tf_op jit(solution)/shard_map/ppermute | solution.py:296
  136.6 0.4 hop.6
  137.0 1.9 %collective-permute-start.17 = (bf16[256,768]{1,0:T(8,128)(2,1)S(1)}, bf16[256,768]{1,0:T(8,128)(2,1)S(1)}, u32[]{:S(2)}, u32[]{:S(2)}) collective-permute-start(bf16[256,768]{1,0:T(8,128)(2,1)S(1)} %hop.6), channel_id=1, source_target_pairs={{0,1},{1,2},{2,3},{3,4},{4,5},{5,6},{6,7},{7,0},{8,9},{9,10},{10,1... | collective-permute-start | bytes 1179656 | tf_op jit(solution)/shard_map/ppermute | solution.py:296
  138.9 0.4 hop.9
  139.3 4.6 %collective-permute-start.21 = (bf16[256,768]{1,0:T(8,128)(2,1)S(1)}, bf16[256,768]{1,0:T(8,128)(2,1)S(1)}, u32[]{:S(2)}, u32[]{:S(2)}) collective-permute-start(bf16[256,768]{1,0:T(8,128)(2,1)S(1)} %hop.9), channel_id=1, source_target_pairs={{0,7},{1,0},{2,1},{3,2},{4,3},{5,4},{6,5},{7,6},{8,15},{9,8},{10,9... | collective-permute-start | bytes 1179656 | tf_op jit(solution)/shard_map/ppermute | solution.py:296
  143.9 4.8 %collective-permute-done.17.left_ref = bf16[256,768]{1,0:T(8,128)(2,1)S(1)} collective-permute-done((bf16[256,768]{1,0:T(8,128)(2,1)S(1)}, bf16[256,768]{1,0:T(8,128)(2,1)S(1)}, u32[]{:S(2)}, u32[]{:S(2)}) %collective-permute-start.17) | collective-permute-done | bytes 393248 | tf_op jit(solution)/shard_map/ppermute | solution.py:296
  148.7 1.3 collective-permute-done.21.right_ref
  150.0 0.4 close.1
  150.4 3.4 %collective-permute-start.22 = (bf16[256,384]{1,0:T(8,128)(2,1)S(1)}, bf16[256,384]{1,0:T(8,128)(2,1)S(1)}, u32[]{:S(2)}, u32[]{:S(2)}) collective-permute-start(bf16[256,384]{1,0:T(8,128)(2,1)S(1)} %get-tuple-element.30), channel_id=1, source_target_pairs={{0,8},{1,9},{2,10},{3,11},{4,12},{5,13},{6,14},{7,15},{8,0},{9,1},... | collective-permute-start | bytes 589832 | tf_op jit(solution)/shard_map/ppermute | solution.py:299
  153.8 4.0 %all-to-all-done.1.arrived_ref = bf16[32,256,128]{2,1,0:T(8,128)(2,1)S(1)} async-done(((bf16[32,256,128]{2,1,0:T(8,128)(2,1)}), bf16[32,256,128]{2,1,0:T(8,128)(2,1)S(1)}, u32[]{:S(2)}, u32[]{:S(2)}) %all-to-all-start.1) | async-done | bytes 2097184 | tf_op jit(solution)/shard_map/all_to_all | solution.py:407
  157.8 1.3 gather.1.cut_ref
  159.2 0.6 collective-permute-done.22.other_ref
  159.7 1.0 last.1
  (55 shorter events, 0.2 us)
Async XLA Ops:
  4.2 26.9 %copy-start.18 = (s32[1,1,16,4]{2,3,1,0:T(4,128)S(1)}, s32[1,1,16,4]{2,3,1,0:T(4,128)}, u32[]{:S(2)}) copy-start(s32[1,1,16,4]{2,3,1,0:T(4,128)} %param.16) | copy-start | bytes 772
  4.2 27.1 %copy-start.7 = (bf16[1,1,32,128,128]{4,3,2,1,0:T(8,128)(2,1)S(1)}, bf16[1,1,32,128,128]{4,3,2,1,0:T(8,128)(2,1)}, u32[]{:S(2)}) copy-start(bf16[1,1,32,128,128]{4,3,2,1,0:T(8,128)(2,1)} %param.18) | copy-start | bytes 3145732
  4.2 27.1 %copy-start.15 = (s32[1,1,32]{2,1,0:T(1,128)S(1)}, s32[1,1,32]{2,1,0:T(1,128)}, u32[]{:S(2)}) copy-start(s32[1,1,32]{2,1,0:T(1,128)} %param.21) | copy-start | bytes 388
  4.2 78.7 %all-to-all-start = ((bf16[32,128,256]{2,1,0:T(8,128)(2,1)}), bf16[32,128,256]{2,1,0:T(8,128)(2,1)}, u32[]{:S(2)}, u32[]{:S(2)}) async-start(bf16[32,128,256]{2,1,0:T(8,128)(2,1)} %fill.1), calls=%async_computation | async-start | bytes 4194304 | tf_op jit(solution)/shard_map/all_to_all | solution.py:328
  15.6 21.1 %collective-permute-start.6 = (bf16[384,256]{1,0:T(8,128)(2,1)S(1)}, bf16[384,256]{1,0:T(8,128)(2,1)}, u32[]{:S(2)}, u32[]{:S(2)}) collective-permute-start(bf16[384,256]{1,0:T(8,128)(2,1)S(1)} %project.1.projected_ref), channel_id=1, source_target_pairs={{0,8},{1,9},{2,10},{3,11},{4,12},{5,13},{6,14},{7,15},{8,0},{9,1},... | collective-permute-start | bytes 589832 | tf_op jit(solution)/shard_map/ppermute | solution.py:299
  18.5 24.6 %collective-permute-start.1 = (bf16[384,256]{1,0:T(8,128)(2,1)S(1)}, bf16[384,256]{1,0:T(8,128)(2,1)}, u32[]{:S(2)}, u32[]{:S(2)}) collective-permute-start(bf16[384,256]{1,0:T(8,128)(2,1)S(1)} %project.1.projected_ref), channel_id=1, source_target_pairs={{0,7},{1,0},{2,1},{3,2},{4,3},{5,4},{6,5},{7,6},{8,15},{9,8},{10,9... | collective-permute-start | bytes 589832 | tf_op jit(solution)/shard_map/ppermute | solution.py:296
  29.1 18.5 %collective-permute-start = (bf16[384,256]{1,0:T(8,128)(2,1)S(1)}, bf16[384,256]{1,0:T(8,128)(2,1)S(1)}, u32[]{:S(2)}, u32[]{:S(2)}) collective-permute-start(bf16[384,256]{1,0:T(8,128)(2,1)S(1)} %project.1.projected_ref), channel_id=1, source_target_pairs={{0,1},{1,2},{2,3},{3,4},{4,5},{5,6},{6,7},{7,0},{8,9},{9,10},{10,1... | collective-permute-start | bytes 589832 | tf_op jit(solution)/shard_map/ppermute | solution.py:296
  31.3 2.9 %copy-start.6 = (bf16[1,1,16,4,128,128]{5,4,3,2,1,0:T(8,128)(2,1)S(1)}, bf16[1,1,16,4,128,128]{5,4,3,2,1,0:T(8,128)(2,1)}, u32[]{:S(2)}) copy-start(bf16[1,1,16,4,128,128]{5,4,3,2,1,0:T(8,128)(2,1)} %param.15) | copy-start | bytes 6291460
  31.3 2.9 %copy-start.16 = (s32[1,1,16]{2,1,0:T(1,128)S(1)}, s32[1,1,16]{2,1,0:T(1,128)}, u32[]{:S(2)}) copy-start(s32[1,1,16]{2,1,0:T(1,128)} %param.17) | copy-start | bytes 196
  36.3 15.9 %copy-start.8 = (bf16[384,768]{1,0:T(8,128)(2,1)}, bf16[384,768]{1,0:T(8,128)(2,1)S(1)}, u32[]{:S(2)}) copy-start(bf16[384,768]{1,0:T(8,128)(2,1)S(1)} %get-tuple-element.17.mat_ref) | copy-start | bytes 1769476
  36.3 40.9 %copy-start.2 = (bf16[384,768]{1,0:T(8,128)(2,1)}, bf16[384,768]{1,0:T(8,128)(2,1)S(1)}, u32[]{:S(2)}) copy-start(bf16[384,768]{1,0:T(8,128)(2,1)S(1)} %get-tuple-element.21.mat_ref) | copy-start | bytes 1769476
  36.3 42.8 %copy-start = (bf16[384,768]{1,0:T(8,128)(2,1)}, bf16[384,768]{1,0:T(8,128)(2,1)S(1)}, u32[]{:S(2)}) copy-start(bf16[384,768]{1,0:T(8,128)(2,1)S(1)} %get-tuple-element.20.mat_ref) | copy-start | bytes 1769476
  36.4 46.2 %copy-start.4 = (bf16[384,768]{1,0:T(8,128)(2,1)}, bf16[384,768]{1,0:T(8,128)(2,1)S(1)}, u32[]{:S(2)}) copy-start(bf16[384,768]{1,0:T(8,128)(2,1)S(1)} %get-tuple-element.22.mat_ref) | copy-start | bytes 1769476
  36.6 15.6 %collective-permute-start.8 = (bf16[384,256]{1,0:T(8,128)(2,1)}, bf16[384,256]{1,0:T(8,128)(2,1)S(1)}, u32[]{:S(2)}, u32[]{:S(2)}) collective-permute-start(bf16[384,256]{1,0:T(8,128)(2,1)} %collective-permute-done.6), channel_id=1, source_target_pairs={{0,7},{1,0},{2,1},{3,2},{4,3},{5,4},{6,5},{7,6},{8,15},{9,8},{10,9... | collective-permute-start | bytes 589832 | tf_op jit(solution)/shard_map/ppermute | solution.py:296
  41.1 15.7 %collective-permute-start.7 = (bf16[384,256]{1,0:T(8,128)(2,1)}, bf16[384,256]{1,0:T(8,128)(2,1)S(1)}, u32[]{:S(2)}, u32[]{:S(2)}) collective-permute-start(bf16[384,256]{1,0:T(8,128)(2,1)} %collective-permute-done.6), channel_id=1, source_target_pairs={{0,1},{1,2},{2,3},{3,4},{4,5},{5,6},{6,7},{7,0},{8,9},{9,10},{10,1... | collective-permute-start | bytes 589832 | tf_op jit(solution)/shard_map/ppermute | solution.py:296
  43.1 15.7 %collective-permute-start.3 = (bf16[384,256]{1,0:T(8,128)(2,1)}, bf16[384,256]{1,0:T(8,128)(2,1)S(1)}, u32[]{:S(2)}, u32[]{:S(2)}) collective-permute-start(bf16[384,256]{1,0:T(8,128)(2,1)} %collective-permute-done.1), channel_id=1, source_target_pairs={{0,7},{1,0},{2,1},{3,2},{4,3},{5,4},{6,5},{7,6},{8,15},{9,8},{10,9... | collective-permute-start | bytes 589832 | tf_op jit(solution)/shard_map/ppermute | solution.py:296
  47.7 15.7 %collective-permute-start.2 = (bf16[384,256]{1,0:T(8,128)(2,1)S(1)}, bf16[384,256]{1,0:T(8,128)(2,1)S(1)}, u32[]{:S(2)}, u32[]{:S(2)}) collective-permute-start(bf16[384,256]{1,0:T(8,128)(2,1)S(1)} %collective-permute-done), channel_id=1, source_target_pairs={{0,1},{1,2},{2,3},{3,4},{4,5},{5,6},{6,7},{7,0},{8,9},{9,10},{10,1... | collective-permute-start | bytes 589832 | tf_op jit(solution)/shard_map/ppermute | solution.py:296
  52.2 13.8 %collective-permute-start.10 = (bf16[384,256]{1,0:T(8,128)(2,1)S(1)}, bf16[384,256]{1,0:T(8,128)(2,1)S(1)}, u32[]{:S(2)}, u32[]{:S(2)}) collective-permute-start(bf16[384,256]{1,0:T(8,128)(2,1)S(1)} %collective-permute-done.8), channel_id=1, source_target_pairs={{0,7},{1,0},{2,1},{3,2},{4,3},{5,4},{6,5},{7,6},{8,15},{9,8},{10,9... | collective-permute-start | bytes 589832 | tf_op jit(solution)/shard_map/ppermute | solution.py:296
  56.8 13.8 %collective-permute-start.9 = (bf16[384,256]{1,0:T(8,128)(2,1)S(1)}, bf16[384,256]{1,0:T(8,128)(2,1)S(1)}, u32[]{:S(2)}, u32[]{:S(2)}) collective-permute-start(bf16[384,256]{1,0:T(8,128)(2,1)S(1)} %collective-permute-done.7), channel_id=1, source_target_pairs={{0,1},{1,2},{2,3},{3,4},{4,5},{5,6},{6,7},{7,0},{8,9},{9,10},{10,1... | collective-permute-start | bytes 589832 | tf_op jit(solution)/shard_map/ppermute | solution.py:296
  58.8 13.8 %collective-permute-start.5 = (bf16[384,256]{1,0:T(8,128)(2,1)S(1)}, bf16[384,256]{1,0:T(8,128)(2,1)}, u32[]{:S(2)}, u32[]{:S(2)}) collective-permute-start(bf16[384,256]{1,0:T(8,128)(2,1)S(1)} %collective-permute-done.3), channel_id=1, source_target_pairs={{0,7},{1,0},{2,1},{3,2},{4,3},{5,4},{6,5},{7,6},{8,15},{9,8},{10,9... | collective-permute-start | bytes 589832 | tf_op jit(solution)/shard_map/ppermute | solution.py:296
  63.4 15.3 %collective-permute-start.4 = (bf16[384,256]{1,0:T(8,128)(2,1)S(1)}, bf16[384,256]{1,0:T(8,128)(2,1)S(1)}, u32[]{:S(2)}, u32[]{:S(2)}) collective-permute-start(bf16[384,256]{1,0:T(8,128)(2,1)S(1)} %collective-permute-done.2), channel_id=1, source_target_pairs={{0,1},{1,2},{2,3},{3,4},{4,5},{5,6},{6,7},{7,0},{8,9},{9,10},{10,1... | collective-permute-start | bytes 589832 | tf_op jit(solution)/shard_map/ppermute | solution.py:296
  66.1 13.4 %collective-permute-start.12 = (bf16[384,256]{1,0:T(8,128)(2,1)S(1)}, bf16[384,256]{1,0:T(8,128)(2,1)}, u32[]{:S(2)}, u32[]{:S(2)}) collective-permute-start(bf16[384,256]{1,0:T(8,128)(2,1)S(1)} %collective-permute-done.10), channel_id=1, source_target_pairs={{0,7},{1,0},{2,1},{3,2},{4,3},{5,4},{6,5},{7,6},{8,15},{9,8},{10,9... | collective-permute-start | bytes 589832 | tf_op jit(solution)/shard_map/ppermute | solution.py:296
  70.7 11.9 %collective-permute-start.11 = (bf16[384,256]{1,0:T(8,128)(2,1)S(1)}, bf16[384,256]{1,0:T(8,128)(2,1)S(1)}, u32[]{:S(2)}, u32[]{:S(2)}) collective-permute-start(bf16[384,256]{1,0:T(8,128)(2,1)S(1)} %collective-permute-done.9), channel_id=1, source_target_pairs={{0,1},{1,2},{2,3},{3,4},{4,5},{5,6},{6,7},{7,0},{8,9},{9,10},{10,1... | collective-permute-start | bytes 589832 | tf_op jit(solution)/shard_map/ppermute | solution.py:296
  72.6 13.7 %collective-permute-start.13 = (bf16[384,256]{1,0:T(8,128)(2,1)}, bf16[384,256]{1,0:T(8,128)(2,1)S(1)}, u32[]{:S(2)}, u32[]{:S(2)}) collective-permute-start(bf16[384,256]{1,0:T(8,128)(2,1)} %collective-permute-done.5), channel_id=1, source_target_pairs={{0,7},{1,0},{2,1},{3,2},{4,3},{5,4},{6,5},{7,6},{8,15},{9,8},{10,9... | collective-permute-start | bytes 589832 | tf_op jit(solution)/shard_map/ppermute | solution.py:296
  79.5 6.9 %collective-permute-start.14 = (bf16[384,256]{1,0:T(8,128)(2,1)}, bf16[384,256]{1,0:T(8,128)(2,1)}, u32[]{:S(2)}, u32[]{:S(2)}) collective-permute-start(bf16[384,256]{1,0:T(8,128)(2,1)} %collective-permute-done.12), channel_id=1, source_target_pairs={{0,7},{1,0},{2,1},{3,2},{4,3},{5,4},{6,5},{7,6},{8,15},{9,8},{10,9... | collective-permute-start | bytes 589832 | tf_op jit(solution)/shard_map/ppermute | solution.py:296
  82.9 4.1 %copy-start.14 = (f32[256]{0:T(256)S(1)}, f32[256]{0:T(256)}, u32[]{:S(2)}) copy-start(f32[256]{0:T(256)} %param.13) | copy-start | bytes 3076
  82.9 4.1 %copy-start.11 = (bf16[384,256]{1,0:T(8,128)(2,1)S(1)}, bf16[384,256]{1,0:T(8,128)(2,1)}, u32[]{:S(2)}) copy-start(bf16[384,256]{1,0:T(8,128)(2,1)} %cotangent_ref.1) | copy-start | bytes 589828
  86.3 0.7 copy-start.17
  93.3 17.7 %collective-permute-start.18 = (bf16[256,768]{1,0:T(8,128)(2,1)}, bf16[256,768]{1,0:T(8,128)(2,1)}, u32[]{:S(2)}, u32[]{:S(2)}) collective-permute-start(bf16[256,768]{1,0:T(8,128)(2,1)} %get-tuple-element.28), channel_id=1, source_target_pairs={{0,7},{1,0},{2,1},{3,2},{4,3},{5,4},{6,5},{7,6},{8,15},{9,8},{10,9... | collective-permute-start | bytes 1179656 | tf_op jit(solution)/shard_map/ppermute | solution.py:296
  97.8 60.1 %all-to-all-start.1 = ((bf16[32,256,128]{2,1,0:T(8,128)(2,1)}), bf16[32,256,128]{2,1,0:T(8,128)(2,1)S(1)}, u32[]{:S(2)}, u32[]{:S(2)}) async-start(bf16[32,256,128]{2,1,0:T(8,128)(2,1)} %get-tuple-element.31), calls=%async_computation.1 | async-start | bytes 4194304 | tf_op jit(solution)/shard_map/all_to_all | solution.py:407
  108.4 17.5 %copy-start.1 = (bf16[384,768]{1,0:T(8,128)(2,1)S(1)}, bf16[384,768]{1,0:T(8,128)(2,1)}, u32[]{:S(2)}) copy-start(bf16[384,768]{1,0:T(8,128)(2,1)} %copy-done) | copy-start | bytes 1769476
  108.4 13.9 %collective-permute-start.15 = (bf16[256,768]{1,0:T(8,128)(2,1)}, bf16[256,768]{1,0:T(8,128)(2,1)S(1)}, u32[]{:S(2)}, u32[]{:S(2)}) collective-permute-start(bf16[256,768]{1,0:T(8,128)(2,1)} %get-tuple-element.27), channel_id=1, source_target_pairs={{0,1},{1,2},{2,3},{3,4},{4,5},{5,6},{6,7},{7,0},{8,9},{9,10},{10,1... | collective-permute-start | bytes 1179656 | tf_op jit(solution)/shard_map/ppermute | solution.py:296
  111.0 1.1 copy-start.5
  113.4 12.4 %collective-permute-start.19 = (bf16[256,768]{1,0:T(8,128)(2,1)S(1)}, bf16[256,768]{1,0:T(8,128)(2,1)S(1)}, u32[]{:S(2)}, u32[]{:S(2)}) collective-permute-start(bf16[256,768]{1,0:T(8,128)(2,1)S(1)} %hop.7), channel_id=1, source_target_pairs={{0,7},{1,0},{2,1},{3,2},{4,3},{5,4},{6,5},{7,6},{8,15},{9,8},{10,9... | collective-permute-start | bytes 1179656 | tf_op jit(solution)/shard_map/ppermute | solution.py:296
  122.4 1.1 copy-start.3
  123.8 26.2 %copy-start.9 = (bf16[384,768]{1,0:T(8,128)(2,1)S(1)}, bf16[384,768]{1,0:T(8,128)(2,1)}, u32[]{:S(2)}) copy-start(bf16[384,768]{1,0:T(8,128)(2,1)} %copy-done.8) | copy-start | bytes 1769476
  123.8 12.8 %collective-permute-start.16 = (bf16[256,768]{1,0:T(8,128)(2,1)S(1)}, bf16[256,768]{1,0:T(8,128)(2,1)S(1)}, u32[]{:S(2)}, u32[]{:S(2)}) collective-permute-start(bf16[256,768]{1,0:T(8,128)(2,1)S(1)} %hop.5), channel_id=1, source_target_pairs={{0,1},{1,2},{2,3},{3,4},{4,5},{5,6},{6,7},{7,0},{8,9},{9,10},{10,1... | collective-permute-start | bytes 1179656 | tf_op jit(solution)/shard_map/ppermute | solution.py:296
  126.3 12.6 %collective-permute-start.20 = (bf16[256,768]{1,0:T(8,128)(2,1)S(1)}, bf16[256,768]{1,0:T(8,128)(2,1)S(1)}, u32[]{:S(2)}, u32[]{:S(2)}) collective-permute-start(bf16[256,768]{1,0:T(8,128)(2,1)S(1)} %hop.8), channel_id=1, source_target_pairs={{0,7},{1,0},{2,1},{3,2},{4,3},{5,4},{6,5},{7,6},{8,15},{9,8},{10,9... | collective-permute-start | bytes 1179656 | tf_op jit(solution)/shard_map/ppermute | solution.py:296
  137.0 11.7 %collective-permute-start.17 = (bf16[256,768]{1,0:T(8,128)(2,1)S(1)}, bf16[256,768]{1,0:T(8,128)(2,1)S(1)}, u32[]{:S(2)}, u32[]{:S(2)}) collective-permute-start(bf16[256,768]{1,0:T(8,128)(2,1)S(1)} %hop.6), channel_id=1, source_target_pairs={{0,1},{1,2},{2,3},{3,4},{4,5},{5,6},{6,7},{7,0},{8,9},{9,10},{10,1... | collective-permute-start | bytes 1179656 | tf_op jit(solution)/shard_map/ppermute | solution.py:296
  139.3 18.5 %copy-start.12 = (s32[1,1,32]{2,1,0:T(1,128)S(1)}, s32[1,1,32]{2,1,0:T(1,128)}, u32[]{:S(2)}) copy-start(s32[1,1,32]{2,1,0:T(1,128)} %param.19) | copy-start | bytes 388
  139.3 18.5 %copy-start.13 = (s32[1,1,32]{2,1,0:T(1,128)S(1)}, s32[1,1,32]{2,1,0:T(1,128)}, u32[]{:S(2)}) copy-start(s32[1,1,32]{2,1,0:T(1,128)} %param.20) | copy-start | bytes 388
  139.3 10.7 %collective-permute-start.21 = (bf16[256,768]{1,0:T(8,128)(2,1)S(1)}, bf16[256,768]{1,0:T(8,128)(2,1)S(1)}, u32[]{:S(2)}, u32[]{:S(2)}) collective-permute-start(bf16[256,768]{1,0:T(8,128)(2,1)S(1)} %hop.9), channel_id=1, source_target_pairs={{0,7},{1,0},{2,1},{3,2},{4,3},{5,4},{6,5},{7,6},{8,15},{9,8},{10,9... | collective-permute-start | bytes 1179656 | tf_op jit(solution)/shard_map/ppermute | solution.py:296
  150.4 9.3 %copy-start.10 = (bf16[256,256]{1,0:T(8,128)(2,1)S(1)}, bf16[256,256]{1,0:T(8,128)(2,1)}, u32[]{:S(2)}) copy-start(bf16[256,256]{1,0:T(8,128)(2,1)} %weight_ref.1) | copy-start | bytes 393220
  150.4 9.3 %collective-permute-start.22 = (bf16[256,384]{1,0:T(8,128)(2,1)S(1)}, bf16[256,384]{1,0:T(8,128)(2,1)S(1)}, u32[]{:S(2)}, u32[]{:S(2)}) collective-permute-start(bf16[256,384]{1,0:T(8,128)(2,1)S(1)} %get-tuple-element.30), channel_id=1, source_target_pairs={{0,8},{1,9},{2,10},{3,11},{4,12},{5,13},{6,14},{7,15},{8,0},{9,1},... | collective-permute-start | bytes 589832 | tf_op jit(solution)/shard_map/ppermute | solution.py:299

commit v9 on v6

--- a/solution.py
+++ b/solution.py
@@ -48,31 +48,39 @@
     return (preact * sigmoid, sigmoid * (1.0 + preact * (1.0 - sigmoid)))
 
 
-def project_kernel(features_hbm, weight_hbm, projected_ref, features, weight, sems):
-    copies = [
-        pltpu.make_async_copy(features_hbm, features, sems.at[0]),
-        pltpu.make_async_copy(weight_hbm, weight, sems.at[1]),
-    ]
-    for copy in copies:
-        copy.start()
-    for copy in copies:
-        copy.wait()
-    projected_ref[...] = product(features[...], weight[...]).astype(BF)
-
-
-def fill_kernel(
-    blk_hbm, live_hbm, projected_ref, outgoing_hbm, blk_ref, live_ref, zeros, load_sems, sems
+def project_kernel(
+    blk_hbm,
+    live_hbm,
+    features_hbm,
+    weight_hbm,
+    projected_ref,
+    outgoing_hbm,
+    blk_ref,
+    live_ref,
+    features,
+    weight,
+    zeros,
+    load_sems,
+    sems,
 ):
     parts = outgoing_hbm.shape[0]
     loads = [
-        pltpu.make_async_copy(blk_hbm, blk_ref, load_sems.at[0]),
-        pltpu.make_async_copy(live_hbm, live_ref, load_sems.at[1]),
+        pltpu.make_async_copy(source, target, load_sems.at[place])
+        for place, (source, target) in enumerate(
+            (
+                (features_hbm, features),
+                (weight_hbm, weight),
+                (blk_hbm, blk_ref),
+                (live_hbm, live_ref),
+            )
+        )
     ]
     for copy in loads:
         copy.start()
     zeros[...] = jnp.zeros(zeros.shape, BF)
     for copy in loads:
         copy.wait()
+    projected_ref[...] = product(features[...], weight[...]).astype(BF)
 
     def start(part, carried):
         @pl.when(live_ref[part] > 0)
@@ -172,13 +180,18 @@
     cotangent_ref,
     far_mat_ref,
     near_mat_ref,
+    left_mat_ref,
+    right_mat_ref,
     cut_hbm,
     hidden_ref,
     grad_ref,
     left_hbm,
     right_hbm,
+    left_term_hbm,
+    right_term_hbm,
     terms_hbm,
     messages,
+    nexts,
     cut,
     terms,
     sems,
@@ -203,6 +216,14 @@
         messages[place] = product(grad, mat_ref[...]).astype(BF)
         stores.append(
             pltpu.make_async_copy(messages.at[place], out_hbm, sems.at[2 * chunks + place])
+        )
+        stores[-1].start()
+    for place, (mat_ref, out_hbm) in enumerate(
+        ((left_mat_ref, left_term_hbm), (right_mat_ref, right_term_hbm))
+    ):
+        nexts[place] = product(grad, mat_ref[...])
+        stores.append(
+            pltpu.make_async_copy(nexts.at[place], out_hbm, sems.at[2 * chunks + 2 + place])
         )
         stores[-1].start()
     for piece in range(chunks):
@@ -295,33 +316,23 @@
     def across(value):
         return lax.ppermute(value, "blk", [(i, (i + ring) % peers) for i in range(peers)])
 
-    projected = call(
+    projected, outgoing = call(
         project_kernel,
         "project",
-        shape((rows, width), BF),
-        [HBM, HBM],
-        VMEM,
-        [
-            pltpu.VMEM(features.shape, BF),
-            pltpu.VMEM(weight.shape, BF),
-            pltpu.SemaphoreType.DMA((2,)),
-        ],
-    )(in_hbm(features), in_hbm(weight))
-    partner = across(projected)
-    outgoing = call(
-        fill_kernel,
-        "fill",
-        pltpu.HBM((parts, TILE, width), BF),
-        [HBM, HBM, VMEM],
-        HBM,
+        (shape((rows, width), BF), pltpu.HBM((parts, TILE, width), BF)),
+        [HBM] * 4,
+        (VMEM, HBM),
         [
             pltpu.SMEM((parts,), jnp.int32),
             pltpu.SMEM((parts,), jnp.int32),
+            pltpu.VMEM(features.shape, BF),
+            pltpu.VMEM(weight.shape, BF),
             pltpu.VMEM((TILE, width), BF),
-            pltpu.SemaphoreType.DMA((2,)),
+            pltpu.SemaphoreType.DMA((4,)),
             pltpu.SemaphoreType.DMA((parts,)),
         ],
-    )(in_hbm(send_to), in_hbm(is_live), projected)
+    )(in_hbm(send_to), in_hbm(is_live), in_hbm(features), in_hbm(weight))
+    partner = across(projected)
     incoming = lax.all_to_all(outgoing, "dom", split_axis=0, concat_axis=0, tiled=True)
 
     dense = call(
@@ -369,19 +380,21 @@
         flops=CUT_COST,
     )(in_hbm(dense_cut), in_hbm(incoming))
 
-    hidden, grad_pre, left, right, terms = call(
+    hidden, grad_pre, left, right, left_term, right_term, terms = call(
         middle_kernel,
         "middle",
         (shape((rows, width), BF), shape((width, rows), BF))
         + (pltpu.HBM((width, wide), BF),) * 2
+        + (pltpu.HBM((width, wide), F32),) * 2
         + (pltpu.HBM((parts, width, TILE), BF),),
-        [VMEM] * 7 + [HBM],
-        (VMEM,) * 2 + (HBM,) * 3,
+        [VMEM] * 9 + [HBM],
+        (VMEM,) * 2 + (HBM,) * 5,
         [
             pltpu.VMEM((2, width, wide), BF),
+            pltpu.VMEM((2, width, wide), F32),
             pltpu.VMEM(dense_cut.shape, BF),
             pltpu.VMEM((parts, width, TILE), BF),
-            pltpu.SemaphoreType.DMA((2 * chunks + 2,)),
+            pltpu.SemaphoreType.DMA((2 * chunks + 4,)),
         ],
     )(
         running,
@@ -391,6 +404,8 @@
         cotangent,
         dense[reach],
         dense[reach - 1],
+        dense[ring - reach + 1],
+        dense[reach - 2],
         in_hbm(dense_cut),
     )
 
@@ -399,12 +414,23 @@
             grad_pre, mat, arrived
         )
 
+    def plus(term, arrived):
+        return (term + arrived.astype(F32)).astype(BF)
+
     left, right = along_ring(left, -1), along_ring(right, 1)
     returned = lax.all_to_all(terms, "dom", split_axis=0, concat_axis=0, tiled=True)
     for hop in range(reach - 1, 0, -1):
-        left = along_ring(add_on(dense[ring - hop], left), -1)
+        if hop == reach - 1:
+            left = plus(left_term, left)
+            if hop > 1:
+                right = plus(right_term, right)
+        else:
+            left = add_on(dense[ring - hop], left)
+            if hop > 1:
+                right = add_on(dense[hop - 1], right)
+        left = along_ring(left, -1)
         if hop > 1:
-            right = along_ring(add_on(dense[hop - 1], right), 1)
+            right = along_ring(right, 1)
     own, other = call(
         close_kernel,
         "close",

time: 150 us -> 151 us (level)
  local copies, waits for them, and re-layouts: 2.38 us -> 0.26 us
  matrix products: 5.26 us -> 7.01 us
    unnamed x37, local copies, waits for them, and re-layouts: 2.29 us -> 0.17 us
    dot_general x7, matrix products: 5.26 us -> 7.01 us  [product(): return jnp.dot(left, right, preferred_element_type=F32)]
    pallas_call x5 -> x3, Pallas kernels: 2.83 us -> 1.1 us  [add_on(): call(hop_kernel, 'hop', shape((width, wide), BF), [VMEM] * 3, VMEM)]
    pallas_call x2 -> x1, Pallas kernels: 3.52 us -> 2.87 us  [on_device(): call(project_kernel, 'project', (shape((rows, width), BF), pltpu.HBM((par...]
  transfers between devices with their start and end apart: 18 -> 18, of which waited for: 10 -> 9; matrix products, arithmetic and copies ran while one was open for 4% -> 6% of each run, Pallas kernels for 10% -> 8%
where the time goes in v9:
time: 151 us; the launch traced here: 149 us
  starting transfers between devices  87.7 us (58%)
  waiting for transfers between devices  29.5 us (20%)
  Pallas kernels  21.8 us (14%)
  matrix products  7.01 us (5%)
    ppermute x14, starting transfers between devices, along_ring(): return lax.ppermute(value, 'blk', moves)  60.8 us
    ppermute x14, waiting for transfers between devices, along_ring(): return lax.ppermute(value, 'blk', moves)  24.5 us
    all_to_all x1, starting transfers between devices, on_device(): lax.all_to_all(terms, 'dom', split_axis=0, concat_axis=0, tiled=True)  9.36 us
    ppermute x2, starting transfers between devices, across(): lax.ppermute(value, 'blk', [(i, (i + ring) % peers) for i in range(peers)])  9.25 us
    all_to_all x1, starting transfers between devices, on_device(): lax.all_to_all(outgoing, 'dom', split_axis=0, concat_axis=0, tiled=True)  8.3 us
    dot_general x7, matrix products, product(): return jnp.dot(left, right, preferred_element_type=F32)  7.01 us
    pallas_call x1, Pallas kernels, on_device(): call(middle_kernel, 'middle', (shape((rows, width), BF), shape((width, ro...  6.62 us
    all_to_all x1, waiting for transfers between devices, on_device(): lax.all_to_all(terms, 'dom', split_axis=0, concat_axis=0, tiled=True)  4.74 us
  transfers between devices with their start and end apart: 18, of which 9 were waited for; matrix products, arithmetic and copies ran while one was open for 6% of the time, Pallas kernels for 8%

profile of v9, /device:TPU:1, one launch (start us, length us, event | category | flops | bytes accessed | tf_op | source)
XLA Modules:
  0.0 148.9 jit_solution(6966484872625074441)
XLA Ops:
  0.6 2.9 %project.1 = (bf16[384,256]{1,0:T(8,128)(2,1)S(1)}, bf16[32,128,256]{2,1,0:T(8,128)(2,1)}) custom-call(s32[32]{0:T(128)} %bitcast.27, s32[32]{0:T(128)} %bitcast.29, bf16[384,256]{1,0:T(8,128)(2,1)} %features_hbm.1, bf16[256,256]{1,0:T(8,128)(2,1)} %weight_ref.1), custom_call_target="tpu_custom_call" | custom-call | tf_op jit(solution)/shard_map/project/pallas_call | solution.py:319
  3.5 5.5 %collective-permute-start = (bf16[384,256]{1,0:T(8,128)(2,1)S(1)}, bf16[384,256]{1,0:T(8,128)(2,1)S(1)}, u32[]{:S(2)}, u32[]{:S(2)}) collective-permute-start(bf16[384,256]{1,0:T(8,128)(2,1)S(1)} %get-tuple-element.22.own_ref), channel_id=1, source_target_pairs={{0,8},{1,9},{2,10},{3,11},{4,12},{5,13},{6,14},{7,15},{8,0},{9,1},... | collective-permute-start | bytes 589832 | tf_op jit(solution)/shard_map/ppermute | solution.py:317
  9.0 8.3 %all-to-all-start = ((bf16[32,128,256]{2,1,0:T(8,128)(2,1)}), bf16[32,128,256]{2,1,0:T(8,128)(2,1)}, u32[]{:S(2)}, u32[]{:S(2)}) async-start(bf16[32,128,256]{2,1,0:T(8,128)(2,1)} %get-tuple-element.29), calls=%async_computation | async-start | bytes 4194304 | tf_op jit(solution)/shard_map/all_to_all | solution.py:336
  17.3 0.0 collective-permute-done.other_ref
  17.3 0.0 copy-start.17
  17.3 0.0 copy-start.4
  17.4 0.0 copy-start.14
  17.4 0.8 pair.1
  18.1 10.7 %collective-permute-start.2 = (bf16[768,256]{1,0:T(8,128)(2,1)}, bf16[768,256]{1,0:T(8,128)(2,1)}, u32[]{:S(2)}, u32[]{:S(2)}) collective-permute-start(bf16[768,256]{1,0:T(8,128)(2,1)} %pair.1), channel_id=1, source_target_pairs={{0,7},{1,0},{2,1},{3,2},{4,3},{5,4},{6,5},{7,6},{8,15},{9,8},{10,9... | collective-permute-start | bytes 1179656 | tf_op jit(solution)/shard_map/ppermute | solution.py:314
  28.8 1.9 %collective-permute-start.1 = (bf16[768,256]{1,0:T(8,128)(2,1)}, bf16[768,256]{1,0:T(8,128)(2,1)}, u32[]{:S(2)}, u32[]{:S(2)}) collective-permute-start(bf16[768,256]{1,0:T(8,128)(2,1)} %pair.1), channel_id=1, source_target_pairs={{0,1},{1,2},{2,3},{3,4},{4,5},{5,6},{6,7},{7,0},{8,9},{9,10},{10,1... | collective-permute-start | bytes 1179656 | tf_op jit(solution)/shard_map/ppermute | solution.py:314
  30.8 0.1 copy.14
  30.8 0.1 reshape_squeeze.3.refs_0_
  31.0 0.0 copy-start.2
  31.0 0.0 copy-start.15
  31.0 2.8 %spread_cut.1.cut_hbm = bf16[8,384,512]{2,1,0:T(8,128)(2,1)} custom-call(s32[32]{0:T(128)S(1)} %bitcast.32, bf16[32,128,128]{2,1,0:T(8,128)(2,1)S(1)} %bitcast.26), custom_call_target="tpu_custom_call" | custom-call | bytes 6291456 | tf_op jit(solution)/shard_map/spread_cut/pallas_call | solution.py:346
  33.8 1.6 %spread.1 = (bf16[384,768]{1,0:T(8,128)(2,1)S(1)}, bf16[384,768]{1,0:T(8,128)(2,1)S(1)}, bf16[384,768]{1,0:T(8,128)(2,1)S(1)}, bf16[384,768]{1,0:T(8,128)(2,1)S(...) custom-call(s32[64]{0:T(128)S(1)} %reshape_squeeze.3.refs_0_, ...), custom_call_target="tpu_custom_call" | custom-call | bytes 10485760 | tf_op jit(solution)/shard_map/spread/pallas_call | solution.py:338
  35.4 1.9 %collective-permute-done.2 = bf16[768,256]{1,0:T(8,128)(2,1)} collective-permute-done((bf16[768,256]{1,0:T(8,128)(2,1)}, bf16[768,256]{1,0:T(8,128)(2,1)}, u32[]{:S(2)}, u32[]{:S(2)}) %collective-permute-start.2) | collective-permute-done | bytes 393248 | tf_op jit(solution)/shard_map/ppermute | solution.py:314
  37.3 5.3 %collective-permute-start.4 = (bf16[768,256]{1,0:T(8,128)(2,1)}, bf16[768,256]{1,0:T(8,128)(2,1)S(1)}, u32[]{:S(2)}, u32[]{:S(2)}) collective-permute-start(bf16[768,256]{1,0:T(8,128)(2,1)} %collective-permute-done.2), channel_id=1, source_target_pairs={{0,7},{1,0},{2,1},{3,2},{4,3},{5,4},{6,5},{7,6},{8,15},{9,8},{10,9... | collective-permute-start | bytes 1179656 | tf_op jit(solution)/shard_map/ppermute | solution.py:314
  42.6 0.0 collective-permute-done.1
  42.6 1.9 %collective-permute-start.3 = (bf16[768,256]{1,0:T(8,128)(2,1)}, bf16[768,256]{1,0:T(8,128)(2,1)S(1)}, u32[]{:S(2)}, u32[]{:S(2)}) collective-permute-start(bf16[768,256]{1,0:T(8,128)(2,1)} %collective-permute-done.1), channel_id=1, source_target_pairs={{0,1},{1,2},{2,3},{3,4},{4,5},{5,6},{6,7},{7,0},{8,9},{9,10},{10,1... | collective-permute-start | bytes 1179656 | tf_op jit(solution)/shard_map/ppermute | solution.py:314
  44.6 1.3 fusion.3
  45.9 1.3 fusion.4
  47.2 1.3 fusion.2
  48.6 1.6 %collective-permute-done.4 = bf16[768,256]{1,0:T(8,128)(2,1)S(1)} collective-permute-done((bf16[768,256]{1,0:T(8,128)(2,1)}, bf16[768,256]{1,0:T(8,128)(2,1)S(1)}, u32[]{:S(2)}, u32[]{:S(2)}) %collective-permute-start.4) | collective-permute-done | bytes 393248 | tf_op jit(solution)/shard_map/ppermute | solution.py:314
  50.2 5.3 %collective-permute-start.6 = (bf16[768,256]{1,0:T(8,128)(2,1)S(1)}, bf16[768,256]{1,0:T(8,128)(2,1)}, u32[]{:S(2)}, u32[]{:S(2)}) collective-permute-start(bf16[768,256]{1,0:T(8,128)(2,1)S(1)} %collective-permute-done.4), channel_id=1, source_target_pairs={{0,7},{1,0},{2,1},{3,2},{4,3},{5,4},{6,5},{7,6},{8,15},{9,8},{10,9... | collective-permute-start | bytes 1179656 | tf_op jit(solution)/shard_map/ppermute | solution.py:314
  55.5 0.0 collective-permute-done.3
  55.5 1.9 %collective-permute-start.5 = (bf16[768,256]{1,0:T(8,128)(2,1)S(1)}, bf16[768,256]{1,0:T(8,128)(2,1)S(1)}, u32[]{:S(2)}, u32[]{:S(2)}) collective-permute-start(bf16[768,256]{1,0:T(8,128)(2,1)S(1)} %collective-permute-done.3), channel_id=1, source_target_pairs={{0,1},{1,2},{2,3},{3,4},{4,5},{5,6},{6,7},{7,0},{8,9},{9,10},{10,1... | collective-permute-start | bytes 1179656 | tf_op jit(solution)/shard_map/ppermute | solution.py:314
  57.4 0.3 fusion.5
  57.8 0.3 fusion.1
  58.1 3.8 %collective-permute-done.6 = bf16[768,256]{1,0:T(8,128)(2,1)} collective-permute-done((bf16[768,256]{1,0:T(8,128)(2,1)S(1)}, bf16[768,256]{1,0:T(8,128)(2,1)}, u32[]{:S(2)}, u32[]{:S(2)}) %collective-permute-start.6) | collective-permute-done | bytes 393248 | tf_op jit(solution)/shard_map/ppermute | solution.py:314
  61.9 5.4 %collective-permute-start.7 = (bf16[768,256]{1,0:T(8,128)(2,1)}, bf16[768,256]{1,0:T(8,128)(2,1)}, u32[]{:S(2)}, u32[]{:S(2)}) collective-permute-start(bf16[768,256]{1,0:T(8,128)(2,1)} %collective-permute-done.6), channel_id=1, source_target_pairs={{0,7},{1,0},{2,1},{3,2},{4,3},{5,4},{6,5},{7,6},{8,15},{9,8},{10,9... | collective-permute-start | bytes 1179656 | tf_op jit(solution)/shard_map/ppermute | solution.py:314
  67.4 1.3 fusion.6
  68.7 0.0 collective-permute-done.5
  68.7 1.1 fusion.sum_ref
  69.8 3.4 %cut_sum.1.cut_sum_ref = f32[384,256]{1,0:T(8,128)S(1)} custom-call(bf16[8,384,512]{2,1,0:T(8,128)(2,1)} %spread_cut.1.cut_hbm, bf16[32,128,256]{2,1,0:T(8,128)(2,1)} %all-to-all-done.far_hbm), custom_call_target="tpu_custom_call" | custom-call | flops 2000000000 | tf_op jit(solution)/shard_map/cut_sum/pallas_call | solution.py:369
  73.3 0.0 collective-permute-done.7.last_ref
  73.3 6.6 %middle.1 = (bf16[384,256]{1,0:T(8,128)(2,1)}, bf16[256,384]{1,0:T(8,128)(2,1)S(1)}, bf16[256,768]{1,0:T(8,128)(2,1)}, bf16[256,768]{1,0:T(8,128)(2,1)}, f32[256...) custom-call(f32[384,256]{1,0:T(8,128)S(1)} %copy-done.3, f32[384,256]{1,0:T(8,128)S(1)} %cut_sum.1.cut_sum_ref, ...), custom_call_target="tpu_custom_call" | custom-call | tf_op jit(solution)/shard_map/middle/pallas_call | solution.py:383
  79.9 7.6 %collective-permute-start.11 = (bf16[256,768]{1,0:T(8,128)(2,1)}, bf16[256,768]{1,0:T(8,128)(2,1)}, u32[]{:S(2)}, u32[]{:S(2)}) collective-permute-start(bf16[256,768]{1,0:T(8,128)(2,1)} %get-tuple-element.36), channel_id=1, source_target_pairs={{0,7},{1,0},{2,1},{3,2},{4,3},{5,4},{6,5},{7,6},{8,15},{9,8},{10,9... | collective-permute-start | bytes 1179656 | tf_op jit(solution)/shard_map/ppermute | solution.py:314
  87.6 9.4 %all-to-all-start.1 = ((bf16[32,256,128]{2,1,0:T(8,128)(2,1)}), bf16[32,256,128]{2,1,0:T(8,128)(2,1)S(1)}, u32[]{:S(2)}, u32[]{:S(2)}) async-start(bf16[32,256,128]{2,1,0:T(8,128)(2,1)} %get-tuple-element.39), calls=%async_computation.1 | async-start | bytes 4194304 | tf_op jit(solution)/shard_map/all_to_all | solution.py:421
  96.9 2.1 %collective-permute-start.8 = (bf16[256,768]{1,0:T(8,128)(2,1)}, bf16[256,768]{1,0:T(8,128)(2,1)S(1)}, u32[]{:S(2)}, u32[]{:S(2)}) collective-permute-start(bf16[256,768]{1,0:T(8,128)(2,1)} %get-tuple-element.34), channel_id=1, source_target_pairs={{0,1},{1,2},{2,3},{3,4},{4,5},{5,6},{6,7},{7,0},{8,9},{9,10},{10,1... | collective-permute-start | bytes 1179656 | tf_op jit(solution)/shard_map/ppermute | solution.py:314
  99.0 1.3 add_convert_fusion
  100.3 4.6 %collective-permute-start.12 = (bf16[256,768]{1,0:T(8,128)(2,1)S(1)}, bf16[256,768]{1,0:T(8,128)(2,1)S(1)}, u32[]{:S(2)}, u32[]{:S(2)}) collective-permute-start(bf16[256,768]{1,0:T(8,128)(2,1)S(1)} %add_convert_fusion), channel_id=1, source_target_pairs={{0,7},{1,0},{2,1},{3,2},{4,3},{5,4},{6,5},{7,6},{8,15},{9,8},{10,9... | collective-permute-start | bytes 1179656 | tf_op jit(solution)/shard_map/ppermute | solution.py:314
  104.9 6.0 %collective-permute-done.8 = bf16[256,768]{1,0:T(8,128)(2,1)S(1)} collective-permute-done((bf16[256,768]{1,0:T(8,128)(2,1)}, bf16[256,768]{1,0:T(8,128)(2,1)S(1)}, u32[]{:S(2)}, u32[]{:S(2)}) %collective-permute-start.8) | collective-permute-done | bytes 393248 | tf_op jit(solution)/shard_map/ppermute | solution.py:314
  110.9 0.1 add_convert_fusion.1
  111.0 1.9 %collective-permute-start.9 = (bf16[256,768]{1,0:T(8,128)(2,1)S(1)}, bf16[256,768]{1,0:T(8,128)(2,1)S(1)}, u32[]{:S(2)}, u32[]{:S(2)}) collective-permute-start(bf16[256,768]{1,0:T(8,128)(2,1)S(1)} %add_convert_fusion.1), channel_id=1, source_target_pairs={{0,1},{1,2},{2,3},{3,4},{4,5},{5,6},{6,7},{7,0},{8,9},{9,10},{10,1... | collective-permute-start | bytes 1179656 | tf_op jit(solution)/shard_map/ppermute | solution.py:314
  112.9 0.0 collective-permute-done.12.arrived_ref
  112.9 0.4 hop.4
  113.3 5.3 %collective-permute-start.13 = (bf16[256,768]{1,0:T(8,128)(2,1)S(1)}, bf16[256,768]{1,0:T(8,128)(2,1)S(1)}, u32[]{:S(2)}, u32[]{:S(2)}) collective-permute-start(bf16[256,768]{1,0:T(8,128)(2,1)S(1)} %hop.4), channel_id=1, source_target_pairs={{0,7},{1,0},{2,1},{3,2},{4,3},{5,4},{6,5},{7,6},{8,15},{9,8},{10,9... | collective-permute-start | bytes 1179656 | tf_op jit(solution)/shard_map/ppermute | solution.py:314
  118.6 5.1 %collective-permute-done.9.arrived_ref = bf16[256,768]{1,0:T(8,128)(2,1)S(1)} collective-permute-done((bf16[256,768]{1,0:T(8,128)(2,1)S(1)}, bf16[256,768]{1,0:T(8,128)(2,1)S(1)}, u32[]{:S(2)}, u32[]{:S(2)}) %collective-permute-start.9) | collective-permute-done | bytes 393248 | tf_op jit(solution)/shard_map/ppermute | solution.py:314
  123.6 0.4 hop.3
  124.0 1.9 %collective-permute-start.10 = (bf16[256,768]{1,0:T(8,128)(2,1)S(1)}, bf16[256,768]{1,0:T(8,128)(2,1)S(1)}, u32[]{:S(2)}, u32[]{:S(2)}) collective-permute-start(bf16[256,768]{1,0:T(8,128)(2,1)S(1)} %hop.3), channel_id=1, source_target_pairs={{0,1},{1,2},{2,3},{3,4},{4,5},{5,6},{6,7},{7,0},{8,9},{9,10},{10,1... | collective-permute-start | bytes 1179656 | tf_op jit(solution)/shard_map/ppermute | solution.py:314
  125.9 0.4 hop.5
  126.3 0.0 copy-start.11
  126.3 0.0 copy-start.12
  126.3 5.0 %collective-permute-start.14 = (bf16[256,768]{1,0:T(8,128)(2,1)S(1)}, bf16[256,768]{1,0:T(8,128)(2,1)S(1)}, u32[]{:S(2)}, u32[]{:S(2)}) collective-permute-start(bf16[256,768]{1,0:T(8,128)(2,1)S(1)} %hop.5), channel_id=1, source_target_pairs={{0,7},{1,0},{2,1},{3,2},{4,3},{5,4},{6,5},{7,6},{8,15},{9,8},{10,9... | collective-permute-start | bytes 1179656 | tf_op jit(solution)/shard_map/ppermute | solution.py:314
  131.3 4.4 %collective-permute-done.10.left_ref = bf16[256,768]{1,0:T(8,128)(2,1)S(1)} collective-permute-done((bf16[256,768]{1,0:T(8,128)(2,1)S(1)}, bf16[256,768]{1,0:T(8,128)(2,1)S(1)}, u32[]{:S(2)}, u32[]{:S(2)}) %collective-permute-start.10) | collective-permute-done | bytes 393248 | tf_op jit(solution)/shard_map/ppermute | solution.py:314
  135.7 1.7 %collective-permute-done.14.right_ref = bf16[256,768]{1,0:T(8,128)(2,1)S(1)} collective-permute-done((bf16[256,768]{1,0:T(8,128)(2,1)S(1)}, bf16[256,768]{1,0:T(8,128)(2,1)S(1)}, u32[]{:S(2)}, u32[]{:S(2)}) %collective-permute-start.14) | collective-permute-done | bytes 393248 | tf_op jit(solution)/shard_map/ppermute | solution.py:314
  137.4 0.4 close.1
  137.8 0.0 copy-start.9
  137.8 3.8 %collective-permute-start.15 = (bf16[256,384]{1,0:T(8,128)(2,1)S(1)}, bf16[256,384]{1,0:T(8,128)(2,1)S(1)}, u32[]{:S(2)}, u32[]{:S(2)}) collective-permute-start(bf16[256,384]{1,0:T(8,128)(2,1)S(1)} %get-tuple-element.38), channel_id=1, source_target_pairs={{0,8},{1,9},{2,10},{3,11},{4,12},{5,13},{6,14},{7,15},{8,0},{9,1},... | collective-permute-start | bytes 589832 | tf_op jit(solution)/shard_map/ppermute | solution.py:317
  141.6 4.7 %all-to-all-done.1.arrived_ref = bf16[32,256,128]{2,1,0:T(8,128)(2,1)S(1)} async-done(((bf16[32,256,128]{2,1,0:T(8,128)(2,1)}), bf16[32,256,128]{2,1,0:T(8,128)(2,1)S(1)}, u32[]{:S(2)}, u32[]{:S(2)}) %all-to-all-start.1) | async-done | bytes 2097184 | tf_op jit(solution)/shard_map/all_to_all | solution.py:421
  146.3 1.3 gather.1.cut_ref
  147.6 0.3 collective-permute-done.15.other_ref
  147.9 0.9 last.1
  (31 shorter events, 0.1 us)
Async XLA Ops:
  3.5 13.8 %collective-permute-start = (bf16[384,256]{1,0:T(8,128)(2,1)S(1)}, bf16[384,256]{1,0:T(8,128)(2,1)S(1)}, u32[]{:S(2)}, u32[]{:S(2)}) collective-permute-start(bf16[384,256]{1,0:T(8,128)(2,1)S(1)} %get-tuple-element.22.own_ref), channel_id=1, source_target_pairs={{0,8},{1,9},{2,10},{3,11},{4,12},{5,13},{6,14},{7,15},{8,0},{9,1},... | collective-permute-start | bytes 589832 | tf_op jit(solution)/shard_map/ppermute | solution.py:317
  9.0 60.8 %all-to-all-start = ((bf16[32,128,256]{2,1,0:T(8,128)(2,1)}), bf16[32,128,256]{2,1,0:T(8,128)(2,1)}, u32[]{:S(2)}, u32[]{:S(2)}) async-start(bf16[32,128,256]{2,1,0:T(8,128)(2,1)} %get-tuple-element.29), calls=%async_computation | async-start | bytes 4194304 | tf_op jit(solution)/shard_map/all_to_all | solution.py:336
  17.3 13.4 %copy-start.17 = (s32[1,1,16,4]{2,3,1,0:T(4,128)S(1)}, s32[1,1,16,4]{2,3,1,0:T(4,128)}, u32[]{:S(2)}) copy-start(s32[1,1,16,4]{2,3,1,0:T(4,128)} %param.16) | copy-start | bytes 772
  17.3 13.6 %copy-start.4 = (bf16[1,1,32,128,128]{4,3,2,1,0:T(8,128)(2,1)S(1)}, bf16[1,1,32,128,128]{4,3,2,1,0:T(8,128)(2,1)}, u32[]{:S(2)}) copy-start(bf16[1,1,32,128,128]{4,3,2,1,0:T(8,128)(2,1)} %param.18) | copy-start | bytes 3145732
  17.4 13.6 %copy-start.14 = (s32[1,1,32]{2,1,0:T(1,128)S(1)}, s32[1,1,32]{2,1,0:T(1,128)}, u32[]{:S(2)}) copy-start(s32[1,1,32]{2,1,0:T(1,128)} %param.21) | copy-start | bytes 388
  18.1 19.2 %collective-permute-start.2 = (bf16[768,256]{1,0:T(8,128)(2,1)}, bf16[768,256]{1,0:T(8,128)(2,1)}, u32[]{:S(2)}, u32[]{:S(2)}) collective-permute-start(bf16[768,256]{1,0:T(8,128)(2,1)} %pair.1), channel_id=1, source_target_pairs={{0,7},{1,0},{2,1},{3,2},{4,3},{5,4},{6,5},{7,6},{8,15},{9,8},{10,9... | collective-permute-start | bytes 1179656 | tf_op jit(solution)/shard_map/ppermute | solution.py:314
  28.8 13.8 %collective-permute-start.1 = (bf16[768,256]{1,0:T(8,128)(2,1)}, bf16[768,256]{1,0:T(8,128)(2,1)}, u32[]{:S(2)}, u32[]{:S(2)}) collective-permute-start(bf16[768,256]{1,0:T(8,128)(2,1)} %pair.1), channel_id=1, source_target_pairs={{0,1},{1,2},{2,3},{3,4},{4,5},{5,6},{6,7},{7,0},{8,9},{9,10},{10,1... | collective-permute-start | bytes 1179656 | tf_op jit(solution)/shard_map/ppermute | solution.py:314
  31.0 2.8 %copy-start.2 = (bf16[1,1,16,4,128,128]{5,4,3,2,1,0:T(8,128)(2,1)S(1)}, bf16[1,1,16,4,128,128]{5,4,3,2,1,0:T(8,128)(2,1)}, u32[]{:S(2)}) copy-start(bf16[1,1,16,4,128,128]{5,4,3,2,1,0:T(8,128)(2,1)} %param.15) | copy-start | bytes 6291460
  31.0 2.8 %copy-start.15 = (s32[1,1,16]{2,1,0:T(1,128)S(1)}, s32[1,1,16]{2,1,0:T(1,128)}, u32[]{:S(2)}) copy-start(s32[1,1,16]{2,1,0:T(1,128)} %param.17) | copy-start | bytes 196
  35.4 13.2 %copy-start.5 = (bf16[384,768]{1,0:T(8,128)(2,1)}, bf16[384,768]{1,0:T(8,128)(2,1)S(1)}, u32[]{:S(2)}) copy-start(bf16[384,768]{1,0:T(8,128)(2,1)S(1)} %get-tuple-element.30.far_mat_ref) | copy-start | bytes 1769476
  35.4 13.2 %copy-start.7 = (bf16[384,768]{1,0:T(8,128)(2,1)}, bf16[384,768]{1,0:T(8,128)(2,1)S(1)}, u32[]{:S(2)}) copy-start(bf16[384,768]{1,0:T(8,128)(2,1)S(1)} %get-tuple-element.21.mat_ref) | copy-start | bytes 1769476
  35.4 22.4 %copy-start = (bf16[384,768]{1,0:T(8,128)(2,1)}, bf16[384,768]{1,0:T(8,128)(2,1)S(1)}, u32[]{:S(2)}) copy-start(bf16[384,768]{1,0:T(8,128)(2,1)S(1)} %get-tuple-element.25.mat_ref) | copy-start | bytes 1769476
  37.3 12.9 %collective-permute-start.4 = (bf16[768,256]{1,0:T(8,128)(2,1)}, bf16[768,256]{1,0:T(8,128)(2,1)S(1)}, u32[]{:S(2)}, u32[]{:S(2)}) collective-permute-start(bf16[768,256]{1,0:T(8,128)(2,1)} %collective-permute-done.2), channel_id=1, source_target_pairs={{0,7},{1,0},{2,1},{3,2},{4,3},{5,4},{6,5},{7,6},{8,15},{9,8},{10,9... | collective-permute-start | bytes 1179656 | tf_op jit(solution)/shard_map/ppermute | solution.py:314
  42.6 12.9 %collective-permute-start.3 = (bf16[768,256]{1,0:T(8,128)(2,1)}, bf16[768,256]{1,0:T(8,128)(2,1)S(1)}, u32[]{:S(2)}, u32[]{:S(2)}) collective-permute-start(bf16[768,256]{1,0:T(8,128)(2,1)} %collective-permute-done.1), channel_id=1, source_target_pairs={{0,1},{1,2},{2,3},{3,4},{4,5},{5,6},{6,7},{7,0},{8,9},{9,10},{10,1... | collective-permute-start | bytes 1179656 | tf_op jit(solution)/shard_map/ppermute | solution.py:314
  50.2 11.7 %collective-permute-start.6 = (bf16[768,256]{1,0:T(8,128)(2,1)S(1)}, bf16[768,256]{1,0:T(8,128)(2,1)}, u32[]{:S(2)}, u32[]{:S(2)}) collective-permute-start(bf16[768,256]{1,0:T(8,128)(2,1)S(1)} %collective-permute-done.4), channel_id=1, source_target_pairs={{0,7},{1,0},{2,1},{3,2},{4,3},{5,4},{6,5},{7,6},{8,15},{9,8},{10,9... | collective-permute-start | bytes 1179656 | tf_op jit(solution)/shard_map/ppermute | solution.py:314
  55.5 13.2 %collective-permute-start.5 = (bf16[768,256]{1,0:T(8,128)(2,1)S(1)}, bf16[768,256]{1,0:T(8,128)(2,1)S(1)}, u32[]{:S(2)}, u32[]{:S(2)}) collective-permute-start(bf16[768,256]{1,0:T(8,128)(2,1)S(1)} %collective-permute-done.3), channel_id=1, source_target_pairs={{0,1},{1,2},{2,3},{3,4},{4,5},{5,6},{6,7},{7,0},{8,9},{9,10},{10,1... | collective-permute-start | bytes 1179656 | tf_op jit(solution)/shard_map/ppermute | solution.py:314
  61.9 11.3 %collective-permute-start.7 = (bf16[768,256]{1,0:T(8,128)(2,1)}, bf16[768,256]{1,0:T(8,128)(2,1)}, u32[]{:S(2)}, u32[]{:S(2)}) collective-permute-start(bf16[768,256]{1,0:T(8,128)(2,1)} %collective-permute-done.6), channel_id=1, source_target_pairs={{0,7},{1,0},{2,1},{3,2},{4,3},{5,4},{6,5},{7,6},{8,15},{9,8},{10,9... | collective-permute-start | bytes 1179656 | tf_op jit(solution)/shard_map/ppermute | solution.py:314
  69.8 3.5 %copy-start.10 = (bf16[384,256]{1,0:T(8,128)(2,1)S(1)}, bf16[384,256]{1,0:T(8,128)(2,1)}, u32[]{:S(2)}) copy-start(bf16[384,256]{1,0:T(8,128)(2,1)} %cotangent_ref.1) | copy-start | bytes 589828
  69.8 3.5 %copy-start.13 = (f32[256]{0:T(256)S(1)}, f32[256]{0:T(256)}, u32[]{:S(2)}) copy-start(f32[256]{0:T(256)} %param.13) | copy-start | bytes 3076
  69.8 3.5 %copy-start.3 = (f32[384,256]{1,0:T(8,128)S(1)}, f32[384,256]{1,0:T(8,128)}, u32[]{:S(2)}) copy-start(f32[384,256]{1,0:T(8,128)} %fusion.sum_ref) | copy-start | bytes 1179652
  69.8 3.5 %copy-start.6 = (bf16[384,768]{1,0:T(8,128)(2,1)S(1)}, bf16[384,768]{1,0:T(8,128)(2,1)}, u32[]{:S(2)}) copy-start(bf16[384,768]{1,0:T(8,128)(2,1)} %copy-done.5) | copy-start | bytes 1769476
  79.9 19.1 %collective-permute-start.11 = (bf16[256,768]{1,0:T(8,128)(2,1)}, bf16[256,768]{1,0:T(8,128)(2,1)}, u32[]{:S(2)}, u32[]{:S(2)}) collective-permute-start(bf16[256,768]{1,0:T(8,128)(2,1)} %get-tuple-element.36), channel_id=1, source_target_pairs={{0,7},{1,0},{2,1},{3,2},{4,3},{5,4},{6,5},{7,6},{8,15},{9,8},{10,9... | collective-permute-start | bytes 1179656 | tf_op jit(solution)/shard_map/ppermute | solution.py:314
  87.6 58.8 %all-to-all-start.1 = ((bf16[32,256,128]{2,1,0:T(8,128)(2,1)}), bf16[32,256,128]{2,1,0:T(8,128)(2,1)S(1)}, u32[]{:S(2)}, u32[]{:S(2)}) async-start(bf16[32,256,128]{2,1,0:T(8,128)(2,1)} %get-tuple-element.39), calls=%async_computation.1 | async-start | bytes 4194304 | tf_op jit(solution)/shard_map/all_to_all | solution.py:421
  96.9 14.0 %copy-start.16 = (f32[256,768]{1,0:T(8,128)S(1)}, f32[256,768]{1,0:T(8,128)}, u32[]{:S(2)}) copy-start(f32[256,768]{1,0:T(8,128)} %get-tuple-element.33) | copy-start | bytes 2359300
  96.9 16.0 %copy-start.1 = (bf16[384,768]{1,0:T(8,128)(2,1)S(1)}, bf16[384,768]{1,0:T(8,128)(2,1)}, u32[]{:S(2)}) copy-start(bf16[384,768]{1,0:T(8,128)(2,1)} %copy-done) | copy-start | bytes 1769476
  96.9 13.9 %collective-permute-start.8 = (bf16[256,768]{1,0:T(8,128)(2,1)}, bf16[256,768]{1,0:T(8,128)(2,1)S(1)}, u32[]{:S(2)}, u32[]{:S(2)}) collective-permute-start(bf16[256,768]{1,0:T(8,128)(2,1)} %get-tuple-element.34), channel_id=1, source_target_pairs={{0,1},{1,2},{2,3},{3,4},{4,5},{5,6},{6,7},{7,0},{8,9},{9,10},{10,1... | collective-permute-start | bytes 1179656 | tf_op jit(solution)/shard_map/ppermute | solution.py:314
  100.3 12.6 %collective-permute-start.12 = (bf16[256,768]{1,0:T(8,128)(2,1)S(1)}, bf16[256,768]{1,0:T(8,128)(2,1)S(1)}, u32[]{:S(2)}, u32[]{:S(2)}) collective-permute-start(bf16[256,768]{1,0:T(8,128)(2,1)S(1)} %add_convert_fusion), channel_id=1, source_target_pairs={{0,7},{1,0},{2,1},{3,2},{4,3},{5,4},{6,5},{7,6},{8,15},{9,8},{10,9... | collective-permute-start | bytes 1179656 | tf_op jit(solution)/shard_map/ppermute | solution.py:314
  111.0 12.7 %collective-permute-start.9 = (bf16[256,768]{1,0:T(8,128)(2,1)S(1)}, bf16[256,768]{1,0:T(8,128)(2,1)S(1)}, u32[]{:S(2)}, u32[]{:S(2)}) collective-permute-start(bf16[256,768]{1,0:T(8,128)(2,1)S(1)} %add_convert_fusion.1), channel_id=1, source_target_pairs={{0,1},{1,2},{2,3},{3,4},{4,5},{5,6},{6,7},{7,0},{8,9},{9,10},{10,1... | collective-permute-start | bytes 1179656 | tf_op jit(solution)/shard_map/ppermute | solution.py:314
  112.9 24.5 %copy-start.8 = (bf16[384,768]{1,0:T(8,128)(2,1)S(1)}, bf16[384,768]{1,0:T(8,128)(2,1)}, u32[]{:S(2)}) copy-start(bf16[384,768]{1,0:T(8,128)(2,1)} %copy-done.7) | copy-start | bytes 1769476
  113.3 12.6 %collective-permute-start.13 = (bf16[256,768]{1,0:T(8,128)(2,1)S(1)}, bf16[256,768]{1,0:T(8,128)(2,1)S(1)}, u32[]{:S(2)}, u32[]{:S(2)}) collective-permute-start(bf16[256,768]{1,0:T(8,128)(2,1)S(1)} %hop.4), channel_id=1, source_target_pairs={{0,7},{1,0},{2,1},{3,2},{4,3},{5,4},{6,5},{7,6},{8,15},{9,8},{10,9... | collective-permute-start | bytes 1179656 | tf_op jit(solution)/shard_map/ppermute | solution.py:314
  124.0 11.7 %collective-permute-start.10 = (bf16[256,768]{1,0:T(8,128)(2,1)S(1)}, bf16[256,768]{1,0:T(8,128)(2,1)S(1)}, u32[]{:S(2)}, u32[]{:S(2)}) collective-permute-start(bf16[256,768]{1,0:T(8,128)(2,1)S(1)} %hop.3), channel_id=1, source_target_pairs={{0,1},{1,2},{2,3},{3,4},{4,5},{5,6},{6,7},{7,0},{8,9},{9,10},{10,1... | collective-permute-start | bytes 1179656 | tf_op jit(solution)/shard_map/ppermute | solution.py:314
  126.3 20.0 %copy-start.11 = (s32[1,1,32]{2,1,0:T(1,128)S(1)}, s32[1,1,32]{2,1,0:T(1,128)}, u32[]{:S(2)}) copy-start(s32[1,1,32]{2,1,0:T(1,128)} %param.19) | copy-start | bytes 388
  126.3 20.0 %copy-start.12 = (s32[1,1,32]{2,1,0:T(1,128)S(1)}, s32[1,1,32]{2,1,0:T(1,128)}, u32[]{:S(2)}) copy-start(s32[1,1,32]{2,1,0:T(1,128)} %param.20) | copy-start | bytes 388
  126.3 11.1 %collective-permute-start.14 = (bf16[256,768]{1,0:T(8,128)(2,1)S(1)}, bf16[256,768]{1,0:T(8,128)(2,1)S(1)}, u32[]{:S(2)}, u32[]{:S(2)}) collective-permute-start(bf16[256,768]{1,0:T(8,128)(2,1)S(1)} %hop.5), channel_id=1, source_target_pairs={{0,7},{1,0},{2,1},{3,2},{4,3},{5,4},{6,5},{7,6},{8,15},{9,8},{10,9... | collective-permute-start | bytes 1179656 | tf_op jit(solution)/shard_map/ppermute | solution.py:314
  137.8 10.1 %copy-start.9 = (bf16[256,256]{1,0:T(8,128)(2,1)S(1)}, bf16[256,256]{1,0:T(8,128)(2,1)}, u32[]{:S(2)}) copy-start(bf16[256,256]{1,0:T(8,128)(2,1)} %weight_ref.1) | copy-start | bytes 393220
  137.8 10.1 %collective-permute-start.15 = (bf16[256,384]{1,0:T(8,128)(2,1)S(1)}, bf16[256,384]{1,0:T(8,128)(2,1)S(1)}, u32[]{:S(2)}, u32[]{:S(2)}) collective-permute-start(bf16[256,384]{1,0:T(8,128)(2,1)S(1)} %get-tuple-element.38), channel_id=1, source_target_pairs={{0,8},{1,9},{2,10},{3,11},{4,12},{5,13},{6,14},{7,15},{8,0},{9,1},... | collective-permute-start | bytes 589832 | tf_op jit(solution)/shard_map/ppermute | solution.py:317

commit v10 on v6

--- a/solution.py
+++ b/solution.py
@@ -11,7 +11,7 @@
 CHUNKS = 8
 VMEM_LIMIT = 16 * 1024 * 1024
 PAIR_COST = 100_000_000_000
-CLOSE_COST = 26_500_000_000
+CLOSE_COST = 30_000_000_000
 CUT_COST = 2_000_000_000
 
 
@@ -238,21 +238,30 @@
     out_ref[...] = term.astype(BF)
 
 
-def close_kernel(half_ref, grad_ref, mat_ref, left_ref, right_ref, own_ref, other_ref):
-    rows = grad_ref.shape[1]
+def halves(half_ref, rows):
     mine = pl.ds(pl.multiple_of(half_ref[0] * rows, TILE), rows)
     theirs = pl.ds(pl.multiple_of((1 - half_ref[0]) * rows, TILE), rows)
-
-    def total(columns):
-        arrived = left_ref[:, columns].astype(F32) + right_ref[:, columns].astype(F32)
-        return product(grad_ref[...], mat_ref[:, columns]) + arrived
-
-    other_ref[...] = total(theirs).astype(BF)
-    own_ref[...] = total(mine)
-
-
-def last_kernel(own_ref, other_ref, cut_ref, weight_ref, out_ref):
-    total = own_ref[...] + other_ref[...].astype(F32) + cut_ref[...]
+    return mine, theirs
+
+
+def last_hop_kernel(half_ref, grad_ref, mat_ref, arrived_ref, own_ref, other_ref):
+    mine, theirs = halves(half_ref, grad_ref.shape[1])
+    for columns, out_ref in ((theirs, other_ref), (mine, own_ref)):
+        term = product(grad_ref[...], mat_ref[:, columns]) + arrived_ref[:, columns].astype(F32)
+        out_ref[...] = term.astype(BF)
+
+
+def own_place_kernel(half_ref, grad_ref, mat_ref, own_ref, other_ref):
+    mine, theirs = halves(half_ref, grad_ref.shape[1])
+    other_ref[...] = product(grad_ref[...], mat_ref[:, theirs]).astype(BF)
+    own_ref[...] = product(grad_ref[...], mat_ref[:, mine])
+
+
+def last_kernel(own_ref, *refs):
+    *arrived_refs, cut_ref, weight_ref, out_ref = refs
+    total = own_ref[...] + cut_ref[...]
+    for arrived_ref in arrived_refs:
+        total += arrived_ref[...].astype(F32)
     out_ref[...] = lax.dot_general(
         total.T.astype(BF), weight_ref[...], (((1,), (1,)), ((), ())), preferred_element_type=F32
     ).astype(BF)
@@ -287,6 +296,17 @@
     def along_ring(value, by):
         moves = [
             (side * ring + spot, side * ring + (spot + by) % ring)
+            for side in range(FAR)
+            for spot in range(ring)
+        ]
+        return lax.ppermute(value, "blk", moves)
+
+    def across_and_along(value, by):
+        moves = [
+            (
+                side * ring + spot,
+                (side + 1) % FAR * ring + (spot + by) % ring,
+            )
             for side in range(FAR)
             for spot in range(ring)
         ]
@@ -401,25 +421,42 @@
 
     left, right = along_ring(left, -1), along_ring(right, 1)
     returned = lax.all_to_all(terms, "dom", split_axis=0, concat_axis=0, tiled=True)
+    own_half = half.reshape(1)
+
+    def deliver(mat, arrived, by, flops):
+        own, other = call(
+            last_hop_kernel,
+            "last_hop",
+            (shape((width, rows), BF),) * 2,
+            [SMEM] + [VMEM] * 3,
+            (VMEM, VMEM),
+            flops=flops,
+        )(own_half, grad_pre, mat, arrived)
+        return across_and_along(other, by), along_ring(own, by)
+
+    own, other = call(
+        own_place_kernel,
+        "own_place",
+        (shape((width, rows), F32), shape((width, rows), BF)),
+        [SMEM] + [VMEM] * 2,
+        (VMEM, VMEM),
+    )(own_half, grad_pre, dense[0])
+    arrived = (across(other),)
     for hop in range(reach - 1, 0, -1):
-        left = along_ring(add_on(dense[ring - hop], left), -1)
         if hop > 1:
+            left = along_ring(add_on(dense[ring - hop], left), -1)
+        else:
+            arrived += deliver(dense[ring - hop], left, -1, CLOSE_COST)
+        if hop > 2:
             right = along_ring(add_on(dense[hop - 1], right), 1)
-    own, other = call(
-        close_kernel,
-        "close",
-        (shape((width, rows), F32), shape((width, rows), BF)),
-        [SMEM] + [VMEM] * 4,
-        (VMEM, VMEM),
-        flops=CLOSE_COST,
-    )(half.reshape(1), grad_pre, dense[0], right, left)
-    other = across(other)
+        elif hop == 2:
+            arrived += deliver(dense[hop - 1], right, 1, 0)
     from_cuts = call(
         gather_kernel, "gather", shape((width, rows), F32), [SMEM, SMEM, VMEM], VMEM, moved=2 << 20
     )(send_to, is_live, returned)
     grad_features = call(
-        last_kernel, "last", shape((rows, width), BF), [VMEM] * 4, VMEM
-    )(own, other, from_cuts, weight)
+        last_kernel, "last", shape((rows, width), BF), [VMEM] * (3 + len(arrived)), VMEM
+    )(own, *arrived, from_cuts, weight)
     return (hidden, grad_features)
 
 

time: 150 us -> 152 us (1.013)
  the two profiles are of different devices: /device:TPU:1 before, /device:TPU:8 now
where the time goes in v10:
time: 152 us; the launch traced here: 151 us
  starting transfers between devices  94.6 us (62%)
  Pallas kernels  25.9 us (17%)
  waiting for transfers between devices  25.1 us (17%)
  matrix products  3.25 us (2%)
    ppermute x14, starting transfers between devices, along_ring(): return lax.ppermute(value, 'blk', moves)  61.5 us
    ppermute x14, waiting for transfers between devices, along_ring(): return lax.ppermute(value, 'blk', moves)  20.5 us
    ppermute x2, starting transfers between devices, across_and_along(): return lax.ppermute(value, 'blk', moves)  9.56 us
    ppermute x2, starting transfers between devices, across(): lax.ppermute(value, 'blk', [(i, (i + ring) % peers) for i in range(peers)])  8.85 us
    all_to_all x1, starting transfers between devices, on_device(): lax.all_to_all(outgoing, 'dom', split_axis=0, concat_axis=0, tiled=True)  7.8 us
    all_to_all x1, starting transfers between devices, on_device(): lax.all_to_all(terms, 'dom', split_axis=0, concat_axis=0, tiled=True)  6.9 us
    pallas_call x1, Pallas kernels, on_device(): call(middle_kernel, 'middle', (shape((rows, width), BF), shape((width, ro...  5.25 us
    all_to_all x1, waiting for transfers between devices, on_device(): lax.all_to_all(terms, 'dom', split_axis=0, concat_axis=0, tiled=True)  3.67 us
  transfers between devices with their start and end apart: 20, of which 9 were waited for; matrix products, arithmetic and copies ran while one was open for 2% of the time, Pallas kernels for 12%

profile of v10, /device:TPU:8, one launch (start us, length us, event | category | flops | bytes accessed | tf_op | source)
XLA Modules:
  0.0 151.4 jit_solution(2902887022855824095)
XLA Ops:
  0.6 1.2 project.1.own_ref.projected_ref
  1.9 4.9 %collective-permute-start = (bf16[384,256]{1,0:T(8,128)(2,1)S(1)}, bf16[384,256]{1,0:T(8,128)(2,1)S(1)}, u32[]{:S(2)}, u32[]{:S(2)}) collective-permute-start(bf16[384,256]{1,0:T(8,128)(2,1)S(1)} %project.1.own_ref.projected_ref), channel_id=1, source_target_pairs={{0,8},{1,9},{2,10},{3,11},{4,12},{5,13},{6,14},{7,15},{8,0},{9,1},... | collective-permute-start | bytes 589832 | tf_op jit(solution)/shard_map/ppermute | solution.py:316
  6.8 2.3 %fill.1 = bf16[32,128,256]{2,1,0:T(8,128)(2,1)} custom-call(s32[32]{0:T(128)} %bitcast.27, s32[32]{0:T(128)} %bitcast.29, bf16[384,256]{1,0:T(8,128)(2,1)S(1)} %project.1.own_ref.projected_ref), custom_call_target="tpu_custom_call" | custom-call | tf_op jit(solution)/shard_map/fill/pallas_call | solution.py:331
  9.1 7.8 %all-to-all-start = ((bf16[32,128,256]{2,1,0:T(8,128)(2,1)}), bf16[32,128,256]{2,1,0:T(8,128)(2,1)}, u32[]{:S(2)}, u32[]{:S(2)}) async-start(bf16[32,128,256]{2,1,0:T(8,128)(2,1)} %fill.1), calls=%async_computation | async-start | bytes 4194304 | tf_op jit(solution)/shard_map/all_to_all | solution.py:345
  16.9 0.0 collective-permute-done.other_ref
  17.0 0.0 copy-start.17
  17.0 0.0 copy-start.7
  17.0 0.0 copy-start.15
  17.0 0.8 pair.1
  17.8 10.9 %collective-permute-start.2 = (bf16[768,256]{1,0:T(8,128)(2,1)}, bf16[768,256]{1,0:T(8,128)(2,1)S(1)}, u32[]{:S(2)}, u32[]{:S(2)}) collective-permute-start(bf16[768,256]{1,0:T(8,128)(2,1)} %pair.1), channel_id=1, source_target_pairs={{0,7},{1,0},{2,1},{3,2},{4,3},{5,4},{6,5},{7,6},{8,15},{9,8},{10,9... | collective-permute-start | bytes 1179656 | tf_op jit(solution)/shard_map/ppermute | solution.py:302
  28.7 1.9 %collective-permute-start.1 = (bf16[768,256]{1,0:T(8,128)(2,1)}, bf16[768,256]{1,0:T(8,128)(2,1)S(1)}, u32[]{:S(2)}, u32[]{:S(2)}) collective-permute-start(bf16[768,256]{1,0:T(8,128)(2,1)} %pair.1), channel_id=1, source_target_pairs={{0,1},{1,2},{2,3},{3,4},{4,5},{5,6},{6,7},{7,0},{8,9},{9,10},{10,1... | collective-permute-start | bytes 1179656 | tf_op jit(solution)/shard_map/ppermute | solution.py:302
  30.7 0.1 copy.14
  30.8 0.1 reshape_squeeze.3.refs_0_
  30.9 0.0 copy-start.6
  30.9 0.0 copy-start.16
  30.9 2.8 %spread_cut.1.cut_hbm = bf16[8,384,512]{2,1,0:T(8,128)(2,1)} custom-call(s32[32]{0:T(128)S(1)} %bitcast.32, bf16[32,128,128]{2,1,0:T(8,128)(2,1)S(1)} %bitcast.26), custom_call_target="tpu_custom_call" | custom-call | bytes 6291456 | tf_op jit(solution)/shard_map/spread_cut/pallas_call | solution.py:355
  33.7 1.5 %spread.1 = (bf16[384,768]{1,0:T(8,128)(2,1)S(1)}, bf16[384,768]{1,0:T(8,128)(2,1)S(1)}, bf16[384,768]{1,0:T(8,128)(2,1)S(1)}, bf16[384,768]{1,0:T(8,128)(2,1)S(...) custom-call(s32[64]{0:T(128)S(1)} %reshape_squeeze.3.refs_0_, ...), custom_call_target="tpu_custom_call" | custom-call | bytes 10485760 | tf_op jit(solution)/shard_map/spread/pallas_call | solution.py:347
  35.3 2.4 %collective-permute-done.2 = bf16[768,256]{1,0:T(8,128)(2,1)S(1)} collective-permute-done((bf16[768,256]{1,0:T(8,128)(2,1)}, bf16[768,256]{1,0:T(8,128)(2,1)S(1)}, u32[]{:S(2)}, u32[]{:S(2)}) %collective-permute-start.2) | collective-permute-done | bytes 393248 | tf_op jit(solution)/shard_map/ppermute | solution.py:302
  37.7 5.5 %collective-permute-start.4 = (bf16[768,256]{1,0:T(8,128)(2,1)S(1)}, bf16[768,256]{1,0:T(8,128)(2,1)S(1)}, u32[]{:S(2)}, u32[]{:S(2)}) collective-permute-start(bf16[768,256]{1,0:T(8,128)(2,1)S(1)} %collective-permute-done.2), channel_id=1, source_target_pairs={{0,7},{1,0},{2,1},{3,2},{4,3},{5,4},{6,5},{7,6},{8,15},{9,8},{10,9... | collective-permute-start | bytes 1179656 | tf_op jit(solution)/shard_map/ppermute | solution.py:302
  43.2 1.9 %collective-permute-start.3 = (bf16[768,256]{1,0:T(8,128)(2,1)S(1)}, bf16[768,256]{1,0:T(8,128)(2,1)S(1)}, u32[]{:S(2)}, u32[]{:S(2)}) collective-permute-start(bf16[768,256]{1,0:T(8,128)(2,1)S(1)} %collective-permute-done.1), channel_id=1, source_target_pairs={{0,1},{1,2},{2,3},{3,4},{4,5},{5,6},{6,7},{7,0},{8,9},{9,10},{10,1... | collective-permute-start | bytes 1179656 | tf_op jit(solution)/shard_map/ppermute | solution.py:302
  45.2 0.3 fusion.3
  45.5 0.3 fusion.4
  45.8 1.3 fusion.2
  47.2 3.9 %collective-permute-done.4 = bf16[768,256]{1,0:T(8,128)(2,1)S(1)} collective-permute-done((bf16[768,256]{1,0:T(8,128)(2,1)S(1)}, bf16[768,256]{1,0:T(8,128)(2,1)S(1)}, u32[]{:S(2)}, u32[]{:S(2)}) %collective-permute-start.4) | collective-permute-done | bytes 393248 | tf_op jit(solution)/shard_map/ppermute | solution.py:302
  51.1 5.6 %collective-permute-start.6 = (bf16[768,256]{1,0:T(8,128)(2,1)S(1)}, bf16[768,256]{1,0:T(8,128)(2,1)S(1)}, u32[]{:S(2)}, u32[]{:S(2)}) collective-permute-start(bf16[768,256]{1,0:T(8,128)(2,1)S(1)} %collective-permute-done.4), channel_id=1, source_target_pairs={{0,7},{1,0},{2,1},{3,2},{4,3},{5,4},{6,5},{7,6},{8,15},{9,8},{10,9... | collective-permute-start | bytes 1179656 | tf_op jit(solution)/shard_map/ppermute | solution.py:302
  56.7 1.9 %collective-permute-start.5 = (bf16[768,256]{1,0:T(8,128)(2,1)S(1)}, bf16[768,256]{1,0:T(8,128)(2,1)S(1)}, u32[]{:S(2)}, u32[]{:S(2)}) collective-permute-start(bf16[768,256]{1,0:T(8,128)(2,1)S(1)} %collective-permute-done.3), channel_id=1, source_target_pairs={{0,1},{1,2},{2,3},{3,4},{4,5},{5,6},{6,7},{7,0},{8,9},{9,10},{10,1... | collective-permute-start | bytes 1179656 | tf_op jit(solution)/shard_map/ppermute | solution.py:302
  58.6 0.3 fusion.5
  58.9 0.3 fusion.1
  59.3 4.4 %collective-permute-done.6 = bf16[768,256]{1,0:T(8,128)(2,1)S(1)} collective-permute-done((bf16[768,256]{1,0:T(8,128)(2,1)S(1)}, bf16[768,256]{1,0:T(8,128)(2,1)S(1)}, u32[]{:S(2)}, u32[]{:S(2)}) %collective-permute-start.6) | collective-permute-done | bytes 393248 | tf_op jit(solution)/shard_map/ppermute | solution.py:302
  63.7 5.6 %collective-permute-start.7 = (bf16[768,256]{1,0:T(8,128)(2,1)S(1)}, bf16[768,256]{1,0:T(8,128)(2,1)S(1)}, u32[]{:S(2)}, u32[]{:S(2)}) collective-permute-start(bf16[768,256]{1,0:T(8,128)(2,1)S(1)} %collective-permute-done.6), channel_id=1, source_target_pairs={{0,7},{1,0},{2,1},{3,2},{4,3},{5,4},{6,5},{7,6},{8,15},{9,8},{10,9... | collective-permute-start | bytes 1179656 | tf_op jit(solution)/shard_map/ppermute | solution.py:302
  69.3 0.3 fusion.6
  69.6 0.3 fusion.sum_ref
  70.0 0.0 copy-start.14
  70.0 0.0 copy-start.11
  70.0 3.4 %cut_sum.1.cut_sum_ref = f32[384,256]{1,0:T(8,128)S(1)} custom-call(bf16[8,384,512]{2,1,0:T(8,128)(2,1)} %spread_cut.1.cut_hbm, bf16[32,128,256]{2,1,0:T(8,128)(2,1)} %all-to-all-done.far_hbm), custom_call_target="tpu_custom_call" | custom-call | flops 2000000000 | tf_op jit(solution)/shard_map/cut_sum/pallas_call | solution.py:378
  73.4 2.1 %collective-permute-done.7.last_ref = bf16[768,256]{1,0:T(8,128)(2,1)S(1)} collective-permute-done((bf16[768,256]{1,0:T(8,128)(2,1)S(1)}, bf16[768,256]{1,0:T(8,128)(2,1)S(1)}, u32[]{:S(2)}, u32[]{:S(2)}) %collective-permute-start.7) | collective-permute-done | bytes 393248 | tf_op jit(solution)/shard_map/ppermute | solution.py:302
  75.5 5.2 %middle.1 = (bf16[384,256]{1,0:T(8,128)(2,1)}, bf16[256,384]{1,0:T(8,128)(2,1)S(1)}, bf16[256,768]{1,0:T(8,128)(2,1)}, bf16[256,768]{1,0:T(8,128)(2,1)}, bf16[32,256,128]{2,1,0:T(8,128)(2,1)}) custom-call(f32[384,256]{1,0:T(8,128)S(1)} %fusion.sum_ref, f32[384,256]{1,0:T(8,128)S(1)} %cut_sum.1.cut_sum_ref, ...), custom_call_target="tpu_custom_call" | custom-call | tf_op jit(solution)/shard_map/middle/pallas_call | solution.py:392
  80.7 7.3 %collective-permute-start.13 = (bf16[256,768]{1,0:T(8,128)(2,1)}, bf16[256,768]{1,0:T(8,128)(2,1)}, u32[]{:S(2)}, u32[]{:S(2)}) collective-permute-start(bf16[256,768]{1,0:T(8,128)(2,1)} %get-tuple-element.36), channel_id=1, source_target_pairs={{0,7},{1,0},{2,1},{3,2},{4,3},{5,4},{6,5},{7,6},{8,15},{9,8},{10,9... | collective-permute-start | bytes 1179656 | tf_op jit(solution)/shard_map/ppermute | solution.py:302
  88.1 6.9 %all-to-all-start.1 = ((bf16[32,256,128]{2,1,0:T(8,128)(2,1)}), bf16[32,256,128]{2,1,0:T(8,128)(2,1)S(1)}, u32[]{:S(2)}, u32[]{:S(2)}) async-start(bf16[32,256,128]{2,1,0:T(8,128)(2,1)} %get-tuple-element.39), calls=%async_computation.1 | async-start | bytes 4194304 | tf_op jit(solution)/shard_map/all_to_all | solution.py:423
  95.0 1.9 %collective-permute-start.9 = (bf16[256,768]{1,0:T(8,128)(2,1)}, bf16[256,768]{1,0:T(8,128)(2,1)S(1)}, u32[]{:S(2)}, u32[]{:S(2)}) collective-permute-start(bf16[256,768]{1,0:T(8,128)(2,1)} %get-tuple-element.33), channel_id=1, source_target_pairs={{0,1},{1,2},{2,3},{3,4},{4,5},{5,6},{6,7},{7,0},{8,9},{9,10},{10,1... | collective-permute-start | bytes 1179656 | tf_op jit(solution)/shard_map/ppermute | solution.py:302
  96.9 1.1 copy-done.1
  98.0 1.4 hop.4
  99.4 5.4 %collective-permute-start.14 = (bf16[256,768]{1,0:T(8,128)(2,1)S(1)}, bf16[256,768]{1,0:T(8,128)(2,1)S(1)}, u32[]{:S(2)}, u32[]{:S(2)}) collective-permute-start(bf16[256,768]{1,0:T(8,128)(2,1)S(1)} %hop.4), channel_id=1, source_target_pairs={{0,7},{1,0},{2,1},{3,2},{4,3},{5,4},{6,5},{7,6},{8,15},{9,8},{10,9... | collective-permute-start | bytes 1179656 | tf_op jit(solution)/shard_map/ppermute | solution.py:302
  104.8 4.7 %collective-permute-done.9.arrived_ref = bf16[256,768]{1,0:T(8,128)(2,1)S(1)} collective-permute-done((bf16[256,768]{1,0:T(8,128)(2,1)}, bf16[256,768]{1,0:T(8,128)(2,1)S(1)}, u32[]{:S(2)}, u32[]{:S(2)}) %collective-permute-start.9) | collective-permute-done | bytes 393248 | tf_op jit(solution)/shard_map/ppermute | solution.py:302
  109.5 0.4 hop.3
  109.9 2.1 %collective-permute-start.10 = (bf16[256,768]{1,0:T(8,128)(2,1)S(1)}, bf16[256,768]{1,0:T(8,128)(2,1)S(1)}, u32[]{:S(2)}, u32[]{:S(2)}) collective-permute-start(bf16[256,768]{1,0:T(8,128)(2,1)S(1)} %hop.3), channel_id=1, source_target_pairs={{0,1},{1,2},{2,3},{3,4},{4,5},{5,6},{6,7},{7,0},{8,9},{9,10},{10,1... | collective-permute-start | bytes 1179656 | tf_op jit(solution)/shard_map/ppermute | solution.py:302
  111.9 1.2 collective-permute-done.14.arrived_ref
  113.1 0.4 hop.5
  113.5 5.6 %collective-permute-start.15 = (bf16[256,768]{1,0:T(8,128)(2,1)S(1)}, bf16[256,768]{1,0:T(8,128)(2,1)S(1)}, u32[]{:S(2)}, u32[]{:S(2)}) collective-permute-start(bf16[256,768]{1,0:T(8,128)(2,1)S(1)} %hop.5), channel_id=1, source_target_pairs={{0,7},{1,0},{2,1},{3,2},{4,3},{5,4},{6,5},{7,6},{8,15},{9,8},{10,9... | collective-permute-start | bytes 1179656 | tf_op jit(solution)/shard_map/ppermute | solution.py:302
  119.1 1.0 own_place.1
  120.1 3.9 %collective-permute-start.8 = (bf16[256,384]{1,0:T(8,128)(2,1)}, bf16[256,384]{1,0:T(8,128)(2,1)S(1)}, u32[]{:S(2)}, u32[]{:S(2)}) collective-permute-start(bf16[256,384]{1,0:T(8,128)(2,1)} %get-tuple-element.32), channel_id=1, source_target_pairs={{0,8},{1,9},{2,10},{3,11},{4,12},{5,13},{6,14},{7,15},{8,0},{9,1},... | collective-permute-start | bytes 589832 | tf_op jit(solution)/shard_map/ppermute | solution.py:316
  124.0 1.1 last_hop.2
  125.1 1.9 %collective-permute-start.11 = (bf16[256,384]{1,0:T(8,128)(2,1)}, bf16[256,384]{1,0:T(8,128)(2,1)S(1)}, u32[]{:S(2)}, u32[]{:S(2)}) collective-permute-start(bf16[256,384]{1,0:T(8,128)(2,1)} %get-tuple-element.34), channel_id=1, source_target_pairs={{0,9},{1,10},{2,11},{3,12},{4,13},{5,14},{6,15},{7,8},{8,1},{9,2},... | collective-permute-start | bytes 589832 | tf_op jit(solution)/shard_map/ppermute | solution.py:313
  127.0 0.0 copy-start.12
  127.0 0.0 copy-start.13
  127.0 1.9 %collective-permute-start.12 = (bf16[256,384]{1,0:T(8,128)(2,1)}, bf16[256,384]{1,0:T(8,128)(2,1)S(1)}, u32[]{:S(2)}, u32[]{:S(2)}) collective-permute-start(bf16[256,384]{1,0:T(8,128)(2,1)} %get-tuple-element.35), channel_id=1, source_target_pairs={{0,1},{1,2},{2,3},{3,4},{4,5},{5,6},{6,7},{7,0},{8,9},{9,10},{10,1... | collective-permute-start | bytes 589832 | tf_op jit(solution)/shard_map/ppermute | solution.py:302
  129.0 1.1 last_hop.3
  130.1 7.7 %collective-permute-start.16 = (bf16[256,384]{1,0:T(8,128)(2,1)}, bf16[256,384]{1,0:T(8,128)(2,1)S(1)}, u32[]{:S(2)}, u32[]{:S(2)}) collective-permute-start(bf16[256,384]{1,0:T(8,128)(2,1)} %get-tuple-element.37), channel_id=1, source_target_pairs={{0,15},{1,8},{2,9},{3,10},{4,11},{5,12},{6,13},{7,14},{8,7},{9,0},... | collective-permute-start | bytes 589832 | tf_op jit(solution)/shard_map/ppermute | solution.py:313
  137.7 3.9 %collective-permute-start.17 = (bf16[256,384]{1,0:T(8,128)(2,1)}, bf16[256,384]{1,0:T(8,128)(2,1)}, u32[]{:S(2)}, u32[]{:S(2)}) collective-permute-start(bf16[256,384]{1,0:T(8,128)(2,1)} %get-tuple-element.38), channel_id=1, source_target_pairs={{0,7},{1,0},{2,1},{3,2},{4,3},{5,4},{6,5},{7,6},{8,15},{9,8},{10,9... | collective-permute-start | bytes 589832 | tf_op jit(solution)/shard_map/ppermute | solution.py:302
  141.6 3.7 %all-to-all-done.1.arrived_ref = bf16[32,256,128]{2,1,0:T(8,128)(2,1)S(1)} async-done(((bf16[32,256,128]{2,1,0:T(8,128)(2,1)}), bf16[32,256,128]{2,1,0:T(8,128)(2,1)S(1)}, u32[]{:S(2)}, u32[]{:S(2)}) %all-to-all-start.1) | async-done | bytes 2097184 | tf_op jit(solution)/shard_map/all_to_all | solution.py:423
  145.3 1.4 gather.1.refs_5_
  146.7 0.9 collective-permute-done.16.refs_3_
  147.6 1.8 %collective-permute-done.17.refs_4_ = bf16[256,384]{1,0:T(8,128)(2,1)} collective-permute-done((bf16[256,384]{1,0:T(8,128)(2,1)}, bf16[256,384]{1,0:T(8,128)(2,1)}, u32[]{:S(2)}, u32[]{:S(2)}) %collective-permute-start.17) | collective-permute-done | bytes 196640 | tf_op jit(solution)/shard_map/ppermute | solution.py:302
  149.4 2.0 %last.1 = bf16[384,256]{1,0:T(8,128)(2,1)} custom-call(f32[256,384]{1,0:T(8,128)S(1)} %get-tuple-element.31.own_ref, bf16[256,384]{1,0:T(8,128)(2,1)S(1)} %collective-permute-done.8.refs_0_, bf16[256,384]{1,0:T(8,128)(2,1)S(1)} %collective-permute-done.11.refs_1_, bf16[256,384]{1,0:T(8,128)(2,1)S(1)} %collective-permute-done.12.refs_2_, ...), custom_call_target="tpu_custom_call" | custom-call | tf_op jit(solution)/shard_map/last/pallas_call | solution.py:457
  (36 shorter events, 0.1 us)
Async XLA Ops:
  1.9 15.1 %collective-permute-start = (bf16[384,256]{1,0:T(8,128)(2,1)S(1)}, bf16[384,256]{1,0:T(8,128)(2,1)S(1)}, u32[]{:S(2)}, u32[]{:S(2)}) collective-permute-start(bf16[384,256]{1,0:T(8,128)(2,1)S(1)} %project.1.own_ref.projected_ref), channel_id=1, source_target_pairs={{0,8},{1,9},{2,10},{3,11},{4,12},{5,13},{6,14},{7,15},{8,0},{9,1},... | collective-permute-start | bytes 589832 | tf_op jit(solution)/shard_map/ppermute | solution.py:316
  9.1 60.8 %all-to-all-start = ((bf16[32,128,256]{2,1,0:T(8,128)(2,1)}), bf16[32,128,256]{2,1,0:T(8,128)(2,1)}, u32[]{:S(2)}, u32[]{:S(2)}) async-start(bf16[32,128,256]{2,1,0:T(8,128)(2,1)} %fill.1), calls=%async_computation | async-start | bytes 4194304 | tf_op jit(solution)/shard_map/all_to_all | solution.py:345
  17.0 13.7 %copy-start.17 = (s32[1,1,16,4]{2,3,1,0:T(4,128)S(1)}, s32[1,1,16,4]{2,3,1,0:T(4,128)}, u32[]{:S(2)}) copy-start(s32[1,1,16,4]{2,3,1,0:T(4,128)} %param.16) | copy-start | bytes 772
  17.0 13.9 %copy-start.7 = (bf16[1,1,32,128,128]{4,3,2,1,0:T(8,128)(2,1)S(1)}, bf16[1,1,32,128,128]{4,3,2,1,0:T(8,128)(2,1)}, u32[]{:S(2)}) copy-start(bf16[1,1,32,128,128]{4,3,2,1,0:T(8,128)(2,1)} %param.18) | copy-start | bytes 3145732
  17.0 13.9 %copy-start.15 = (s32[1,1,32]{2,1,0:T(1,128)S(1)}, s32[1,1,32]{2,1,0:T(1,128)}, u32[]{:S(2)}) copy-start(s32[1,1,32]{2,1,0:T(1,128)} %param.21) | copy-start | bytes 388
  17.8 19.9 %collective-permute-start.2 = (bf16[768,256]{1,0:T(8,128)(2,1)}, bf16[768,256]{1,0:T(8,128)(2,1)S(1)}, u32[]{:S(2)}, u32[]{:S(2)}) collective-permute-start(bf16[768,256]{1,0:T(8,128)(2,1)} %pair.1), channel_id=1, source_target_pairs={{0,7},{1,0},{2,1},{3,2},{4,3},{5,4},{6,5},{7,6},{8,15},{9,8},{10,9... | collective-permute-start | bytes 1179656 | tf_op jit(solution)/shard_map/ppermute | solution.py:302
  28.7 14.5 %collective-permute-start.1 = (bf16[768,256]{1,0:T(8,128)(2,1)}, bf16[768,256]{1,0:T(8,128)(2,1)S(1)}, u32[]{:S(2)}, u32[]{:S(2)}) collective-permute-start(bf16[768,256]{1,0:T(8,128)(2,1)} %pair.1), channel_id=1, source_target_pairs={{0,1},{1,2},{2,3},{3,4},{4,5},{5,6},{6,7},{7,0},{8,9},{9,10},{10,1... | collective-permute-start | bytes 1179656 | tf_op jit(solution)/shard_map/ppermute | solution.py:302
  30.9 2.8 %copy-start.6 = (bf16[1,1,16,4,128,128]{5,4,3,2,1,0:T(8,128)(2,1)S(1)}, bf16[1,1,16,4,128,128]{5,4,3,2,1,0:T(8,128)(2,1)}, u32[]{:S(2)}) copy-start(bf16[1,1,16,4,128,128]{5,4,3,2,1,0:T(8,128)(2,1)} %param.15) | copy-start | bytes 6291460
  30.9 2.8 %copy-start.16 = (s32[1,1,16]{2,1,0:T(1,128)S(1)}, s32[1,1,16]{2,1,0:T(1,128)}, u32[]{:S(2)}) copy-start(s32[1,1,16]{2,1,0:T(1,128)} %param.17) | copy-start | bytes 196
  35.3 11.9 %copy-start.2 = (bf16[384,768]{1,0:T(8,128)(2,1)}, bf16[384,768]{1,0:T(8,128)(2,1)S(1)}, u32[]{:S(2)}) copy-start(bf16[384,768]{1,0:T(8,128)(2,1)S(1)} %get-tuple-element.23.mat_ref) | copy-start | bytes 1769476
  35.3 11.9 %copy-start.4 = (bf16[384,768]{1,0:T(8,128)(2,1)}, bf16[384,768]{1,0:T(8,128)(2,1)S(1)}, u32[]{:S(2)}) copy-start(bf16[384,768]{1,0:T(8,128)(2,1)S(1)} %get-tuple-element.21.mat_ref) | copy-start | bytes 1769476
  35.3 11.9 %copy-start.8 = (bf16[384,768]{1,0:T(8,128)(2,1)}, bf16[384,768]{1,0:T(8,128)(2,1)S(1)}, u32[]{:S(2)}) copy-start(bf16[384,768]{1,0:T(8,128)(2,1)S(1)} %get-tuple-element.22.mat_ref) | copy-start | bytes 1769476
  35.3 34.3 %copy-start = (bf16[384,768]{1,0:T(8,128)(2,1)}, bf16[384,768]{1,0:T(8,128)(2,1)S(1)}, u32[]{:S(2)}) copy-start(bf16[384,768]{1,0:T(8,128)(2,1)S(1)} %get-tuple-element.26.mat_ref) | copy-start | bytes 1769476
  37.7 13.3 %collective-permute-start.4 = (bf16[768,256]{1,0:T(8,128)(2,1)S(1)}, bf16[768,256]{1,0:T(8,128)(2,1)S(1)}, u32[]{:S(2)}, u32[]{:S(2)}) collective-permute-start(bf16[768,256]{1,0:T(8,128)(2,1)S(1)} %collective-permute-done.2), channel_id=1, source_target_pairs={{0,7},{1,0},{2,1},{3,2},{4,3},{5,4},{6,5},{7,6},{8,15},{9,8},{10,9... | collective-permute-start | bytes 1179656 | tf_op jit(solution)/shard_map/ppermute | solution.py:302
  43.2 13.4 %collective-permute-start.3 = (bf16[768,256]{1,0:T(8,128)(2,1)S(1)}, bf16[768,256]{1,0:T(8,128)(2,1)S(1)}, u32[]{:S(2)}, u32[]{:S(2)}) collective-permute-start(bf16[768,256]{1,0:T(8,128)(2,1)S(1)} %collective-permute-done.1), channel_id=1, source_target_pairs={{0,1},{1,2},{2,3},{3,4},{4,5},{5,6},{6,7},{7,0},{8,9},{9,10},{10,1... | collective-permute-start | bytes 1179656 | tf_op jit(solution)/shard_map/ppermute | solution.py:302
  51.1 12.6 %collective-permute-start.6 = (bf16[768,256]{1,0:T(8,128)(2,1)S(1)}, bf16[768,256]{1,0:T(8,128)(2,1)S(1)}, u32[]{:S(2)}, u32[]{:S(2)}) collective-permute-start(bf16[768,256]{1,0:T(8,128)(2,1)S(1)} %collective-permute-done.4), channel_id=1, source_target_pairs={{0,7},{1,0},{2,1},{3,2},{4,3},{5,4},{6,5},{7,6},{8,15},{9,8},{10,9... | collective-permute-start | bytes 1179656 | tf_op jit(solution)/shard_map/ppermute | solution.py:302
  56.7 12.9 %collective-permute-start.5 = (bf16[768,256]{1,0:T(8,128)(2,1)S(1)}, bf16[768,256]{1,0:T(8,128)(2,1)S(1)}, u32[]{:S(2)}, u32[]{:S(2)}) collective-permute-start(bf16[768,256]{1,0:T(8,128)(2,1)S(1)} %collective-permute-done.3), channel_id=1, source_target_pairs={{0,1},{1,2},{2,3},{3,4},{4,5},{5,6},{6,7},{7,0},{8,9},{9,10},{10,1... | collective-permute-start | bytes 1179656 | tf_op jit(solution)/shard_map/ppermute | solution.py:302
  63.7 11.8 %collective-permute-start.7 = (bf16[768,256]{1,0:T(8,128)(2,1)S(1)}, bf16[768,256]{1,0:T(8,128)(2,1)S(1)}, u32[]{:S(2)}, u32[]{:S(2)}) collective-permute-start(bf16[768,256]{1,0:T(8,128)(2,1)S(1)} %collective-permute-done.6), channel_id=1, source_target_pairs={{0,7},{1,0},{2,1},{3,2},{4,3},{5,4},{6,5},{7,6},{8,15},{9,8},{10,9... | collective-permute-start | bytes 1179656 | tf_op jit(solution)/shard_map/ppermute | solution.py:302
  70.0 5.5 %copy-start.14 = (f32[256]{0:T(256)S(1)}, f32[256]{0:T(256)}, u32[]{:S(2)}) copy-start(f32[256]{0:T(256)} %param.13) | copy-start | bytes 3076
  70.0 5.5 %copy-start.11 = (bf16[384,256]{1,0:T(8,128)(2,1)S(1)}, bf16[384,256]{1,0:T(8,128)(2,1)}, u32[]{:S(2)}) copy-start(bf16[384,256]{1,0:T(8,128)(2,1)} %cotangent_ref.1) | copy-start | bytes 589828
  80.7 16.2 %collective-permute-start.13 = (bf16[256,768]{1,0:T(8,128)(2,1)}, bf16[256,768]{1,0:T(8,128)(2,1)}, u32[]{:S(2)}, u32[]{:S(2)}) collective-permute-start(bf16[256,768]{1,0:T(8,128)(2,1)} %get-tuple-element.36), channel_id=1, source_target_pairs={{0,7},{1,0},{2,1},{3,2},{4,3},{5,4},{6,5},{7,6},{8,15},{9,8},{10,9... | collective-permute-start | bytes 1179656 | tf_op jit(solution)/shard_map/ppermute | solution.py:302
  88.1 57.2 %all-to-all-start.1 = ((bf16[32,256,128]{2,1,0:T(8,128)(2,1)}), bf16[32,256,128]{2,1,0:T(8,128)(2,1)S(1)}, u32[]{:S(2)}, u32[]{:S(2)}) async-start(bf16[32,256,128]{2,1,0:T(8,128)(2,1)} %get-tuple-element.39), calls=%async_computation.1 | async-start | bytes 4194304 | tf_op jit(solution)/shard_map/all_to_all | solution.py:423
  95.0 14.5 %collective-permute-start.9 = (bf16[256,768]{1,0:T(8,128)(2,1)}, bf16[256,768]{1,0:T(8,128)(2,1)S(1)}, u32[]{:S(2)}, u32[]{:S(2)}) collective-permute-start(bf16[256,768]{1,0:T(8,128)(2,1)} %get-tuple-element.33), channel_id=1, source_target_pairs={{0,1},{1,2},{2,3},{3,4},{4,5},{5,6},{6,7},{7,0},{8,9},{9,10},{10,1... | collective-permute-start | bytes 1179656 | tf_op jit(solution)/shard_map/ppermute | solution.py:302
  96.9 1.1 copy-start.1
  98.0 21.1 %copy-start.5 = (bf16[384,768]{1,0:T(8,128)(2,1)S(1)}, bf16[384,768]{1,0:T(8,128)(2,1)}, u32[]{:S(2)}) copy-start(bf16[384,768]{1,0:T(8,128)(2,1)} %copy-done.4) | copy-start | bytes 1769476
  99.4 24.6 %copy-start.3 = (bf16[384,768]{1,0:T(8,128)(2,1)S(1)}, bf16[384,768]{1,0:T(8,128)(2,1)}, u32[]{:S(2)}) copy-start(bf16[384,768]{1,0:T(8,128)(2,1)} %copy-done.2) | copy-start | bytes 1769476
  99.4 13.7 %collective-permute-start.14 = (bf16[256,768]{1,0:T(8,128)(2,1)S(1)}, bf16[256,768]{1,0:T(8,128)(2,1)S(1)}, u32[]{:S(2)}, u32[]{:S(2)}) collective-permute-start(bf16[256,768]{1,0:T(8,128)(2,1)S(1)} %hop.4), channel_id=1, source_target_pairs={{0,7},{1,0},{2,1},{3,2},{4,3},{5,4},{6,5},{7,6},{8,15},{9,8},{10,9... | collective-permute-start | bytes 1179656 | tf_op jit(solution)/shard_map/ppermute | solution.py:302
  109.8 19.1 %copy-start.9 = (bf16[384,768]{1,0:T(8,128)(2,1)S(1)}, bf16[384,768]{1,0:T(8,128)(2,1)}, u32[]{:S(2)}) copy-start(bf16[384,768]{1,0:T(8,128)(2,1)} %copy-done.8) | copy-start | bytes 1769476
  109.9 14.1 %collective-permute-start.10 = (bf16[256,768]{1,0:T(8,128)(2,1)S(1)}, bf16[256,768]{1,0:T(8,128)(2,1)S(1)}, u32[]{:S(2)}, u32[]{:S(2)}) collective-permute-start(bf16[256,768]{1,0:T(8,128)(2,1)S(1)} %hop.3), channel_id=1, source_target_pairs={{0,1},{1,2},{2,3},{3,4},{4,5},{5,6},{6,7},{7,0},{8,9},{9,10},{10,1... | collective-permute-start | bytes 1179656 | tf_op jit(solution)/shard_map/ppermute | solution.py:302
  113.5 15.5 %collective-permute-start.15 = (bf16[256,768]{1,0:T(8,128)(2,1)S(1)}, bf16[256,768]{1,0:T(8,128)(2,1)S(1)}, u32[]{:S(2)}, u32[]{:S(2)}) collective-permute-start(bf16[256,768]{1,0:T(8,128)(2,1)S(1)} %hop.5), channel_id=1, source_target_pairs={{0,7},{1,0},{2,1},{3,2},{4,3},{5,4},{6,5},{7,6},{8,15},{9,8},{10,9... | collective-permute-start | bytes 1179656 | tf_op jit(solution)/shard_map/ppermute | solution.py:302
  120.1 26.6 %collective-permute-start.8 = (bf16[256,384]{1,0:T(8,128)(2,1)}, bf16[256,384]{1,0:T(8,128)(2,1)S(1)}, u32[]{:S(2)}, u32[]{:S(2)}) collective-permute-start(bf16[256,384]{1,0:T(8,128)(2,1)} %get-tuple-element.32), channel_id=1, source_target_pairs={{0,8},{1,9},{2,10},{3,11},{4,12},{5,13},{6,14},{7,15},{8,0},{9,1},... | collective-permute-start | bytes 589832 | tf_op jit(solution)/shard_map/ppermute | solution.py:316
  125.1 21.6 %collective-permute-start.11 = (bf16[256,384]{1,0:T(8,128)(2,1)}, bf16[256,384]{1,0:T(8,128)(2,1)S(1)}, u32[]{:S(2)}, u32[]{:S(2)}) collective-permute-start(bf16[256,384]{1,0:T(8,128)(2,1)} %get-tuple-element.34), channel_id=1, source_target_pairs={{0,9},{1,10},{2,11},{3,12},{4,13},{5,14},{6,15},{7,8},{8,1},{9,2},... | collective-permute-start | bytes 589832 | tf_op jit(solution)/shard_map/ppermute | solution.py:313
  127.0 18.3 %copy-start.12 = (s32[1,1,32]{2,1,0:T(1,128)S(1)}, s32[1,1,32]{2,1,0:T(1,128)}, u32[]{:S(2)}) copy-start(s32[1,1,32]{2,1,0:T(1,128)} %param.19) | copy-start | bytes 388
  127.0 18.3 %copy-start.13 = (s32[1,1,32]{2,1,0:T(1,128)S(1)}, s32[1,1,32]{2,1,0:T(1,128)}, u32[]{:S(2)}) copy-start(s32[1,1,32]{2,1,0:T(1,128)} %param.20) | copy-start | bytes 388
  127.0 19.7 %collective-permute-start.12 = (bf16[256,384]{1,0:T(8,128)(2,1)}, bf16[256,384]{1,0:T(8,128)(2,1)S(1)}, u32[]{:S(2)}, u32[]{:S(2)}) collective-permute-start(bf16[256,384]{1,0:T(8,128)(2,1)} %get-tuple-element.35), channel_id=1, source_target_pairs={{0,1},{1,2},{2,3},{3,4},{4,5},{5,6},{6,7},{7,0},{8,9},{9,10},{10,1... | collective-permute-start | bytes 589832 | tf_op jit(solution)/shard_map/ppermute | solution.py:302
  130.0 19.4 %copy-start.10 = (bf16[256,256]{1,0:T(8,128)(2,1)S(1)}, bf16[256,256]{1,0:T(8,128)(2,1)}, u32[]{:S(2)}) copy-start(bf16[256,256]{1,0:T(8,128)(2,1)} %refs_6_.1) | copy-start | bytes 393220
  130.1 17.5 %collective-permute-start.16 = (bf16[256,384]{1,0:T(8,128)(2,1)}, bf16[256,384]{1,0:T(8,128)(2,1)S(1)}, u32[]{:S(2)}, u32[]{:S(2)}) collective-permute-start(bf16[256,384]{1,0:T(8,128)(2,1)} %get-tuple-element.37), channel_id=1, source_target_pairs={{0,15},{1,8},{2,9},{3,10},{4,11},{5,12},{6,13},{7,14},{8,7},{9,0},... | collective-permute-start | bytes 589832 | tf_op jit(solution)/shard_map/ppermute | solution.py:313
  137.7 11.7 %collective-permute-start.17 = (bf16[256,384]{1,0:T(8,128)(2,1)}, bf16[256,384]{1,0:T(8,128)(2,1)}, u32[]{:S(2)}, u32[]{:S(2)}) collective-permute-start(bf16[256,384]{1,0:T(8,128)(2,1)} %get-tuple-element.38), channel_id=1, source_target_pairs={{0,7},{1,0},{2,1},{3,2},{4,3},{5,4},{6,5},{7,6},{8,15},{9,8},{10,9... | collective-permute-start | bytes 589832 | tf_op jit(solution)/shard_map/ppermute | solution.py:302

commit v11 on v10

--- a/solution.py
+++ b/solution.py
@@ -13,6 +13,7 @@
 PAIR_COST = 100_000_000_000
 CLOSE_COST = 30_000_000_000
 CUT_COST = 2_000_000_000
+COLLECT_COST = 2_000_000
 
 
 def spec(space):
@@ -219,20 +220,6 @@
         copy.wait()
 
 
-def gather_kernel(blk_ref, live_ref, arrived_ref, total_ref):
-    total_ref[...] = jnp.zeros(total_ref.shape, F32)
-
-    def add(part, carried):
-        @pl.when(live_ref[part] > 0)
-        def _():
-            columns = pl.ds(pl.multiple_of(blk_ref[part] * TILE, TILE), TILE)
-            total_ref[:, columns] += arrived_ref[part].astype(F32)
-
-        return carried
-
-    lax.fori_loop(0, arrived_ref.shape[0], add, 0)
-
-
 def hop_kernel(grad_ref, mat_ref, arrived_ref, out_ref):
     term = product(grad_ref[...], mat_ref[...]) + arrived_ref[...].astype(F32)
     out_ref[...] = term.astype(BF)
@@ -257,13 +244,39 @@
     own_ref[...] = product(grad_ref[...], mat_ref[:, mine])
 
 
-def last_kernel(own_ref, *refs):
-    *arrived_refs, cut_ref, weight_ref, out_ref = refs
-    total = own_ref[...] + cut_ref[...]
+def collect_kernel(own_ref, *refs):
+    *arrived_refs, total_ref = refs
+    total = own_ref[...]
     for arrived_ref in arrived_refs:
         total += arrived_ref[...].astype(F32)
+    total_ref[...] = total
+
+
+def last_kernel(
+    blk_ref, live_ref, terms_ref, sum_hbm, weight_hbm, out_ref, total, collected, weight, sems
+):
+    loads = [
+        pltpu.make_async_copy(sum_hbm, collected, sems.at[0]),
+        pltpu.make_async_copy(weight_hbm, weight, sems.at[1]),
+    ]
+    for copy in loads:
+        copy.start()
+    total[...] = jnp.zeros(total.shape, F32)
+
+    def add(part, carried):
+        @pl.when(live_ref[part] > 0)
+        def _():
+            columns = pl.ds(pl.multiple_of(blk_ref[part] * TILE, TILE), TILE)
+            total[:, columns] += terms_ref[part].astype(F32)
+
+        return carried
+
+    lax.fori_loop(0, terms_ref.shape[0], add, 0)
+    for copy in loads:
+        copy.wait()
+    rows = (total[...] + collected[...]).T.astype(BF)
     out_ref[...] = lax.dot_general(
-        total.T.astype(BF), weight_ref[...], (((1,), (1,)), ((), ())), preferred_element_type=F32
+        rows, weight[...], (((1,), (1,)), ((), ())), preferred_element_type=F32
     ).astype(BF)
 
 
@@ -451,12 +464,27 @@
             right = along_ring(add_on(dense[hop - 1], right), 1)
         elif hop == 2:
             arrived += deliver(dense[hop - 1], right, 1, 0)
-    from_cuts = call(
-        gather_kernel, "gather", shape((width, rows), F32), [SMEM, SMEM, VMEM], VMEM, moved=2 << 20
-    )(send_to, is_live, returned)
+    collected = call(
+        collect_kernel,
+        "collect",
+        shape((width, rows), F32),
+        [VMEM] * (1 + len(arrived)),
+        VMEM,
+        flops=COLLECT_COST,
+    )(own, *arrived)
     grad_features = call(
-        last_kernel, "last", shape((rows, width), BF), [VMEM] * (3 + len(arrived)), VMEM
-    )(own, *arrived, from_cuts, weight)
+        last_kernel,
+        "last",
+        shape((rows, width), BF),
+        [SMEM, SMEM, VMEM, HBM, HBM],
+        VMEM,
+        [
+            pltpu.VMEM((width, rows), F32),
+            pltpu.VMEM((width, rows), F32),
+            pltpu.VMEM(weight.shape, BF),
+            pltpu.SemaphoreType.DMA((2,)),
+        ],
+    )(send_to, is_live, returned, in_hbm(collected), in_hbm(weight))
     return (hidden, grad_features)
 
 

time: 152 us -> 152 us (level)
  Pallas kernels: 25.9 us -> 23.7 us
    ppermute x2, waiting for transfers between devices: 0.89 us -> 6.81 us  [across_and_along(): return lax.ppermute(value, 'blk', moves)]
    all_to_all x1, waiting for transfers between devices: 3.67 us -> 0.01 us  [on_device(): lax.all_to_all(terms, 'dom', split_axis=0, concat_axis=0, tiled=True)]
  transfers between devices with their start and end apart: 20 -> 20, of which waited for: 9 -> 9; matrix products, arithmetic and copies ran while one was open for 2% -> 2% of each run, Pallas kernels for 12% -> 10%
where the time goes in v11:
time: 152 us; the launch traced here: 151 us
  starting transfers between devices  94.5 us (62%)
  waiting for transfers between devices  26.3 us (17%)
  Pallas kernels  23.7 us (16%)
  matrix products  3.25 us (2%)
  local copies, waits for them, and re-layouts  2.05 us (1%)
    ppermute x14, starting transfers between devices, along_ring(): return lax.ppermute(value, 'blk', moves)  61.5 us
    ppermute x14, waiting for transfers between devices, along_ring(): return lax.ppermute(value, 'blk', moves)  19.5 us
    ppermute x2, starting transfers between devices, across_and_along(): return lax.ppermute(value, 'blk', moves)  9.46 us
    ppermute x2, starting transfers between devices, across(): lax.ppermute(value, 'blk', [(i, (i + ring) % peers) for i in range(peers)])  8.86 us
    all_to_all x1, starting transfers between devices, on_device(): lax.all_to_all(outgoing, 'dom', split_axis=0, concat_axis=0, tiled=True)  7.8 us
    all_to_all x1, starting transfers between devices, on_device(): lax.all_to_all(terms, 'dom', split_axis=0, concat_axis=0, tiled=True)  6.9 us
    ppermute x2, waiting for transfers between devices, across_and_along(): return lax.ppermute(value, 'blk', moves)  6.81 us
    pallas_call x1, Pallas kernels, on_device(): call(middle_kernel, 'middle', (shape((rows, width), BF), shape((width, ro...  5.25 us
  transfers between devices with their start and end apart: 20, of which 9 were waited for; matrix products, arithmetic and copies ran while one was open for 2% of the time, Pallas kernels for 10%

profile of v11, /device:TPU:8, one launch (start us, length us, event | category | flops | bytes accessed | tf_op | source)
XLA Modules:
  0.0 151.1 jit_solution(12281258559956372039)
XLA Ops:
  0.6 1.2 project.1.own_ref.projected_ref
  1.9 4.9 %collective-permute-start = (bf16[384,256]{1,0:T(8,128)(2,1)S(1)}, bf16[384,256]{1,0:T(8,128)(2,1)S(1)}, u32[]{:S(2)}, u32[]{:S(2)}) collective-permute-start(bf16[384,256]{1,0:T(8,128)(2,1)S(1)} %project.1.own_ref.projected_ref), channel_id=1, source_target_pairs={{0,8},{1,9},{2,10},{3,11},{4,12},{5,13},{6,14},{7,15},{8,0},{9,1},... | collective-permute-start | bytes 589832 | tf_op jit(solution)/shard_map/ppermute | solution.py:329
  6.8 2.3 %fill.1 = bf16[32,128,256]{2,1,0:T(8,128)(2,1)} custom-call(s32[32]{0:T(128)} %bitcast.27, s32[32]{0:T(128)} %bitcast.29, bf16[384,256]{1,0:T(8,128)(2,1)S(1)} %project.1.own_ref.projected_ref), custom_call_target="tpu_custom_call" | custom-call | tf_op jit(solution)/shard_map/fill/pallas_call | solution.py:344
  9.1 7.8 %all-to-all-start = ((bf16[32,128,256]{2,1,0:T(8,128)(2,1)}), bf16[32,128,256]{2,1,0:T(8,128)(2,1)}, u32[]{:S(2)}, u32[]{:S(2)}) async-start(bf16[32,128,256]{2,1,0:T(8,128)(2,1)} %fill.1), calls=%async_computation | async-start | bytes 4194304 | tf_op jit(solution)/shard_map/all_to_all | solution.py:358
  17.0 0.0 copy-start.17
  17.0 0.0 copy-start.8
  17.0 0.0 copy-start.15
  17.0 0.8 pair.1
  17.8 10.9 %collective-permute-start.2 = (bf16[768,256]{1,0:T(8,128)(2,1)}, bf16[768,256]{1,0:T(8,128)(2,1)S(1)}, u32[]{:S(2)}, u32[]{:S(2)}) collective-permute-start(bf16[768,256]{1,0:T(8,128)(2,1)} %pair.1), channel_id=1, source_target_pairs={{0,7},{1,0},{2,1},{3,2},{4,3},{5,4},{6,5},{7,6},{8,15},{9,8},{10,9... | collective-permute-start | bytes 1179656 | tf_op jit(solution)/shard_map/ppermute | solution.py:315
  28.7 1.9 %collective-permute-start.1 = (bf16[768,256]{1,0:T(8,128)(2,1)}, bf16[768,256]{1,0:T(8,128)(2,1)S(1)}, u32[]{:S(2)}, u32[]{:S(2)}) collective-permute-start(bf16[768,256]{1,0:T(8,128)(2,1)} %pair.1), channel_id=1, source_target_pairs={{0,1},{1,2},{2,3},{3,4},{4,5},{5,6},{6,7},{7,0},{8,9},{9,10},{10,1... | collective-permute-start | bytes 1179656 | tf_op jit(solution)/shard_map/ppermute | solution.py:315
  30.7 0.1 copy.14
  30.8 0.1 reshape_squeeze.3.refs_0_
  30.9 0.0 copy-start.6
  30.9 0.0 copy-start.16
  30.9 2.8 %spread_cut.1.cut_hbm = bf16[8,384,512]{2,1,0:T(8,128)(2,1)} custom-call(s32[32]{0:T(128)S(1)} %bitcast.32, bf16[32,128,128]{2,1,0:T(8,128)(2,1)S(1)} %bitcast.26), custom_call_target="tpu_custom_call" | custom-call | bytes 6291456 | tf_op jit(solution)/shard_map/spread_cut/pallas_call | solution.py:368
  33.7 2.0 %spread.1 = (bf16[384,768]{1,0:T(8,128)(2,1)S(1)}, bf16[384,768]{1,0:T(8,128)(2,1)S(1)}, bf16[384,768]{1,0:T(8,128)(2,1)S(1)}, bf16[384,768]{1,0:T(8,128)(2,1)S(...) custom-call(s32[64]{0:T(128)S(1)} %reshape_squeeze.3.refs_0_, ...), custom_call_target="tpu_custom_call" | custom-call | bytes 10485760 | tf_op jit(solution)/shard_map/spread/pallas_call | solution.py:360
  35.7 2.0 %collective-permute-done.2 = bf16[768,256]{1,0:T(8,128)(2,1)S(1)} collective-permute-done((bf16[768,256]{1,0:T(8,128)(2,1)}, bf16[768,256]{1,0:T(8,128)(2,1)S(1)}, u32[]{:S(2)}, u32[]{:S(2)}) %collective-permute-start.2) | collective-permute-done | bytes 393248 | tf_op jit(solution)/shard_map/ppermute | solution.py:315
  37.7 5.5 %collective-permute-start.4 = (bf16[768,256]{1,0:T(8,128)(2,1)S(1)}, bf16[768,256]{1,0:T(8,128)(2,1)S(1)}, u32[]{:S(2)}, u32[]{:S(2)}) collective-permute-start(bf16[768,256]{1,0:T(8,128)(2,1)S(1)} %collective-permute-done.2), channel_id=1, source_target_pairs={{0,7},{1,0},{2,1},{3,2},{4,3},{5,4},{6,5},{7,6},{8,15},{9,8},{10,9... | collective-permute-start | bytes 1179656 | tf_op jit(solution)/shard_map/ppermute | solution.py:315
  43.2 1.9 %collective-permute-start.3 = (bf16[768,256]{1,0:T(8,128)(2,1)S(1)}, bf16[768,256]{1,0:T(8,128)(2,1)S(1)}, u32[]{:S(2)}, u32[]{:S(2)}) collective-permute-start(bf16[768,256]{1,0:T(8,128)(2,1)S(1)} %collective-permute-done.1), channel_id=1, source_target_pairs={{0,1},{1,2},{2,3},{3,4},{4,5},{5,6},{6,7},{7,0},{8,9},{9,10},{10,1... | collective-permute-start | bytes 1179656 | tf_op jit(solution)/shard_map/ppermute | solution.py:315
  45.2 0.3 fusion.3
  45.5 0.3 fusion.4
  45.8 1.3 fusion.2
  47.2 3.9 %collective-permute-done.4 = bf16[768,256]{1,0:T(8,128)(2,1)S(1)} collective-permute-done((bf16[768,256]{1,0:T(8,128)(2,1)S(1)}, bf16[768,256]{1,0:T(8,128)(2,1)S(1)}, u32[]{:S(2)}, u32[]{:S(2)}) %collective-permute-start.4) | collective-permute-done | bytes 393248 | tf_op jit(solution)/shard_map/ppermute | solution.py:315
  51.1 5.6 %collective-permute-start.6 = (bf16[768,256]{1,0:T(8,128)(2,1)S(1)}, bf16[768,256]{1,0:T(8,128)(2,1)S(1)}, u32[]{:S(2)}, u32[]{:S(2)}) collective-permute-start(bf16[768,256]{1,0:T(8,128)(2,1)S(1)} %collective-permute-done.4), channel_id=1, source_target_pairs={{0,7},{1,0},{2,1},{3,2},{4,3},{5,4},{6,5},{7,6},{8,15},{9,8},{10,9... | collective-permute-start | bytes 1179656 | tf_op jit(solution)/shard_map/ppermute | solution.py:315
  56.7 1.9 %collective-permute-start.5 = (bf16[768,256]{1,0:T(8,128)(2,1)S(1)}, bf16[768,256]{1,0:T(8,128)(2,1)S(1)}, u32[]{:S(2)}, u32[]{:S(2)}) collective-permute-start(bf16[768,256]{1,0:T(8,128)(2,1)S(1)} %collective-permute-done.3), channel_id=1, source_target_pairs={{0,1},{1,2},{2,3},{3,4},{4,5},{5,6},{6,7},{7,0},{8,9},{9,10},{10,1... | collective-permute-start | bytes 1179656 | tf_op jit(solution)/shard_map/ppermute | solution.py:315
  58.6 0.3 fusion.5
  58.9 0.3 fusion.1
  59.3 4.4 %collective-permute-done.6 = bf16[768,256]{1,0:T(8,128)(2,1)S(1)} collective-permute-done((bf16[768,256]{1,0:T(8,128)(2,1)S(1)}, bf16[768,256]{1,0:T(8,128)(2,1)S(1)}, u32[]{:S(2)}, u32[]{:S(2)}) %collective-permute-start.6) | collective-permute-done | bytes 393248 | tf_op jit(solution)/shard_map/ppermute | solution.py:315
  63.7 5.6 %collective-permute-start.7 = (bf16[768,256]{1,0:T(8,128)(2,1)S(1)}, bf16[768,256]{1,0:T(8,128)(2,1)S(1)}, u32[]{:S(2)}, u32[]{:S(2)}) collective-permute-start(bf16[768,256]{1,0:T(8,128)(2,1)S(1)} %collective-permute-done.6), channel_id=1, source_target_pairs={{0,7},{1,0},{2,1},{3,2},{4,3},{5,4},{6,5},{7,6},{8,15},{9,8},{10,9... | collective-permute-start | bytes 1179656 | tf_op jit(solution)/shard_map/ppermute | solution.py:315
  69.3 0.3 fusion.6
  69.6 0.3 fusion.sum_ref
  70.0 0.0 copy-start.14
  70.0 0.0 copy-start.11
  70.0 3.4 %cut_sum.1.cut_sum_ref = f32[384,256]{1,0:T(8,128)S(1)} custom-call(bf16[8,384,512]{2,1,0:T(8,128)(2,1)} %spread_cut.1.cut_hbm, bf16[32,128,256]{2,1,0:T(8,128)(2,1)} %all-to-all-done.far_hbm), custom_call_target="tpu_custom_call" | custom-call | flops 2000000000 | tf_op jit(solution)/shard_map/cut_sum/pallas_call | solution.py:391
  73.4 2.1 %collective-permute-done.7.last_ref = bf16[768,256]{1,0:T(8,128)(2,1)S(1)} collective-permute-done((bf16[768,256]{1,0:T(8,128)(2,1)S(1)}, bf16[768,256]{1,0:T(8,128)(2,1)S(1)}, u32[]{:S(2)}, u32[]{:S(2)}) %collective-permute-start.7) | collective-permute-done | bytes 393248 | tf_op jit(solution)/shard_map/ppermute | solution.py:315
  75.5 5.2 %middle.1 = (bf16[384,256]{1,0:T(8,128)(2,1)}, bf16[256,384]{1,0:T(8,128)(2,1)S(1)}, bf16[256,768]{1,0:T(8,128)(2,1)}, bf16[256,768]{1,0:T(8,128)(2,1)}, bf16[32,256,128]{2,1,0:T(8,128)(2,1)}) custom-call(f32[384,256]{1,0:T(8,128)S(1)} %fusion.sum_ref, f32[384,256]{1,0:T(8,128)S(1)} %cut_sum.1.cut_sum_ref, ...), custom_call_target="tpu_custom_call" | custom-call | tf_op jit(solution)/shard_map/middle/pallas_call | solution.py:405
  80.7 7.3 %collective-permute-start.13 = (bf16[256,768]{1,0:T(8,128)(2,1)}, bf16[256,768]{1,0:T(8,128)(2,1)}, u32[]{:S(2)}, u32[]{:S(2)}) collective-permute-start(bf16[256,768]{1,0:T(8,128)(2,1)} %get-tuple-element.37), channel_id=1, source_target_pairs={{0,7},{1,0},{2,1},{3,2},{4,3},{5,4},{6,5},{7,6},{8,15},{9,8},{10,9... | collective-permute-start | bytes 1179656 | tf_op jit(solution)/shard_map/ppermute | solution.py:315
  88.1 6.9 %all-to-all-start.1 = ((bf16[32,256,128]{2,1,0:T(8,128)(2,1)}), bf16[32,256,128]{2,1,0:T(8,128)(2,1)S(1)}, u32[]{:S(2)}, u32[]{:S(2)}) async-start(bf16[32,256,128]{2,1,0:T(8,128)(2,1)} %get-tuple-element.30), calls=%async_computation.1 | async-start | bytes 4194304 | tf_op jit(solution)/shard_map/all_to_all | solution.py:436
  95.0 1.9 %collective-permute-start.9 = (bf16[256,768]{1,0:T(8,128)(2,1)}, bf16[256,768]{1,0:T(8,128)(2,1)S(1)}, u32[]{:S(2)}, u32[]{:S(2)}) collective-permute-start(bf16[256,768]{1,0:T(8,128)(2,1)} %get-tuple-element.34), channel_id=1, source_target_pairs={{0,1},{1,2},{2,3},{3,4},{4,5},{5,6},{6,7},{7,0},{8,9},{9,10},{10,1... | collective-permute-start | bytes 1179656 | tf_op jit(solution)/shard_map/ppermute | solution.py:315
  96.9 1.1 copy-done.1
  98.0 1.4 hop.4
  99.4 5.4 %collective-permute-start.14 = (bf16[256,768]{1,0:T(8,128)(2,1)S(1)}, bf16[256,768]{1,0:T(8,128)(2,1)S(1)}, u32[]{:S(2)}, u32[]{:S(2)}) collective-permute-start(bf16[256,768]{1,0:T(8,128)(2,1)S(1)} %hop.4), channel_id=1, source_target_pairs={{0,7},{1,0},{2,1},{3,2},{4,3},{5,4},{6,5},{7,6},{8,15},{9,8},{10,9... | collective-permute-start | bytes 1179656 | tf_op jit(solution)/shard_map/ppermute | solution.py:315
  104.8 4.7 %collective-permute-done.9.arrived_ref = bf16[256,768]{1,0:T(8,128)(2,1)S(1)} collective-permute-done((bf16[256,768]{1,0:T(8,128)(2,1)}, bf16[256,768]{1,0:T(8,128)(2,1)S(1)}, u32[]{:S(2)}, u32[]{:S(2)}) %collective-permute-start.9) | collective-permute-done | bytes 393248 | tf_op jit(solution)/shard_map/ppermute | solution.py:315
  109.5 0.4 hop.3
  109.9 2.1 %collective-permute-start.10 = (bf16[256,768]{1,0:T(8,128)(2,1)S(1)}, bf16[256,768]{1,0:T(8,128)(2,1)S(1)}, u32[]{:S(2)}, u32[]{:S(2)}) collective-permute-start(bf16[256,768]{1,0:T(8,128)(2,1)S(1)} %hop.3), channel_id=1, source_target_pairs={{0,1},{1,2},{2,3},{3,4},{4,5},{5,6},{6,7},{7,0},{8,9},{9,10},{10,1... | collective-permute-start | bytes 1179656 | tf_op jit(solution)/shard_map/ppermute | solution.py:315
  111.9 1.2 collective-permute-done.14.arrived_ref
  113.1 0.4 hop.5
  113.5 5.6 %collective-permute-start.15 = (bf16[256,768]{1,0:T(8,128)(2,1)S(1)}, bf16[256,768]{1,0:T(8,128)(2,1)S(1)}, u32[]{:S(2)}, u32[]{:S(2)}) collective-permute-start(bf16[256,768]{1,0:T(8,128)(2,1)S(1)} %hop.5), channel_id=1, source_target_pairs={{0,7},{1,0},{2,1},{3,2},{4,3},{5,4},{6,5},{7,6},{8,15},{9,8},{10,9... | collective-permute-start | bytes 1179656 | tf_op jit(solution)/shard_map/ppermute | solution.py:315
  119.1 0.4 own_place.1
  119.5 3.9 %collective-permute-start.8 = (bf16[256,384]{1,0:T(8,128)(2,1)S(1)}, bf16[256,384]{1,0:T(8,128)(2,1)S(1)}, u32[]{:S(2)}, u32[]{:S(2)}) collective-permute-start(bf16[256,384]{1,0:T(8,128)(2,1)S(1)} %get-tuple-element.33), channel_id=1, source_target_pairs={{0,8},{1,9},{2,10},{3,11},{4,12},{5,13},{6,14},{7,15},{8,0},{9,1},... | collective-permute-start | bytes 589832 | tf_op jit(solution)/shard_map/ppermute | solution.py:329
  123.4 0.0 collective-permute-done.10.arrived_ref
  123.4 0.4 last_hop.2
  123.8 2.4 %collective-permute-start.11 = (bf16[256,384]{1,0:T(8,128)(2,1)S(1)}, bf16[256,384]{1,0:T(8,128)(2,1)S(1)}, u32[]{:S(2)}, u32[]{:S(2)}) collective-permute-start(bf16[256,384]{1,0:T(8,128)(2,1)S(1)} %get-tuple-element.35), channel_id=1, source_target_pairs={{0,9},{1,10},{2,11},{3,12},{4,13},{5,14},{6,15},{7,8},{8,1},{9,2},... | collective-permute-start | bytes 589832 | tf_op jit(solution)/shard_map/ppermute | solution.py:326
  126.3 0.0 copy-start.12
  126.3 1.9 %collective-permute-start.12 = (bf16[256,384]{1,0:T(8,128)(2,1)S(1)}, bf16[256,384]{1,0:T(8,128)(2,1)S(1)}, u32[]{:S(2)}, u32[]{:S(2)}) collective-permute-start(bf16[256,384]{1,0:T(8,128)(2,1)S(1)} %get-tuple-element.36), channel_id=1, source_target_pairs={{0,1},{1,2},{2,3},{3,4},{4,5},{5,6},{6,7},{7,0},{8,9},{9,10},{10,1... | collective-permute-start | bytes 589832 | tf_op jit(solution)/shard_map/ppermute | solution.py:315
  128.3 0.4 last_hop.3
  128.7 7.0 %collective-permute-start.16 = (bf16[256,384]{1,0:T(8,128)(2,1)S(1)}, bf16[256,384]{1,0:T(8,128)(2,1)S(1)}, u32[]{:S(2)}, u32[]{:S(2)}) collective-permute-start(bf16[256,384]{1,0:T(8,128)(2,1)S(1)} %get-tuple-element.38), channel_id=1, source_target_pairs={{0,15},{1,8},{2,9},{3,10},{4,11},{5,12},{6,13},{7,14},{8,7},{9,0},... | collective-permute-start | bytes 589832 | tf_op jit(solution)/shard_map/ppermute | solution.py:326
  135.7 3.9 %collective-permute-start.17 = (bf16[256,384]{1,0:T(8,128)(2,1)S(1)}, bf16[256,384]{1,0:T(8,128)(2,1)S(1)}, u32[]{:S(2)}, u32[]{:S(2)}) collective-permute-start(bf16[256,384]{1,0:T(8,128)(2,1)S(1)} %get-tuple-element.39), channel_id=1, source_target_pairs={{0,7},{1,0},{2,1},{3,2},{4,3},{5,4},{6,5},{7,6},{8,15},{9,8},{10,9... | collective-permute-start | bytes 589832 | tf_op jit(solution)/shard_map/ppermute | solution.py:315
  139.6 0.8 collective-permute-done.11.refs_1_
  140.4 6.1 %collective-permute-done.16.refs_3_ = bf16[256,384]{1,0:T(8,128)(2,1)S(1)} collective-permute-done((bf16[256,384]{1,0:T(8,128)(2,1)S(1)}, bf16[256,384]{1,0:T(8,128)(2,1)S(1)}, u32[]{:S(2)}, u32[]{:S(2)}) %collective-permute-start.16) | collective-permute-done | bytes 196640 | tf_op jit(solution)/shard_map/ppermute | solution.py:326
  146.4 1.2 collective-permute-done.17.refs_4_
  147.7 0.2 collect.1.sum_hbm
  147.8 0.7 copy-done.7
  148.6 2.5 %last.1 = bf16[384,256]{1,0:T(8,128)(2,1)} custom-call(s32[32]{0:T(128)S(1)} %bitcast.28, s32[32]{0:T(128)S(1)} %bitcast.30, bf16[32,256,128]{2,1,0:T(8,128)(2,1)S(1)} %all-to-all-done.1.terms_ref, f32[256,384]{1,0:T(8,128)} %copy-done.7, bf16[256,256]{1,0:T(8,128)(2,1)} %weight_hbm.3), custom_call_target="tpu_custom_call" | custom-call | tf_op jit(solution)/shard_map/last/pallas_call | solution.py:475
  (36 shorter events, 0.1 us)
Async XLA Ops:
  1.9 15.1 %collective-permute-start = (bf16[384,256]{1,0:T(8,128)(2,1)S(1)}, bf16[384,256]{1,0:T(8,128)(2,1)S(1)}, u32[]{:S(2)}, u32[]{:S(2)}) collective-permute-start(bf16[384,256]{1,0:T(8,128)(2,1)S(1)} %project.1.own_ref.projected_ref), channel_id=1, source_target_pairs={{0,8},{1,9},{2,10},{3,11},{4,12},{5,13},{6,14},{7,15},{8,0},{9,1},... | collective-permute-start | bytes 589832 | tf_op jit(solution)/shard_map/ppermute | solution.py:329
  9.1 60.8 %all-to-all-start = ((bf16[32,128,256]{2,1,0:T(8,128)(2,1)}), bf16[32,128,256]{2,1,0:T(8,128)(2,1)}, u32[]{:S(2)}, u32[]{:S(2)}) async-start(bf16[32,128,256]{2,1,0:T(8,128)(2,1)} %fill.1), calls=%async_computation | async-start | bytes 4194304 | tf_op jit(solution)/shard_map/all_to_all | solution.py:358
  17.0 13.7 %copy-start.17 = (s32[1,1,16,4]{2,3,1,0:T(4,128)S(1)}, s32[1,1,16,4]{2,3,1,0:T(4,128)}, u32[]{:S(2)}) copy-start(s32[1,1,16,4]{2,3,1,0:T(4,128)} %param.16) | copy-start | bytes 772
  17.0 13.9 %copy-start.8 = (bf16[1,1,32,128,128]{4,3,2,1,0:T(8,128)(2,1)S(1)}, bf16[1,1,32,128,128]{4,3,2,1,0:T(8,128)(2,1)}, u32[]{:S(2)}) copy-start(bf16[1,1,32,128,128]{4,3,2,1,0:T(8,128)(2,1)} %param.18) | copy-start | bytes 3145732
  17.0 13.9 %copy-start.15 = (s32[1,1,32]{2,1,0:T(1,128)S(1)}, s32[1,1,32]{2,1,0:T(1,128)}, u32[]{:S(2)}) copy-start(s32[1,1,32]{2,1,0:T(1,128)} %param.21) | copy-start | bytes 388
  17.8 19.9 %collective-permute-start.2 = (bf16[768,256]{1,0:T(8,128)(2,1)}, bf16[768,256]{1,0:T(8,128)(2,1)S(1)}, u32[]{:S(2)}, u32[]{:S(2)}) collective-permute-start(bf16[768,256]{1,0:T(8,128)(2,1)} %pair.1), channel_id=1, source_target_pairs={{0,7},{1,0},{2,1},{3,2},{4,3},{5,4},{6,5},{7,6},{8,15},{9,8},{10,9... | collective-permute-start | bytes 1179656 | tf_op jit(solution)/shard_map/ppermute | solution.py:315
  28.7 14.5 %collective-permute-start.1 = (bf16[768,256]{1,0:T(8,128)(2,1)}, bf16[768,256]{1,0:T(8,128)(2,1)S(1)}, u32[]{:S(2)}, u32[]{:S(2)}) collective-permute-start(bf16[768,256]{1,0:T(8,128)(2,1)} %pair.1), channel_id=1, source_target_pairs={{0,1},{1,2},{2,3},{3,4},{4,5},{5,6},{6,7},{7,0},{8,9},{9,10},{10,1... | collective-permute-start | bytes 1179656 | tf_op jit(solution)/shard_map/ppermute | solution.py:315
  30.9 2.8 %copy-start.6 = (bf16[1,1,16,4,128,128]{5,4,3,2,1,0:T(8,128)(2,1)S(1)}, bf16[1,1,16,4,128,128]{5,4,3,2,1,0:T(8,128)(2,1)}, u32[]{:S(2)}) copy-start(bf16[1,1,16,4,128,128]{5,4,3,2,1,0:T(8,128)(2,1)} %param.15) | copy-start | bytes 6291460
  30.9 2.8 %copy-start.16 = (s32[1,1,16]{2,1,0:T(1,128)S(1)}, s32[1,1,16]{2,1,0:T(1,128)}, u32[]{:S(2)}) copy-start(s32[1,1,16]{2,1,0:T(1,128)} %param.17) | copy-start | bytes 196
  35.7 11.5 %copy-start.2 = (bf16[384,768]{1,0:T(8,128)(2,1)}, bf16[384,768]{1,0:T(8,128)(2,1)S(1)}, u32[]{:S(2)}) copy-start(bf16[384,768]{1,0:T(8,128)(2,1)S(1)} %get-tuple-element.23.mat_ref) | copy-start | bytes 1769476
  35.7 11.5 %copy-start.4 = (bf16[384,768]{1,0:T(8,128)(2,1)}, bf16[384,768]{1,0:T(8,128)(2,1)S(1)}, u32[]{:S(2)}) copy-start(bf16[384,768]{1,0:T(8,128)(2,1)S(1)} %get-tuple-element.21.mat_ref) | copy-start | bytes 1769476
  35.7 11.5 %copy-start.9 = (bf16[384,768]{1,0:T(8,128)(2,1)}, bf16[384,768]{1,0:T(8,128)(2,1)S(1)}, u32[]{:S(2)}) copy-start(bf16[384,768]{1,0:T(8,128)(2,1)S(1)} %get-tuple-element.22.mat_ref) | copy-start | bytes 1769476
  35.7 33.9 %copy-start = (bf16[384,768]{1,0:T(8,128)(2,1)}, bf16[384,768]{1,0:T(8,128)(2,1)S(1)}, u32[]{:S(2)}) copy-start(bf16[384,768]{1,0:T(8,128)(2,1)S(1)} %get-tuple-element.26.mat_ref) | copy-start | bytes 1769476
  37.7 13.3 %collective-permute-start.4 = (bf16[768,256]{1,0:T(8,128)(2,1)S(1)}, bf16[768,256]{1,0:T(8,128)(2,1)S(1)}, u32[]{:S(2)}, u32[]{:S(2)}) collective-permute-start(bf16[768,256]{1,0:T(8,128)(2,1)S(1)} %collective-permute-done.2), channel_id=1, source_target_pairs={{0,7},{1,0},{2,1},{3,2},{4,3},{5,4},{6,5},{7,6},{8,15},{9,8},{10,9... | collective-permute-start | bytes 1179656 | tf_op jit(solution)/shard_map/ppermute | solution.py:315
  43.2 13.4 %collective-permute-start.3 = (bf16[768,256]{1,0:T(8,128)(2,1)S(1)}, bf16[768,256]{1,0:T(8,128)(2,1)S(1)}, u32[]{:S(2)}, u32[]{:S(2)}) collective-permute-start(bf16[768,256]{1,0:T(8,128)(2,1)S(1)} %collective-permute-done.1), channel_id=1, source_target_pairs={{0,1},{1,2},{2,3},{3,4},{4,5},{5,6},{6,7},{7,0},{8,9},{9,10},{10,1... | collective-permute-start | bytes 1179656 | tf_op jit(solution)/shard_map/ppermute | solution.py:315
  51.1 12.6 %collective-permute-start.6 = (bf16[768,256]{1,0:T(8,128)(2,1)S(1)}, bf16[768,256]{1,0:T(8,128)(2,1)S(1)}, u32[]{:S(2)}, u32[]{:S(2)}) collective-permute-start(bf16[768,256]{1,0:T(8,128)(2,1)S(1)} %collective-permute-done.4), channel_id=1, source_target_pairs={{0,7},{1,0},{2,1},{3,2},{4,3},{5,4},{6,5},{7,6},{8,15},{9,8},{10,9... | collective-permute-start | bytes 1179656 | tf_op jit(solution)/shard_map/ppermute | solution.py:315
  56.7 12.9 %collective-permute-start.5 = (bf16[768,256]{1,0:T(8,128)(2,1)S(1)}, bf16[768,256]{1,0:T(8,128)(2,1)S(1)}, u32[]{:S(2)}, u32[]{:S(2)}) collective-permute-start(bf16[768,256]{1,0:T(8,128)(2,1)S(1)} %collective-permute-done.3), channel_id=1, source_target_pairs={{0,1},{1,2},{2,3},{3,4},{4,5},{5,6},{6,7},{7,0},{8,9},{9,10},{10,1... | collective-permute-start | bytes 1179656 | tf_op jit(solution)/shard_map/ppermute | solution.py:315
  63.7 11.8 %collective-permute-start.7 = (bf16[768,256]{1,0:T(8,128)(2,1)S(1)}, bf16[768,256]{1,0:T(8,128)(2,1)S(1)}, u32[]{:S(2)}, u32[]{:S(2)}) collective-permute-start(bf16[768,256]{1,0:T(8,128)(2,1)S(1)} %collective-permute-done.6), channel_id=1, source_target_pairs={{0,7},{1,0},{2,1},{3,2},{4,3},{5,4},{6,5},{7,6},{8,15},{9,8},{10,9... | collective-permute-start | bytes 1179656 | tf_op jit(solution)/shard_map/ppermute | solution.py:315
  70.0 5.5 %copy-start.14 = (f32[256]{0:T(256)S(1)}, f32[256]{0:T(256)}, u32[]{:S(2)}) copy-start(f32[256]{0:T(256)} %param.13) | copy-start | bytes 3076
  70.0 5.5 %copy-start.11 = (bf16[384,256]{1,0:T(8,128)(2,1)S(1)}, bf16[384,256]{1,0:T(8,128)(2,1)}, u32[]{:S(2)}) copy-start(bf16[384,256]{1,0:T(8,128)(2,1)} %cotangent_ref.1) | copy-start | bytes 589828
  80.7 16.2 %collective-permute-start.13 = (bf16[256,768]{1,0:T(8,128)(2,1)}, bf16[256,768]{1,0:T(8,128)(2,1)}, u32[]{:S(2)}, u32[]{:S(2)}) collective-permute-start(bf16[256,768]{1,0:T(8,128)(2,1)} %get-tuple-element.37), channel_id=1, source_target_pairs={{0,7},{1,0},{2,1},{3,2},{4,3},{5,4},{6,5},{7,6},{8,15},{9,8},{10,9... | collective-permute-start | bytes 1179656 | tf_op jit(solution)/shard_map/ppermute | solution.py:315
  88.1 60.5 %all-to-all-start.1 = ((bf16[32,256,128]{2,1,0:T(8,128)(2,1)}), bf16[32,256,128]{2,1,0:T(8,128)(2,1)S(1)}, u32[]{:S(2)}, u32[]{:S(2)}) async-start(bf16[32,256,128]{2,1,0:T(8,128)(2,1)} %get-tuple-element.30), calls=%async_computation.1 | async-start | bytes 4194304 | tf_op jit(solution)/shard_map/all_to_all | solution.py:436
  95.0 14.5 %collective-permute-start.9 = (bf16[256,768]{1,0:T(8,128)(2,1)}, bf16[256,768]{1,0:T(8,128)(2,1)S(1)}, u32[]{:S(2)}, u32[]{:S(2)}) collective-permute-start(bf16[256,768]{1,0:T(8,128)(2,1)} %get-tuple-element.34), channel_id=1, source_target_pairs={{0,1},{1,2},{2,3},{3,4},{4,5},{5,6},{6,7},{7,0},{8,9},{9,10},{10,1... | collective-permute-start | bytes 1179656 | tf_op jit(solution)/shard_map/ppermute | solution.py:315
  96.9 1.1 copy-start.1
  98.0 21.1 %copy-start.5 = (bf16[384,768]{1,0:T(8,128)(2,1)S(1)}, bf16[384,768]{1,0:T(8,128)(2,1)}, u32[]{:S(2)}) copy-start(bf16[384,768]{1,0:T(8,128)(2,1)} %copy-done.4) | copy-start | bytes 1769476
  99.4 24.0 %copy-start.3 = (bf16[384,768]{1,0:T(8,128)(2,1)S(1)}, bf16[384,768]{1,0:T(8,128)(2,1)}, u32[]{:S(2)}) copy-start(bf16[384,768]{1,0:T(8,128)(2,1)} %copy-done.2) | copy-start | bytes 1769476
  99.4 13.7 %collective-permute-start.14 = (bf16[256,768]{1,0:T(8,128)(2,1)S(1)}, bf16[256,768]{1,0:T(8,128)(2,1)S(1)}, u32[]{:S(2)}, u32[]{:S(2)}) collective-permute-start(bf16[256,768]{1,0:T(8,128)(2,1)S(1)} %hop.4), channel_id=1, source_target_pairs={{0,7},{1,0},{2,1},{3,2},{4,3},{5,4},{6,5},{7,6},{8,15},{9,8},{10,9... | collective-permute-start | bytes 1179656 | tf_op jit(solution)/shard_map/ppermute | solution.py:315
  109.8 18.4 %copy-start.10 = (bf16[384,768]{1,0:T(8,128)(2,1)S(1)}, bf16[384,768]{1,0:T(8,128)(2,1)}, u32[]{:S(2)}) copy-start(bf16[384,768]{1,0:T(8,128)(2,1)} %copy-done.9) | copy-start | bytes 1769476
  109.9 13.6 %collective-permute-start.10 = (bf16[256,768]{1,0:T(8,128)(2,1)S(1)}, bf16[256,768]{1,0:T(8,128)(2,1)S(1)}, u32[]{:S(2)}, u32[]{:S(2)}) collective-permute-start(bf16[256,768]{1,0:T(8,128)(2,1)S(1)} %hop.3), channel_id=1, source_target_pairs={{0,1},{1,2},{2,3},{3,4},{4,5},{5,6},{6,7},{7,0},{8,9},{9,10},{10,1... | collective-permute-start | bytes 1179656 | tf_op jit(solution)/shard_map/ppermute | solution.py:315
  113.5 14.8 %collective-permute-start.15 = (bf16[256,768]{1,0:T(8,128)(2,1)S(1)}, bf16[256,768]{1,0:T(8,128)(2,1)S(1)}, u32[]{:S(2)}, u32[]{:S(2)}) collective-permute-start(bf16[256,768]{1,0:T(8,128)(2,1)S(1)} %hop.5), channel_id=1, source_target_pairs={{0,7},{1,0},{2,1},{3,2},{4,3},{5,4},{6,5},{7,6},{8,15},{9,8},{10,9... | collective-permute-start | bytes 1179656 | tf_op jit(solution)/shard_map/ppermute | solution.py:315
  119.5 20.1 %collective-permute-start.8 = (bf16[256,384]{1,0:T(8,128)(2,1)S(1)}, bf16[256,384]{1,0:T(8,128)(2,1)S(1)}, u32[]{:S(2)}, u32[]{:S(2)}) collective-permute-start(bf16[256,384]{1,0:T(8,128)(2,1)S(1)} %get-tuple-element.33), channel_id=1, source_target_pairs={{0,8},{1,9},{2,10},{3,11},{4,12},{5,13},{6,14},{7,15},{8,0},{9,1},... | collective-permute-start | bytes 589832 | tf_op jit(solution)/shard_map/ppermute | solution.py:329
  123.8 16.5 %collective-permute-start.11 = (bf16[256,384]{1,0:T(8,128)(2,1)S(1)}, bf16[256,384]{1,0:T(8,128)(2,1)S(1)}, u32[]{:S(2)}, u32[]{:S(2)}) collective-permute-start(bf16[256,384]{1,0:T(8,128)(2,1)S(1)} %get-tuple-element.35), channel_id=1, source_target_pairs={{0,9},{1,10},{2,11},{3,12},{4,13},{5,14},{6,15},{7,8},{8,1},{9,2},... | collective-permute-start | bytes 589832 | tf_op jit(solution)/shard_map/ppermute | solution.py:326
  126.3 22.3 %copy-start.12 = (s32[1,1,32]{2,1,0:T(1,128)S(1)}, s32[1,1,32]{2,1,0:T(1,128)}, u32[]{:S(2)}) copy-start(s32[1,1,32]{2,1,0:T(1,128)} %param.19) | copy-start | bytes 388
  126.3 22.3 %copy-start.13 = (s32[1,1,32]{2,1,0:T(1,128)S(1)}, s32[1,1,32]{2,1,0:T(1,128)}, u32[]{:S(2)}) copy-start(s32[1,1,32]{2,1,0:T(1,128)} %param.20) | copy-start | bytes 388
  126.3 14.1 %collective-permute-start.12 = (bf16[256,384]{1,0:T(8,128)(2,1)S(1)}, bf16[256,384]{1,0:T(8,128)(2,1)S(1)}, u32[]{:S(2)}, u32[]{:S(2)}) collective-permute-start(bf16[256,384]{1,0:T(8,128)(2,1)S(1)} %get-tuple-element.36), channel_id=1, source_target_pairs={{0,1},{1,2},{2,3},{3,4},{4,5},{5,6},{6,7},{7,0},{8,9},{9,10},{10,1... | collective-permute-start | bytes 589832 | tf_op jit(solution)/shard_map/ppermute | solution.py:315
  128.7 17.8 %collective-permute-start.16 = (bf16[256,384]{1,0:T(8,128)(2,1)S(1)}, bf16[256,384]{1,0:T(8,128)(2,1)S(1)}, u32[]{:S(2)}, u32[]{:S(2)}) collective-permute-start(bf16[256,384]{1,0:T(8,128)(2,1)S(1)} %get-tuple-element.38), channel_id=1, source_target_pairs={{0,15},{1,8},{2,9},{3,10},{4,11},{5,12},{6,13},{7,14},{8,7},{9,0},... | collective-permute-start | bytes 589832 | tf_op jit(solution)/shard_map/ppermute | solution.py:326
  135.7 12.0 %collective-permute-start.17 = (bf16[256,384]{1,0:T(8,128)(2,1)S(1)}, bf16[256,384]{1,0:T(8,128)(2,1)S(1)}, u32[]{:S(2)}, u32[]{:S(2)}) collective-permute-start(bf16[256,384]{1,0:T(8,128)(2,1)S(1)} %get-tuple-element.39), channel_id=1, source_target_pairs={{0,7},{1,0},{2,1},{3,2},{4,3},{5,4},{6,5},{7,6},{8,15},{9,8},{10,9... | collective-permute-start | bytes 589832 | tf_op jit(solution)/shard_map/ppermute | solution.py:315
  147.8 0.7 copy-start.7

commit v12 on v6

--- a/solution.py
+++ b/solution.py
@@ -238,7 +238,9 @@
     out_ref[...] = term.astype(BF)
 
 
-def close_kernel(half_ref, grad_ref, mat_ref, left_ref, right_ref, own_ref, other_ref):
+def close_kernel(
+    half_ref, grad_ref, mat_ref, left_ref, right_ref, own_ref, upper_ref, lower_ref
+):
     rows = grad_ref.shape[1]
     mine = pl.ds(pl.multiple_of(half_ref[0] * rows, TILE), rows)
     theirs = pl.ds(pl.multiple_of((1 - half_ref[0]) * rows, TILE), rows)
@@ -247,12 +249,16 @@
         arrived = left_ref[:, columns].astype(F32) + right_ref[:, columns].astype(F32)
         return product(grad_ref[...], mat_ref[:, columns]) + arrived
 
-    other_ref[...] = total(theirs).astype(BF)
+    middle = upper_ref.shape[0]
+    other = total(theirs).astype(BF)
+    upper_ref[...] = other[:middle]
+    lower_ref[...] = other[middle:]
     own_ref[...] = total(mine)
 
 
-def last_kernel(own_ref, other_ref, cut_ref, weight_ref, out_ref):
-    total = own_ref[...] + other_ref[...].astype(F32) + cut_ref[...]
+def last_kernel(own_ref, upper_ref, lower_ref, cut_ref, weight_ref, out_ref):
+    other = jnp.concatenate([upper_ref[...], lower_ref[...]]).astype(F32)
+    total = own_ref[...] + other + cut_ref[...]
     out_ref[...] = lax.dot_general(
         total.T.astype(BF), weight_ref[...], (((1,), (1,)), ((), ())), preferred_element_type=F32
     ).astype(BF)
@@ -405,21 +411,21 @@
         left = along_ring(add_on(dense[ring - hop], left), -1)
         if hop > 1:
             right = along_ring(add_on(dense[hop - 1], right), 1)
-    own, other = call(
+    own, upper, lower = call(
         close_kernel,
         "close",
-        (shape((width, rows), F32), shape((width, rows), BF)),
+        (shape((width, rows), F32),) + (shape((width // 2, rows), BF),) * 2,
         [SMEM] + [VMEM] * 4,
-        (VMEM, VMEM),
+        (VMEM,) * 3,
         flops=CLOSE_COST,
     )(half.reshape(1), grad_pre, dense[0], right, left)
-    other = across(other)
+    upper, lower = across(upper), across(lower)
     from_cuts = call(
         gather_kernel, "gather", shape((width, rows), F32), [SMEM, SMEM, VMEM], VMEM, moved=2 << 20
     )(send_to, is_live, returned)
     grad_features = call(
-        last_kernel, "last", shape((rows, width), BF), [VMEM] * 4, VMEM
-    )(own, other, from_cuts, weight)
+        last_kernel, "last", shape((rows, width), BF), [VMEM] * 5, VMEM
+    )(own, upper, lower, from_cuts, weight)
     return (hidden, grad_features)
 
 

time: 150 us -> 153 us (1.020)
  starting transfers between devices: 87.5 us -> 90.6 us
  matrix products: 5.26 us -> 2.25 us
  waiting for transfers between devices: 29 us -> 31.4 us
    all_to_all x1, waiting for transfers between devices: 3.64 us -> 0.48 us  [on_device(): lax.all_to_all(terms, 'dom', split_axis=0, concat_axis=0, tiled=True)]
    ppermute x2 -> x3, starting transfers between devices: 9.24 us -> 12.4 us  [across(): lax.ppermute(value, 'blk', [(i, (i + ring) % peers) for i in range(peers)])]
    ppermute x14, waiting for transfers between devices: 24.6 us -> 27.7 us  [along_ring(): return lax.ppermute(value, 'blk', moves)]
    dot_general x7, matrix products: 5.26 us -> 2.25 us  [product(): return jnp.dot(left, right, preferred_element_type=F32)]
    ppermute x2 -> x3, waiting for transfers between devices: 0.75 us -> 3.18 us  [across(): lax.ppermute(value, 'blk', [(i, (i + ring) % peers) for i in range(peers)])]
  transfers between devices with their start and end apart: 18 -> 19, of which waited for: 10 -> 10; matrix products, arithmetic and copies ran while one was open for 4% -> 2% of each run, Pallas kernels for 10% -> 10%
where the time goes in v12:
time: 153 us; the launch traced here: 150 us
  starting transfers between devices  90.6 us (59%)
  waiting for transfers between devices  31.4 us (21%)
  Pallas kernels  22.2 us (15%)
  local copies, waits for them, and re-layouts  2.38 us (2%)
  matrix products  2.25 us (1%)
    ppermute x14, starting transfers between devices, along_ring(): return lax.ppermute(value, 'blk', moves)  61.5 us
    ppermute x14, waiting for transfers between devices, along_ring(): return lax.ppermute(value, 'blk', moves)  27.7 us
    ppermute x3, starting transfers between devices, across(): lax.ppermute(value, 'blk', [(i, (i + ring) % peers) for i in range(peers)])  12.4 us
    all_to_all x1, starting transfers between devices, on_device(): lax.all_to_all(terms, 'dom', split_axis=0, concat_axis=0, tiled=True)  8.39 us
    all_to_all x1, starting transfers between devices, on_device(): lax.all_to_all(outgoing, 'dom', split_axis=0, concat_axis=0, tiled=True)  8.3 us
    pallas_call x1, Pallas kernels, on_device(): call(middle_kernel, 'middle', (shape((rows, width), BF), shape((width, ro...  5.23 us
    pallas_call x1, Pallas kernels, on_device(): call(cut_sum_kernel, 'cut_sum', shape((rows, width), F32), [HBM, HBM], VM...  3.38 us
    ppermute x3, waiting for transfers between devices, across(): lax.ppermute(value, 'blk', [(i, (i + ring) % peers) for i in range(peers)])  3.18 us
  transfers between devices with their start and end apart: 19, of which 10 were waited for; matrix products, arithmetic and copies ran while one was open for 2% of the time, Pallas kernels for 10%

profile of v12, /device:TPU:1, one launch (start us, length us, event | category | flops | bytes accessed | tf_op | source)
XLA Modules:
  0.0 150.1 jit_solution(5335510995256459143)
XLA Ops:
  0.6 1.2 project.1.own_ref.projected_ref
  1.9 5.5 %collective-permute-start = (bf16[384,256]{1,0:T(8,128)(2,1)S(1)}, bf16[384,256]{1,0:T(8,128)(2,1)S(1)}, u32[]{:S(2)}, u32[]{:S(2)}) collective-permute-start(bf16[384,256]{1,0:T(8,128)(2,1)S(1)} %project.1.own_ref.projected_ref), channel_id=1, source_target_pairs={{0,8},{1,9},{2,10},{3,11},{4,12},{5,13},{6,14},{7,15},{8,0},{9,1},... | collective-permute-start | bytes 589832 | tf_op jit(solution)/shard_map/ppermute | solution.py:302
  7.4 2.3 %fill.1 = bf16[32,128,256]{2,1,0:T(8,128)(2,1)} custom-call(s32[32]{0:T(128)} %bitcast.27, s32[32]{0:T(128)} %bitcast.29, bf16[384,256]{1,0:T(8,128)(2,1)S(1)} %project.1.own_ref.projected_ref), custom_call_target="tpu_custom_call" | custom-call | tf_op jit(solution)/shard_map/fill/pallas_call | solution.py:317
  9.7 8.3 %all-to-all-start = ((bf16[32,128,256]{2,1,0:T(8,128)(2,1)}), bf16[32,128,256]{2,1,0:T(8,128)(2,1)}, u32[]{:S(2)}, u32[]{:S(2)}) async-start(bf16[32,128,256]{2,1,0:T(8,128)(2,1)} %fill.1), calls=%async_computation | async-start | bytes 4194304 | tf_op jit(solution)/shard_map/all_to_all | solution.py:331
  18.0 0.0 copy-start.17
  18.0 0.0 copy-start.7
  18.0 0.0 copy-start.15
  18.1 10.8 %collective-permute-start.2 = (bf16[768,256]{1,0:T(8,128)(2,1)S(1)}, bf16[768,256]{1,0:T(8,128)(2,1)S(1)}, u32[]{:S(2)}, u32[]{:S(2)}) collective-permute-start(bf16[768,256]{1,0:T(8,128)(2,1)S(1)} %pair.1), channel_id=1, source_target_pairs={{0,7},{1,0},{2,1},{3,2},{4,3},{5,4},{6,5},{7,6},{8,15},{9,8},{10,9... | collective-permute-start | bytes 1179656 | tf_op jit(solution)/shard_map/ppermute | solution.py:299
  28.9 1.9 %collective-permute-start.1 = (bf16[768,256]{1,0:T(8,128)(2,1)S(1)}, bf16[768,256]{1,0:T(8,128)(2,1)S(1)}, u32[]{:S(2)}, u32[]{:S(2)}) collective-permute-start(bf16[768,256]{1,0:T(8,128)(2,1)S(1)} %pair.1), channel_id=1, source_target_pairs={{0,1},{1,2},{2,3},{3,4},{4,5},{5,6},{6,7},{7,0},{8,9},{9,10},{10,1... | collective-permute-start | bytes 1179656 | tf_op jit(solution)/shard_map/ppermute | solution.py:299
  30.8 0.1 copy.14
  30.9 0.1 reshape_squeeze.3.refs_0_
  31.0 0.0 copy-start.6
  31.1 0.0 copy-start.16
  31.1 2.8 %spread_cut.1.cut_hbm = bf16[8,384,512]{2,1,0:T(8,128)(2,1)} custom-call(s32[32]{0:T(128)S(1)} %bitcast.32, bf16[32,128,128]{2,1,0:T(8,128)(2,1)S(1)} %bitcast.26), custom_call_target="tpu_custom_call" | custom-call | bytes 6291456 | tf_op jit(solution)/shard_map/spread_cut/pallas_call | solution.py:341
  33.8 1.8 %spread.1 = (bf16[384,768]{1,0:T(8,128)(2,1)S(1)}, bf16[384,768]{1,0:T(8,128)(2,1)S(1)}, bf16[384,768]{1,0:T(8,128)(2,1)S(1)}, bf16[384,768]{1,0:T(8,128)(2,1)S(...) custom-call(s32[64]{0:T(128)S(1)} %reshape_squeeze.3.refs_0_, ...), custom_call_target="tpu_custom_call" | custom-call | bytes 10485760 | tf_op jit(solution)/shard_map/spread/pallas_call | solution.py:333
  35.7 1.4 collective-permute-done.2
  37.1 5.4 %collective-permute-start.4 = (bf16[768,256]{1,0:T(8,128)(2,1)S(1)}, bf16[768,256]{1,0:T(8,128)(2,1)S(1)}, u32[]{:S(2)}, u32[]{:S(2)}) collective-permute-start(bf16[768,256]{1,0:T(8,128)(2,1)S(1)} %collective-permute-done.2), channel_id=1, source_target_pairs={{0,7},{1,0},{2,1},{3,2},{4,3},{5,4},{6,5},{7,6},{8,15},{9,8},{10,9... | collective-permute-start | bytes 1179656 | tf_op jit(solution)/shard_map/ppermute | solution.py:299
  42.5 1.9 %collective-permute-start.3 = (bf16[768,256]{1,0:T(8,128)(2,1)S(1)}, bf16[768,256]{1,0:T(8,128)(2,1)S(1)}, u32[]{:S(2)}, u32[]{:S(2)}) collective-permute-start(bf16[768,256]{1,0:T(8,128)(2,1)S(1)} %collective-permute-done.1), channel_id=1, source_target_pairs={{0,1},{1,2},{2,3},{3,4},{4,5},{5,6},{6,7},{7,0},{8,9},{9,10},{10,1... | collective-permute-start | bytes 1179656 | tf_op jit(solution)/shard_map/ppermute | solution.py:299
  44.4 0.3 fusion.3
  44.8 0.3 fusion.4
  45.1 0.3 fusion.2
  45.4 4.4 %collective-permute-done.4 = bf16[768,256]{1,0:T(8,128)(2,1)S(1)} collective-permute-done((bf16[768,256]{1,0:T(8,128)(2,1)S(1)}, bf16[768,256]{1,0:T(8,128)(2,1)S(1)}, u32[]{:S(2)}, u32[]{:S(2)}) %collective-permute-start.4) | collective-permute-done | bytes 393248 | tf_op jit(solution)/shard_map/ppermute | solution.py:299
  49.8 5.4 %collective-permute-start.6 = (bf16[768,256]{1,0:T(8,128)(2,1)S(1)}, bf16[768,256]{1,0:T(8,128)(2,1)S(1)}, u32[]{:S(2)}, u32[]{:S(2)}) collective-permute-start(bf16[768,256]{1,0:T(8,128)(2,1)S(1)} %collective-permute-done.4), channel_id=1, source_target_pairs={{0,7},{1,0},{2,1},{3,2},{4,3},{5,4},{6,5},{7,6},{8,15},{9,8},{10,9... | collective-permute-start | bytes 1179656 | tf_op jit(solution)/shard_map/ppermute | solution.py:299
  55.3 1.9 %collective-permute-start.5 = (bf16[768,256]{1,0:T(8,128)(2,1)S(1)}, bf16[768,256]{1,0:T(8,128)(2,1)S(1)}, u32[]{:S(2)}, u32[]{:S(2)}) collective-permute-start(bf16[768,256]{1,0:T(8,128)(2,1)S(1)} %collective-permute-done.3), channel_id=1, source_target_pairs={{0,1},{1,2},{2,3},{3,4},{4,5},{5,6},{6,7},{7,0},{8,9},{9,10},{10,1... | collective-permute-start | bytes 1179656 | tf_op jit(solution)/shard_map/ppermute | solution.py:299
  57.2 0.3 fusion.5
  57.5 0.3 fusion.1
  57.9 3.9 %collective-permute-done.6 = bf16[768,256]{1,0:T(8,128)(2,1)S(1)} collective-permute-done((bf16[768,256]{1,0:T(8,128)(2,1)S(1)}, bf16[768,256]{1,0:T(8,128)(2,1)S(1)}, u32[]{:S(2)}, u32[]{:S(2)}) %collective-permute-start.6) | collective-permute-done | bytes 393248 | tf_op jit(solution)/shard_map/ppermute | solution.py:299
  61.8 5.4 %collective-permute-start.7 = (bf16[768,256]{1,0:T(8,128)(2,1)S(1)}, bf16[768,256]{1,0:T(8,128)(2,1)S(1)}, u32[]{:S(2)}, u32[]{:S(2)}) collective-permute-start(bf16[768,256]{1,0:T(8,128)(2,1)S(1)} %collective-permute-done.6), channel_id=1, source_target_pairs={{0,7},{1,0},{2,1},{3,2},{4,3},{5,4},{6,5},{7,6},{8,15},{9,8},{10,9... | collective-permute-start | bytes 1179656 | tf_op jit(solution)/shard_map/ppermute | solution.py:299
  67.2 0.3 fusion.6
  67.6 0.3 fusion.sum_ref
  67.9 0.0 copy-start.14
  67.9 0.0 copy-start.11
  67.9 3.4 %cut_sum.1.cut_sum_ref = f32[384,256]{1,0:T(8,128)S(1)} custom-call(bf16[8,384,512]{2,1,0:T(8,128)(2,1)} %spread_cut.1.cut_hbm, bf16[32,128,256]{2,1,0:T(8,128)(2,1)} %all-to-all-done.far_hbm), custom_call_target="tpu_custom_call" | custom-call | flops 2000000000 | tf_op jit(solution)/shard_map/cut_sum/pallas_call | solution.py:364
  71.3 1.6 %collective-permute-done.7.last_ref = bf16[768,256]{1,0:T(8,128)(2,1)S(1)} collective-permute-done((bf16[768,256]{1,0:T(8,128)(2,1)S(1)}, bf16[768,256]{1,0:T(8,128)(2,1)S(1)}, u32[]{:S(2)}, u32[]{:S(2)}) %collective-permute-start.7) | collective-permute-done | bytes 393248 | tf_op jit(solution)/shard_map/ppermute | solution.py:299
  72.9 5.2 %middle.1 = (bf16[384,256]{1,0:T(8,128)(2,1)}, bf16[256,384]{1,0:T(8,128)(2,1)S(1)}, bf16[256,768]{1,0:T(8,128)(2,1)}, bf16[256,768]{1,0:T(8,128)(2,1)}, bf16[32,256,128]{2,1,0:T(8,128)(2,1)}) custom-call(f32[384,256]{1,0:T(8,128)S(1)} %fusion.sum_ref, f32[384,256]{1,0:T(8,128)S(1)} %cut_sum.1.cut_sum_ref, ...), custom_call_target="tpu_custom_call" | custom-call | tf_op jit(solution)/shard_map/middle/pallas_call | solution.py:378
  78.2 8.6 %collective-permute-start.11 = (bf16[256,768]{1,0:T(8,128)(2,1)}, bf16[256,768]{1,0:T(8,128)(2,1)}, u32[]{:S(2)}, u32[]{:S(2)}) collective-permute-start(bf16[256,768]{1,0:T(8,128)(2,1)} %get-tuple-element.29), channel_id=1, source_target_pairs={{0,7},{1,0},{2,1},{3,2},{4,3},{5,4},{6,5},{7,6},{8,15},{9,8},{10,9... | collective-permute-start | bytes 1179656 | tf_op jit(solution)/shard_map/ppermute | solution.py:299
  86.8 8.4 %all-to-all-start.1 = ((bf16[32,256,128]{2,1,0:T(8,128)(2,1)}), bf16[32,256,128]{2,1,0:T(8,128)(2,1)S(1)}, u32[]{:S(2)}, u32[]{:S(2)}) async-start(bf16[32,256,128]{2,1,0:T(8,128)(2,1)} %get-tuple-element.33), calls=%async_computation.1 | async-start | bytes 4194304 | tf_op jit(solution)/shard_map/all_to_all | solution.py:409
  95.2 2.1 %collective-permute-start.8 = (bf16[256,768]{1,0:T(8,128)(2,1)}, bf16[256,768]{1,0:T(8,128)(2,1)S(1)}, u32[]{:S(2)}, u32[]{:S(2)}) collective-permute-start(bf16[256,768]{1,0:T(8,128)(2,1)} %get-tuple-element.28), channel_id=1, source_target_pairs={{0,1},{1,2},{2,3},{3,4},{4,5},{5,6},{6,7},{7,0},{8,9},{9,10},{10,1... | collective-permute-start | bytes 1179656 | tf_op jit(solution)/shard_map/ppermute | solution.py:299
  97.3 1.1 copy-done.5
  98.3 1.4 hop.7
  99.7 4.6 %collective-permute-start.12 = (bf16[256,768]{1,0:T(8,128)(2,1)S(1)}, bf16[256,768]{1,0:T(8,128)(2,1)S(1)}, u32[]{:S(2)}, u32[]{:S(2)}) collective-permute-start(bf16[256,768]{1,0:T(8,128)(2,1)S(1)} %hop.7), channel_id=1, source_target_pairs={{0,7},{1,0},{2,1},{3,2},{4,3},{5,4},{6,5},{7,6},{8,15},{9,8},{10,9... | collective-permute-start | bytes 1179656 | tf_op jit(solution)/shard_map/ppermute | solution.py:299
  104.3 4.8 %collective-permute-done.8.arrived_ref = bf16[256,768]{1,0:T(8,128)(2,1)S(1)} collective-permute-done((bf16[256,768]{1,0:T(8,128)(2,1)}, bf16[256,768]{1,0:T(8,128)(2,1)S(1)}, u32[]{:S(2)}, u32[]{:S(2)}) %collective-permute-start.8) | collective-permute-done | bytes 393248 | tf_op jit(solution)/shard_map/ppermute | solution.py:299
  109.1 1.1 copy-done.3
  110.2 0.4 hop.5
  110.6 2.1 %collective-permute-start.9 = (bf16[256,768]{1,0:T(8,128)(2,1)S(1)}, bf16[256,768]{1,0:T(8,128)(2,1)S(1)}, u32[]{:S(2)}, u32[]{:S(2)}) collective-permute-start(bf16[256,768]{1,0:T(8,128)(2,1)S(1)} %hop.5), channel_id=1, source_target_pairs={{0,1},{1,2},{2,3},{3,4},{4,5},{5,6},{6,7},{7,0},{8,9},{9,10},{10,1... | collective-permute-start | bytes 1179656 | tf_op jit(solution)/shard_map/ppermute | solution.py:299
  112.6 0.4 hop.8
  113.0 4.9 %collective-permute-start.13 = (bf16[256,768]{1,0:T(8,128)(2,1)S(1)}, bf16[256,768]{1,0:T(8,128)(2,1)S(1)}, u32[]{:S(2)}, u32[]{:S(2)}) collective-permute-start(bf16[256,768]{1,0:T(8,128)(2,1)S(1)} %hop.8), channel_id=1, source_target_pairs={{0,7},{1,0},{2,1},{3,2},{4,3},{5,4},{6,5},{7,6},{8,15},{9,8},{10,9... | collective-permute-start | bytes 1179656 | tf_op jit(solution)/shard_map/ppermute | solution.py:299
  117.9 5.4 %collective-permute-done.9.arrived_ref = bf16[256,768]{1,0:T(8,128)(2,1)S(1)} collective-permute-done((bf16[256,768]{1,0:T(8,128)(2,1)S(1)}, bf16[256,768]{1,0:T(8,128)(2,1)S(1)}, u32[]{:S(2)}, u32[]{:S(2)}) %collective-permute-start.9) | collective-permute-done | bytes 393248 | tf_op jit(solution)/shard_map/ppermute | solution.py:299
  123.4 0.4 hop.6
  123.7 1.9 %collective-permute-start.10 = (bf16[256,768]{1,0:T(8,128)(2,1)S(1)}, bf16[256,768]{1,0:T(8,128)(2,1)S(1)}, u32[]{:S(2)}, u32[]{:S(2)}) collective-permute-start(bf16[256,768]{1,0:T(8,128)(2,1)S(1)} %hop.6), channel_id=1, source_target_pairs={{0,1},{1,2},{2,3},{3,4},{4,5},{5,6},{6,7},{7,0},{8,9},{9,10},{10,1... | collective-permute-start | bytes 1179656 | tf_op jit(solution)/shard_map/ppermute | solution.py:299
  125.7 0.4 hop.9
  126.0 0.0 copy-start.12
  126.0 0.0 copy-start.13
  126.1 4.6 %collective-permute-start.14 = (bf16[256,768]{1,0:T(8,128)(2,1)S(1)}, bf16[256,768]{1,0:T(8,128)(2,1)S(1)}, u32[]{:S(2)}, u32[]{:S(2)}) collective-permute-start(bf16[256,768]{1,0:T(8,128)(2,1)S(1)} %hop.9), channel_id=1, source_target_pairs={{0,7},{1,0},{2,1},{3,2},{4,3},{5,4},{6,5},{7,6},{8,15},{9,8},{10,9... | collective-permute-start | bytes 1179656 | tf_op jit(solution)/shard_map/ppermute | solution.py:299
  130.7 4.8 %collective-permute-done.10.left_ref = bf16[256,768]{1,0:T(8,128)(2,1)S(1)} collective-permute-done((bf16[256,768]{1,0:T(8,128)(2,1)S(1)}, bf16[256,768]{1,0:T(8,128)(2,1)S(1)}, u32[]{:S(2)}, u32[]{:S(2)}) %collective-permute-start.10) | collective-permute-done | bytes 393248 | tf_op jit(solution)/shard_map/ppermute | solution.py:299
  135.5 1.3 collective-permute-done.14.right_ref
  136.8 0.4 close.1
  137.2 0.0 copy-start.10
  137.2 3.8 %collective-permute-start.15 = (bf16[128,384]{1,0:T(8,128)(2,1)S(1)}, bf16[128,384]{1,0:T(8,128)(2,1)S(1)}, u32[]{:S(2)}, u32[]{:S(2)}) collective-permute-start(bf16[128,384]{1,0:T(8,128)(2,1)S(1)} %get-tuple-element.31), channel_id=1, source_target_pairs={{0,8},{1,9},{2,10},{3,11},{4,12},{5,13},{6,14},{7,15},{8,0},{9,1},... | collective-permute-start | bytes 294920 | tf_op jit(solution)/shard_map/ppermute | solution.py:302
  140.9 3.2 %collective-permute-start.16 = (bf16[128,384]{1,0:T(8,128)(2,1)S(1)}, bf16[128,384]{1,0:T(8,128)(2,1)S(1)}, u32[]{:S(2)}, u32[]{:S(2)}) collective-permute-start(bf16[128,384]{1,0:T(8,128)(2,1)S(1)} %get-tuple-element.32), channel_id=1, source_target_pairs={{0,8},{1,9},{2,10},{3,11},{4,12},{5,13},{6,14},{7,15},{8,0},{9,1},... | collective-permute-start | bytes 294920 | tf_op jit(solution)/shard_map/ppermute | solution.py:302
  144.1 0.5 all-to-all-done.1.arrived_ref
  144.6 1.3 gather.1.cut_ref
  145.9 3.2 %collective-permute-done.16.lower_ref = bf16[128,384]{1,0:T(8,128)(2,1)S(1)} collective-permute-done((bf16[128,384]{1,0:T(8,128)(2,1)S(1)}, bf16[128,384]{1,0:T(8,128)(2,1)S(1)}, u32[]{:S(2)}, u32[]{:S(2)}) %collective-permute-start.16) | collective-permute-done | bytes 98336 | tf_op jit(solution)/shard_map/ppermute | solution.py:302
  149.1 1.0 last.1
  (34 shorter events, 0.1 us)
Async XLA Ops:
  1.9 16.1 %collective-permute-start = (bf16[384,256]{1,0:T(8,128)(2,1)S(1)}, bf16[384,256]{1,0:T(8,128)(2,1)S(1)}, u32[]{:S(2)}, u32[]{:S(2)}) collective-permute-start(bf16[384,256]{1,0:T(8,128)(2,1)S(1)} %project.1.own_ref.projected_ref), channel_id=1, source_target_pairs={{0,8},{1,9},{2,10},{3,11},{4,12},{5,13},{6,14},{7,15},{8,0},{9,1},... | collective-permute-start | bytes 589832 | tf_op jit(solution)/shard_map/ppermute | solution.py:302
  9.7 58.2 %all-to-all-start = ((bf16[32,128,256]{2,1,0:T(8,128)(2,1)}), bf16[32,128,256]{2,1,0:T(8,128)(2,1)}, u32[]{:S(2)}, u32[]{:S(2)}) async-start(bf16[32,128,256]{2,1,0:T(8,128)(2,1)} %fill.1), calls=%async_computation | async-start | bytes 4194304 | tf_op jit(solution)/shard_map/all_to_all | solution.py:331
  18.0 12.8 %copy-start.17 = (s32[1,1,16,4]{2,3,1,0:T(4,128)S(1)}, s32[1,1,16,4]{2,3,1,0:T(4,128)}, u32[]{:S(2)}) copy-start(s32[1,1,16,4]{2,3,1,0:T(4,128)} %param.16) | copy-start | bytes 772
  18.0 13.0 %copy-start.7 = (bf16[1,1,32,128,128]{4,3,2,1,0:T(8,128)(2,1)S(1)}, bf16[1,1,32,128,128]{4,3,2,1,0:T(8,128)(2,1)}, u32[]{:S(2)}) copy-start(bf16[1,1,32,128,128]{4,3,2,1,0:T(8,128)(2,1)} %param.18) | copy-start | bytes 3145732
  18.0 13.0 %copy-start.15 = (s32[1,1,32]{2,1,0:T(1,128)S(1)}, s32[1,1,32]{2,1,0:T(1,128)}, u32[]{:S(2)}) copy-start(s32[1,1,32]{2,1,0:T(1,128)} %param.21) | copy-start | bytes 388
  18.1 19.0 %collective-permute-start.2 = (bf16[768,256]{1,0:T(8,128)(2,1)S(1)}, bf16[768,256]{1,0:T(8,128)(2,1)S(1)}, u32[]{:S(2)}, u32[]{:S(2)}) collective-permute-start(bf16[768,256]{1,0:T(8,128)(2,1)S(1)} %pair.1), channel_id=1, source_target_pairs={{0,7},{1,0},{2,1},{3,2},{4,3},{5,4},{6,5},{7,6},{8,15},{9,8},{10,9... | collective-permute-start | bytes 1179656 | tf_op jit(solution)/shard_map/ppermute | solution.py:299
  28.9 13.6 %collective-permute-start.1 = (bf16[768,256]{1,0:T(8,128)(2,1)S(1)}, bf16[768,256]{1,0:T(8,128)(2,1)S(1)}, u32[]{:S(2)}, u32[]{:S(2)}) collective-permute-start(bf16[768,256]{1,0:T(8,128)(2,1)S(1)} %pair.1), channel_id=1, source_target_pairs={{0,1},{1,2},{2,3},{3,4},{4,5},{5,6},{6,7},{7,0},{8,9},{9,10},{10,1... | collective-permute-start | bytes 1179656 | tf_op jit(solution)/shard_map/ppermute | solution.py:299
  31.0 2.8 %copy-start.6 = (bf16[1,1,16,4,128,128]{5,4,3,2,1,0:T(8,128)(2,1)S(1)}, bf16[1,1,16,4,128,128]{5,4,3,2,1,0:T(8,128)(2,1)}, u32[]{:S(2)}) copy-start(bf16[1,1,16,4,128,128]{5,4,3,2,1,0:T(8,128)(2,1)} %param.15) | copy-start | bytes 6291460
  31.1 2.8 %copy-start.16 = (s32[1,1,16]{2,1,0:T(1,128)S(1)}, s32[1,1,16]{2,1,0:T(1,128)}, u32[]{:S(2)}) copy-start(s32[1,1,16]{2,1,0:T(1,128)} %param.17) | copy-start | bytes 196
  35.7 9.8 %copy-start.8 = (bf16[384,768]{1,0:T(8,128)(2,1)}, bf16[384,768]{1,0:T(8,128)(2,1)S(1)}, u32[]{:S(2)}) copy-start(bf16[384,768]{1,0:T(8,128)(2,1)S(1)} %get-tuple-element.18.mat_ref) | copy-start | bytes 1769476
  35.7 21.5 %copy-start.2 = (bf16[384,768]{1,0:T(8,128)(2,1)}, bf16[384,768]{1,0:T(8,128)(2,1)S(1)}, u32[]{:S(2)}) copy-start(bf16[384,768]{1,0:T(8,128)(2,1)S(1)} %get-tuple-element.22.mat_ref) | copy-start | bytes 1769476
  35.7 21.9 %copy-start = (bf16[384,768]{1,0:T(8,128)(2,1)}, bf16[384,768]{1,0:T(8,128)(2,1)S(1)}, u32[]{:S(2)}) copy-start(bf16[384,768]{1,0:T(8,128)(2,1)S(1)} %get-tuple-element.21.mat_ref) | copy-start | bytes 1769476
  35.7 31.9 %copy-start.4 = (bf16[384,768]{1,0:T(8,128)(2,1)}, bf16[384,768]{1,0:T(8,128)(2,1)S(1)}, u32[]{:S(2)}) copy-start(bf16[384,768]{1,0:T(8,128)(2,1)S(1)} %get-tuple-element.23.mat_ref) | copy-start | bytes 1769476
  37.1 12.8 %collective-permute-start.4 = (bf16[768,256]{1,0:T(8,128)(2,1)S(1)}, bf16[768,256]{1,0:T(8,128)(2,1)S(1)}, u32[]{:S(2)}, u32[]{:S(2)}) collective-permute-start(bf16[768,256]{1,0:T(8,128)(2,1)S(1)} %collective-permute-done.2), channel_id=1, source_target_pairs={{0,7},{1,0},{2,1},{3,2},{4,3},{5,4},{6,5},{7,6},{8,15},{9,8},{10,9... | collective-permute-start | bytes 1179656 | tf_op jit(solution)/shard_map/ppermute | solution.py:299
  42.5 12.8 %collective-permute-start.3 = (bf16[768,256]{1,0:T(8,128)(2,1)S(1)}, bf16[768,256]{1,0:T(8,128)(2,1)S(1)}, u32[]{:S(2)}, u32[]{:S(2)}) collective-permute-start(bf16[768,256]{1,0:T(8,128)(2,1)S(1)} %collective-permute-done.1), channel_id=1, source_target_pairs={{0,1},{1,2},{2,3},{3,4},{4,5},{5,6},{6,7},{7,0},{8,9},{9,10},{10,1... | collective-permute-start | bytes 1179656 | tf_op jit(solution)/shard_map/ppermute | solution.py:299
  49.8 12.0 %collective-permute-start.6 = (bf16[768,256]{1,0:T(8,128)(2,1)S(1)}, bf16[768,256]{1,0:T(8,128)(2,1)S(1)}, u32[]{:S(2)}, u32[]{:S(2)}) collective-permute-start(bf16[768,256]{1,0:T(8,128)(2,1)S(1)} %collective-permute-done.4), channel_id=1, source_target_pairs={{0,7},{1,0},{2,1},{3,2},{4,3},{5,4},{6,5},{7,6},{8,15},{9,8},{10,9... | collective-permute-start | bytes 1179656 | tf_op jit(solution)/shard_map/ppermute | solution.py:299
  55.3 12.3 %collective-permute-start.5 = (bf16[768,256]{1,0:T(8,128)(2,1)S(1)}, bf16[768,256]{1,0:T(8,128)(2,1)S(1)}, u32[]{:S(2)}, u32[]{:S(2)}) collective-permute-start(bf16[768,256]{1,0:T(8,128)(2,1)S(1)} %collective-permute-done.3), channel_id=1, source_target_pairs={{0,1},{1,2},{2,3},{3,4},{4,5},{5,6},{6,7},{7,0},{8,9},{9,10},{10,1... | collective-permute-start | bytes 1179656 | tf_op jit(solution)/shard_map/ppermute | solution.py:299
  61.8 11.1 %collective-permute-start.7 = (bf16[768,256]{1,0:T(8,128)(2,1)S(1)}, bf16[768,256]{1,0:T(8,128)(2,1)S(1)}, u32[]{:S(2)}, u32[]{:S(2)}) collective-permute-start(bf16[768,256]{1,0:T(8,128)(2,1)S(1)} %collective-permute-done.6), channel_id=1, source_target_pairs={{0,7},{1,0},{2,1},{3,2},{4,3},{5,4},{6,5},{7,6},{8,15},{9,8},{10,9... | collective-permute-start | bytes 1179656 | tf_op jit(solution)/shard_map/ppermute | solution.py:299
  67.9 5.0 %copy-start.14 = (f32[256]{0:T(256)S(1)}, f32[256]{0:T(256)}, u32[]{:S(2)}) copy-start(f32[256]{0:T(256)} %param.13) | copy-start | bytes 3076
  67.9 5.0 %copy-start.11 = (bf16[384,256]{1,0:T(8,128)(2,1)S(1)}, bf16[384,256]{1,0:T(8,128)(2,1)}, u32[]{:S(2)}) copy-start(bf16[384,256]{1,0:T(8,128)(2,1)} %cotangent_ref.1) | copy-start | bytes 589828
  78.2 19.1 %collective-permute-start.11 = (bf16[256,768]{1,0:T(8,128)(2,1)}, bf16[256,768]{1,0:T(8,128)(2,1)}, u32[]{:S(2)}, u32[]{:S(2)}) collective-permute-start(bf16[256,768]{1,0:T(8,128)(2,1)} %get-tuple-element.29), channel_id=1, source_target_pairs={{0,7},{1,0},{2,1},{3,2},{4,3},{5,4},{6,5},{7,6},{8,15},{9,8},{10,9... | collective-permute-start | bytes 1179656 | tf_op jit(solution)/shard_map/ppermute | solution.py:299
  86.8 57.8 %all-to-all-start.1 = ((bf16[32,256,128]{2,1,0:T(8,128)(2,1)}), bf16[32,256,128]{2,1,0:T(8,128)(2,1)S(1)}, u32[]{:S(2)}, u32[]{:S(2)}) async-start(bf16[32,256,128]{2,1,0:T(8,128)(2,1)} %get-tuple-element.33), calls=%async_computation.1 | async-start | bytes 4194304 | tf_op jit(solution)/shard_map/all_to_all | solution.py:409
  95.2 17.5 %copy-start.1 = (bf16[384,768]{1,0:T(8,128)(2,1)S(1)}, bf16[384,768]{1,0:T(8,128)(2,1)}, u32[]{:S(2)}) copy-start(bf16[384,768]{1,0:T(8,128)(2,1)} %copy-done) | copy-start | bytes 1769476
  95.2 13.9 %collective-permute-start.8 = (bf16[256,768]{1,0:T(8,128)(2,1)}, bf16[256,768]{1,0:T(8,128)(2,1)S(1)}, u32[]{:S(2)}, u32[]{:S(2)}) collective-permute-start(bf16[256,768]{1,0:T(8,128)(2,1)} %get-tuple-element.28), channel_id=1, source_target_pairs={{0,1},{1,2},{2,3},{3,4},{4,5},{5,6},{6,7},{7,0},{8,9},{9,10},{10,1... | collective-permute-start | bytes 1179656 | tf_op jit(solution)/shard_map/ppermute | solution.py:299
  97.3 1.1 copy-start.5
  99.7 12.9 %collective-permute-start.12 = (bf16[256,768]{1,0:T(8,128)(2,1)S(1)}, bf16[256,768]{1,0:T(8,128)(2,1)S(1)}, u32[]{:S(2)}, u32[]{:S(2)}) collective-permute-start(bf16[256,768]{1,0:T(8,128)(2,1)S(1)} %hop.7), channel_id=1, source_target_pairs={{0,7},{1,0},{2,1},{3,2},{4,3},{5,4},{6,5},{7,6},{8,15},{9,8},{10,9... | collective-permute-start | bytes 1179656 | tf_op jit(solution)/shard_map/ppermute | solution.py:299
  109.1 1.1 copy-start.3
  110.5 26.2 %copy-start.9 = (bf16[384,768]{1,0:T(8,128)(2,1)S(1)}, bf16[384,768]{1,0:T(8,128)(2,1)}, u32[]{:S(2)}) copy-start(bf16[384,768]{1,0:T(8,128)(2,1)} %copy-done.8) | copy-start | bytes 1769476
  110.6 12.8 %collective-permute-start.9 = (bf16[256,768]{1,0:T(8,128)(2,1)S(1)}, bf16[256,768]{1,0:T(8,128)(2,1)S(1)}, u32[]{:S(2)}, u32[]{:S(2)}) collective-permute-start(bf16[256,768]{1,0:T(8,128)(2,1)S(1)} %hop.5), channel_id=1, source_target_pairs={{0,1},{1,2},{2,3},{3,4},{4,5},{5,6},{6,7},{7,0},{8,9},{9,10},{10,1... | collective-permute-start | bytes 1179656 | tf_op jit(solution)/shard_map/ppermute | solution.py:299
  113.0 12.6 %collective-permute-start.13 = (bf16[256,768]{1,0:T(8,128)(2,1)S(1)}, bf16[256,768]{1,0:T(8,128)(2,1)S(1)}, u32[]{:S(2)}, u32[]{:S(2)}) collective-permute-start(bf16[256,768]{1,0:T(8,128)(2,1)S(1)} %hop.8), channel_id=1, source_target_pairs={{0,7},{1,0},{2,1},{3,2},{4,3},{5,4},{6,5},{7,6},{8,15},{9,8},{10,9... | collective-permute-start | bytes 1179656 | tf_op jit(solution)/shard_map/ppermute | solution.py:299
  123.7 11.7 %collective-permute-start.10 = (bf16[256,768]{1,0:T(8,128)(2,1)S(1)}, bf16[256,768]{1,0:T(8,128)(2,1)S(1)}, u32[]{:S(2)}, u32[]{:S(2)}) collective-permute-start(bf16[256,768]{1,0:T(8,128)(2,1)S(1)} %hop.6), channel_id=1, source_target_pairs={{0,1},{1,2},{2,3},{3,4},{4,5},{5,6},{6,7},{7,0},{8,9},{9,10},{10,1... | collective-permute-start | bytes 1179656 | tf_op jit(solution)/shard_map/ppermute | solution.py:299
  126.0 18.5 %copy-start.12 = (s32[1,1,32]{2,1,0:T(1,128)S(1)}, s32[1,1,32]{2,1,0:T(1,128)}, u32[]{:S(2)}) copy-start(s32[1,1,32]{2,1,0:T(1,128)} %param.19) | copy-start | bytes 388
  126.0 18.5 %copy-start.13 = (s32[1,1,32]{2,1,0:T(1,128)S(1)}, s32[1,1,32]{2,1,0:T(1,128)}, u32[]{:S(2)}) copy-start(s32[1,1,32]{2,1,0:T(1,128)} %param.20) | copy-start | bytes 388
  126.1 10.7 %collective-permute-start.14 = (bf16[256,768]{1,0:T(8,128)(2,1)S(1)}, bf16[256,768]{1,0:T(8,128)(2,1)S(1)}, u32[]{:S(2)}, u32[]{:S(2)}) collective-permute-start(bf16[256,768]{1,0:T(8,128)(2,1)S(1)} %hop.9), channel_id=1, source_target_pairs={{0,7},{1,0},{2,1},{3,2},{4,3},{5,4},{6,5},{7,6},{8,15},{9,8},{10,9... | collective-permute-start | bytes 1179656 | tf_op jit(solution)/shard_map/ppermute | solution.py:299
  137.2 12.0 %copy-start.10 = (bf16[256,256]{1,0:T(8,128)(2,1)S(1)}, bf16[256,256]{1,0:T(8,128)(2,1)}, u32[]{:S(2)}) copy-start(bf16[256,256]{1,0:T(8,128)(2,1)} %weight_ref.1) | copy-start | bytes 393220
  137.2 8.8 %collective-permute-start.15 = (bf16[128,384]{1,0:T(8,128)(2,1)S(1)}, bf16[128,384]{1,0:T(8,128)(2,1)S(1)}, u32[]{:S(2)}, u32[]{:S(2)}) collective-permute-start(bf16[128,384]{1,0:T(8,128)(2,1)S(1)} %get-tuple-element.31), channel_id=1, source_target_pairs={{0,8},{1,9},{2,10},{3,11},{4,12},{5,13},{6,14},{7,15},{8,0},{9,1},... | collective-permute-start | bytes 294920 | tf_op jit(solution)/shard_map/ppermute | solution.py:302
  140.9 8.2 %collective-permute-start.16 = (bf16[128,384]{1,0:T(8,128)(2,1)S(1)}, bf16[128,384]{1,0:T(8,128)(2,1)S(1)}, u32[]{:S(2)}, u32[]{:S(2)}) collective-permute-start(bf16[128,384]{1,0:T(8,128)(2,1)S(1)} %get-tuple-element.32), channel_id=1, source_target_pairs={{0,8},{1,9},{2,10},{3,11},{4,12},{5,13},{6,14},{7,15},{8,0},{9,1},... | collective-permute-start | bytes 294920 | tf_op jit(solution)/shard_map/ppermute | solution.py:302
